TPU v7x, 32 devices: a whole 2x2x4 slice. The times are simulated.
32 devices in a mesh: group: 4 (over y, x), sub: 8 (over z, core).
Axes of the slice: x: 2, y: 2, z: 4, core: 2. Of those that a mesh axis runs over, the one named last changes fastest.
Arguments:
- load_cases: bfloat16 [4, 8, 1536, 256], P('group', 'sub'), may hold values from -6 to 6
- inv_schur: bfloat16 [4, 8, 1536, 1536], P('group', 'sub'), may hold values from -0.15625 to 0.15625
- schur_blocks: bfloat16 [4, 8, 1536, 1536], P('group', 'sub'), may hold values from -0.15625 to 0.15625
- coarse_basis: float32 [4, 8, 1536], P('group', 'sub'), may hold values from -0.53033006 to 0.53033006
- coarse_map: int32 [4, 8, 12], P('group', 'sub'), may hold values from 0 to 1023
- multiplicity: int32 [4, 8, 12], P('group', 'sub'), may hold values from 2 to 4
- recv_code: int32 [4, 8, 12], P('group', 'sub'), may hold values from 0 to 23, as said below
- send_blocks: int32 [4, 8, 24], P('group', 'sub'), may hold values from -1 to 11, as said below
- coarse_inv: float32 [4, 1024, 1024], P('group', 'sub'), may hold values from -0.1875 to 0.1875
Outputs:
- multipliers: float32 [4, 8, 1536, 256], P('group', 'sub')
Inputs may be any that keep to these rules, and one draw needn't show every extreme that they name: `recv_code`: within one subdomain the blocks read distinct codes; in every subdomain all 4 slots of one direction are read. `send_blocks`: entry d * 4 + j is the block a subdomain sends as slot j of direction d, to the subdomain that reads direction d from it; it is -1 exactly where that subdomain reads nothing from the slot.
All inputs are finite; a program needn't handle non-finite values.
Results may differ from a plain program's by a relative error of at most 0.0085.
Values may be sent and summed in bfloat16 or wider, within the bound.
No kernel may reach another device: no remote copies, remote signals or barrier semaphores. Data moves between devices by JAX's collectives and lax.ppermute only.
A program may use at most 64 MiB of HBM per device.

v0:
```python
import jax
import jax.numpy as jnp
from jax import lax
from jax.sharding import PartitionSpec as P

BLK = 128
DIRS = 6
CAP = 4
ITERS = 2


OFFSETS = (1, -1, 2, -2, 1, -1)
HIGHEST = lax.Precision.HIGHEST


def passed_along(block, axis, distance):
    devices = range(lax.axis_size(axis))
    route = [((i - distance) % len(devices), i) for i in devices]
    return lax.ppermute(block, axis, route)


def jump(values, read_codes, outgoing):
    block_count, block_size, case_count = values.shape
    picked = jnp.take(values, jnp.maximum(outgoing, 0), axis=0)
    picked = jnp.where((outgoing >= 0)[:, None, None], picked, jnp.zeros((), jnp.bfloat16))
    send_slabs = picked.reshape(DIRS, CAP, block_size, case_count)
    arrived = []
    for direction in range(4):
        arrived.append(passed_along(send_slabs[direction], "sub", OFFSETS[direction]))
    for direction in (4, 5):
        arrived.append(passed_along(send_slabs[direction], "group", OFFSETS[direction]))
    received = jnp.stack(arrived).reshape(DIRS * CAP, block_size, case_count)
    remote = jnp.take(received, read_codes, axis=0)
    return values.astype(jnp.float32) - remote.astype(jnp.float32)


def on_device(
    load_cases,
    inv_schur,
    schur_blocks,
    coarse_basis,
    coarse_map,
    multiplicity,
    recv_code,
    send_blocks,
    coarse_inv,
):
    dof_count = inv_schur.shape[2]
    case_count = load_cases.shape[3]
    block_count = dof_count // BLK
    solve_matrix = inv_schur[0, 0]
    dirichlet_matrix = schur_blocks[0, 0]
    basis_rows = coarse_basis[0, 0].reshape(block_count, BLK)
    read_codes = recv_code[0, 0]
    outgoing = send_blocks[0, 0]
    weights = (1.0 / multiplicity[0, 0].astype(jnp.float32))[:, None, None]
    own_rows = coarse_inv[0]
    own_map = coarse_map[0, 0]
    every_map = lax.all_gather(own_map, "sub", axis=0, tiled=True)
    wanted_columns = jnp.take(own_rows, every_map, axis=1)
    my_columns = lax.all_to_all(
        wanted_columns.astype(jnp.bfloat16), "sub", split_axis=1, concat_axis=0, tiled=True
    ).astype(wanted_columns.dtype)
    column_rows = jnp.take(my_columns, every_map, axis=0)
    multipliers = jnp.zeros((dof_count, case_count), jnp.float32)
    for iteration in range(ITERS):
        residual_load = (load_cases[0, 0].astype(jnp.float32) - multipliers).astype(jnp.bfloat16)
        displacement = jnp.dot(
            solve_matrix, residual_load, preferred_element_type=jnp.float32
        ).reshape(block_count, BLK, case_count)
        projected = jnp.sum(basis_rows[:, :, None] * displacement, axis=1)
        every_projected = lax.all_gather(projected, "sub", axis=0, tiled=True)
        coarse_here = jnp.einsum("nb,nc->bc", column_rows, every_projected, precision=HIGHEST)
        corrected = (displacement + basis_rows[:, :, None] * coarse_here[:, None, :]).astype(
            jnp.bfloat16
        )
        scaled = (jump(corrected, read_codes, outgoing) * weights).astype(jnp.bfloat16)
        dirichlet = jnp.dot(
            dirichlet_matrix,
            scaled.reshape(dof_count, case_count),
            preferred_element_type=jnp.float32,
        ).reshape(block_count, BLK, case_count)
        dual_step = (dirichlet * weights).astype(jnp.bfloat16)
        multipliers = multipliers + jump(dual_step, read_codes, outgoing).reshape(
            dof_count, case_count
        )
    return multipliers[None, None]


def solution(mesh):
    placed = (
        P("group", "sub", None, None),
        P("group", "sub", None, None),
        P("group", "sub", None, None),
        P("group", "sub", None),
        P("group", "sub", None),
        P("group", "sub", None),
        P("group", "sub", None),
        P("group", "sub", None),
        P("group", "sub", None),
    )
    return jax.shard_map(
        on_device,
        mesh=mesh,
        in_specs=placed,
        out_specs=P("group", "sub", None, None),
        check_vma=False,
    )
```

profile of v0, /device:TPU:0, one launch (start us, length us, event | category | flops | bytes accessed | tf_op | source)
XLA Modules:
  0.0 205.5 jit_solution(13215983132533416774)
XLA Ops:
  2.7 10.6 %all-reduce = s32[96]{0:T(128)S(1)} all-reduce(s32[96]{0:T(128)S(1)} %bitcast_dynamic-update-slice_fusion.24), channel_id=2, replica_groups=mesh['group'=4,'sub'=8] {'sub'}, use_global_device_ids=true, to_apply=%add | all-reduce | flops 96 | bytes 768 | tf_op jit(solution)/shard_map/all_gather | solution.py:59
  16.0 3.3 %all-to-all-start = ((bf16[128,8,12]{0,2,1:T(8,128)(2,1)}), bf16[128,8,12]{0,2,1:T(8,128)(2,1)S(1)}, u32[]{:S(2)}, u32[]{:S(2)}) async-start(bf16[128,8,12]{0,2,1:T(8,128)(2,1)} %select_convert_fusion), calls=%async_computation | async-start | bytes 65536 | tf_op jit(solution)/shard_map/all_to_all | solution.py:61
  22.7 4.0 %multiply_reduce_fusion.1 = (f32[12,256]{1,0:T(8,128)S(1)}, f32[12,128,256]{2,1,0:T(8,128)S(1)}) fusion(f32[12,128]{1,0:T(8,128)S(1)} %bitcast.135, bf16[12,128,1536]{2,1,0:T(8,128)(2,1)} %bitcast.144, bf16[1,1,1536,256]{3,2,1,0:T(8,128)(2,1)} %param.13), kind=kOutput, calls=%fused_computation.34 | convolution fusion | flops 1208742912 | bytes 7096320 | tf_op jit(solution)/shard_map/dot_general | solution.py:68
  26.7 14.5 %all-gather.1 = f32[8,12,256]{2,1,0:T(8,128)S(1)} all-gather(f32[1,12,256]{2,1,0:T(8,128)S(1)} %bitcast.143), channel_id=1, replica_groups=mesh['group'=4,'sub'=8] {'sub'}, dimensions={0}, use_global_device_ids=true | all-gather | bytes 110592 | tf_op jit(solution)/shard_map/all_gather | solution.py:72
  46.9 3.2 %collective-permute-start.1 = (bf16[4,128,256]{2,1,0:T(8,128)(2,1)S(1)}, bf16[4,128,256]{2,1,0:T(8,128)(2,1)S(1)}, u32[]{:S(2)}, u32[]{:S(2)}) collective-permute-start(bf16[4,128,256]{2,1,0:T(8,128)(2,1)S(1)} %get-tuple-element.31), channel_id=1, source_target_pairs={{1,0},{2,1},{3,2},{4,3},{5,4},{6,5},{7,6},{0,7},{9,8},{10,9},{11,1... | collective-permute-start | bytes 786440 | tf_op jit(solution)/shard_map/ppermute | solution.py:19
  50.0 2.4 %collective-permute-start.5 = (bf16[4,128,256]{2,1,0:T(8,128)(2,1)S(1)}, bf16[4,128,256]{2,1,0:T(8,128)(2,1)S(1)}, u32[]{:S(2)}, u32[]{:S(2)}) collective-permute-start(bf16[4,128,256]{2,1,0:T(8,128)(2,1)S(1)} %get-tuple-element.27), channel_id=1, source_target_pairs={{8,0},{16,8},{24,16},{0,24},{9,1},{17,9},{25,17},{1,25},{10,2},{18... | collective-permute-start | bytes 786440 | tf_op jit(solution)/shard_map/ppermute | solution.py:19
  55.1 13.0 %collective-permute-done.2 = bf16[4,128,256]{2,1,0:T(8,128)(2,1)S(1)} collective-permute-done((bf16[4,128,256]{2,1,0:T(8,128)(2,1)S(1)}, bf16[4,128,256]{2,1,0:T(8,128)(2,1)S(1)}, u32[]{:S(2)}, u32[]{:S(2)}) %collective-permute-start.2) | collective-permute-done | bytes 262176 | tf_op jit(solution)/shard_map/ppermute | solution.py:19
  69.3 2.0 gather_fusion.3
  71.8 3.8 %fusion.6 = f32[1536,256]{0,1:T(8,128)S(1)} fusion(bf16[1536,256]{1,0:T(8,128)(2,1)S(1)} %bitcast.131, bf16[1,1,1536,1536]{3,2,1,0:T(8,128)(2,1)} %param.15), kind=kOutput, calls=%fused_computation.16 | convolution fusion | flops 1207959552 | bytes 7077888 | tf_op jit(solution)/shard_map/dot_general | solution.py:78
  80.0 3.5 %collective-permute-start.7 = (bf16[4,128,256]{2,1,0:T(8,128)(2,1)S(1)}, bf16[4,128,256]{2,1,0:T(8,128)(2,1)S(1)}, u32[]{:S(2)}, u32[]{:S(2)}) collective-permute-start(bf16[4,128,256]{2,1,0:T(8,128)(2,1)S(1)} %get-tuple-element.25), channel_id=1, source_target_pairs={{1,0},{2,1},{3,2},{4,3},{5,4},{6,5},{7,6},{0,7},{9,8},{10,9},{11,1... | collective-permute-start | bytes 786440 | tf_op jit(solution)/shard_map/ppermute | solution.py:19
  83.5 2.4 %collective-permute-start.11 = (bf16[4,128,256]{2,1,0:T(8,128)(2,1)S(1)}, bf16[4,128,256]{2,1,0:T(8,128)(2,1)S(1)}, u32[]{:S(2)}, u32[]{:S(2)}) collective-permute-start(bf16[4,128,256]{2,1,0:T(8,128)(2,1)S(1)} %get-tuple-element.21), channel_id=1, source_target_pairs={{8,0},{16,8},{24,16},{0,24},{9,1},{17,9},{25,17},{1,25},{10,2},{18... | collective-permute-start | bytes 786440 | tf_op jit(solution)/shard_map/ppermute | solution.py:19
  85.9 4.4 %collective-permute-done.6 = bf16[4,128,256]{2,1,0:T(8,128)(2,1)S(1)} collective-permute-done((bf16[4,128,256]{2,1,0:T(8,128)(2,1)S(1)}, bf16[4,128,256]{2,1,0:T(8,128)(2,1)S(1)}, u32[]{:S(2)}, u32[]{:S(2)}) %collective-permute-start.6) | collective-permute-done | bytes 262176 | tf_op jit(solution)/shard_map/ppermute | solution.py:19
  90.4 11.0 %collective-permute-done.8 = bf16[4,128,256]{2,1,0:T(8,128)(2,1)S(1)} collective-permute-done((bf16[4,128,256]{2,1,0:T(8,128)(2,1)S(1)}, bf16[4,128,256]{2,1,0:T(8,128)(2,1)S(1)}, u32[]{:S(2)}, u32[]{:S(2)}) %collective-permute-start.8) | collective-permute-done | bytes 262176 | tf_op jit(solution)/shard_map/ppermute | solution.py:19
  102.7 2.0 gather_fusion.5
  105.6 4.9 %fusion.12 = f32[1536,256]{0,1:T(8,128)} fusion(bf16[1536,256]{1,0:T(8,128)(2,1)S(1)} %bitcast.132, bf16[1,1,1536,1536]{3,2,1,0:T(8,128)(2,1)} %param.14), kind=kOutput, calls=%fused_computation.18 | convolution fusion | flops 1207959552 | bytes 7077888 | tf_op jit(solution)/shard_map/dot_general | solution.py:68
  110.5 1.9 copy.23
  112.7 14.1 %all-gather.2 = f32[8,12,256]{2,1,0:T(8,128)S(1)} all-gather(f32[1,12,256]{2,1,0:T(8,128)S(1)} %bitcast.142), channel_id=1, replica_groups=mesh['group'=4,'sub'=8] {'sub'}, dimensions={0}, use_global_device_ids=true | all-gather | bytes 110592 | tf_op jit(solution)/shard_map/all_gather | solution.py:72
  128.4 3.0 %gather_fusion.6 = bf16[24,128,256]{2,1,0:T(8,128)(2,1)} fusion(bf16[12,128,256]{2,1,0:T(8,128)(2,1)} %add_convert_fusion, s32[1024]{0:T(1024)S(1)} %pad_clamp_fusion.1), kind=kCustom, calls=%fused_computation.3.clone | custom fusion | bytes 3145824 | tf_op jit(solution)/shard_map/jit(_take)/gather | solution.py:24
  133.6 3.2 %collective-permute-start.13 = (bf16[4,128,256]{2,1,0:T(8,128)(2,1)S(1)}, bf16[4,128,256]{2,1,0:T(8,128)(2,1)S(1)}, u32[]{:S(2)}, u32[]{:S(2)}) collective-permute-start(bf16[4,128,256]{2,1,0:T(8,128)(2,1)S(1)} %get-tuple-element.19), channel_id=1, source_target_pairs={{1,0},{2,1},{3,2},{4,3},{5,4},{6,5},{7,6},{0,7},{9,8},{10,9},{11,1... | collective-permute-start | bytes 786440 | tf_op jit(solution)/shard_map/ppermute | solution.py:19
  136.8 2.5 %collective-permute-start.17 = (bf16[4,128,256]{2,1,0:T(8,128)(2,1)S(1)}, bf16[4,128,256]{2,1,0:T(8,128)(2,1)S(1)}, u32[]{:S(2)}, u32[]{:S(2)}) collective-permute-start(bf16[4,128,256]{2,1,0:T(8,128)(2,1)S(1)} %get-tuple-element.15), channel_id=1, source_target_pairs={{8,0},{16,8},{24,16},{0,24},{9,1},{17,9},{25,17},{1,25},{10,2},{18... | collective-permute-start | bytes 786440 | tf_op jit(solution)/shard_map/ppermute | solution.py:19
  139.2 4.4 %collective-permute-done.12 = bf16[4,128,256]{2,1,0:T(8,128)(2,1)S(1)} collective-permute-done((bf16[4,128,256]{2,1,0:T(8,128)(2,1)S(1)}, bf16[4,128,256]{2,1,0:T(8,128)(2,1)S(1)}, u32[]{:S(2)}, u32[]{:S(2)}) %collective-permute-start.12) | collective-permute-done | bytes 262176 | tf_op jit(solution)/shard_map/ppermute | solution.py:19
  145.1 9.8 %collective-permute-done.14 = bf16[4,128,256]{2,1,0:T(8,128)(2,1)S(1)} collective-permute-done((bf16[4,128,256]{2,1,0:T(8,128)(2,1)S(1)}, bf16[4,128,256]{2,1,0:T(8,128)(2,1)S(1)}, u32[]{:S(2)}, u32[]{:S(2)}) %collective-permute-start.14) | collective-permute-done | bytes 262176 | tf_op jit(solution)/shard_map/ppermute | solution.py:19
  157.8 3.0 %gather_fusion.7 = bf16[12,128,256]{2,1,0:T(8,128)(2,1)} fusion(bf16[24,128,256]{2,1,0:T(8,128)(2,1)} %bitcast.44, s32[1024]{0:T(1024)S(1)} %pad_clamp_fusion), kind=kCustom, calls=%fused_computation.6.clone | custom fusion | bytes 1572912 | tf_op jit(solution)/shard_map/jit(_take)/gather | solution.py:33
  162.3 4.9 %fusion.9 = f32[1536,256]{0,1:T(8,128)} fusion(bf16[1536,256]{1,0:T(8,128)(2,1)S(1)} %bitcast.130, bf16[1,1,1536,1536]{3,2,1,0:T(8,128)(2,1)} %param.15), kind=kOutput, calls=%fused_computation.17 | convolution fusion | flops 1207959552 | bytes 7077888 | tf_op jit(solution)/shard_map/dot_general | solution.py:78
  167.2 1.9 copy.24
  170.2 3.0 %gather_fusion.8 = bf16[24,128,256]{2,1,0:T(8,128)(2,1)} fusion(bf16[12,128,256]{2,1,0:T(8,128)(2,1)} %multiply_convert_fusion, s32[1024]{0:T(1024)S(1)} %pad_clamp_fusion.1), kind=kCustom, calls=%fused_computation.4.clone | custom fusion | bytes 3145824 | tf_op jit(solution)/shard_map/jit(_take)/gather | solution.py:24
  175.2 3.4 %collective-permute-start.19 = (bf16[4,128,256]{2,1,0:T(8,128)(2,1)S(1)}, bf16[4,128,256]{2,1,0:T(8,128)(2,1)S(1)}, u32[]{:S(2)}, u32[]{:S(2)}) collective-permute-start(bf16[4,128,256]{2,1,0:T(8,128)(2,1)S(1)} %get-tuple-element.13), channel_id=1, source_target_pairs={{1,0},{2,1},{3,2},{4,3},{5,4},{6,5},{7,6},{0,7},{9,8},{10,9},{11,1... | collective-permute-start | bytes 786440 | tf_op jit(solution)/shard_map/ppermute | solution.py:19
  178.7 2.4 %collective-permute-start.23 = (bf16[4,128,256]{2,1,0:T(8,128)(2,1)S(1)}, bf16[4,128,256]{2,1,0:T(8,128)(2,1)S(1)}, u32[]{:S(2)}, u32[]{:S(2)}) collective-permute-start(bf16[4,128,256]{2,1,0:T(8,128)(2,1)S(1)} %get-tuple-element.9), channel_id=1, source_target_pairs={{8,0},{16,8},{24,16},{0,24},{9,1},{17,9},{25,17},{1,25},{10,2},{18... | collective-permute-start | bytes 786440 | tf_op jit(solution)/shard_map/ppermute | solution.py:19
  181.1 4.4 %collective-permute-done.18 = bf16[4,128,256]{2,1,0:T(8,128)(2,1)S(1)} collective-permute-done((bf16[4,128,256]{2,1,0:T(8,128)(2,1)S(1)}, bf16[4,128,256]{2,1,0:T(8,128)(2,1)S(1)}, u32[]{:S(2)}, u32[]{:S(2)}) %collective-permute-start.18) | collective-permute-done | bytes 262176 | tf_op jit(solution)/shard_map/ppermute | solution.py:19
  187.0 9.6 %collective-permute-done.20 = bf16[4,128,256]{2,1,0:T(8,128)(2,1)S(1)} collective-permute-done((bf16[4,128,256]{2,1,0:T(8,128)(2,1)S(1)}, bf16[4,128,256]{2,1,0:T(8,128)(2,1)S(1)}, u32[]{:S(2)}, u32[]{:S(2)}) %collective-permute-start.20) | collective-permute-done | bytes 262176 | tf_op jit(solution)/shard_map/ppermute | solution.py:19
  199.5 3.0 %gather_fusion.9 = bf16[12,128,256]{2,1,0:T(8,128)(2,1)} fusion(bf16[24,128,256]{2,1,0:T(8,128)(2,1)} %bitcast.54, s32[1024]{0:T(1024)S(1)} %pad_clamp_fusion), kind=kCustom, calls=%fused_computation.7.clone | custom fusion | bytes 1572912 | tf_op jit(solution)/shard_map/jit(_take)/gather | solution.py:33
  202.4 3.1 %subtract_add_fusion = f32[12,128,256]{2,1,0:T(8,128)} fusion(bf16[12,128,256]{2,1,0:T(8,128)(2,1)} %gather_fusion.9, pred[12]{0:T(512)(128)(4,1)S(1)} %compare_and_fusion, bf16[12,128,256]{2,1,0:T(8,128)(2,1)} %copy-done, f32[12,128,256]{2,1,0:T(8,128)S(1)} %bitcast.126, f32[12]{0:T(128)S(1)} %divide_bitcast_fusion, f32[12,128,256]{2,1,0:T(8,128)S(1)} %bitcast.124), kind=kLoop, calls=%fused_computation.25 | loop fusion | flops 5111808 | bytes 6291516 | tf_op jit(solution)/shard_map/add | solution.py:84
  (113 shorter events, 41.8 us)
Async XLA Ops:
  16.0 25.2 %all-to-all-start = ((bf16[128,8,12]{0,2,1:T(8,128)(2,1)}), bf16[128,8,12]{0,2,1:T(8,128)(2,1)S(1)}, u32[]{:S(2)}, u32[]{:S(2)}) async-start(bf16[128,8,12]{0,2,1:T(8,128)(2,1)} %select_convert_fusion), calls=%async_computation | async-start | bytes 65536 | tf_op jit(solution)/shard_map/all_to_all | solution.py:61
  46.2 0.7 copy-start.4
  46.3 8.7 %collective-permute-start = (bf16[4,128,256]{2,1,0:T(8,128)(2,1)S(1)}, bf16[4,128,256]{2,1,0:T(8,128)(2,1)S(1)}, u32[]{:S(2)}, u32[]{:S(2)}) collective-permute-start(bf16[4,128,256]{2,1,0:T(8,128)(2,1)S(1)} %get-tuple-element.32), channel_id=1, source_target_pairs={{7,0},{0,1},{1,2},{2,3},{3,4},{4,5},{5,6},{6,7},{15,8},{8,9},{9,10... | collective-permute-start | bytes 786440 | tf_op jit(solution)/shard_map/ppermute | solution.py:19
  46.9 8.2 %collective-permute-start.1 = (bf16[4,128,256]{2,1,0:T(8,128)(2,1)S(1)}, bf16[4,128,256]{2,1,0:T(8,128)(2,1)S(1)}, u32[]{:S(2)}, u32[]{:S(2)}) collective-permute-start(bf16[4,128,256]{2,1,0:T(8,128)(2,1)S(1)} %get-tuple-element.31), channel_id=1, source_target_pairs={{1,0},{2,1},{3,2},{4,3},{5,4},{6,5},{7,6},{0,7},{9,8},{10,9},{11,1... | collective-permute-start | bytes 786440 | tf_op jit(solution)/shard_map/ppermute | solution.py:19
  50.0 18.1 %collective-permute-start.5 = (bf16[4,128,256]{2,1,0:T(8,128)(2,1)S(1)}, bf16[4,128,256]{2,1,0:T(8,128)(2,1)S(1)}, u32[]{:S(2)}, u32[]{:S(2)}) collective-permute-start(bf16[4,128,256]{2,1,0:T(8,128)(2,1)S(1)} %get-tuple-element.27), channel_id=1, source_target_pairs={{8,0},{16,8},{24,16},{0,24},{9,1},{17,9},{25,17},{1,25},{10,2},{18... | collective-permute-start | bytes 786440 | tf_op jit(solution)/shard_map/ppermute | solution.py:19
  52.5 15.6 %collective-permute-start.4 = (bf16[4,128,256]{2,1,0:T(8,128)(2,1)S(1)}, bf16[4,128,256]{2,1,0:T(8,128)(2,1)S(1)}, u32[]{:S(2)}, u32[]{:S(2)}) collective-permute-start(bf16[4,128,256]{2,1,0:T(8,128)(2,1)S(1)} %get-tuple-element.28), channel_id=1, source_target_pairs={{24,0},{0,8},{8,16},{16,24},{25,1},{1,9},{9,17},{17,25},{26,2},{2,... | collective-permute-start | bytes 786440 | tf_op jit(solution)/shard_map/ppermute | solution.py:19
  52.5 15.6 %collective-permute-start.3 = (bf16[4,128,256]{2,1,0:T(8,128)(2,1)S(1)}, bf16[4,128,256]{2,1,0:T(8,128)(2,1)S(1)}, u32[]{:S(2)}, u32[]{:S(2)}) collective-permute-start(bf16[4,128,256]{2,1,0:T(8,128)(2,1)S(1)} %get-tuple-element.29), channel_id=1, source_target_pairs={{2,0},{3,1},{4,2},{5,3},{6,4},{7,5},{0,6},{1,7},{10,8},{11,9},{12,... | collective-permute-start | bytes 786440 | tf_op jit(solution)/shard_map/ppermute | solution.py:19
  55.0 13.0 %collective-permute-start.2 = (bf16[4,128,256]{2,1,0:T(8,128)(2,1)S(1)}, bf16[4,128,256]{2,1,0:T(8,128)(2,1)S(1)}, u32[]{:S(2)}, u32[]{:S(2)}) collective-permute-start(bf16[4,128,256]{2,1,0:T(8,128)(2,1)S(1)} %get-tuple-element.30), channel_id=1, source_target_pairs={{6,0},{7,1},{0,2},{1,3},{2,4},{3,5},{4,6},{5,7},{14,8},{15,9},{8,1... | collective-permute-start | bytes 786440 | tf_op jit(solution)/shard_map/ppermute | solution.py:19
  68.2 1.1 copy-start.2
  79.9 10.5 %collective-permute-start.6 = (bf16[4,128,256]{2,1,0:T(8,128)(2,1)S(1)}, bf16[4,128,256]{2,1,0:T(8,128)(2,1)S(1)}, u32[]{:S(2)}, u32[]{:S(2)}) collective-permute-start(bf16[4,128,256]{2,1,0:T(8,128)(2,1)S(1)} %get-tuple-element.26), channel_id=1, source_target_pairs={{7,0},{0,1},{1,2},{2,3},{3,4},{4,5},{5,6},{6,7},{15,8},{8,9},{9,10... | collective-permute-start | bytes 786440 | tf_op jit(solution)/shard_map/ppermute | solution.py:19
  80.0 10.4 %collective-permute-start.7 = (bf16[4,128,256]{2,1,0:T(8,128)(2,1)S(1)}, bf16[4,128,256]{2,1,0:T(8,128)(2,1)S(1)}, u32[]{:S(2)}, u32[]{:S(2)}) collective-permute-start(bf16[4,128,256]{2,1,0:T(8,128)(2,1)S(1)} %get-tuple-element.25), channel_id=1, source_target_pairs={{1,0},{2,1},{3,2},{4,3},{5,4},{6,5},{7,6},{0,7},{9,8},{10,9},{11,1... | collective-permute-start | bytes 786440 | tf_op jit(solution)/shard_map/ppermute | solution.py:19
  83.5 18.0 %collective-permute-start.11 = (bf16[4,128,256]{2,1,0:T(8,128)(2,1)S(1)}, bf16[4,128,256]{2,1,0:T(8,128)(2,1)S(1)}, u32[]{:S(2)}, u32[]{:S(2)}) collective-permute-start(bf16[4,128,256]{2,1,0:T(8,128)(2,1)S(1)} %get-tuple-element.21), channel_id=1, source_target_pairs={{8,0},{16,8},{24,16},{0,24},{9,1},{17,9},{25,17},{1,25},{10,2},{18... | collective-permute-start | bytes 786440 | tf_op jit(solution)/shard_map/ppermute | solution.py:19
  85.9 15.5 %collective-permute-start.10 = (bf16[4,128,256]{2,1,0:T(8,128)(2,1)S(1)}, bf16[4,128,256]{2,1,0:T(8,128)(2,1)S(1)}, u32[]{:S(2)}, u32[]{:S(2)}) collective-permute-start(bf16[4,128,256]{2,1,0:T(8,128)(2,1)S(1)} %get-tuple-element.22), channel_id=1, source_target_pairs={{24,0},{0,8},{8,16},{16,24},{25,1},{1,9},{9,17},{17,25},{26,2},{2,... | collective-permute-start | bytes 786440 | tf_op jit(solution)/shard_map/ppermute | solution.py:19
  85.9 15.5 %collective-permute-start.9 = (bf16[4,128,256]{2,1,0:T(8,128)(2,1)S(1)}, bf16[4,128,256]{2,1,0:T(8,128)(2,1)S(1)}, u32[]{:S(2)}, u32[]{:S(2)}) collective-permute-start(bf16[4,128,256]{2,1,0:T(8,128)(2,1)S(1)} %get-tuple-element.23), channel_id=1, source_target_pairs={{2,0},{3,1},{4,2},{5,3},{6,4},{7,5},{0,6},{1,7},{10,8},{11,9},{12,... | collective-permute-start | bytes 786440 | tf_op jit(solution)/shard_map/ppermute | solution.py:19
  90.4 11.0 %collective-permute-start.8 = (bf16[4,128,256]{2,1,0:T(8,128)(2,1)S(1)}, bf16[4,128,256]{2,1,0:T(8,128)(2,1)S(1)}, u32[]{:S(2)}, u32[]{:S(2)}) collective-permute-start(bf16[4,128,256]{2,1,0:T(8,128)(2,1)S(1)} %get-tuple-element.24), channel_id=1, source_target_pairs={{6,0},{7,1},{0,2},{1,3},{2,4},{3,5},{4,6},{5,7},{14,8},{15,9},{8,1... | collective-permute-start | bytes 786440 | tf_op jit(solution)/shard_map/ppermute | solution.py:19
  101.4 3.3 %copy-start.1 = (bf16[1,1,1536,256]{3,2,1,0:T(8,128)(2,1)S(1)}, bf16[1,1,1536,256]{3,2,1,0:T(8,128)(2,1)}, u32[]{:S(2)}) copy-start(bf16[1,1,1536,256]{3,2,1,0:T(8,128)(2,1)} %param.13) | copy-start | bytes 2359300
  101.5 1.1 copy-start.3
  104.7 0.9 copy-start
  133.2 10.4 %collective-permute-start.12 = (bf16[4,128,256]{2,1,0:T(8,128)(2,1)S(1)}, bf16[4,128,256]{2,1,0:T(8,128)(2,1)S(1)}, u32[]{:S(2)}, u32[]{:S(2)}) collective-permute-start(bf16[4,128,256]{2,1,0:T(8,128)(2,1)S(1)} %get-tuple-element.20), channel_id=1, source_target_pairs={{7,0},{0,1},{1,2},{2,3},{3,4},{4,5},{5,6},{6,7},{15,8},{8,9},{9,10... | collective-permute-start | bytes 786440 | tf_op jit(solution)/shard_map/ppermute | solution.py:19
  133.6 10.8 %collective-permute-start.13 = (bf16[4,128,256]{2,1,0:T(8,128)(2,1)S(1)}, bf16[4,128,256]{2,1,0:T(8,128)(2,1)S(1)}, u32[]{:S(2)}, u32[]{:S(2)}) collective-permute-start(bf16[4,128,256]{2,1,0:T(8,128)(2,1)S(1)} %get-tuple-element.19), channel_id=1, source_target_pairs={{1,0},{2,1},{3,2},{4,3},{5,4},{6,5},{7,6},{0,7},{9,8},{10,9},{11,1... | collective-permute-start | bytes 786440 | tf_op jit(solution)/shard_map/ppermute | solution.py:19
  136.8 20.3 %collective-permute-start.17 = (bf16[4,128,256]{2,1,0:T(8,128)(2,1)S(1)}, bf16[4,128,256]{2,1,0:T(8,128)(2,1)S(1)}, u32[]{:S(2)}, u32[]{:S(2)}) collective-permute-start(bf16[4,128,256]{2,1,0:T(8,128)(2,1)S(1)} %get-tuple-element.15), channel_id=1, source_target_pairs={{8,0},{16,8},{24,16},{0,24},{9,1},{17,9},{25,17},{1,25},{10,2},{18... | collective-permute-start | bytes 786440 | tf_op jit(solution)/shard_map/ppermute | solution.py:19
  139.2 17.1 %collective-permute-start.16 = (bf16[4,128,256]{2,1,0:T(8,128)(2,1)S(1)}, bf16[4,128,256]{2,1,0:T(8,128)(2,1)S(1)}, u32[]{:S(2)}, u32[]{:S(2)}) collective-permute-start(bf16[4,128,256]{2,1,0:T(8,128)(2,1)S(1)} %get-tuple-element.16), channel_id=1, source_target_pairs={{24,0},{0,8},{8,16},{16,24},{25,1},{1,9},{9,17},{17,25},{26,2},{2,... | collective-permute-start | bytes 786440 | tf_op jit(solution)/shard_map/ppermute | solution.py:19
  139.2 16.4 %collective-permute-start.15 = (bf16[4,128,256]{2,1,0:T(8,128)(2,1)S(1)}, bf16[4,128,256]{2,1,0:T(8,128)(2,1)S(1)}, u32[]{:S(2)}, u32[]{:S(2)}) collective-permute-start(bf16[4,128,256]{2,1,0:T(8,128)(2,1)S(1)} %get-tuple-element.17), channel_id=1, source_target_pairs={{2,0},{3,1},{4,2},{5,3},{6,4},{7,5},{0,6},{1,7},{10,8},{11,9},{12,... | collective-permute-start | bytes 786440 | tf_op jit(solution)/shard_map/ppermute | solution.py:19
  143.6 11.2 %collective-permute-start.14 = (bf16[4,128,256]{2,1,0:T(8,128)(2,1)S(1)}, bf16[4,128,256]{2,1,0:T(8,128)(2,1)S(1)}, u32[]{:S(2)}, u32[]{:S(2)}) collective-permute-start(bf16[4,128,256]{2,1,0:T(8,128)(2,1)S(1)} %get-tuple-element.18), channel_id=1, source_target_pairs={{6,0},{7,1},{0,2},{1,3},{2,4},{3,5},{4,6},{5,7},{14,8},{15,9},{8,1... | collective-permute-start | bytes 786440 | tf_op jit(solution)/shard_map/ppermute | solution.py:19
  175.1 10.5 %collective-permute-start.18 = (bf16[4,128,256]{2,1,0:T(8,128)(2,1)S(1)}, bf16[4,128,256]{2,1,0:T(8,128)(2,1)S(1)}, u32[]{:S(2)}, u32[]{:S(2)}) collective-permute-start(bf16[4,128,256]{2,1,0:T(8,128)(2,1)S(1)} %get-tuple-element.14), channel_id=1, source_target_pairs={{7,0},{0,1},{1,2},{2,3},{3,4},{4,5},{5,6},{6,7},{15,8},{8,9},{9,10... | collective-permute-start | bytes 786440 | tf_op jit(solution)/shard_map/ppermute | solution.py:19
  175.2 11.0 %collective-permute-start.19 = (bf16[4,128,256]{2,1,0:T(8,128)(2,1)S(1)}, bf16[4,128,256]{2,1,0:T(8,128)(2,1)S(1)}, u32[]{:S(2)}, u32[]{:S(2)}) collective-permute-start(bf16[4,128,256]{2,1,0:T(8,128)(2,1)S(1)} %get-tuple-element.13), channel_id=1, source_target_pairs={{1,0},{2,1},{3,2},{4,3},{5,4},{6,5},{7,6},{0,7},{9,8},{10,9},{11,1... | collective-permute-start | bytes 786440 | tf_op jit(solution)/shard_map/ppermute | solution.py:19
  178.7 20.1 %collective-permute-start.23 = (bf16[4,128,256]{2,1,0:T(8,128)(2,1)S(1)}, bf16[4,128,256]{2,1,0:T(8,128)(2,1)S(1)}, u32[]{:S(2)}, u32[]{:S(2)}) collective-permute-start(bf16[4,128,256]{2,1,0:T(8,128)(2,1)S(1)} %get-tuple-element.9), channel_id=1, source_target_pairs={{8,0},{16,8},{24,16},{0,24},{9,1},{17,9},{25,17},{1,25},{10,2},{18... | collective-permute-start | bytes 786440 | tf_op jit(solution)/shard_map/ppermute | solution.py:19
  181.1 16.9 %collective-permute-start.22 = (bf16[4,128,256]{2,1,0:T(8,128)(2,1)S(1)}, bf16[4,128,256]{2,1,0:T(8,128)(2,1)S(1)}, u32[]{:S(2)}, u32[]{:S(2)}) collective-permute-start(bf16[4,128,256]{2,1,0:T(8,128)(2,1)S(1)} %get-tuple-element.10), channel_id=1, source_target_pairs={{24,0},{0,8},{8,16},{16,24},{25,1},{1,9},{9,17},{17,25},{26,2},{2,... | collective-permute-start | bytes 786440 | tf_op jit(solution)/shard_map/ppermute | solution.py:19
  181.1 16.2 %collective-permute-start.21 = (bf16[4,128,256]{2,1,0:T(8,128)(2,1)S(1)}, bf16[4,128,256]{2,1,0:T(8,128)(2,1)S(1)}, u32[]{:S(2)}, u32[]{:S(2)}) collective-permute-start(bf16[4,128,256]{2,1,0:T(8,128)(2,1)S(1)} %get-tuple-element.11), channel_id=1, source_target_pairs={{2,0},{3,1},{4,2},{5,3},{6,4},{7,5},{0,6},{1,7},{10,8},{11,9},{12,... | collective-permute-start | bytes 786440 | tf_op jit(solution)/shard_map/ppermute | solution.py:19
  185.5 11.0 %collective-permute-start.20 = (bf16[4,128,256]{2,1,0:T(8,128)(2,1)S(1)}, bf16[4,128,256]{2,1,0:T(8,128)(2,1)S(1)}, u32[]{:S(2)}, u32[]{:S(2)}) collective-permute-start(bf16[4,128,256]{2,1,0:T(8,128)(2,1)S(1)} %get-tuple-element.12), channel_id=1, source_target_pairs={{6,0},{7,1},{0,2},{1,3},{2,4},{3,5},{4,6},{5,7},{14,8},{15,9},{8,1... | collective-permute-start | bytes 786440 | tf_op jit(solution)/shard_map/ppermute | solution.py:19
where the time goes:
time: 206 us; the launch traced here: 205 us
  waiting for transfers between devices  57.8 us (28%)
  local copies, waits for them, and re-layouts  40.8 us (20%)
  blocking collectives  39.3 us (19%)
  starting transfers between devices  28.8 us (14%)
  other arithmetic  19.6 us (10%)
  matrix products  18.1 us (9%)
    ppermute x24, waiting for transfers between devices, passed_along(): return lax.ppermute(block, axis, route)  57.8 us
    all_gather x2, blocking collectives, on_device(): every_projected = lax.all_gather(projected, 'sub', axis=0, tiled=True)  28.7 us
    ppermute x24, starting transfers between devices, passed_along(): return lax.ppermute(block, axis, route)  25.5 us
    unnamed x36, local copies, waits for them, and re-layouts  13.5 us
    all_gather x1, blocking collectives, on_device(): every_map = lax.all_gather(own_map, 'sub', axis=0, tiled=True)  10.6 us
    gather x4, local copies, waits for them, and re-layouts, jump(): remote = jnp.take(received, read_codes, axis=0)  9.92 us
    gather x4, local copies, waits for them, and re-layouts, jump(): picked = jnp.take(values, jnp.maximum(outgoing, 0), axis=0)  9.63 us
    dot_general x2, matrix products, on_device(): jnp.dot(solve_matrix, residual_load, preferred_element_type=jnp.float32)  8.87 us
  transfers between devices with their start and end apart: 25, of which 8 were waited for; matrix products, arithmetic and copies ran while one was open for 7% of the time, Pallas kernels for 0%

commit v1 on v0

v1 whole, which is shorter than its diff:
```python
import functools

import jax
import jax.numpy as jnp
from jax import lax
from jax.experimental import pallas as pl
from jax.experimental.pallas import tpu as pltpu
from jax.sharding import PartitionSpec as P

BLK = 128
DIRS = 6
CAP = 4
ITERS = 2
ROWS = 256
SHIFTS = (("sub", 1), ("sub", -1), ("sub", 2), ("sub", -2), ("group", 1), ("group", -1))
ORDER = (2, 0, 1, 3, 4, 5)
HIGHEST = lax.Precision.HIGHEST
VMEM = pl.BlockSpec(memory_space=pltpu.VMEM)
SMEM = pl.BlockSpec(memory_space=pltpu.SMEM)
ANY = pl.BlockSpec(memory_space=pl.ANY)
PARAMS = pltpu.CompilerParams(vmem_limit_bytes=40 * 1024 * 1024)


def passed_along(block, direction):
    axis, distance = SHIFTS[direction]
    count = lax.axis_size(axis)
    return lax.ppermute(block, axis, [((i - distance) % count, i) for i in range(count)])


def jump_slabs(slabs):
    arrived = {d: passed_along(slabs[d], d) for d in ORDER}
    return [arrived[d] for d in range(DIRS)]


def matrix_copies(matrix, held, sems):
    steps = held.shape[0] // ROWS
    return [
        pltpu.make_async_copy(
            matrix.at[pl.ds(i * ROWS, ROWS)], held.at[pl.ds(i * ROWS, ROWS)], sems.at[i]
        )
        for i in range(steps)
    ]


def slab_copies(slabs, received, sems):
    return [
        pltpu.make_async_copy(slab, received.at[pl.ds(d * CAP, CAP)], sems.at[d])
        for d, slab in enumerate(slabs)
    ]


def pick_blocks(send, values, slabs):
    for d in range(DIRS):
        for j in range(CAP):
            slabs[d][j] = values[send[d * CAP + j]]


def solve_tail(send, held, rhs, copies, basis, disp, proj, slabs, narrow):
    block_count, _, cases = disp.shape
    per = ROWS // BLK
    wide = cases // BLK
    for i, copy in enumerate(copies):
        copy.wait()
        part = jnp.dot(
            held[pl.ds(i * ROWS, ROWS), :], rhs[...], preferred_element_type=jnp.float32
        )
        for k in range(per):
            b = i * per + k
            mine = part[k * BLK : (k + 1) * BLK]
            disp[b] = mine
            narrow[b] = mine.astype(jnp.bfloat16)
            column = basis[b]
            for w in range(wide):
                proj[b, pl.ds(w * BLK, BLK)] = jnp.sum(
                    column * mine[:, w * BLK : (w + 1) * BLK], axis=0
                )
    pick_blocks(send, narrow, slabs)


def first_solve_kernel(send, matrix, load, basis, disp, proj, *rest):
    slabs, (held, narrow, sems) = rest[:DIRS], rest[DIRS:]
    copies = matrix_copies(matrix, held, sems)
    for copy in copies:
        copy.start()
    solve_tail(send, held, load, copies, basis, disp, proj, slabs, narrow)


def next_solve_kernel(send, read, matrix, load, basis, dual, *rest):
    arrived, (mult, disp, proj), rest = rest[:DIRS], rest[DIRS : DIRS + 3], rest[DIRS + 3 :]
    slabs, (held, narrow, received, rhs, sems, slab_sems) = rest[:DIRS], rest[DIRS:]
    incoming = slab_copies(arrived, received, slab_sems)
    copies = matrix_copies(matrix, held, sems)
    for copy in incoming + copies:
        copy.start()
    for copy in incoming:
        copy.wait()
    for b in range(disp.shape[0]):
        step = dual[b].astype(jnp.float32) - received[read[b]].astype(jnp.float32)
        mult[b] = step
        rows = pl.ds(b * BLK, BLK)
        rhs[rows, :] = (load[rows, :].astype(jnp.float32) - step).astype(jnp.bfloat16)
    solve_tail(send, held, rhs, copies, basis, disp, proj, slabs, narrow)


def dirichlet_kernel(
    send, read, weights, matrix, disp, basis, far_basis, coarse, near_rows, up_rows, down_rows, *rest
):
    arrived, dual, rest = rest[:DIRS], rest[DIRS], rest[DIRS + 1 :]
    slabs, (held, received, rows24, rhs, sems, slab_sems) = rest[:DIRS], rest[DIRS:]
    incoming = slab_copies(arrived, received, slab_sems)
    copies = matrix_copies(matrix, held, sems)
    for copy in incoming + copies:
        copy.start()
    near = near_rows.shape[0]
    for k in range(near):
        rows24[k] = near_rows[k : k + 1]
    for j in range(CAP):
        rows24[near + j] = up_rows[j : j + 1]
        rows24[near + CAP + j] = down_rows[j : j + 1]
    for copy in incoming:
        copy.wait()
    block_count, _, cases = disp.shape
    for b in range(block_count):
        code = read[b]
        for w in range(cases // BLK):
            cols = pl.ds(w * BLK, BLK)
            own = disp[b, :, cols] + basis[b] * coarse[pl.ds(b, 1), cols]
            far = received[code, :, cols].astype(jnp.float32) + far_basis[b] * rows24[
                code, :, cols
            ]
            gap = own.astype(jnp.bfloat16).astype(jnp.float32) - far.astype(jnp.bfloat16).astype(
                jnp.float32
            )
            rhs[pl.ds(b * BLK, BLK), cols] = (gap * weights[b]).astype(jnp.bfloat16)
    per = ROWS // BLK
    for i, copy in enumerate(copies):
        copy.wait()
        part = jnp.dot(
            held[pl.ds(i * ROWS, ROWS), :], rhs[...], preferred_element_type=jnp.float32
        )
        for k in range(per):
            b = i * per + k
            dual[b] = (part[k * BLK : (k + 1) * BLK] * weights[b]).astype(jnp.bfloat16)
    pick_blocks(send, dual, slabs)


def finish_kernel(read, mult, dual, *rest):
    arrived, out, received, slab_sems = rest[:DIRS], rest[DIRS], rest[DIRS + 1], rest[DIRS + 2]
    incoming = slab_copies(arrived, received, slab_sems)
    for copy in incoming:
        copy.start()
    for copy in incoming:
        copy.wait()
    for b in range(out.shape[0]):
        gap = dual[b].astype(jnp.float32) - received[read[b]].astype(jnp.float32)
        out[b] = mult[b] + gap


def coarse_kernel(send, table, every, coarse, near_rows, up_rows, down_rows, held):
    block_count = coarse.shape[0]
    near = near_rows.shape[0]
    rows = jnp.dot(
        table[...], every[...], preferred_element_type=jnp.float32, precision=HIGHEST
    )
    coarse[...] = rows[:block_count]
    near_rows[...] = rows[block_count : block_count + near]
    for b in range(block_count):
        held[b] = rows[b : b + 1]
    for j in range(CAP):
        up_rows[pl.ds(j, 1), :] = held[send[near + j]]
        down_rows[pl.ds(j, 1), :] = held[send[near + CAP + j]]


def f32(*shape):
    return jax.ShapeDtypeStruct(shape, jnp.float32)


def bf16(*shape):
    return jax.ShapeDtypeStruct(shape, jnp.bfloat16)


def to_everyone(mine):
    count = lax.axis_size("sub")
    return lax.all_to_all(
        jnp.broadcast_to(mine[None], (count,) + mine.shape), "sub", 0, 0, tiled=True
    )


def on_device(
    load_cases,
    inv_schur,
    schur_blocks,
    coarse_basis,
    coarse_map,
    multiplicity,
    recv_code,
    send_blocks,
    coarse_inv,
):
    dofs = inv_schur.shape[2]
    cases = load_cases.shape[3]
    blocks = dofs // BLK
    near = 4 * CAP
    slots = DIRS * CAP
    subs = lax.axis_size("sub")
    here = lax.axis_index("sub")
    solve_matrix = inv_schur[0, 0]
    dirichlet_matrix = schur_blocks[0, 0]
    load = load_cases[0, 0]
    basis = coarse_basis[0, 0].reshape(blocks, BLK)
    basis_columns = jnp.broadcast_to(basis[:, :, None], (blocks, BLK, BLK))
    read = recv_code[0, 0]
    send = jnp.maximum(send_blocks[0, 0], 0)
    weights = 1.0 / multiplicity[0, 0].astype(jnp.float32)
    steps = dofs // ROWS
    slab_shapes = [bf16(CAP, BLK, cases)] * DIRS
    held = pltpu.VMEM((dofs, dofs), jnp.bfloat16)
    values = pltpu.VMEM((blocks, BLK, cases), jnp.bfloat16)
    received = pltpu.VMEM((slots, BLK, cases), jnp.bfloat16)
    rhs = pltpu.VMEM((dofs, cases), jnp.bfloat16)
    sems = pltpu.SemaphoreType.DMA((steps,))
    slab_sems = pltpu.SemaphoreType.DMA((DIRS,))

    disp, proj, *slabs = pl.pallas_call(
        first_solve_kernel,
        out_shape=[f32(blocks, BLK, cases), f32(blocks, cases)] + slab_shapes,
        in_specs=[SMEM, ANY, VMEM, VMEM],
        out_specs=[VMEM] * (2 + DIRS),
        scratch_shapes=[held, values, sems],
        compiler_params=PARAMS,
    )(send, solve_matrix, load, basis_columns)

    width = -(-(blocks + slots) // BLK) * BLK
    names = jnp.concatenate([coarse_map[0, 0], send]).astype(jnp.float32)
    names = jnp.pad(names, (0, width - blocks - slots)).reshape(-1, BLK)
    told = to_everyone(jnp.concatenate([basis, names])).reshape(subs, -1, BLK)
    every_basis = told[:, :blocks]
    numbers = told[:, blocks:].reshape(subs, -1).astype(jnp.int32)
    every_map = numbers[:, :blocks]
    every_send = numbers[:, blocks : blocks + near]
    chosen = every_send[:, :, None] == jnp.arange(blocks, dtype=jnp.int32)
    slot_dofs = jnp.sum(jnp.where(chosen, every_map[:, None, :], 0), axis=2)

    def to_readers(array):
        parts = array.reshape((subs, 4, CAP) + array.shape[2:])
        moved = [jnp.roll(parts[:, d], SHIFTS[d][1], axis=0) for d in range(4)]
        return jnp.concatenate(moved, axis=1)

    wanted = jnp.concatenate([every_map, to_readers(slot_dofs)], axis=1).reshape(-1)
    orders = jnp.arange(coarse_inv.shape[2], dtype=jnp.int32)
    wanted_hot = (wanted[:, None] == orders).astype(jnp.bfloat16)
    columns = lax.dot_general(
        wanted_hot,
        coarse_inv[0].astype(jnp.bfloat16),
        (((1,), (1,)), ((), ())),
        preferred_element_type=jnp.float32,
    ).astype(jnp.bfloat16)
    columns = lax.all_to_all(columns, "sub", 0, 0, tiled=True)
    columns = columns.reshape(subs, blocks + near, -1).transpose(1, 0, 2).reshape(blocks + near, -1)
    every_hot = (every_map.reshape(-1)[:, None] == orders).astype(jnp.bfloat16)
    table = lax.dot_general(
        columns, every_hot, (((1,), (1,)), ((), ())), preferred_element_type=jnp.float32
    )
    slot_basis = jnp.einsum(
        "skb,sbi->ski", chosen.astype(jnp.float32), every_basis, precision=HIGHEST
    )
    near_basis = lax.dynamic_index_in_dim(to_readers(slot_basis), here, 0, keepdims=False)
    far_hot = (send[near:, None] == jnp.arange(blocks, dtype=jnp.int32)).astype(jnp.float32)
    far_rows = jnp.dot(far_hot, basis, precision=HIGHEST)
    all_rows = jnp.concatenate(
        [near_basis, passed_along(far_rows[:CAP], 4), passed_along(far_rows[CAP:], 5)]
    )
    read_hot = (read[:, None] == jnp.arange(slots, dtype=jnp.int32)).astype(jnp.float32)
    read_basis = jnp.dot(read_hot, all_rows, precision=HIGHEST)
    far_columns = jnp.broadcast_to(read_basis[:, :, None], (blocks, BLK, BLK))

    for iteration in range(ITERS):
        arrived = jump_slabs(slabs)
        every_proj = to_everyone(proj).reshape(-1, cases)
        coarse, near_rows, up_rows, down_rows = pl.pallas_call(
            coarse_kernel,
            out_shape=[f32(blocks, cases), f32(near, cases), f32(CAP, cases), f32(CAP, cases)],
            in_specs=[SMEM, VMEM, VMEM],
            out_specs=[VMEM] * 4,
            scratch_shapes=[pltpu.VMEM((blocks, 1, cases), jnp.float32)],
            compiler_params=PARAMS,
        )(send, table, every_proj)
        up_rows = passed_along(up_rows, 4)
        down_rows = passed_along(down_rows, 5)
        dual, *slabs = pl.pallas_call(
            dirichlet_kernel,
            out_shape=[bf16(blocks, BLK, cases)] + slab_shapes,
            in_specs=[SMEM] * 3 + [ANY] + [VMEM] * 7 + [ANY] * DIRS,
            out_specs=[VMEM] * (1 + DIRS),
            scratch_shapes=[held, received, pltpu.VMEM((slots, 1, cases), jnp.float32), rhs, sems, slab_sems],
            compiler_params=PARAMS,
        )(
            send, read, weights, dirichlet_matrix, disp, basis_columns, far_columns,
            coarse, near_rows, up_rows, down_rows, *arrived,
        )
        arrived = jump_slabs(slabs)
        if iteration + 1 < ITERS:
            mult, disp, proj, *slabs = pl.pallas_call(
                next_solve_kernel,
                out_shape=[f32(blocks, BLK, cases), f32(blocks, BLK, cases), f32(blocks, cases)] + slab_shapes,
                in_specs=[SMEM] * 2 + [ANY] + [VMEM] * 3 + [ANY] * DIRS,
                out_specs=[VMEM] * (3 + DIRS),
                scratch_shapes=[held, values, received, rhs, sems, slab_sems],
                compiler_params=PARAMS,
            )(send, read, solve_matrix, load, basis_columns, dual, *arrived)
    out = pl.pallas_call(
        finish_kernel,
        out_shape=f32(blocks, BLK, cases),
        in_specs=[SMEM] + [VMEM] * 2 + [ANY] * DIRS,
        out_specs=VMEM,
        scratch_shapes=[received, slab_sems],
        compiler_params=PARAMS,
    )(read, mult, dual, *arrived)
    return out.reshape(1, 1, dofs, cases)


def solution(mesh):
    split = P("group", "sub")
    return jax.shard_map(
        on_device, mesh=mesh, in_specs=(split,) * 9, out_specs=split, check_vma=False
    )
```

time: 206 us -> 169 us (0.82)
  blocking collectives: 39.3 us -> 11.4 us
  starting transfers between devices: 28.8 us -> 53.2 us
  Pallas kernels: 0 us -> 24.4 us
  local copies, waits for them, and re-layouts: 40.8 us -> 19.1 us
  other arithmetic: 19.6 us -> 2.52 us
  matrix products: 18.1 us -> 2.23 us
  waiting for transfers between devices: 57.8 us -> 55.2 us
    all_gather x3 -> x0, blocking collectives: 39.3 us -> none  [the longest x2 28.7 us: on_device(): every_projected = lax.all_gather(projected, 'sub', axis=0, tiled=True)]
    pallas_call x0 -> x7, Pallas kernels: none -> 24.4 us  [the longest x2 10.3 us: on_device(): pl.pallas_call(dirichlet_kernel, out_shape=[bf16(blocks, BLK, cases)] + s...]
    gather x11 -> x0, local copies, waits for them, and re-layouts: 20.9 us -> none  [the longest x4 9.92 us: jump(): remote = jnp.take(received, read_codes, axis=0)]
    dot_general x6 -> x5, matrix products: 18.1 us -> 2.23 us  [the longest x1 1.38 us: on_device(): lax.dot_general(wanted_hot, coarse_inv[0].astype(jnp.bfloat16), (((1,), (...]
    ppermute x24 -> x30, starting transfers between devices: 25.5 us -> 39 us  [passed_along(): lax.ppermute(block, axis, [((i - distance) % count, i) for i in range(cou...]
    all_to_all x0 -> x1, blocking collectives: none -> 11.4 us  [to_everyone(): lax.all_to_all(jnp.broadcast_to(mine[None], (count,) + mine.shape), 'sub'...]
    ppermute x24 -> x30, waiting for transfers between devices: 57.8 us -> 46.5 us  [passed_along(): lax.ppermute(block, axis, [((i - distance) % count, i) for i in range(cou...]
    all_to_all x1 -> x3, starting transfers between devices: 3.34 us -> 14.2 us  [the longest x2 10.2 us: to_everyone(): lax.all_to_all(jnp.broadcast_to(mine[None], (count,) + mine.shape), 'sub'...]
  transfers between devices with their start and end apart: 25 -> 33, of which waited for: 8 -> 17; matrix products, arithmetic and copies ran while one was open for 7% -> 4% of each run, Pallas kernels for 0% -> 4%
where the time goes in v1:
time: 169 us
  waiting for transfers between devices  55.2 us (33%)
  starting transfers between devices  53.2 us (31%)
  Pallas kernels  24.4 us (14%)
  local copies, waits for them, and re-layouts  19.1 us (11%)
  blocking collectives  11.4 us (7%)
  other arithmetic  2.52 us (1%)
  matrix products  2.23 us (1%)
    ppermute x30, waiting for transfers between devices, passed_along(): lax.ppermute(block, axis, [((i - distance) % count, i) for i in range(cou...  46.5 us
    ppermute x30, starting transfers between devices, passed_along(): lax.ppermute(block, axis, [((i - distance) % count, i) for i in range(cou...  39 us
    unnamed x32, local copies, waits for them, and re-layouts  14.3 us
    all_to_all x1, blocking collectives, to_everyone(): lax.all_to_all(jnp.broadcast_to(mine[None], (count,) + mine.shape), 'sub'...  11.4 us
    pallas_call x2, Pallas kernels, on_device(): pl.pallas_call(dirichlet_kernel, out_shape=[bf16(blocks, BLK, cases)] + s...  10.3 us
    all_to_all x2, starting transfers between devices, to_everyone(): lax.all_to_all(jnp.broadcast_to(mine[None], (count,) + mine.shape), 'sub'...  10.2 us
    all_to_all x1, waiting for transfers between devices, on_device(): columns = lax.all_to_all(columns, 'sub', 0, 0, tiled=True)  5.82 us
    pallas_call x1, Pallas kernels, on_device(): pl.pallas_call(next_solve_kernel, out_shape=[f32(blocks, BLK, cases), f32...  5.53 us
  transfers between devices with their start and end apart: 33, of which 17 were waited for; matrix products, arithmetic and copies ran while one was open for 4% of the time, Pallas kernels for 4%

profile of v1, /device:TPU:0, one launch (start us, length us, event | category | flops | bytes accessed | tf_op | source)
XLA Modules:
  0.0 168.6 jit_solution(3612086974220362879)
XLA Ops:
  1.7 2.9 %collective-permute-start = (f32[4,128]{1,0:T(4,128)S(1)}, f32[4,128]{1,0:T(4,128)S(1)}, u32[]{:S(2)}, u32[]{:S(2)}) collective-permute-start(f32[4,128]{1,0:T(4,128)S(1)} %get-tuple-element.99), channel_id=1, source_target_pairs={{24,0},{0,8},{8,16},{16,24},{25,1},{1,9},{9,17},{17,25},{26,2},{2,... | collective-permute-start | bytes 6152 | tf_op jit(solution)/shard_map/ppermute | solution.py:27
  7.0 5.3 %all-to-all-start = ((f32[8,13,128]{2,1,0:T(8,128)}), f32[8,13,128]{2,1,0:T(8,128)S(1)}, u32[]{:S(2)}, u32[]{:S(2)}) async-start(f32[8,13,128]{2,1,0:T(8,128)} %broadcast_in_dim.26), calls=%async_computation | async-start | bytes 131072 | tf_op jit(solution)/shard_map/all_to_all | solution.py:184
  12.6 2.3 %copy-done = bf16[1,1,1536,1536]{3,2,1,0:T(8,128)(2,1)S(1)} copy-done((bf16[1,1,1536,1536]{3,2,1,0:T(8,128)(2,1)S(1)}, bf16[1,1,1536,1536]{3,2,1,0:T(8,128)(2,1)}, u32[]{:S(2)}) %copy-start) | copy-done | bytes 4718616
  15.0 5.1 %shard_map.91 = (f32[12,128,256]{2,1,0:T(8,128)S(1)}, f32[12,256]{1,0:T(8,128)S(1)}, bf16[4,128,256]{2,1,0:T(8,128)(2,1)}, bf16[4,128,256]{2,1,0:T(8,128)(2,1)S(...) custom-call(s32[24]{0:T(128)S(1)} %get-tuple-element.102.send, ...), custom_call_target="tpu_custom_call" | custom-call | tf_op jit(solution)/shard_map/pallas_call | solution.py:224
  22.4 4.9 %all-to-all-start.2 = ((f32[8,12,256]{2,1,0:T(8,128)}), f32[8,12,256]{2,1,0:T(8,128)S(1)}, u32[]{:S(2)}, u32[]{:S(2)}) async-start(f32[8,12,256]{2,1,0:T(8,128)} %broadcast_in_dim.30), calls=%async_computation.2 | async-start | bytes 262144 | tf_op jit(solution)/shard_map/all_to_all | solution.py:184
  31.1 2.9 %all-to-all-done.2 = f32[8,12,256]{2,1,0:T(8,128)S(1)} async-done(((f32[8,12,256]{2,1,0:T(8,128)}), f32[8,12,256]{2,1,0:T(8,128)S(1)}, u32[]{:S(2)}, u32[]{:S(2)}) %all-to-all-start.2) | async-done | bytes 98336 | tf_op jit(solution)/shard_map/all_to_all | solution.py:184
  34.0 4.0 %all-to-all-start.1 = ((bf16[8,28,128]{2,1,0:T(8,128)(2,1)}), bf16[8,28,128]{2,1,0:T(8,128)(2,1)}, u32[]{:S(2)}, u32[]{:S(2)}) async-start(bf16[8,28,128]{2,1,0:T(8,128)(2,1)} %all_to_all.16), calls=%async_computation.1 | async-start | bytes 131072 | tf_op jit(solution)/shard_map/all_to_all | solution.py:258
  38.1 5.8 %all-to-all-done.1 = bf16[8,28,128]{2,1,0:T(8,128)(2,1)} async-done(((bf16[8,28,128]{2,1,0:T(8,128)(2,1)}), bf16[8,28,128]{2,1,0:T(8,128)(2,1)}, u32[]{:S(2)}, u32[]{:S(2)}) %all-to-all-start.1) | async-done | bytes 57376 | tf_op jit(solution)/shard_map/all_to_all | solution.py:258
  46.5 2.3 %collective-permute-start.3 = (f32[4,256]{1,0:T(4,128)S(1)}, f32[4,256]{1,0:T(4,128)S(1)}, u32[]{:S(2)}, u32[]{:S(2)}) collective-permute-start(f32[4,256]{1,0:T(4,128)S(1)} %get-tuple-element.49), channel_id=1, source_target_pairs={{8,0},{16,8},{24,16},{0,24},{9,1},{17,9},{25,17},{1,25},{10,2},{18... | collective-permute-start | bytes 12296 | tf_op jit(solution)/shard_map/ppermute | solution.py:27
  50.4 2.3 %collective-permute-start.7 = (bf16[4,128,256]{2,1,0:T(8,128)(2,1)S(1)}, bf16[4,128,256]{2,1,0:T(8,128)(2,1)S(1)}, u32[]{:S(2)}, u32[]{:S(2)}) collective-permute-start(bf16[4,128,256]{2,1,0:T(8,128)(2,1)S(1)} %get-tuple-element.53), channel_id=1, source_target_pairs={{2,0},{3,1},{4,2},{5,3},{6,4},{7,5},{0,6},{1,7},{10,8},{11,9},{12,... | collective-permute-start | bytes 786440 | tf_op jit(solution)/shard_map/ppermute | solution.py:27
  55.9 5.0 %collective-permute-done.6.rest_2_ = bf16[4,128,256]{2,1,0:T(8,128)(2,1)S(1)} collective-permute-done((bf16[4,128,256]{2,1,0:T(8,128)(2,1)S(1)}, bf16[4,128,256]{2,1,0:T(8,128)(2,1)S(1)}, u32[]{:S(2)}, u32[]{:S(2)}) %collective-permute-start.6) | collective-permute-done | bytes 262176 | tf_op jit(solution)/shard_map/ppermute | solution.py:27
  60.8 4.3 %collective-permute-done.7.rest_3_ = bf16[4,128,256]{2,1,0:T(8,128)(2,1)S(1)} collective-permute-done((bf16[4,128,256]{2,1,0:T(8,128)(2,1)S(1)}, bf16[4,128,256]{2,1,0:T(8,128)(2,1)S(1)}, u32[]{:S(2)}, u32[]{:S(2)}) %collective-permute-start.7) | collective-permute-done | bytes 262176 | tf_op jit(solution)/shard_map/ppermute | solution.py:27
  67.7 2.5 %copy-done.1 = bf16[1,1,1536,1536]{3,2,1,0:T(8,128)(2,1)S(1)} copy-done((bf16[1,1,1536,1536]{3,2,1,0:T(8,128)(2,1)S(1)}, bf16[1,1,1536,1536]{3,2,1,0:T(8,128)(2,1)}, u32[]{:S(2)}) %copy-start.1) | copy-done | bytes 4718616
  71.7 5.2 %shard_map.93 = (bf16[12,128,256]{2,1,0:T(8,128)(2,1)S(1)}, bf16[4,128,256]{2,1,0:T(8,128)(2,1)S(1)}, bf16[4,128,256]{2,1,0:T(8,128)(2,1)S(1)}, bf16[4,128,256]{...) custom-call(s32[24]{0:T(128)S(1)} %get-tuple-element.102.send, ...), custom_call_target="tpu_custom_call" | custom-call | tf_op jit(solution)/shard_map/pallas_call | solution.py:290
  77.0 3.5 %collective-permute-start.11 = (bf16[4,128,256]{2,1,0:T(8,128)(2,1)S(1)}, bf16[4,128,256]{2,1,0:T(8,128)(2,1)S(1)}, u32[]{:S(2)}, u32[]{:S(2)}) collective-permute-start(bf16[4,128,256]{2,1,0:T(8,128)(2,1)S(1)} %get-tuple-element.58), channel_id=1, source_target_pairs={{1,0},{2,1},{3,2},{4,3},{5,4},{6,5},{7,6},{0,7},{9,8},{10,9},{11,1... | collective-permute-start | bytes 786440 | tf_op jit(solution)/shard_map/ppermute | solution.py:27
  80.5 3.8 %collective-permute-start.13 = (bf16[4,128,256]{2,1,0:T(8,128)(2,1)S(1)}, bf16[4,128,256]{2,1,0:T(8,128)(2,1)S(1)}, u32[]{:S(2)}, u32[]{:S(2)}) collective-permute-start(bf16[4,128,256]{2,1,0:T(8,128)(2,1)S(1)} %get-tuple-element.60), channel_id=1, source_target_pairs={{2,0},{3,1},{4,2},{5,3},{6,4},{7,5},{0,6},{1,7},{10,8},{11,9},{12,... | collective-permute-start | bytes 786440 | tf_op jit(solution)/shard_map/ppermute | solution.py:27
  84.6 2.8 %collective-permute-done.10.rest_0_ = bf16[4,128,256]{2,1,0:T(8,128)(2,1)S(1)} collective-permute-done((bf16[4,128,256]{2,1,0:T(8,128)(2,1)S(1)}, bf16[4,128,256]{2,1,0:T(8,128)(2,1)S(1)}, u32[]{:S(2)}, u32[]{:S(2)}) %collective-permute-start.10) | collective-permute-done | bytes 262176 | tf_op jit(solution)/shard_map/ppermute | solution.py:27
  87.8 4.1 %collective-permute-done.12.rest_2_ = bf16[4,128,256]{2,1,0:T(8,128)(2,1)S(1)} collective-permute-done((bf16[4,128,256]{2,1,0:T(8,128)(2,1)S(1)}, bf16[4,128,256]{2,1,0:T(8,128)(2,1)S(1)}, u32[]{:S(2)}, u32[]{:S(2)}) %collective-permute-start.12) | collective-permute-done | bytes 262176 | tf_op jit(solution)/shard_map/ppermute | solution.py:27
  91.8 4.2 %collective-permute-done.13.rest_3_ = bf16[4,128,256]{2,1,0:T(8,128)(2,1)S(1)} collective-permute-done((bf16[4,128,256]{2,1,0:T(8,128)(2,1)S(1)}, bf16[4,128,256]{2,1,0:T(8,128)(2,1)S(1)}, u32[]{:S(2)}, u32[]{:S(2)}) %collective-permute-start.13) | collective-permute-done | bytes 262176 | tf_op jit(solution)/shard_map/ppermute | solution.py:27
  96.1 5.5 %shard_map.94 = (f32[12,128,256]{2,1,0:T(8,128)S(1)}, f32[12,128,256]{2,1,0:T(8,128)S(1)}, f32[12,256]{1,0:T(8,128)S(1)}, bf16[4,128,256]{2,1,0:T(8,128)(2,1)}, ...) custom-call(s32[24]{0:T(128)S(1)} %get-tuple-element.102.send, ...), custom_call_target="tpu_custom_call" | custom-call | tf_op jit(solution)/shard_map/pallas_call | solution.py:303
  104.7 11.4 %all_to_all.24 = f32[8,12,256]{2,1,0:T(8,128)S(1)} all-to-all(f32[8,12,256]{2,1,0:T(8,128)S(1)} %broadcast_in_dim.31), channel_id=1, replica_groups=mesh['group'=4,'sub'=8] {'sub'}, dimensions={0} | all-to-all | bytes 196608 | tf_op jit(solution)/shard_map/all_to_all | solution.py:184
  121.4 2.3 %collective-permute-start.21 = (bf16[4,128,256]{2,1,0:T(8,128)(2,1)S(1)}, bf16[4,128,256]{2,1,0:T(8,128)(2,1)S(1)}, u32[]{:S(2)}, u32[]{:S(2)}) collective-permute-start(bf16[4,128,256]{2,1,0:T(8,128)(2,1)S(1)} %get-tuple-element.73), channel_id=1, source_target_pairs={{2,0},{3,1},{4,2},{5,3},{6,4},{7,5},{0,6},{1,7},{10,8},{11,9},{12,... | collective-permute-start | bytes 786440 | tf_op jit(solution)/shard_map/ppermute | solution.py:27
  124.0 2.7 %collective-permute-start.23 = (bf16[4,128,256]{2,1,0:T(8,128)(2,1)S(1)}, bf16[4,128,256]{2,1,0:T(8,128)(2,1)S(1)}, u32[]{:S(2)}, u32[]{:S(2)}) collective-permute-start(bf16[4,128,256]{2,1,0:T(8,128)(2,1)S(1)} %get-tuple-element.75), channel_id=1, source_target_pairs={{8,0},{16,8},{24,16},{0,24},{9,1},{17,9},{25,17},{1,25},{10,2},{18... | collective-permute-start | bytes 786440 | tf_op jit(solution)/shard_map/ppermute | solution.py:27
  126.8 5.6 %collective-permute-done.20.rest_2_ = bf16[4,128,256]{2,1,0:T(8,128)(2,1)S(1)} collective-permute-done((bf16[4,128,256]{2,1,0:T(8,128)(2,1)S(1)}, bf16[4,128,256]{2,1,0:T(8,128)(2,1)S(1)}, u32[]{:S(2)}, u32[]{:S(2)}) %collective-permute-start.20) | collective-permute-done | bytes 262176 | tf_op jit(solution)/shard_map/ppermute | solution.py:27
  132.4 4.1 %collective-permute-done.21.rest_3_ = bf16[4,128,256]{2,1,0:T(8,128)(2,1)S(1)} collective-permute-done((bf16[4,128,256]{2,1,0:T(8,128)(2,1)S(1)}, bf16[4,128,256]{2,1,0:T(8,128)(2,1)S(1)}, u32[]{:S(2)}, u32[]{:S(2)}) %collective-permute-start.21) | collective-permute-done | bytes 262176 | tf_op jit(solution)/shard_map/ppermute | solution.py:27
  138.0 2.3 %copy-done.2 = bf16[1,1,1536,1536]{3,2,1,0:T(8,128)(2,1)S(1)} copy-done((bf16[1,1,1536,1536]{3,2,1,0:T(8,128)(2,1)S(1)}, bf16[1,1,1536,1536]{3,2,1,0:T(8,128)(2,1)}, u32[]{:S(2)}) %copy-start.2) | copy-done | bytes 4718616
  141.7 5.2 %shard_map.96 = (bf16[12,128,256]{2,1,0:T(8,128)(2,1)S(1)}, bf16[4,128,256]{2,1,0:T(8,128)(2,1)S(1)}, bf16[4,128,256]{2,1,0:T(8,128)(2,1)S(1)}, bf16[4,128,256]{...) custom-call(s32[24]{0:T(128)S(1)} %get-tuple-element.102.send, ...), custom_call_target="tpu_custom_call" | custom-call | tf_op jit(solution)/shard_map/pallas_call | solution.py:290
  147.0 3.5 %collective-permute-start.25 = (bf16[4,128,256]{2,1,0:T(8,128)(2,1)S(1)}, bf16[4,128,256]{2,1,0:T(8,128)(2,1)S(1)}, u32[]{:S(2)}, u32[]{:S(2)}) collective-permute-start(bf16[4,128,256]{2,1,0:T(8,128)(2,1)S(1)} %get-tuple-element.78), channel_id=1, source_target_pairs={{1,0},{2,1},{3,2},{4,3},{5,4},{6,5},{7,6},{0,7},{9,8},{10,9},{11,1... | collective-permute-start | bytes 786440 | tf_op jit(solution)/shard_map/ppermute | solution.py:27
  150.5 3.8 %collective-permute-start.27 = (bf16[4,128,256]{2,1,0:T(8,128)(2,1)S(1)}, bf16[4,128,256]{2,1,0:T(8,128)(2,1)S(1)}, u32[]{:S(2)}, u32[]{:S(2)}) collective-permute-start(bf16[4,128,256]{2,1,0:T(8,128)(2,1)S(1)} %get-tuple-element.80), channel_id=1, source_target_pairs={{2,0},{3,1},{4,2},{5,3},{6,4},{7,5},{0,6},{1,7},{10,8},{11,9},{12,... | collective-permute-start | bytes 786440 | tf_op jit(solution)/shard_map/ppermute | solution.py:27
  154.6 2.7 %collective-permute-done.24.rest_0_ = bf16[4,128,256]{2,1,0:T(8,128)(2,1)S(1)} collective-permute-done((bf16[4,128,256]{2,1,0:T(8,128)(2,1)S(1)}, bf16[4,128,256]{2,1,0:T(8,128)(2,1)S(1)}, u32[]{:S(2)}, u32[]{:S(2)}) %collective-permute-start.24) | collective-permute-done | bytes 262176 | tf_op jit(solution)/shard_map/ppermute | solution.py:27
  158.0 5.1 %collective-permute-done.26.rest_2_ = bf16[4,128,256]{2,1,0:T(8,128)(2,1)S(1)} collective-permute-done((bf16[4,128,256]{2,1,0:T(8,128)(2,1)S(1)}, bf16[4,128,256]{2,1,0:T(8,128)(2,1)S(1)}, u32[]{:S(2)}, u32[]{:S(2)}) %collective-permute-start.26) | collective-permute-done | bytes 262176 | tf_op jit(solution)/shard_map/ppermute | solution.py:27
  163.1 3.3 %collective-permute-done.27.rest_3_ = bf16[4,128,256]{2,1,0:T(8,128)(2,1)S(1)} collective-permute-done((bf16[4,128,256]{2,1,0:T(8,128)(2,1)S(1)}, bf16[4,128,256]{2,1,0:T(8,128)(2,1)S(1)}, u32[]{:S(2)}, u32[]{:S(2)}) %collective-permute-start.27) | collective-permute-done | bytes 262176 | tf_op jit(solution)/shard_map/ppermute | solution.py:27
  (121 shorter events, 37.2 us)
Async XLA Ops:
  1.7 47.1 %collective-permute-start = (f32[4,128]{1,0:T(4,128)S(1)}, f32[4,128]{1,0:T(4,128)S(1)}, u32[]{:S(2)}, u32[]{:S(2)}) collective-permute-start(f32[4,128]{1,0:T(4,128)S(1)} %get-tuple-element.99), channel_id=1, source_target_pairs={{24,0},{0,8},{8,16},{16,24},{25,1},{1,9},{9,17},{17,25},{26,2},{2,... | collective-permute-start | bytes 6152 | tf_op jit(solution)/shard_map/ppermute | solution.py:27
  4.7 44.2 %collective-permute-start.1 = (f32[4,128]{1,0:T(4,128)S(1)}, f32[4,128]{1,0:T(4,128)S(1)}, u32[]{:S(2)}, u32[]{:S(2)}) collective-permute-start(f32[4,128]{1,0:T(4,128)S(1)} %get-tuple-element.100), channel_id=1, source_target_pairs={{8,0},{16,8},{24,16},{0,24},{9,1},{17,9},{25,17},{1,25},{10,2},{18... | collective-permute-start | bytes 6152 | tf_op jit(solution)/shard_map/ppermute | solution.py:27
  7.0 14.7 %all-to-all-start = ((f32[8,13,128]{2,1,0:T(8,128)}), f32[8,13,128]{2,1,0:T(8,128)S(1)}, u32[]{:S(2)}, u32[]{:S(2)}) async-start(f32[8,13,128]{2,1,0:T(8,128)} %broadcast_in_dim.26), calls=%async_computation | async-start | bytes 131072 | tf_op jit(solution)/shard_map/all_to_all | solution.py:184
  21.2 32.2 %collective-permute-start.4 = (bf16[4,128,256]{2,1,0:T(8,128)(2,1)}, bf16[4,128,256]{2,1,0:T(8,128)(2,1)S(1)}, u32[]{:S(2)}, u32[]{:S(2)}) collective-permute-start(bf16[4,128,256]{2,1,0:T(8,128)(2,1)} %get-tuple-element.50), channel_id=1, source_target_pairs={{7,0},{0,1},{1,2},{2,3},{3,4},{4,5},{5,6},{6,7},{15,8},{8,9},{9,10... | collective-permute-start | bytes 786440 | tf_op jit(solution)/shard_map/ppermute | solution.py:27
  22.4 11.7 %all-to-all-start.2 = ((f32[8,12,256]{2,1,0:T(8,128)}), f32[8,12,256]{2,1,0:T(8,128)S(1)}, u32[]{:S(2)}, u32[]{:S(2)}) async-start(f32[8,12,256]{2,1,0:T(8,128)} %broadcast_in_dim.30), calls=%async_computation.2 | async-start | bytes 262144 | tf_op jit(solution)/shard_map/all_to_all | solution.py:184
  34.0 9.9 %all-to-all-start.1 = ((bf16[8,28,128]{2,1,0:T(8,128)(2,1)}), bf16[8,28,128]{2,1,0:T(8,128)(2,1)}, u32[]{:S(2)}, u32[]{:S(2)}) async-start(bf16[8,28,128]{2,1,0:T(8,128)(2,1)} %all_to_all.16), calls=%async_computation.1 | async-start | bytes 131072 | tf_op jit(solution)/shard_map/all_to_all | solution.py:258
  45.8 4.6 %collective-permute-start.2 = (f32[4,256]{1,0:T(4,128)S(1)}, f32[4,256]{1,0:T(4,128)S(1)}, u32[]{:S(2)}, u32[]{:S(2)}) collective-permute-start(f32[4,256]{1,0:T(4,128)S(1)} %get-tuple-element.48), channel_id=1, source_target_pairs={{24,0},{0,8},{8,16},{16,24},{25,1},{1,9},{9,17},{17,25},{26,2},{2,... | collective-permute-start | bytes 12296 | tf_op jit(solution)/shard_map/ppermute | solution.py:27
  46.5 6.2 %collective-permute-start.3 = (f32[4,256]{1,0:T(4,128)S(1)}, f32[4,256]{1,0:T(4,128)S(1)}, u32[]{:S(2)}, u32[]{:S(2)}) collective-permute-start(f32[4,256]{1,0:T(4,128)S(1)} %get-tuple-element.49), channel_id=1, source_target_pairs={{8,0},{16,8},{24,16},{0,24},{9,1},{17,9},{25,17},{1,25},{10,2},{18... | collective-permute-start | bytes 12296 | tf_op jit(solution)/shard_map/ppermute | solution.py:27
  48.8 7.1 %collective-permute-start.5 = (bf16[4,128,256]{2,1,0:T(8,128)(2,1)S(1)}, bf16[4,128,256]{2,1,0:T(8,128)(2,1)S(1)}, u32[]{:S(2)}, u32[]{:S(2)}) collective-permute-start(bf16[4,128,256]{2,1,0:T(8,128)(2,1)S(1)} %get-tuple-element.51), channel_id=1, source_target_pairs={{1,0},{2,1},{3,2},{4,3},{5,4},{6,5},{7,6},{0,7},{9,8},{10,9},{11,1... | collective-permute-start | bytes 786440 | tf_op jit(solution)/shard_map/ppermute | solution.py:27
  48.8 12.0 %collective-permute-start.6 = (bf16[4,128,256]{2,1,0:T(8,128)(2,1)S(1)}, bf16[4,128,256]{2,1,0:T(8,128)(2,1)S(1)}, u32[]{:S(2)}, u32[]{:S(2)}) collective-permute-start(bf16[4,128,256]{2,1,0:T(8,128)(2,1)S(1)} %get-tuple-element.52), channel_id=1, source_target_pairs={{6,0},{7,1},{0,2},{1,3},{2,4},{3,5},{4,6},{5,7},{14,8},{15,9},{8,1... | collective-permute-start | bytes 786440 | tf_op jit(solution)/shard_map/ppermute | solution.py:27
  50.4 14.7 %collective-permute-start.7 = (bf16[4,128,256]{2,1,0:T(8,128)(2,1)S(1)}, bf16[4,128,256]{2,1,0:T(8,128)(2,1)S(1)}, u32[]{:S(2)}, u32[]{:S(2)}) collective-permute-start(bf16[4,128,256]{2,1,0:T(8,128)(2,1)S(1)} %get-tuple-element.53), channel_id=1, source_target_pairs={{2,0},{3,1},{4,2},{5,3},{6,4},{7,5},{0,6},{1,7},{10,8},{11,9},{12,... | collective-permute-start | bytes 786440 | tf_op jit(solution)/shard_map/ppermute | solution.py:27
  52.7 12.4 %collective-permute-start.8 = (bf16[4,128,256]{2,1,0:T(8,128)(2,1)S(1)}, bf16[4,128,256]{2,1,0:T(8,128)(2,1)S(1)}, u32[]{:S(2)}, u32[]{:S(2)}) collective-permute-start(bf16[4,128,256]{2,1,0:T(8,128)(2,1)S(1)} %get-tuple-element.54), channel_id=1, source_target_pairs={{24,0},{0,8},{8,16},{16,24},{25,1},{1,9},{9,17},{17,25},{26,2},{2,... | collective-permute-start | bytes 786440 | tf_op jit(solution)/shard_map/ppermute | solution.py:27
  53.4 14.0 %collective-permute-start.9 = (bf16[4,128,256]{2,1,0:T(8,128)(2,1)S(1)}, bf16[4,128,256]{2,1,0:T(8,128)(2,1)S(1)}, u32[]{:S(2)}, u32[]{:S(2)}) collective-permute-start(bf16[4,128,256]{2,1,0:T(8,128)(2,1)S(1)} %get-tuple-element.55), channel_id=1, source_target_pairs={{8,0},{16,8},{24,16},{0,24},{9,1},{17,9},{25,17},{1,25},{10,2},{18... | collective-permute-start | bytes 786440 | tf_op jit(solution)/shard_map/ppermute | solution.py:27
  76.9 10.5 %collective-permute-start.10 = (bf16[4,128,256]{2,1,0:T(8,128)(2,1)S(1)}, bf16[4,128,256]{2,1,0:T(8,128)(2,1)S(1)}, u32[]{:S(2)}, u32[]{:S(2)}) collective-permute-start(bf16[4,128,256]{2,1,0:T(8,128)(2,1)S(1)} %get-tuple-element.57), channel_id=1, source_target_pairs={{7,0},{0,1},{1,2},{2,3},{3,4},{4,5},{5,6},{6,7},{15,8},{8,9},{9,10... | collective-permute-start | bytes 786440 | tf_op jit(solution)/shard_map/ppermute | solution.py:27
  77.0 10.8 %collective-permute-start.11 = (bf16[4,128,256]{2,1,0:T(8,128)(2,1)S(1)}, bf16[4,128,256]{2,1,0:T(8,128)(2,1)S(1)}, u32[]{:S(2)}, u32[]{:S(2)}) collective-permute-start(bf16[4,128,256]{2,1,0:T(8,128)(2,1)S(1)} %get-tuple-element.58), channel_id=1, source_target_pairs={{1,0},{2,1},{3,2},{4,3},{5,4},{6,5},{7,6},{0,7},{9,8},{10,9},{11,1... | collective-permute-start | bytes 786440 | tf_op jit(solution)/shard_map/ppermute | solution.py:27
  80.5 11.3 %collective-permute-start.12 = (bf16[4,128,256]{2,1,0:T(8,128)(2,1)S(1)}, bf16[4,128,256]{2,1,0:T(8,128)(2,1)S(1)}, u32[]{:S(2)}, u32[]{:S(2)}) collective-permute-start(bf16[4,128,256]{2,1,0:T(8,128)(2,1)S(1)} %get-tuple-element.59), channel_id=1, source_target_pairs={{6,0},{7,1},{0,2},{1,3},{2,4},{3,5},{4,6},{5,7},{14,8},{15,9},{8,1... | collective-permute-start | bytes 786440 | tf_op jit(solution)/shard_map/ppermute | solution.py:27
  80.5 15.6 %collective-permute-start.13 = (bf16[4,128,256]{2,1,0:T(8,128)(2,1)S(1)}, bf16[4,128,256]{2,1,0:T(8,128)(2,1)S(1)}, u32[]{:S(2)}, u32[]{:S(2)}) collective-permute-start(bf16[4,128,256]{2,1,0:T(8,128)(2,1)S(1)} %get-tuple-element.60), channel_id=1, source_target_pairs={{2,0},{3,1},{4,2},{5,3},{6,4},{7,5},{0,6},{1,7},{10,8},{11,9},{12,... | collective-permute-start | bytes 786440 | tf_op jit(solution)/shard_map/ppermute | solution.py:27
  84.3 11.7 %collective-permute-start.14 = (bf16[4,128,256]{2,1,0:T(8,128)(2,1)S(1)}, bf16[4,128,256]{2,1,0:T(8,128)(2,1)S(1)}, u32[]{:S(2)}, u32[]{:S(2)}) collective-permute-start(bf16[4,128,256]{2,1,0:T(8,128)(2,1)S(1)} %get-tuple-element.61), channel_id=1, source_target_pairs={{24,0},{0,8},{8,16},{16,24},{25,1},{1,9},{9,17},{17,25},{26,2},{2,... | collective-permute-start | bytes 786440 | tf_op jit(solution)/shard_map/ppermute | solution.py:27
  87.4 8.7 %collective-permute-start.15 = (bf16[4,128,256]{2,1,0:T(8,128)(2,1)S(1)}, bf16[4,128,256]{2,1,0:T(8,128)(2,1)S(1)}, u32[]{:S(2)}, u32[]{:S(2)}) collective-permute-start(bf16[4,128,256]{2,1,0:T(8,128)(2,1)S(1)} %get-tuple-element.62), channel_id=1, source_target_pairs={{8,0},{16,8},{24,16},{0,24},{9,1},{17,9},{25,17},{1,25},{10,2},{18... | collective-permute-start | bytes 786440 | tf_op jit(solution)/shard_map/ppermute | solution.py:27
  104.7 19.3 %collective-permute-start.18 = (bf16[4,128,256]{2,1,0:T(8,128)(2,1)}, bf16[4,128,256]{2,1,0:T(8,128)(2,1)S(1)}, u32[]{:S(2)}, u32[]{:S(2)}) collective-permute-start(bf16[4,128,256]{2,1,0:T(8,128)(2,1)} %get-tuple-element.70), channel_id=1, source_target_pairs={{7,0},{0,1},{1,2},{2,3},{3,4},{4,5},{5,6},{6,7},{15,8},{8,9},{9,10... | collective-permute-start | bytes 786440 | tf_op jit(solution)/shard_map/ppermute | solution.py:27
  117.5 6.3 %collective-permute-start.17 = (f32[4,256]{1,0:T(4,128)S(1)}, f32[4,256]{1,0:T(4,128)S(1)}, u32[]{:S(2)}, u32[]{:S(2)}) collective-permute-start(f32[4,256]{1,0:T(4,128)S(1)} %get-tuple-element.69), channel_id=1, source_target_pairs={{8,0},{16,8},{24,16},{0,24},{9,1},{17,9},{25,17},{1,25},{10,2},{18... | collective-permute-start | bytes 12296 | tf_op jit(solution)/shard_map/ppermute | solution.py:27
  119.8 7.0 %collective-permute-start.19 = (bf16[4,128,256]{2,1,0:T(8,128)(2,1)}, bf16[4,128,256]{2,1,0:T(8,128)(2,1)S(1)}, u32[]{:S(2)}, u32[]{:S(2)}) collective-permute-start(bf16[4,128,256]{2,1,0:T(8,128)(2,1)} %copy-done.11), channel_id=1, source_target_pairs={{1,0},{2,1},{3,2},{4,3},{5,4},{6,5},{7,6},{0,7},{9,8},{10,9},{11,1... | collective-permute-start | bytes 786440 | tf_op jit(solution)/shard_map/ppermute | solution.py:27
  119.9 12.5 %collective-permute-start.20 = (bf16[4,128,256]{2,1,0:T(8,128)(2,1)S(1)}, bf16[4,128,256]{2,1,0:T(8,128)(2,1)S(1)}, u32[]{:S(2)}, u32[]{:S(2)}) collective-permute-start(bf16[4,128,256]{2,1,0:T(8,128)(2,1)S(1)} %get-tuple-element.72), channel_id=1, source_target_pairs={{6,0},{7,1},{0,2},{1,3},{2,4},{3,5},{4,6},{5,7},{14,8},{15,9},{8,1... | collective-permute-start | bytes 786440 | tf_op jit(solution)/shard_map/ppermute | solution.py:27
  121.4 15.1 %collective-permute-start.21 = (bf16[4,128,256]{2,1,0:T(8,128)(2,1)S(1)}, bf16[4,128,256]{2,1,0:T(8,128)(2,1)S(1)}, u32[]{:S(2)}, u32[]{:S(2)}) collective-permute-start(bf16[4,128,256]{2,1,0:T(8,128)(2,1)S(1)} %get-tuple-element.73), channel_id=1, source_target_pairs={{2,0},{3,1},{4,2},{5,3},{6,4},{7,5},{0,6},{1,7},{10,8},{11,9},{12,... | collective-permute-start | bytes 786440 | tf_op jit(solution)/shard_map/ppermute | solution.py:27
  123.7 12.8 %collective-permute-start.22 = (bf16[4,128,256]{2,1,0:T(8,128)(2,1)S(1)}, bf16[4,128,256]{2,1,0:T(8,128)(2,1)S(1)}, u32[]{:S(2)}, u32[]{:S(2)}) collective-permute-start(bf16[4,128,256]{2,1,0:T(8,128)(2,1)S(1)} %get-tuple-element.74), channel_id=1, source_target_pairs={{24,0},{0,8},{8,16},{16,24},{25,1},{1,9},{9,17},{17,25},{26,2},{2,... | collective-permute-start | bytes 786440 | tf_op jit(solution)/shard_map/ppermute | solution.py:27
  124.0 14.0 %collective-permute-start.23 = (bf16[4,128,256]{2,1,0:T(8,128)(2,1)S(1)}, bf16[4,128,256]{2,1,0:T(8,128)(2,1)S(1)}, u32[]{:S(2)}, u32[]{:S(2)}) collective-permute-start(bf16[4,128,256]{2,1,0:T(8,128)(2,1)S(1)} %get-tuple-element.75), channel_id=1, source_target_pairs={{8,0},{16,8},{24,16},{0,24},{9,1},{17,9},{25,17},{1,25},{10,2},{18... | collective-permute-start | bytes 786440 | tf_op jit(solution)/shard_map/ppermute | solution.py:27
  146.9 10.4 %collective-permute-start.24 = (bf16[4,128,256]{2,1,0:T(8,128)(2,1)S(1)}, bf16[4,128,256]{2,1,0:T(8,128)(2,1)S(1)}, u32[]{:S(2)}, u32[]{:S(2)}) collective-permute-start(bf16[4,128,256]{2,1,0:T(8,128)(2,1)S(1)} %get-tuple-element.77), channel_id=1, source_target_pairs={{7,0},{0,1},{1,2},{2,3},{3,4},{4,5},{5,6},{6,7},{15,8},{8,9},{9,10... | collective-permute-start | bytes 786440 | tf_op jit(solution)/shard_map/ppermute | solution.py:27
  147.0 11.0 %collective-permute-start.25 = (bf16[4,128,256]{2,1,0:T(8,128)(2,1)S(1)}, bf16[4,128,256]{2,1,0:T(8,128)(2,1)S(1)}, u32[]{:S(2)}, u32[]{:S(2)}) collective-permute-start(bf16[4,128,256]{2,1,0:T(8,128)(2,1)S(1)} %get-tuple-element.78), channel_id=1, source_target_pairs={{1,0},{2,1},{3,2},{4,3},{5,4},{6,5},{7,6},{0,7},{9,8},{10,9},{11,1... | collective-permute-start | bytes 786440 | tf_op jit(solution)/shard_map/ppermute | solution.py:27
  150.5 12.6 %collective-permute-start.26 = (bf16[4,128,256]{2,1,0:T(8,128)(2,1)S(1)}, bf16[4,128,256]{2,1,0:T(8,128)(2,1)S(1)}, u32[]{:S(2)}, u32[]{:S(2)}) collective-permute-start(bf16[4,128,256]{2,1,0:T(8,128)(2,1)S(1)} %get-tuple-element.79), channel_id=1, source_target_pairs={{6,0},{7,1},{0,2},{1,3},{2,4},{3,5},{4,6},{5,7},{14,8},{15,9},{8,1... | collective-permute-start | bytes 786440 | tf_op jit(solution)/shard_map/ppermute | solution.py:27
  150.5 15.8 %collective-permute-start.27 = (bf16[4,128,256]{2,1,0:T(8,128)(2,1)S(1)}, bf16[4,128,256]{2,1,0:T(8,128)(2,1)S(1)}, u32[]{:S(2)}, u32[]{:S(2)}) collective-permute-start(bf16[4,128,256]{2,1,0:T(8,128)(2,1)S(1)} %get-tuple-element.80), channel_id=1, source_target_pairs={{2,0},{3,1},{4,2},{5,3},{6,4},{7,5},{0,6},{1,7},{10,8},{11,9},{12,... | collective-permute-start | bytes 786440 | tf_op jit(solution)/shard_map/ppermute | solution.py:27
  154.3 12.0 %collective-permute-start.28 = (bf16[4,128,256]{2,1,0:T(8,128)(2,1)S(1)}, bf16[4,128,256]{2,1,0:T(8,128)(2,1)S(1)}, u32[]{:S(2)}, u32[]{:S(2)}) collective-permute-start(bf16[4,128,256]{2,1,0:T(8,128)(2,1)S(1)} %get-tuple-element.81), channel_id=1, source_target_pairs={{24,0},{0,8},{8,16},{16,24},{25,1},{1,9},{9,17},{17,25},{26,2},{2,... | collective-permute-start | bytes 786440 | tf_op jit(solution)/shard_map/ppermute | solution.py:27
  157.3 9.0 %collective-permute-start.29 = (bf16[4,128,256]{2,1,0:T(8,128)(2,1)S(1)}, bf16[4,128,256]{2,1,0:T(8,128)(2,1)S(1)}, u32[]{:S(2)}, u32[]{:S(2)}) collective-permute-start(bf16[4,128,256]{2,1,0:T(8,128)(2,1)S(1)} %get-tuple-element.82), channel_id=1, source_target_pairs={{8,0},{16,8},{24,16},{0,24},{9,1},{17,9},{25,17},{1,25},{10,2},{18... | collective-permute-start | bytes 786440 | tf_op jit(solution)/shard_map/ppermute | solution.py:27
  (16 other events, 150.1 us)

commit v2 on v0

v2 whole, which is shorter than its diff:
```python
import jax
import jax.numpy as jnp
from jax import lax
from jax.experimental import pallas as pl
from jax.experimental.pallas import tpu as pltpu
from jax.sharding import PartitionSpec as P

BLK = 128
DIRS = 6
CAP = 4
ITERS = 2
NEAR = 4 * CAP
WIDE = 16
ROWS = 256
EXCHANGES = (("sub", 1), ("sub", 2), ("group", 1))
OFFSETS = (1, -1, 2, -2)
ORDER = (3, 2, 1, 0, 4, 5)
HIGHEST = lax.Precision.HIGHEST
VMEM = pl.BlockSpec(memory_space=pltpu.VMEM)
SMEM = pl.BlockSpec(memory_space=pltpu.SMEM)
HBM = pl.BlockSpec(memory_space=pltpu.HBM)
PARAMS = pltpu.CompilerParams(vmem_limit_bytes=24 * 1024 * 1024)


def f32(*shape):
    return jax.ShapeDtypeStruct(shape, jnp.float32)


def bf16(*shape):
    return jax.ShapeDtypeStruct(shape, jnp.bfloat16)


def is_lower(pair):
    axis, distance = EXCHANGES[pair]
    return (lax.axis_index(axis) // distance) % 2 == 0


def exchanged(slab, way):
    axis, distance = EXCHANGES[way // 2]
    count = lax.axis_size(axis)
    route = []
    for i in range(count):
        upward = (i // distance) % 2 == way % 2
        route.append((i, (i + distance if upward else i - distance) % count))
    return lax.ppermute(slab, axis, route)


def swapped(value, bit):
    count = lax.axis_size("sub")
    return lax.ppermute(value, "sub", [(i, i ^ bit) for i in range(count)])


def bits_of(count):
    return [1 << k for k in range(count.bit_length() - 1)]


def gathered(mine):
    held = mine[None]
    for bit in bits_of(lax.axis_size("sub")):
        held = jnp.concatenate([held, swapped(held, bit)])
    return held


def slot_block(send, way, j):
    direction = jnp.where(is_lower(way // 2), way, way ^ 1)
    return jnp.maximum(send[direction * CAP + j], 0)


def slot_read(read, b):
    code = read[b]
    pair = code // (2 * CAP)
    lower = jnp.where(pair == 0, is_lower(0), jnp.where(pair == 1, is_lower(1), is_lower(2)))
    return jnp.where(lower, code ^ CAP, code)


def pick_blocks(send, values, slabs, ways):
    for slab, way in zip(slabs, ways):
        for j in range(CAP):
            slab[j] = values[slot_block(send, way, j)]


def stack_slabs(arrived, received):
    for way, slab in enumerate(arrived):
        for j in range(CAP):
            received[way * CAP + j] = slab[j]


def solve_rows(matrix, rhs, basis, disp, narrow, proj, i):
    per = ROWS // BLK
    part = jnp.dot(matrix[pl.ds(i * ROWS, ROWS), :], rhs[...], preferred_element_type=jnp.float32)
    for k in range(per):
        b = i * per + k
        mine = part[k * BLK : (k + 1) * BLK]
        disp[b] = mine
        narrow[b] = mine.astype(jnp.bfloat16)
        for w in range(mine.shape[1] // BLK):
            cols = slice(w * BLK, (w + 1) * BLK)
            proj[b : b + 1, cols] = jnp.sum(basis[b] * mine[:, cols], axis=0, keepdims=True)


def clear_rest(proj, blocks):
    proj[blocks:, :] = jnp.zeros((proj.shape[0] - blocks, proj.shape[1]), jnp.float32)


def basis_column(row):
    return jnp.broadcast_to(row, (BLK, BLK)).T


def first_solve_kernel(send, matrix, load, basis, disp, proj, basis_columns, *rest):
    slabs, (held, narrow, sems) = rest[:4], rest[4:]
    blocks = disp.shape[0]
    copies = [
        pltpu.make_async_copy(
            matrix.at[pl.ds(i * ROWS, ROWS)], held.at[pl.ds(i * ROWS, ROWS)], sems.at[i]
        )
        for i in range(held.shape[0] // ROWS)
    ]
    for copy in copies:
        copy.start()
    for b in range(blocks):
        basis_columns[b] = basis_column(basis[b : b + 1, :])
    for i, copy in enumerate(copies):
        copy.wait()
        solve_rows(held, load, basis_columns, disp, narrow, proj, i)
    clear_rest(proj, blocks)
    pick_blocks(send, narrow, slabs, range(4))


def next_solve_kernel(send, read, matrix, load, basis_columns, dual, *rest):
    arrived, (mult, disp, proj), rest = rest[:DIRS], rest[DIRS : DIRS + 3], rest[DIRS + 3 :]
    slabs, (narrow, received, rhs) = rest[:4], rest[4:]
    blocks = disp.shape[0]
    stack_slabs(arrived, received)
    for b in range(blocks):
        far = received[slot_read(read, b)]
        step = dual[b].astype(jnp.float32) - far.astype(jnp.float32)
        mult[b] = step
        rows = pl.ds(b * BLK, BLK)
        rhs[rows, :] = (load[rows, :].astype(jnp.float32) - step).astype(jnp.bfloat16)
    for i in range(blocks * BLK // ROWS):
        solve_rows(matrix, rhs, basis_columns, disp, narrow, proj, i)
    clear_rest(proj, blocks)
    pick_blocks(send, narrow, slabs, range(4))


def coarse_kernel(send, table, every, disp, basis_columns, corrected, near_rows, *rest):
    slabs, (ordered,) = rest[:2], rest[2:]
    here = lax.axis_index("sub")
    for t in range(every.shape[0]):
        ordered[t * WIDE : (t + 1) * WIDE, :] = every[t ^ here]
    rows = jnp.dot(
        table[...], ordered[...], preferred_element_type=jnp.float32, precision=HIGHEST
    )
    near_rows[...] = rows[WIDE:]
    for b in range(disp.shape[0]):
        for w in range(disp.shape[2] // BLK):
            cols = slice(w * BLK, (w + 1) * BLK)
            corrected[b, :, cols] = (
                disp[b, :, cols] + basis_columns[b] * rows[b : b + 1, cols]
            ).astype(jnp.bfloat16)
    pick_blocks(send, corrected, slabs, (4, 5))


def dirichlet_kernel(send, read, weights, matrix, corrected, far_basis, near_rows, *rest):
    arrived, dual, rest = rest[:DIRS], rest[DIRS], rest[DIRS + 1 :]
    slabs, (received, rows, rhs) = rest[:DIRS], rest[DIRS:]
    blocks, _, cases = corrected.shape
    stack_slabs(arrived, received)
    for k in range(NEAR):
        rows[k] = near_rows[k : k + 1, :]
    for k in range(NEAR, DIRS * CAP):
        rows[k] = jnp.zeros((1, cases), jnp.float32)
    for b in range(blocks):
        place, code = slot_read(read, b), read[b]
        for w in range(cases // BLK):
            cols = slice(w * BLK, (w + 1) * BLK)
            far = received[place, :, cols].astype(jnp.float32) + far_basis[b] * rows[code, :, cols]
            far = far.astype(jnp.bfloat16).astype(jnp.float32)
            gap = corrected[b, :, cols].astype(jnp.float32) - far
            rhs[b * BLK : (b + 1) * BLK, cols] = (gap * weights[b]).astype(jnp.bfloat16)
    per = ROWS // BLK
    for i in range(blocks // per):
        part = jnp.dot(
            matrix[pl.ds(i * ROWS, ROWS), :], rhs[...], preferred_element_type=jnp.float32
        )
        for k in range(per):
            b = i * per + k
            dual[b] = (part[k * BLK : (k + 1) * BLK] * weights[b]).astype(jnp.bfloat16)
    pick_blocks(send, dual, slabs, range(DIRS))


def finish_kernel(read, mult, dual, *rest):
    arrived, out, received = rest[:DIRS], rest[DIRS], rest[DIRS + 1]
    stack_slabs(arrived, received)
    for b in range(out.shape[0]):
        far = received[slot_read(read, b)]
        out[b] = mult[b] + (dual[b].astype(jnp.float32) - far.astype(jnp.float32))


def share_kernel(dofs, own_rows, share):
    height, order = own_rows.shape
    width = dofs.shape[1]
    here = lax.axis_index("sub")
    hot = (lax.broadcasted_iota(jnp.int32, (order, width), 0) == dofs[...]).astype(jnp.float32)
    columns = jnp.dot(
        own_rows[...].astype(jnp.bfloat16),
        hot.astype(jnp.bfloat16),
        preferred_element_type=jnp.float32,
    )
    mine = lax.broadcasted_iota(jnp.int32, (height, width), 0) + here * height
    rows = (mine == dofs[...]).astype(jnp.float32)
    share[...] = lax.dot_general(
        columns.astype(jnp.bfloat16),
        rows.astype(jnp.bfloat16),
        (((0,), (0,)), ((), ())),
        preferred_element_type=jnp.float32,
    ).astype(jnp.bfloat16)


def table_kernel(read, every_send, shares, every_basis, table, far_columns, hot):
    here = lax.axis_index("sub")
    subs = lax.axis_size("sub")
    width = shares.shape[1]
    blocks = far_columns.shape[0]
    lanes = lax.broadcasted_iota(jnp.int32, (1, width), 1)
    sources = [lax.rem(here - offset + subs, subs) for offset in OFFSETS]
    for b in range(WIDE):
        hot[b : b + 1, :] = (lanes == here * WIDE + b).astype(jnp.float32)
    for k in range(NEAR):
        source = sources[k // CAP]
        place = source * WIDE + every_send[source * NEAR + k]
        hot[WIDE + k : WIDE + k + 1, :] = (lanes == place).astype(jnp.float32)
    table[...] = jnp.dot(
        hot[...].astype(jnp.bfloat16), shares[...], preferred_element_type=jnp.float32
    )
    for b in range(blocks):
        code = jnp.minimum(read[b], NEAR - 1)
        direction = code // CAP
        source = sources[3]
        for d in range(3):
            source = jnp.where(direction == d, sources[d], source)
        block = every_send[source * NEAR + code]
        far_columns[b] = basis_column(every_basis[(source ^ here) * blocks + block])


def on_device(
    load_cases,
    inv_schur,
    schur_blocks,
    coarse_basis,
    coarse_map,
    multiplicity,
    recv_code,
    send_blocks,
    coarse_inv,
):
    dofs = inv_schur.shape[2]
    cases = load_cases.shape[3]
    blocks = dofs // BLK
    subs = lax.axis_size("sub")
    here = lax.axis_index("sub")
    solve_matrix = inv_schur[0, 0]
    dirichlet_matrix = schur_blocks[0, 0]
    load = load_cases[0, 0]
    basis = coarse_basis[0, 0].reshape(blocks, BLK)
    read = recv_code[0, 0]
    send = send_blocks[0, 0]
    weights = 1.0 / multiplicity[0, 0].astype(jnp.float32)
    whole = f32(blocks, BLK, cases)
    halved = bf16(blocks, BLK, cases)
    slab = bf16(CAP, BLK, cases)
    columns = f32(blocks, BLK, BLK)
    values = pltpu.VMEM(halved.shape, jnp.bfloat16)
    received = pltpu.VMEM((DIRS * CAP, BLK, cases), jnp.bfloat16)
    rhs = pltpu.VMEM((dofs, cases), jnp.bfloat16)

    disp, proj, basis_columns, *slabs = pl.pallas_call(
        first_solve_kernel,
        out_shape=[whole, f32(WIDE, cases), columns] + [slab] * 4,
        in_specs=[SMEM, HBM, VMEM, VMEM],
        out_specs=[VMEM] * 7,
        scratch_shapes=[
            pltpu.VMEM((dofs, dofs), jnp.bfloat16),
            values,
            pltpu.SemaphoreType.DMA((dofs // ROWS,)),
        ],
        compiler_params=PARAMS,
    )(send, solve_matrix, load, basis)

    lanes = -(-subs * WIDE // BLK) * BLK
    names = jnp.stack([jnp.pad(coarse_map[0, 0] + 1, (0, WIDE - blocks)), jnp.maximum(send[:NEAR], 0)])
    names = lax.dynamic_update_slice(
        jnp.zeros((2, lanes), jnp.float32), names.astype(jnp.float32), (0, here * WIDE)
    )
    told = gathered(jnp.concatenate([basis, names.reshape(-1, BLK)]))
    every_basis = told[:, :blocks].reshape(subs * blocks, 1, BLK)
    names = jnp.sum(told[:, blocks:], axis=0).reshape(2, lanes).astype(jnp.int32)
    share = pl.pallas_call(
        share_kernel,
        out_shape=bf16(lanes, lanes),
        in_specs=[VMEM] * 2,
        out_specs=VMEM,
        compiler_params=PARAMS,
    )(names[:1] - 1, coarse_inv[0])
    for bit in bits_of(subs):
        share = share + swapped(share, bit)
    table, far_columns = pl.pallas_call(
        table_kernel,
        out_shape=[f32(WIDE + NEAR, lanes), columns],
        in_specs=[SMEM, SMEM, VMEM, VMEM],
        out_specs=[VMEM] * 2,
        scratch_shapes=[pltpu.VMEM((WIDE + NEAR, lanes), jnp.float32)],
        compiler_params=PARAMS,
    )(read, names[1], share, every_basis)

    for iteration in range(ITERS):
        arrived = {way: exchanged(slabs[way], way) for way in ORDER[:4]}
        corrected, near_rows, *far_slabs = pl.pallas_call(
            coarse_kernel,
            out_shape=[halved, f32(NEAR, cases), slab, slab],
            in_specs=[SMEM] + [VMEM] * 4,
            out_specs=[VMEM] * 4,
            scratch_shapes=[pltpu.VMEM((lanes, cases), jnp.float32)],
            compiler_params=PARAMS,
        )(send, table, gathered(proj), disp, basis_columns)
        for way in ORDER[4:]:
            arrived[way] = exchanged(far_slabs[way - 4], way)
        dual, *slabs = pl.pallas_call(
            dirichlet_kernel,
            out_shape=[halved] + [slab] * DIRS,
            in_specs=[SMEM] * 3 + [VMEM] * (4 + DIRS),
            out_specs=[VMEM] * (1 + DIRS),
            scratch_shapes=[received, pltpu.VMEM((DIRS * CAP, 1, cases), jnp.float32), rhs],
            compiler_params=PARAMS,
        )(
            send, read, weights, dirichlet_matrix, corrected, far_columns, near_rows,
            *[arrived[way] for way in range(DIRS)],
        )
        arrived = {way: exchanged(slabs[way], way) for way in ORDER}
        arrived = [arrived[way] for way in range(DIRS)]
        if iteration + 1 < ITERS:
            mult, disp, proj, *slabs = pl.pallas_call(
                next_solve_kernel,
                out_shape=[whole, whole, f32(WIDE, cases)] + [slab] * 4,
                in_specs=[SMEM] * 2 + [VMEM] * (4 + DIRS),
                out_specs=[VMEM] * 7,
                scratch_shapes=[values, received, rhs],
                compiler_params=PARAMS,
            )(send, read, solve_matrix, load, basis_columns, dual, *arrived)
    out = pl.pallas_call(
        finish_kernel,
        out_shape=whole,
        in_specs=[SMEM] + [VMEM] * (2 + DIRS),
        out_specs=VMEM,
        scratch_shapes=[received],
        compiler_params=PARAMS,
    )(read, mult, dual, *arrived)
    return out.reshape(1, 1, dofs, cases)


def solution(mesh):
    split = P("group", "sub")
    return jax.shard_map(
        on_device, mesh=mesh, in_specs=(split,) * 9, out_specs=split, check_vma=False
    )
```

time: 206 us -> 150 us (0.73)
  blocking collectives: 39.3 us -> 0 us
  local copies, waits for them, and re-layouts: 40.8 us -> 6.68 us
  waiting for transfers between devices: 57.8 us -> 82.8 us
  matrix products: 18.1 us -> 0 us
  Pallas kernels: 0 us -> 17.7 us
  other arithmetic: 19.6 us -> 5.02 us
  starting transfers between devices: 28.8 us -> 36.1 us
    all_gather x3 -> x0, blocking collectives: 39.3 us -> none  [the longest x2 28.7 us: on_device(): every_projected = lax.all_gather(projected, 'sub', axis=0, tiled=True)]
    ppermute x24 -> x36, waiting for transfers between devices: 57.8 us -> 82.8 us  [the longest x24 51.2 us: exchanged(): return lax.ppermute(slab, axis, route)]
    gather x11 -> x0, local copies, waits for them, and re-layouts: 20.9 us -> none  [the longest x4 9.92 us: jump(): remote = jnp.take(received, read_codes, axis=0)]
    dot_general x6 -> x0, matrix products: 18.1 us -> none  [the longest x2 8.87 us: on_device(): jnp.dot(solve_matrix, residual_load, preferred_element_type=jnp.float32)]
    pallas_call x0 -> x9, Pallas kernels: none -> 17.7 us  [the longest x1 5.47 us: on_device(): pl.pallas_call(first_solve_kernel, out_shape=[whole, f32(WIDE, cases), co...]
    ppermute x24 -> x36, starting transfers between devices: 25.5 us -> 36.1 us  [the longest x24 26.2 us: exchanged(): return lax.ppermute(slab, axis, route)]
    select_n x6 -> x0, other arithmetic: 7.41 us -> none  [the longest x4 6.75 us: jump(): jnp.where((outgoing >= 0)[:, None, None], picked, jnp.zeros((), jnp.bfloa...]
    unnamed x36 -> x30, local copies, waits for them, and re-layouts: 13.5 us -> 6.51 us
  transfers between devices with their start and end apart: 25 -> 36, of which waited for: 8 -> 18; matrix products, arithmetic and copies ran while one was open for 7% -> 2% of each run, Pallas kernels for 0% -> 6%
where the time goes in v2:
time: 150 us; the launch traced here: 149 us
  waiting for transfers between devices  82.8 us (55%)
  starting transfers between devices  36.1 us (24%)
  Pallas kernels  17.7 us (12%)
  local copies, waits for them, and re-layouts  6.68 us (4%)
  other arithmetic  5.02 us (3%)
    ppermute x24, waiting for transfers between devices, exchanged(): return lax.ppermute(slab, axis, route)  51.2 us
    ppermute x12, waiting for transfers between devices, swapped(): return lax.ppermute(value, 'sub', [(i, i ^ bit) for i in range(count)])  31.6 us
    ppermute x24, starting transfers between devices, exchanged(): return lax.ppermute(slab, axis, route)  26.2 us
    ppermute x12, starting transfers between devices, swapped(): return lax.ppermute(value, 'sub', [(i, i ^ bit) for i in range(count)])  9.91 us
    unnamed x30, local copies, waits for them, and re-layouts  6.51 us
    pallas_call x1, Pallas kernels, on_device(): pl.pallas_call(first_solve_kernel, out_shape=[whole, f32(WIDE, cases), co...  5.47 us
    pallas_call x2, Pallas kernels, on_device(): pl.pallas_call(dirichlet_kernel, out_shape=[halved] + [slab] * DIRS, in_s...  4.78 us
  transfers between devices with their start and end apart: 36, of which 18 were waited for; matrix products, arithmetic and copies ran while one was open for 2% of the time, Pallas kernels for 6%

profile of v2, /device:TPU:0, one launch (start us, length us, event | category | flops | bytes accessed | tf_op | source)
XLA Modules:
  0.0 148.6 jit_solution(12582745382893634866)
XLA Ops:
  3.7 2.9 %collective-permute-start.1 = (f32[2,14,128]{2,1,0:T(8,128)S(1)}, f32[2,14,128]{2,1,0:T(8,128)S(1)}, u32[]{:S(2)}, u32[]{:S(2)}) collective-permute-start(f32[2,14,128]{2,1,0:T(8,128)S(1)} %pad_maximum_fusion.10), channel_id=1, source_target_pairs={{0,2},{1,3},{2,0},{3,1},{4,6},{5,7},{6,4},{7,5},{8,10},{9,11},{10,... | collective-permute-start | bytes 43016 | tf_op jit(solution)/shard_map/ppermute | solution.py:50
  6.6 2.3 %copy-done = bf16[1,1,1536,1536]{3,2,1,0:T(8,128)(2,1)S(1)} copy-done((bf16[1,1,1536,1536]{3,2,1,0:T(8,128)(2,1)S(1)}, bf16[1,1,1536,1536]{3,2,1,0:T(8,128)(2,1)}, u32[]{:S(2)}) %copy-start) | copy-done | bytes 4718616
  10.7 5.5 %shard_map.91 = (f32[12,128,256]{2,1,0:T(8,128)S(1)}, f32[16,256]{1,0:T(8,128)S(1)}, f32[12,128,128]{2,1,0:T(8,128)S(1)}, bf16[4,128,256]{2,1,0:T(8,128)(2,1)}, ...) custom-call(s32[24]{0:T(128)S(1)} %bitcast.45, ...), custom_call_target="tpu_custom_call" | custom-call | tf_op jit(solution)/shard_map/pallas_call | solution.py:277
  16.8 2.2 %collective-permute-start.10 = (bf16[4,128,256]{2,1,0:T(8,128)(2,1)}, bf16[4,128,256]{2,1,0:T(8,128)(2,1)S(1)}, u32[]{:S(2)}, u32[]{:S(2)}) collective-permute-start(bf16[4,128,256]{2,1,0:T(8,128)(2,1)} %get-tuple-element.51), channel_id=1, source_target_pairs={{0,7},{1,2},{2,1},{3,4},{4,3},{5,6},{6,5},{7,0},{8,15},{9,10},{10,... | collective-permute-start | bytes 786440 | tf_op jit(solution)/shard_map/ppermute | solution.py:45
  19.0 2.2 %collective-permute-start.2 = (f32[4,14,128]{2,1,0:T(8,128)S(1)}, f32[4,14,128]{2,1,0:T(8,128)S(1)}, u32[]{:S(2)}, u32[]{:S(2)}) collective-permute-start(f32[4,14,128]{2,1,0:T(8,128)S(1)} %pad_maximum_fusion.7), channel_id=1, source_target_pairs={{0,4},{1,5},{2,6},{3,7},{4,0},{5,1},{6,2},{7,3},{8,12},{9,13},{10,... | collective-permute-start | bytes 86024 | tf_op jit(solution)/shard_map/ppermute | solution.py:50
  21.6 8.2 %collective-permute-done.2 = f32[4,14,128]{2,1,0:T(8,128)S(1)} collective-permute-done((f32[4,14,128]{2,1,0:T(8,128)S(1)}, f32[4,14,128]{2,1,0:T(8,128)S(1)}, u32[]{:S(2)}, u32[]{:S(2)}) %collective-permute-start.2) | collective-permute-done | bytes 28704 | tf_op jit(solution)/shard_map/ppermute | solution.py:50
  30.3 2.6 %collective-permute-done.7 = f32[2,16,256]{2,1,0:T(8,128)S(1)} collective-permute-done((f32[2,16,256]{2,1,0:T(8,128)S(1)}, f32[2,16,256]{2,1,0:T(8,128)S(1)}, u32[]{:S(2)}, u32[]{:S(2)}) %collective-permute-start.7) | collective-permute-done | bytes 32800 | tf_op jit(solution)/shard_map/ppermute | solution.py:50
  33.5 2.1 %collective-permute-start.8 = (f32[4,16,256]{2,1,0:T(8,128)}, f32[4,16,256]{2,1,0:T(8,128)}, u32[]{:S(2)}, u32[]{:S(2)}) collective-permute-start(f32[4,16,256]{2,1,0:T(8,128)} %pad_maximum_fusion.5), channel_id=1, source_target_pairs={{0,4},{1,5},{2,6},{3,7},{4,0},{5,1},{6,2},{7,3},{8,12},{9,13},{10,... | collective-permute-start | bytes 196616 | tf_op jit(solution)/shard_map/ppermute | solution.py:50
  37.0 3.5 %collective-permute-done.4 = bf16[128,128]{1,0:T(8,128)(2,1)} collective-permute-done((bf16[128,128]{1,0:T(8,128)(2,1)}, bf16[128,128]{1,0:T(8,128)(2,1)}, u32[]{:S(2)}, u32[]{:S(2)}) %collective-permute-start.4) | collective-permute-done | bytes 32800 | tf_op jit(solution)/shard_map/ppermute | solution.py:50
  40.5 2.6 %collective-permute-start.12 = (bf16[4,128,256]{2,1,0:T(8,128)(2,1)S(1)}, bf16[4,128,256]{2,1,0:T(8,128)(2,1)S(1)}, u32[]{:S(2)}, u32[]{:S(2)}) collective-permute-start(bf16[4,128,256]{2,1,0:T(8,128)(2,1)S(1)} %get-tuple-element.53), channel_id=1, source_target_pairs={{0,6},{1,7},{2,4},{3,5},{4,2},{5,3},{6,0},{7,1},{8,14},{9,15},{10,... | collective-permute-start | bytes 786440 | tf_op jit(solution)/shard_map/ppermute | solution.py:45
  44.8 10.3 %collective-permute-done.5 = bf16[128,128]{1,0:T(8,128)(2,1)S(1)} collective-permute-done((bf16[128,128]{1,0:T(8,128)(2,1)S(1)}, bf16[128,128]{1,0:T(8,128)(2,1)S(1)}, u32[]{:S(2)}, u32[]{:S(2)}) %collective-permute-start.5) | collective-permute-done | bytes 32800 | tf_op jit(solution)/shard_map/ppermute | solution.py:50
  57.0 1.6 %collective-permute-start.13 = (bf16[4,128,256]{2,1,0:T(8,128)(2,1)S(1)}, bf16[4,128,256]{2,1,0:T(8,128)(2,1)S(1)}, u32[]{:S(2)}, u32[]{:S(2)}) collective-permute-start(bf16[4,128,256]{2,1,0:T(8,128)(2,1)S(1)} %get-tuple-element.54), channel_id=1, source_target_pairs={{0,8},{8,0},{16,24},{24,16},{1,9},{9,1},{17,25},{25,17},{2,10},{10... | collective-permute-start | bytes 786440 | tf_op jit(solution)/shard_map/ppermute | solution.py:45
  60.1 6.2 %collective-permute-done.13.rest_4_ = bf16[4,128,256]{2,1,0:T(8,128)(2,1)S(1)} collective-permute-done((bf16[4,128,256]{2,1,0:T(8,128)(2,1)S(1)}, bf16[4,128,256]{2,1,0:T(8,128)(2,1)S(1)}, u32[]{:S(2)}, u32[]{:S(2)}) %collective-permute-start.13) | collective-permute-done | bytes 262176 | tf_op jit(solution)/shard_map/ppermute | solution.py:45
  66.3 3.9 %collective-permute-done.14.rest_5_ = bf16[4,128,256]{2,1,0:T(8,128)(2,1)S(1)} collective-permute-done((bf16[4,128,256]{2,1,0:T(8,128)(2,1)S(1)}, bf16[4,128,256]{2,1,0:T(8,128)(2,1)S(1)}, u32[]{:S(2)}, u32[]{:S(2)}) %collective-permute-start.14) | collective-permute-done | bytes 262176 | tf_op jit(solution)/shard_map/ppermute | solution.py:45
  70.2 2.3 %copy-done.1 = bf16[1,1,1536,1536]{3,2,1,0:T(8,128)(2,1)S(1)} copy-done((bf16[1,1,1536,1536]{3,2,1,0:T(8,128)(2,1)S(1)}, bf16[1,1,1536,1536]{3,2,1,0:T(8,128)(2,1)}, u32[]{:S(2)}) %copy-start.1) | copy-done | bytes 4718616
  72.5 2.4 %shard_map.95 = (bf16[12,128,256]{2,1,0:T(8,128)(2,1)S(1)}, bf16[4,128,256]{2,1,0:T(8,128)(2,1)S(1)}, bf16[4,128,256]{2,1,0:T(8,128)(2,1)S(1)}, bf16[4,128,256]{...) custom-call(s32[24]{0:T(128)S(1)} %bitcast.47, ...), custom_call_target="tpu_custom_call" | custom-call | tf_op jit(solution)/shard_map/pallas_call | solution.py:328
  75.0 2.6 %collective-permute-start.16 = (bf16[4,128,256]{2,1,0:T(8,128)(2,1)S(1)}, bf16[4,128,256]{2,1,0:T(8,128)(2,1)S(1)}, u32[]{:S(2)}, u32[]{:S(2)}) collective-permute-start(bf16[4,128,256]{2,1,0:T(8,128)(2,1)S(1)} %get-tuple-element.58), channel_id=1, source_target_pairs={{0,7},{1,2},{2,1},{3,4},{4,3},{5,6},{6,5},{7,0},{8,15},{9,10},{10,... | collective-permute-start | bytes 786440 | tf_op jit(solution)/shard_map/ppermute | solution.py:45
  80.0 5.4 %collective-permute-done.16.rest_1_ = bf16[4,128,256]{2,1,0:T(8,128)(2,1)S(1)} collective-permute-done((bf16[4,128,256]{2,1,0:T(8,128)(2,1)S(1)}, bf16[4,128,256]{2,1,0:T(8,128)(2,1)S(1)}, u32[]{:S(2)}, u32[]{:S(2)}) %collective-permute-start.16) | collective-permute-done | bytes 262176 | tf_op jit(solution)/shard_map/ppermute | solution.py:45
  85.4 4.5 %collective-permute-done.17.rest_2_ = bf16[4,128,256]{2,1,0:T(8,128)(2,1)S(1)} collective-permute-done((bf16[4,128,256]{2,1,0:T(8,128)(2,1)S(1)}, bf16[4,128,256]{2,1,0:T(8,128)(2,1)S(1)}, u32[]{:S(2)}, u32[]{:S(2)}) %collective-permute-start.17) | collective-permute-done | bytes 262176 | tf_op jit(solution)/shard_map/ppermute | solution.py:45
  89.9 5.4 %collective-permute-done.18.rest_3_ = bf16[4,128,256]{2,1,0:T(8,128)(2,1)S(1)} collective-permute-done((bf16[4,128,256]{2,1,0:T(8,128)(2,1)S(1)}, bf16[4,128,256]{2,1,0:T(8,128)(2,1)S(1)}, u32[]{:S(2)}, u32[]{:S(2)}) %collective-permute-start.18) | collective-permute-done | bytes 262176 | tf_op jit(solution)/shard_map/ppermute | solution.py:45
  95.3 2.2 %shard_map.96 = (f32[12,128,256]{2,1,0:T(8,128)S(1)}, f32[12,128,256]{2,1,0:T(8,128)S(1)}, f32[16,256]{1,0:T(8,128)S(1)}, bf16[4,128,256]{2,1,0:T(8,128)(2,1)S(1...) custom-call(s32[24]{0:T(128)S(1)} %bitcast.48, ...), custom_call_target="tpu_custom_call" | custom-call | tf_op jit(solution)/shard_map/pallas_call | solution.py:342
  99.3 3.6 %collective-permute-done.22 = f32[2,16,256]{2,1,0:T(8,128)S(1)} collective-permute-done((f32[2,16,256]{2,1,0:T(8,128)S(1)}, f32[2,16,256]{2,1,0:T(8,128)S(1)}, u32[]{:S(2)}, u32[]{:S(2)}) %collective-permute-start.22) | collective-permute-done | bytes 32800 | tf_op jit(solution)/shard_map/ppermute | solution.py:50
  105.1 2.2 %collective-permute-start.27 = (bf16[4,128,256]{2,1,0:T(8,128)(2,1)S(1)}, bf16[4,128,256]{2,1,0:T(8,128)(2,1)S(1)}, u32[]{:S(2)}, u32[]{:S(2)}) collective-permute-start(bf16[4,128,256]{2,1,0:T(8,128)(2,1)S(1)} %get-tuple-element.71), channel_id=1, source_target_pairs={{0,6},{1,7},{2,4},{3,5},{4,2},{5,3},{6,0},{7,1},{8,14},{9,15},{10,... | collective-permute-start | bytes 786440 | tf_op jit(solution)/shard_map/ppermute | solution.py:45
  107.3 1.8 %collective-permute-done.23 = f32[4,16,256]{2,1,0:T(8,128)S(1)} collective-permute-done((f32[4,16,256]{2,1,0:T(8,128)S(1)}, f32[4,16,256]{2,1,0:T(8,128)S(1)}, u32[]{:S(2)}, u32[]{:S(2)}) %collective-permute-start.23) | collective-permute-done | bytes 65568 | tf_op jit(solution)/shard_map/ppermute | solution.py:50
  113.5 11.1 %collective-permute-done.26.rest_2_ = bf16[4,128,256]{2,1,0:T(8,128)(2,1)S(1)} collective-permute-done((bf16[4,128,256]{2,1,0:T(8,128)(2,1)S(1)}, bf16[4,128,256]{2,1,0:T(8,128)(2,1)S(1)}, u32[]{:S(2)}, u32[]{:S(2)}) %collective-permute-start.26) | collective-permute-done | bytes 262176 | tf_op jit(solution)/shard_map/ppermute | solution.py:45
  124.6 2.4 %shard_map.98 = (bf16[12,128,256]{2,1,0:T(8,128)(2,1)S(1)}, bf16[4,128,256]{2,1,0:T(8,128)(2,1)S(1)}, bf16[4,128,256]{2,1,0:T(8,128)(2,1)S(1)}, bf16[4,128,256]{...) custom-call(s32[24]{0:T(128)S(1)} %bitcast.50, ...), custom_call_target="tpu_custom_call" | custom-call | tf_op jit(solution)/shard_map/pallas_call | solution.py:328
  127.1 2.1 %collective-permute-start.31 = (bf16[4,128,256]{2,1,0:T(8,128)(2,1)S(1)}, bf16[4,128,256]{2,1,0:T(8,128)(2,1)S(1)}, u32[]{:S(2)}, u32[]{:S(2)}) collective-permute-start(bf16[4,128,256]{2,1,0:T(8,128)(2,1)S(1)} %get-tuple-element.76), channel_id=1, source_target_pairs={{0,7},{1,2},{2,1},{3,4},{4,3},{5,6},{6,5},{7,0},{8,15},{9,10},{10,... | collective-permute-start | bytes 786440 | tf_op jit(solution)/shard_map/ppermute | solution.py:45
  129.2 2.2 %collective-permute-start.33 = (bf16[4,128,256]{2,1,0:T(8,128)(2,1)S(1)}, bf16[4,128,256]{2,1,0:T(8,128)(2,1)S(1)}, u32[]{:S(2)}, u32[]{:S(2)}) collective-permute-start(bf16[4,128,256]{2,1,0:T(8,128)(2,1)S(1)} %get-tuple-element.78), channel_id=1, source_target_pairs={{0,6},{1,7},{2,4},{3,5},{4,2},{5,3},{6,0},{7,1},{8,14},{9,15},{10,... | collective-permute-start | bytes 786440 | tf_op jit(solution)/shard_map/ppermute | solution.py:45
  133.4 4.2 %collective-permute-done.31.rest_1_ = bf16[4,128,256]{2,1,0:T(8,128)(2,1)S(1)} collective-permute-done((bf16[4,128,256]{2,1,0:T(8,128)(2,1)S(1)}, bf16[4,128,256]{2,1,0:T(8,128)(2,1)S(1)}, u32[]{:S(2)}, u32[]{:S(2)}) %collective-permute-start.31) | collective-permute-done | bytes 262176 | tf_op jit(solution)/shard_map/ppermute | solution.py:45
  137.5 5.5 %collective-permute-done.32.rest_2_ = bf16[4,128,256]{2,1,0:T(8,128)(2,1)S(1)} collective-permute-done((bf16[4,128,256]{2,1,0:T(8,128)(2,1)S(1)}, bf16[4,128,256]{2,1,0:T(8,128)(2,1)S(1)}, u32[]{:S(2)}, u32[]{:S(2)}) %collective-permute-start.32) | collective-permute-done | bytes 262176 | tf_op jit(solution)/shard_map/ppermute | solution.py:45
  143.1 3.5 %collective-permute-done.33.rest_3_ = bf16[4,128,256]{2,1,0:T(8,128)(2,1)S(1)} collective-permute-done((bf16[4,128,256]{2,1,0:T(8,128)(2,1)S(1)}, bf16[4,128,256]{2,1,0:T(8,128)(2,1)S(1)}, u32[]{:S(2)}, u32[]{:S(2)}) %collective-permute-start.33) | collective-permute-done | bytes 262176 | tf_op jit(solution)/shard_map/ppermute | solution.py:45
  146.6 2.0 %shard_map.99 = f32[12,128,256]{2,1,0:T(8,128)} custom-call(s32[12]{0:T(128)S(1)} %bitcast.55, f32[12,128,256]{2,1,0:T(8,128)S(1)} %get-tuple-element.63.mult, bf16[12,128,256]{2,1,0:T(8,128)(2,1)S(1)} %get-tuple-element.74.dual, bf16[4,128,256]{2,1,0:T(8,128)(2,1)S(1)} %collective-permute-done.30.rest_0_, ...), custom_call_target="tpu_custom_call" | custom-call | tf_op jit(solution)/shard_map/pallas_call | solution.py:350
  (106 shorter events, 26.9 us)
Async XLA Ops:
  3.7 15.3 %collective-permute-start.1 = (f32[2,14,128]{2,1,0:T(8,128)S(1)}, f32[2,14,128]{2,1,0:T(8,128)S(1)}, u32[]{:S(2)}, u32[]{:S(2)}) collective-permute-start(f32[2,14,128]{2,1,0:T(8,128)S(1)} %pad_maximum_fusion.10), channel_id=1, source_target_pairs={{0,2},{1,3},{2,0},{3,1},{4,6},{5,7},{6,4},{7,5},{8,10},{9,11},{10,... | collective-permute-start | bytes 43016 | tf_op jit(solution)/shard_map/ppermute | solution.py:50
  16.2 5.0 %collective-permute-start.6 = (f32[1,16,256]{2,1,0:T(8,128)S(1)}, f32[1,16,256]{2,1,0:T(8,128)S(1)}, u32[]{:S(2)}, u32[]{:S(2)}) collective-permute-start(f32[1,16,256]{2,1,0:T(8,128)S(1)} %bitcast.35), channel_id=1, source_target_pairs={{0,1},{1,0},{2,3},{3,2},{4,5},{5,4},{6,7},{7,6},{8,9},{9,8},{10,11... | collective-permute-start | bytes 49160 | tf_op jit(solution)/shard_map/ppermute | solution.py:50
  16.3 42.3 %collective-permute-start.9 = (bf16[4,128,256]{2,1,0:T(8,128)(2,1)}, bf16[4,128,256]{2,1,0:T(8,128)(2,1)S(1)}, u32[]{:S(2)}, u32[]{:S(2)}) collective-permute-start(bf16[4,128,256]{2,1,0:T(8,128)(2,1)} %get-tuple-element.50), channel_id=1, source_target_pairs={{0,1},{1,0},{2,3},{3,2},{4,5},{5,4},{6,7},{7,6},{8,9},{9,8},{10,11... | collective-permute-start | bytes 786440 | tf_op jit(solution)/shard_map/ppermute | solution.py:45
  16.8 43.3 %collective-permute-start.10 = (bf16[4,128,256]{2,1,0:T(8,128)(2,1)}, bf16[4,128,256]{2,1,0:T(8,128)(2,1)S(1)}, u32[]{:S(2)}, u32[]{:S(2)}) collective-permute-start(bf16[4,128,256]{2,1,0:T(8,128)(2,1)} %get-tuple-element.51), channel_id=1, source_target_pairs={{0,7},{1,2},{2,1},{3,4},{4,3},{5,6},{6,5},{7,0},{8,15},{9,10},{10,... | collective-permute-start | bytes 786440 | tf_op jit(solution)/shard_map/ppermute | solution.py:45
  19.0 41.1 %collective-permute-start.11 = (bf16[4,128,256]{2,1,0:T(8,128)(2,1)}, bf16[4,128,256]{2,1,0:T(8,128)(2,1)S(1)}, u32[]{:S(2)}, u32[]{:S(2)}) collective-permute-start(bf16[4,128,256]{2,1,0:T(8,128)(2,1)} %get-tuple-element.52), channel_id=1, source_target_pairs={{0,2},{1,3},{2,0},{3,1},{4,6},{5,7},{6,4},{7,5},{8,10},{9,11},{10,... | collective-permute-start | bytes 786440 | tf_op jit(solution)/shard_map/ppermute | solution.py:45
  19.0 10.8 %collective-permute-start.2 = (f32[4,14,128]{2,1,0:T(8,128)S(1)}, f32[4,14,128]{2,1,0:T(8,128)S(1)}, u32[]{:S(2)}, u32[]{:S(2)}) collective-permute-start(f32[4,14,128]{2,1,0:T(8,128)S(1)} %pad_maximum_fusion.7), channel_id=1, source_target_pairs={{0,4},{1,5},{2,6},{3,7},{4,0},{5,1},{6,2},{7,3},{8,12},{9,13},{10,... | collective-permute-start | bytes 86024 | tf_op jit(solution)/shard_map/ppermute | solution.py:50
  21.2 11.7 %collective-permute-start.7 = (f32[2,16,256]{2,1,0:T(8,128)S(1)}, f32[2,16,256]{2,1,0:T(8,128)S(1)}, u32[]{:S(2)}, u32[]{:S(2)}) collective-permute-start(f32[2,16,256]{2,1,0:T(8,128)S(1)} %pad_maximum_fusion.8), channel_id=1, source_target_pairs={{0,2},{1,3},{2,0},{3,1},{4,6},{5,7},{6,4},{7,5},{8,10},{9,11},{10,... | collective-permute-start | bytes 98312 | tf_op jit(solution)/shard_map/ppermute | solution.py:50
  30.3 5.4 %collective-permute-start.3 = (bf16[128,128]{1,0:T(8,128)(2,1)S(1)}, bf16[128,128]{1,0:T(8,128)(2,1)S(1)}, u32[]{:S(2)}, u32[]{:S(2)}) collective-permute-start(bf16[128,128]{1,0:T(8,128)(2,1)S(1)} %shard_map.92), channel_id=1, source_target_pairs={{0,1},{1,0},{2,3},{3,2},{4,5},{5,4},{6,7},{7,6},{8,9},{9,8},{10,11... | collective-permute-start | bytes 98312 | tf_op jit(solution)/shard_map/ppermute | solution.py:50
  33.5 10.3 %collective-permute-start.8 = (f32[4,16,256]{2,1,0:T(8,128)}, f32[4,16,256]{2,1,0:T(8,128)}, u32[]{:S(2)}, u32[]{:S(2)}) collective-permute-start(f32[4,16,256]{2,1,0:T(8,128)} %pad_maximum_fusion.5), channel_id=1, source_target_pairs={{0,4},{1,5},{2,6},{3,7},{4,0},{5,1},{6,2},{7,3},{8,12},{9,13},{10,... | collective-permute-start | bytes 196616 | tf_op jit(solution)/shard_map/ppermute | solution.py:50
  40.5 19.6 %collective-permute-start.12 = (bf16[4,128,256]{2,1,0:T(8,128)(2,1)S(1)}, bf16[4,128,256]{2,1,0:T(8,128)(2,1)S(1)}, u32[]{:S(2)}, u32[]{:S(2)}) collective-permute-start(bf16[4,128,256]{2,1,0:T(8,128)(2,1)S(1)} %get-tuple-element.53), channel_id=1, source_target_pairs={{0,6},{1,7},{2,4},{3,5},{4,2},{5,3},{6,0},{7,1},{8,14},{9,15},{10,... | collective-permute-start | bytes 786440 | tf_op jit(solution)/shard_map/ppermute | solution.py:45
  43.9 11.3 %collective-permute-start.5 = (bf16[128,128]{1,0:T(8,128)(2,1)S(1)}, bf16[128,128]{1,0:T(8,128)(2,1)S(1)}, u32[]{:S(2)}, u32[]{:S(2)}) collective-permute-start(bf16[128,128]{1,0:T(8,128)(2,1)S(1)} %add.25), channel_id=1, source_target_pairs={{0,4},{1,5},{2,6},{3,7},{4,0},{5,1},{6,2},{7,3},{8,12},{9,13},{10,... | collective-permute-start | bytes 98312 | tf_op jit(solution)/shard_map/ppermute | solution.py:50
  57.0 9.3 %collective-permute-start.13 = (bf16[4,128,256]{2,1,0:T(8,128)(2,1)S(1)}, bf16[4,128,256]{2,1,0:T(8,128)(2,1)S(1)}, u32[]{:S(2)}, u32[]{:S(2)}) collective-permute-start(bf16[4,128,256]{2,1,0:T(8,128)(2,1)S(1)} %get-tuple-element.54), channel_id=1, source_target_pairs={{0,8},{8,0},{16,24},{24,16},{1,9},{9,1},{17,25},{25,17},{2,10},{10... | collective-permute-start | bytes 786440 | tf_op jit(solution)/shard_map/ppermute | solution.py:45
  58.6 11.6 %collective-permute-start.14 = (bf16[4,128,256]{2,1,0:T(8,128)(2,1)S(1)}, bf16[4,128,256]{2,1,0:T(8,128)(2,1)S(1)}, u32[]{:S(2)}, u32[]{:S(2)}) collective-permute-start(bf16[4,128,256]{2,1,0:T(8,128)(2,1)S(1)} %get-tuple-element.55), channel_id=1, source_target_pairs={{0,24},{8,16},{16,8},{24,0},{1,25},{9,17},{17,9},{25,1},{2,26},{10... | collective-permute-start | bytes 786440 | tf_op jit(solution)/shard_map/ppermute | solution.py:45
  74.9 4.6 %collective-permute-start.15 = (bf16[4,128,256]{2,1,0:T(8,128)(2,1)S(1)}, bf16[4,128,256]{2,1,0:T(8,128)(2,1)S(1)}, u32[]{:S(2)}, u32[]{:S(2)}) collective-permute-start(bf16[4,128,256]{2,1,0:T(8,128)(2,1)S(1)} %get-tuple-element.57), channel_id=1, source_target_pairs={{0,1},{1,0},{2,3},{3,2},{4,5},{5,4},{6,7},{7,6},{8,9},{9,8},{10,11... | collective-permute-start | bytes 786440 | tf_op jit(solution)/shard_map/ppermute | solution.py:45
  75.0 10.4 %collective-permute-start.16 = (bf16[4,128,256]{2,1,0:T(8,128)(2,1)S(1)}, bf16[4,128,256]{2,1,0:T(8,128)(2,1)S(1)}, u32[]{:S(2)}, u32[]{:S(2)}) collective-permute-start(bf16[4,128,256]{2,1,0:T(8,128)(2,1)S(1)} %get-tuple-element.58), channel_id=1, source_target_pairs={{0,7},{1,2},{2,1},{3,4},{4,3},{5,6},{6,5},{7,0},{8,15},{9,10},{10,... | collective-permute-start | bytes 786440 | tf_op jit(solution)/shard_map/ppermute | solution.py:45
  77.6 12.3 %collective-permute-start.17 = (bf16[4,128,256]{2,1,0:T(8,128)(2,1)S(1)}, bf16[4,128,256]{2,1,0:T(8,128)(2,1)S(1)}, u32[]{:S(2)}, u32[]{:S(2)}) collective-permute-start(bf16[4,128,256]{2,1,0:T(8,128)(2,1)S(1)} %get-tuple-element.59), channel_id=1, source_target_pairs={{0,2},{1,3},{2,0},{3,1},{4,6},{5,7},{6,4},{7,5},{8,10},{9,11},{10,... | collective-permute-start | bytes 786440 | tf_op jit(solution)/shard_map/ppermute | solution.py:45
  77.6 17.7 %collective-permute-start.18 = (bf16[4,128,256]{2,1,0:T(8,128)(2,1)S(1)}, bf16[4,128,256]{2,1,0:T(8,128)(2,1)S(1)}, u32[]{:S(2)}, u32[]{:S(2)}) collective-permute-start(bf16[4,128,256]{2,1,0:T(8,128)(2,1)S(1)} %get-tuple-element.60), channel_id=1, source_target_pairs={{0,6},{1,7},{2,4},{3,5},{4,2},{5,3},{6,0},{7,1},{8,14},{9,15},{10,... | collective-permute-start | bytes 786440 | tf_op jit(solution)/shard_map/ppermute | solution.py:45
  78.0 17.3 %collective-permute-start.19 = (bf16[4,128,256]{2,1,0:T(8,128)(2,1)S(1)}, bf16[4,128,256]{2,1,0:T(8,128)(2,1)S(1)}, u32[]{:S(2)}, u32[]{:S(2)}) collective-permute-start(bf16[4,128,256]{2,1,0:T(8,128)(2,1)S(1)} %get-tuple-element.61), channel_id=1, source_target_pairs={{0,8},{8,0},{16,24},{24,16},{1,9},{9,1},{17,25},{25,17},{2,10},{10... | collective-permute-start | bytes 786440 | tf_op jit(solution)/shard_map/ppermute | solution.py:45
  79.5 15.8 %collective-permute-start.20 = (bf16[4,128,256]{2,1,0:T(8,128)(2,1)S(1)}, bf16[4,128,256]{2,1,0:T(8,128)(2,1)S(1)}, u32[]{:S(2)}, u32[]{:S(2)}) collective-permute-start(bf16[4,128,256]{2,1,0:T(8,128)(2,1)S(1)} %get-tuple-element.62), channel_id=1, source_target_pairs={{0,24},{8,16},{16,8},{24,0},{1,25},{9,17},{17,9},{25,1},{2,26},{10... | collective-permute-start | bytes 786440 | tf_op jit(solution)/shard_map/ppermute | solution.py:45
  99.0 12.6 %collective-permute-start.24 = (bf16[4,128,256]{2,1,0:T(8,128)(2,1)S(1)}, bf16[4,128,256]{2,1,0:T(8,128)(2,1)S(1)}, u32[]{:S(2)}, u32[]{:S(2)}) collective-permute-start(bf16[4,128,256]{2,1,0:T(8,128)(2,1)S(1)} %get-tuple-element.68), channel_id=1, source_target_pairs={{0,1},{1,0},{2,3},{3,2},{4,5},{5,4},{6,7},{7,6},{8,9},{9,8},{10,11... | collective-permute-start | bytes 786440 | tf_op jit(solution)/shard_map/ppermute | solution.py:45
  102.9 6.2 %collective-permute-start.23 = (f32[4,16,256]{2,1,0:T(8,128)S(1)}, f32[4,16,256]{2,1,0:T(8,128)S(1)}, u32[]{:S(2)}, u32[]{:S(2)}) collective-permute-start(f32[4,16,256]{2,1,0:T(8,128)S(1)} %pad_maximum_fusion.6), channel_id=1, source_target_pairs={{0,4},{1,5},{2,6},{3,7},{4,0},{5,1},{6,2},{7,3},{8,12},{9,13},{10,... | collective-permute-start | bytes 196616 | tf_op jit(solution)/shard_map/ppermute | solution.py:50
  103.1 10.4 %collective-permute-start.25 = (bf16[4,128,256]{2,1,0:T(8,128)(2,1)S(1)}, bf16[4,128,256]{2,1,0:T(8,128)(2,1)S(1)}, u32[]{:S(2)}, u32[]{:S(2)}) collective-permute-start(bf16[4,128,256]{2,1,0:T(8,128)(2,1)S(1)} %get-tuple-element.69), channel_id=1, source_target_pairs={{0,7},{1,2},{2,1},{3,4},{4,3},{5,6},{6,5},{7,0},{8,15},{9,10},{10,... | collective-permute-start | bytes 786440 | tf_op jit(solution)/shard_map/ppermute | solution.py:45
  104.4 20.2 %collective-permute-start.26 = (bf16[4,128,256]{2,1,0:T(8,128)(2,1)S(1)}, bf16[4,128,256]{2,1,0:T(8,128)(2,1)S(1)}, u32[]{:S(2)}, u32[]{:S(2)}) collective-permute-start(bf16[4,128,256]{2,1,0:T(8,128)(2,1)S(1)} %get-tuple-element.70), channel_id=1, source_target_pairs={{0,2},{1,3},{2,0},{3,1},{4,6},{5,7},{6,4},{7,5},{8,10},{9,11},{10,... | collective-permute-start | bytes 786440 | tf_op jit(solution)/shard_map/ppermute | solution.py:45
  105.1 19.4 %collective-permute-start.27 = (bf16[4,128,256]{2,1,0:T(8,128)(2,1)S(1)}, bf16[4,128,256]{2,1,0:T(8,128)(2,1)S(1)}, u32[]{:S(2)}, u32[]{:S(2)}) collective-permute-start(bf16[4,128,256]{2,1,0:T(8,128)(2,1)S(1)} %get-tuple-element.71), channel_id=1, source_target_pairs={{0,6},{1,7},{2,4},{3,5},{4,2},{5,3},{6,0},{7,1},{8,14},{9,15},{10,... | collective-permute-start | bytes 786440 | tf_op jit(solution)/shard_map/ppermute | solution.py:45
  110.1 14.5 %collective-permute-start.28 = (bf16[4,128,256]{2,1,0:T(8,128)(2,1)S(1)}, bf16[4,128,256]{2,1,0:T(8,128)(2,1)S(1)}, u32[]{:S(2)}, u32[]{:S(2)}) collective-permute-start(bf16[4,128,256]{2,1,0:T(8,128)(2,1)S(1)} %get-tuple-element.72), channel_id=1, source_target_pairs={{0,8},{8,0},{16,24},{24,16},{1,9},{9,1},{17,25},{25,17},{2,10},{10... | collective-permute-start | bytes 786440 | tf_op jit(solution)/shard_map/ppermute | solution.py:45
  111.6 12.9 %collective-permute-start.29 = (bf16[4,128,256]{2,1,0:T(8,128)(2,1)S(1)}, bf16[4,128,256]{2,1,0:T(8,128)(2,1)S(1)}, u32[]{:S(2)}, u32[]{:S(2)}) collective-permute-start(bf16[4,128,256]{2,1,0:T(8,128)(2,1)S(1)} %get-tuple-element.73), channel_id=1, source_target_pairs={{0,24},{8,16},{16,8},{24,0},{1,25},{9,17},{17,9},{25,1},{2,26},{10... | collective-permute-start | bytes 786440 | tf_op jit(solution)/shard_map/ppermute | solution.py:45
  127.0 5.9 %collective-permute-start.30 = (bf16[4,128,256]{2,1,0:T(8,128)(2,1)S(1)}, bf16[4,128,256]{2,1,0:T(8,128)(2,1)S(1)}, u32[]{:S(2)}, u32[]{:S(2)}) collective-permute-start(bf16[4,128,256]{2,1,0:T(8,128)(2,1)S(1)} %get-tuple-element.75), channel_id=1, source_target_pairs={{0,1},{1,0},{2,3},{3,2},{4,5},{5,4},{6,7},{7,6},{8,9},{9,8},{10,11... | collective-permute-start | bytes 786440 | tf_op jit(solution)/shard_map/ppermute | solution.py:45
  127.1 10.5 %collective-permute-start.31 = (bf16[4,128,256]{2,1,0:T(8,128)(2,1)S(1)}, bf16[4,128,256]{2,1,0:T(8,128)(2,1)S(1)}, u32[]{:S(2)}, u32[]{:S(2)}) collective-permute-start(bf16[4,128,256]{2,1,0:T(8,128)(2,1)S(1)} %get-tuple-element.76), channel_id=1, source_target_pairs={{0,7},{1,2},{2,1},{3,4},{4,3},{5,6},{6,5},{7,0},{8,15},{9,10},{10,... | collective-permute-start | bytes 786440 | tf_op jit(solution)/shard_map/ppermute | solution.py:45
  129.1 13.9 %collective-permute-start.32 = (bf16[4,128,256]{2,1,0:T(8,128)(2,1)S(1)}, bf16[4,128,256]{2,1,0:T(8,128)(2,1)S(1)}, u32[]{:S(2)}, u32[]{:S(2)}) collective-permute-start(bf16[4,128,256]{2,1,0:T(8,128)(2,1)S(1)} %get-tuple-element.77), channel_id=1, source_target_pairs={{0,2},{1,3},{2,0},{3,1},{4,6},{5,7},{6,4},{7,5},{8,10},{9,11},{10,... | collective-permute-start | bytes 786440 | tf_op jit(solution)/shard_map/ppermute | solution.py:45
  129.2 17.4 %collective-permute-start.33 = (bf16[4,128,256]{2,1,0:T(8,128)(2,1)S(1)}, bf16[4,128,256]{2,1,0:T(8,128)(2,1)S(1)}, u32[]{:S(2)}, u32[]{:S(2)}) collective-permute-start(bf16[4,128,256]{2,1,0:T(8,128)(2,1)S(1)} %get-tuple-element.78), channel_id=1, source_target_pairs={{0,6},{1,7},{2,4},{3,5},{4,2},{5,3},{6,0},{7,1},{8,14},{9,15},{10,... | collective-permute-start | bytes 786440 | tf_op jit(solution)/shard_map/ppermute | solution.py:45
  131.4 15.2 %collective-permute-start.34 = (bf16[4,128,256]{2,1,0:T(8,128)(2,1)S(1)}, bf16[4,128,256]{2,1,0:T(8,128)(2,1)S(1)}, u32[]{:S(2)}, u32[]{:S(2)}) collective-permute-start(bf16[4,128,256]{2,1,0:T(8,128)(2,1)S(1)} %get-tuple-element.79), channel_id=1, source_target_pairs={{0,8},{8,0},{16,24},{24,16},{1,9},{9,1},{17,25},{25,17},{2,10},{10... | collective-permute-start | bytes 786440 | tf_op jit(solution)/shard_map/ppermute | solution.py:45
  132.9 13.7 %collective-permute-start.35 = (bf16[4,128,256]{2,1,0:T(8,128)(2,1)S(1)}, bf16[4,128,256]{2,1,0:T(8,128)(2,1)S(1)}, u32[]{:S(2)}, u32[]{:S(2)}) collective-permute-start(bf16[4,128,256]{2,1,0:T(8,128)(2,1)S(1)} %get-tuple-element.80), channel_id=1, source_target_pairs={{0,24},{8,16},{16,8},{24,0},{1,25},{9,17},{17,9},{25,1},{2,26},{10... | collective-permute-start | bytes 786440 | tf_op jit(solution)/shard_map/ppermute | solution.py:45
  (19 other events, 301.7 us)

commit v3 on v2

v3 whole, which is shorter than its diff:
```python
import functools

import jax
import jax.numpy as jnp
from jax import lax
from jax.experimental import pallas as pl
from jax.experimental.pallas import tpu as pltpu
from jax.sharding import PartitionSpec as P

BLK = 128
DIRS = 6
CAP = 4
NEAR = 4 * CAP
ITERS = 2
ROWS = 512
EXCHANGES = (("sub", 1), ("sub", 2), ("group", 1))
OFFSETS = (1, -1, 2, -2)
ORDER = (3, 2, 1, 0, 4, 5)
HIGHEST = lax.Precision.HIGHEST
VMEM = pl.BlockSpec(memory_space=pltpu.VMEM)
SMEM = pl.BlockSpec(memory_space=pltpu.SMEM)
HBM = pl.BlockSpec(memory_space=pltpu.HBM)
MIB = 1024 * 1024
PARAMS = pltpu.CompilerParams(vmem_limit_bytes=20 * MIB)


def f32(*shape):
    return jax.ShapeDtypeStruct(shape, jnp.float32)


def bf16(*shape):
    return jax.ShapeDtypeStruct(shape, jnp.bfloat16)


def in_hbm(array):
    return pltpu.with_memory_space_constraint(array, pltpu.HBM)


def is_lower(pair):
    axis, distance = EXCHANGES[pair]
    return (lax.axis_index(axis) // distance) % 2 == 0


def exchanged(slab, way):
    axis, distance = EXCHANGES[way // 2]
    count = lax.axis_size(axis)
    route = []
    for i in range(count):
        upward = (i // distance) % 2 == way % 2
        route.append((i, (i + distance if upward else i - distance) % count))
    return lax.ppermute(slab, axis, route)


def swapped(value, mask):
    count = lax.axis_size("sub")
    return lax.ppermute(value, "sub", [(i, i ^ mask) for i in range(count)])


def to_chips(chunks):
    return [chunks[0]] + [swapped(chunk, 2 * p) for p, chunk in enumerate(chunks) if p]


def slot_block(send, way, j):
    direction = jnp.where(is_lower(way // 2), way, way ^ 1)
    return jnp.maximum(send[direction * CAP + j], 0)


def slot_read(read, b):
    code = read[b]
    pair = code // (2 * CAP)
    lower = jnp.where(pair == 0, is_lower(0), jnp.where(pair == 1, is_lower(1), is_lower(2)))
    return jnp.where(lower, code ^ CAP, code)


def pick_blocks(send, values, slabs, ways):
    for slab, way in zip(slabs, ways):
        for j in range(CAP):
            slab[j] = values[slot_block(send, way, j)]


def stack_slabs(arrived, received):
    for way, slab in zip(ORDER, arrived):
        for j in range(CAP):
            received[way * CAP + j] = slab[j]


def as_column(row):
    return jnp.broadcast_to(row, (BLK, BLK)).T


def column_parts(cases):
    return [slice(w * BLK, (w + 1) * BLK) for w in range(cases // BLK)]


def matrix_copies(matrix, held, sems):
    return [
        pltpu.make_async_copy(
            matrix.at[pl.ds(i * ROWS, ROWS)], held.at[pl.ds(i * ROWS, ROWS)], sems.at[i]
        )
        for i in range(held.shape[0] // ROWS)
    ]


def each_rows(copies, matrix, rhs, consume):
    per = ROWS // BLK
    for i in range(matrix.shape[0] // ROWS):
        if copies:
            copies[i].wait()
            if i + 2 < len(copies):
                copies[i + 2].start()
        part = jnp.dot(
            matrix[pl.ds(i * ROWS, ROWS), :], rhs[...], preferred_element_type=jnp.float32
        )
        for k in range(per):
            consume(i * per + k, part[k * BLK : (k + 1) * BLK])


def solve(copies, matrix, rhs, columns, disp, narrow, proj):
    blocks = disp.shape[0]

    def consume(b, mine):
        disp[b] = mine
        narrow[b] = mine.astype(jnp.bfloat16)
        for cols in column_parts(mine.shape[1]):
            proj[b : b + 1, cols] = jnp.sum(columns[b] * mine[:, cols], axis=0, keepdims=True)

    proj[blocks:, :] = jnp.zeros((proj.shape[0] - blocks, proj.shape[1]), jnp.float32)
    each_rows(copies, matrix, rhs, consume)


def tell(wide, coarse_map, send, basis, told):
    subs = lax.axis_size("sub")
    here = lax.axis_index("sub")
    blocks = basis.shape[0]
    tall = (told.shape[0] - NEAR) // 2
    place = lax.broadcasted_iota(jnp.int32, (tall, BLK), 0) * BLK + lax.broadcasted_iota(
        jnp.int32, (tall, BLK), 1
    )
    own = jnp.zeros((tall, BLK), jnp.int32)
    for b in range(blocks):
        own = jnp.where(place == here * wide + b, coarse_map[0, b] + 1, own)
    theirs = jnp.zeros((tall, BLK), jnp.int32)
    for k in range(NEAR):
        block = jnp.maximum(send[0, k], 0)
        reader = lax.rem(here + OFFSETS[k // CAP] + subs, subs)
        theirs = jnp.where(place == reader * wide + k, coarse_map[0, block] + 1, theirs)
        told[k : k + 1, :] = basis[block]
    told[NEAR : NEAR + tall, :] = own.astype(jnp.float32)
    told[NEAR + tall :, :] = theirs.astype(jnp.float32)


def first_solve_kernel(wide, send, coarse_map, matrix, load, basis, disp, proj, columns, told, *rest):
    slabs, rest = rest[:4], rest[4:]
    held, rhs, narrow, send_held, map_held, basis_held, rows, sems, more_sems = rest
    blocks = disp.shape[0]
    copies = matrix_copies(matrix, held, sems)
    pairs = ((send, send_held), (coarse_map, map_held), (basis, basis_held), (load, rhs))
    small = [
        pltpu.make_async_copy(source, target, more_sems.at[i])
        for i, (source, target) in enumerate(pairs)
    ]
    for copy in small + copies[:2]:
        copy.start()
    for copy in small[:3]:
        copy.wait()
    for b in range(blocks):
        row = basis_held[:, b * BLK : (b + 1) * BLK]
        rows[b] = row
        columns[b] = as_column(row)
    tell(wide, map_held, send_held, rows, told)
    small[3].wait()
    solve(copies, held, rhs, columns, disp, narrow, proj)
    pick_blocks(send_held.at[0], narrow, slabs, range(4))


def next_solve_kernel(send, read, matrix, load, columns, dual, *rest):
    arrived, (mult, disp, proj), rest = rest[:DIRS], rest[DIRS : DIRS + 3], rest[DIRS + 3 :]
    slabs, (received, rhs, narrow) = rest[:4], rest[4:]
    stack_slabs(arrived, received)
    for b in range(disp.shape[0]):
        far = received[slot_read(read, b)]
        step = dual[b].astype(jnp.float32) - far.astype(jnp.float32)
        mult[b] = step
        rows = pl.ds(b * BLK, BLK)
        rhs[rows, :] = (load[rows, :].astype(jnp.float32) - step).astype(jnp.bfloat16)
    solve([], matrix, rhs, columns, disp, narrow, proj)
    pick_blocks(send, narrow, slabs, range(4))


def coarse_kernel(wide, send, mine, theirs, part, partner, disp, columns, corrected, near, *rest):
    slabs, (ordered,) = rest[:2], rest[2:]
    here = lax.axis_index("sub")
    chips = mine.shape[0]
    cases = disp.shape[2]
    for p in range(chips):
        for e, values in ((0, mine), (1, theirs)):
            at = ((here ^ (2 * p + e)) * wide) // 8 * 8
            ordered[pl.ds(pl.multiple_of(at, 8), wide), :] = values[p, :wide, :].astype(jnp.float32)
    rows = [0.0, 0.0]
    for q, kind, group, cols in pieces_of(ordered.shape[0], cases):
        span = slice(group * wide, (group + 1) * wide)
        table = part[span, cols].astype(jnp.float32) + partner[span, cols].astype(jnp.float32)
        rows[kind] += jnp.dot(
            table,
            ordered[q * BLK : (q + 1) * BLK, :],
            preferred_element_type=jnp.float32,
            precision=HIGHEST,
        )
    near[...] = rows[1]
    for b in range(disp.shape[0]):
        for cols in column_parts(cases):
            corrected[b, :, cols] = (
                disp[b, :, cols] + columns[b] * rows[0][b : b + 1, cols]
            ).astype(jnp.bfloat16)
    pick_blocks(send, corrected, slabs, (4, 5))


def dirichlet_kernel(streamed, send, read, weights, matrix, corrected, far_columns, near, *rest):
    arrived, dual, rest = rest[:DIRS], rest[DIRS], rest[DIRS + 1 :]
    slabs, (received, rows, rhs, *stream) = rest[:DIRS], rest[DIRS:]
    blocks, _, cases = corrected.shape
    copies = []
    if streamed:
        copies = matrix_copies(matrix, *stream)
        matrix = stream[0]
        for copy in copies[:2]:
            copy.start()
    stack_slabs(arrived, received)
    for k in range(NEAR):
        rows[k] = near[k : k + 1, :]
    for k in range(NEAR, DIRS * CAP):
        rows[k] = jnp.zeros((1, cases), jnp.float32)
    for b in range(blocks):
        place, code = slot_read(read, b), read[b]
        for cols in column_parts(cases):
            far = received[place, :, cols].astype(jnp.float32) + far_columns[b] * rows[code, :, cols]
            far = far.astype(jnp.bfloat16).astype(jnp.float32)
            gap = corrected[b, :, cols].astype(jnp.float32) - far
            rhs[b * BLK : (b + 1) * BLK, cols] = (gap * weights[b]).astype(jnp.bfloat16)

    def consume(b, mine):
        dual[b] = (mine * weights[b]).astype(jnp.bfloat16)

    each_rows(copies, matrix, rhs, consume)
    pick_blocks(send, dual, slabs, range(DIRS))


def finish_kernel(read, mult, dual, *rest):
    arrived, (out, received) = rest[:DIRS], rest[DIRS:]
    stack_slabs(arrived, received)
    for b in range(out.shape[0]):
        far = received[slot_read(read, b)]
        out[b] = mult[b] + (dual[b].astype(jnp.float32) - far.astype(jnp.float32))


def pieces_of(lanes, cases):
    across = cases // BLK
    return [
        (i // 2, i % 2, i // across, slice(i % across * BLK, (i % across + 1) * BLK))
        for i in range(2 * (lanes // BLK))
    ]


def share_kernel(wide, read, own_rows, mine, theirs, proj, far_columns, held, *chunks):
    held, chunks = chunks[-1], (held,) + chunks[:-1]
    high, order = own_rows.shape
    subs, here = lax.axis_size("sub"), lax.axis_index("sub")
    chips = mine.shape[0]
    tall = (mine.shape[1] - NEAR) // 2
    blocks = far_columns.shape[0]
    sums = sum(names[p, NEAR:, :] for p in range(chips) for names in (mine, theirs))
    sums = sums.astype(jnp.int32) - 1

    def lanes_of(first):
        return jnp.concatenate([sums[first + r : first + r + 1] for r in range(tall)], axis=1)

    dofs, lanes = (lanes_of(0), lanes_of(tall)), subs * wide
    local = (lax.broadcasted_iota(jnp.int32, (high, lanes), 0) + here * high == dofs[0][:, :lanes])
    local = local.astype(jnp.float32).astype(jnp.bfloat16)
    source = own_rows[...].astype(jnp.bfloat16)
    for kind in range(2):
        pick = lax.broadcasted_iota(jnp.int32, (order, lanes), 0) == dofs[kind][:, :lanes]
        chosen = jnp.dot(
            source,
            pick.astype(jnp.float32).astype(jnp.bfloat16),
            preferred_element_type=jnp.float32,
        )
        held[kind] = lax.dot_general(
            chosen.astype(jnp.bfloat16),
            local,
            (((0,), (0,)), ((), ())),
            preferred_element_type=jnp.float32,
        )
    groups = (chunks[0].shape[0] // wide - 1) // 2
    for p, chunk in enumerate(chunks):
        chunk[:wide, :] = proj[...].astype(jnp.bfloat16)
        for e in range(2):
            reader = 2 * ((here // 2) ^ p) + e
            at = pl.ds(pl.multiple_of(reader * wide, wide), wide)
            for q, kind, group, cols in pieces_of(lanes, chunk.shape[1]):
                top = (1 + e * groups + group) * wide
                chunk[top : top + wide, cols] = held[
                    kind, at, q * BLK : (q + 1) * BLK
                ].astype(jnp.bfloat16)
    for b in range(blocks):
        code = jnp.minimum(read[b], NEAR - 1)
        direction = code // CAP
        offset = jnp.where(
            direction == 0, OFFSETS[0],
            jnp.where(direction == 1, OFFSETS[1], jnp.where(direction == 2, OFFSETS[2], OFFSETS[3])),
        )
        sender = lax.rem(here - offset + subs, subs) ^ here
        found = jnp.zeros((1, BLK), jnp.float32)
        rows = jnp.where(sender % 2 == 0, mine[sender // 2, :NEAR], theirs[sender // 2, :NEAR])
        line = lax.broadcasted_iota(jnp.int32, (NEAR, BLK), 0)
        found = jnp.sum(jnp.where(line == code, rows, 0.0), axis=0, keepdims=True)
        far_columns[b] = as_column(found)


def merge_kernel(wide, *refs):
    arrived, (outgoing, part) = refs[:-2], refs[-2:]
    chips = len(arrived)
    core = lax.axis_index("sub") % 2
    span = part.shape[0]
    for p, chunk in enumerate(arrived):
        outgoing[p, :wide, :] = chunk[:wide, :]
    tables = [
        sum(chunk[wide + e * span : wide + (e + 1) * span, :].astype(jnp.float32) for chunk in arrived)
        for e in range(2)
    ]
    part[...] = jnp.where(core == 0, tables[0], tables[1]).astype(jnp.bfloat16)
    outgoing[chips, :, :] = jnp.where(core == 0, tables[1], tables[0]).astype(jnp.bfloat16)


def on_device(
    load_cases,
    inv_schur,
    schur_blocks,
    coarse_basis,
    coarse_map,
    multiplicity,
    recv_code,
    send_blocks,
    coarse_inv,
):
    dofs = inv_schur.shape[2]
    cases = load_cases.shape[3]
    blocks = dofs // BLK
    subs = lax.axis_size("sub")
    chips = subs // 2
    wide = NEAR * -(-blocks // NEAR)
    lanes = subs * wide
    tall = 4 * -(-lanes // (4 * BLK))
    groups = -(-2 * (lanes // BLK) // (cases // BLK))
    solve_matrix = inv_schur[0, 0]
    dirichlet_matrix = schur_blocks[0, 0]
    load = load_cases[0, 0]
    read = recv_code[0, 0]
    send = send_blocks[0, 0]
    weights = 1.0 / multiplicity[0, 0].astype(jnp.float32)
    whole = f32(blocks, BLK, cases)
    halved = bf16(blocks, BLK, cases)
    slab = bf16(CAP, BLK, cases)
    block_columns = f32(blocks, BLK, BLK)
    received = pltpu.VMEM((DIRS * CAP, BLK, cases), jnp.bfloat16)
    narrow = pltpu.VMEM((blocks, BLK, cases), jnp.bfloat16)
    rhs = pltpu.VMEM((dofs, cases), jnp.bfloat16)
    steps = pltpu.SemaphoreType.DMA((dofs // ROWS,))
    held = pltpu.VMEM((dofs, dofs), jnp.bfloat16)

    disp, proj, columns, told, *slabs = pl.pallas_call(
        functools.partial(first_solve_kernel, wide),
        out_shape=[whole, f32(wide, cases), block_columns, f32(NEAR + 2 * tall, BLK)] + [slab] * 4,
        in_specs=[HBM] * 5,
        out_specs=[VMEM] * 8,
        scratch_shapes=[
            held,
            rhs,
            narrow,
            pltpu.SMEM((1, DIRS * CAP), jnp.int32),
            pltpu.SMEM((1, blocks), jnp.int32),
            pltpu.VMEM((1, dofs), jnp.float32),
            pltpu.VMEM((blocks, 1, BLK), jnp.float32),
            steps,
            pltpu.SemaphoreType.DMA((4,)),
        ],
        compiler_params=PARAMS,
    )(
        in_hbm(send_blocks[0]), in_hbm(coarse_map[0]), in_hbm(solve_matrix), in_hbm(load),
        in_hbm(coarse_basis[0]),
    )
    mine = jnp.stack(to_chips([told] * chips))
    theirs = swapped(mine, 1)
    far_columns, *chunks = pl.pallas_call(
        functools.partial(share_kernel, wide),
        out_shape=[block_columns] + [bf16((1 + 2 * groups) * wide, cases)] * chips,
        in_specs=[SMEM] + [VMEM] * 4,
        out_specs=[VMEM] * (1 + chips),
        scratch_shapes=[pltpu.VMEM((2, lanes, lanes), jnp.float32)],
        compiler_params=PARAMS,
    )(read, coarse_inv[0], mine, theirs, proj)
    outgoing, part = pl.pallas_call(
        functools.partial(merge_kernel, wide),
        out_shape=[bf16(chips + 1, groups * wide, cases), bf16(groups * wide, cases)],
        in_specs=[VMEM] * chips,
        out_specs=[VMEM] * 2,
        compiler_params=PARAMS,
    )(*to_chips(chunks))
    incoming = swapped(outgoing, 1)
    partner = incoming[chips]

    for iteration in range(ITERS):
        arrived = {way: exchanged(slabs[way], way) for way in range(4)}
        if iteration:
            outgoing = jnp.stack(to_chips([proj.astype(jnp.bfloat16)] * chips))
            incoming = swapped(outgoing, 1)
        corrected, near, *far_slabs = pl.pallas_call(
            functools.partial(coarse_kernel, wide),
            out_shape=[halved, f32(NEAR, cases), slab, slab],
            in_specs=[SMEM] + [VMEM] * 6,
            out_specs=[VMEM] * 4,
            scratch_shapes=[pltpu.VMEM((lanes, cases), jnp.float32)],
            compiler_params=PARAMS,
        )(send, outgoing[:chips], incoming[:chips], part, partner, disp, columns)
        for way in (4, 5):
            arrived[way] = exchanged(far_slabs[way - 4], way)
        streamed = iteration == 0
        dual, *slabs = pl.pallas_call(
            functools.partial(dirichlet_kernel, streamed),
            out_shape=[halved] + [slab] * DIRS,
            in_specs=[SMEM] * 3 + [HBM if streamed else VMEM] + [VMEM] * (3 + DIRS),
            out_specs=[VMEM] * (1 + DIRS),
            scratch_shapes=[received, pltpu.VMEM((DIRS * CAP, 1, cases), jnp.float32), rhs]
            + ([held, steps] if streamed else []),
            compiler_params=PARAMS,
        )(
            send, read, weights, in_hbm(dirichlet_matrix) if streamed else dirichlet_matrix,
            corrected, far_columns, near, *[arrived[way] for way in ORDER],
        )
        arrived = [exchanged(slabs[way], way) for way in ORDER]
        if iteration + 1 < ITERS:
            mult, disp, proj, *slabs = pl.pallas_call(
                next_solve_kernel,
                out_shape=[whole, whole, f32(wide, cases)] + [slab] * 4,
                in_specs=[SMEM] * 2 + [VMEM] * (4 + DIRS),
                out_specs=[VMEM] * 7,
                scratch_shapes=[received, rhs, narrow],
                compiler_params=PARAMS,
            )(send, read, solve_matrix, load, columns, dual, *arrived)
    out = pl.pallas_call(
        finish_kernel,
        out_shape=whole,
        in_specs=[SMEM] + [VMEM] * (2 + DIRS),
        out_specs=VMEM,
        scratch_shapes=[received],
        compiler_params=PARAMS,
    )(read, mult, dual, *arrived)
    return out.reshape(1, 1, dofs, cases)


def solution(mesh):
    split = P("group", "sub")
    return jax.shard_map(
        on_device, mesh=mesh, in_specs=(split,) * 9, out_specs=split, check_vma=False
    )
```

time: 150 us -> 125 us (0.83)
  waiting for transfers between devices: 82.8 us -> 58 us
  starting transfers between devices: 36.1 us -> 46.4 us
  local copies, waits for them, and re-layouts: 6.68 us -> 0.06 us
  other arithmetic: 5.02 us -> 0.02 us
    ppermute x12, waiting for transfers between devices: 31.6 us -> 10.2 us  [swapped(): return lax.ppermute(value, 'sub', [(i, i ^ mask) for i in range(count)])]
    unnamed x30 -> x18, local copies, waits for them, and re-layouts: 6.51 us -> 0.05 us
    ppermute x24, starting transfers between devices: 26.2 us -> 31.6 us  [exchanged(): return lax.ppermute(slab, axis, route)]
    ppermute x12, starting transfers between devices: 9.91 us -> 14.9 us  [swapped(): return lax.ppermute(value, 'sub', [(i, i ^ mask) for i in range(count)])]
    ppermute x24, waiting for transfers between devices: 51.2 us -> 47.8 us  [exchanged(): return lax.ppermute(slab, axis, route)]
    add x4 -> x0, other arithmetic: 2.07 us -> none  [the longest x3 1.41 us: on_device(): share = share + swapped(share, bit)]
    concatenate x9 -> x0, other arithmetic: 1.52 us -> none  [gathered(): held = jnp.concatenate([held, swapped(held, bit)])]
  transfers between devices with their start and end apart: 36 -> 36, of which waited for: 18 -> 19; matrix products, arithmetic and copies ran while one was open for 2% -> 0% of each run, Pallas kernels for 6% -> 2%
where the time goes in v3:
time: 125 us; the launch traced here: 124 us
  waiting for transfers between devices  58 us (46%)
  starting transfers between devices  46.4 us (37%)
  Pallas kernels  18.9 us (15%)
    ppermute x24, waiting for transfers between devices, exchanged(): return lax.ppermute(slab, axis, route)  47.8 us
    ppermute x24, starting transfers between devices, exchanged(): return lax.ppermute(slab, axis, route)  31.6 us
    ppermute x12, starting transfers between devices, swapped(): return lax.ppermute(value, 'sub', [(i, i ^ mask) for i in range(count)])  14.9 us
    ppermute x12, waiting for transfers between devices, swapped(): return lax.ppermute(value, 'sub', [(i, i ^ mask) for i in range(count)])  10.2 us
    pallas_call x2, Pallas kernels, on_device(): pl.pallas_call(functools.partial(dirichlet_kernel, streamed), out_shape=[...  7.05 us
    pallas_call x1, Pallas kernels, on_device(): pl.pallas_call(functools.partial(first_solve_kernel, wide), out_shape=[wh...  4.33 us
  transfers between devices with their start and end apart: 36, of which 19 were waited for; matrix products, arithmetic and copies ran while one was open for 0% of the time, Pallas kernels for 2%

profile of v3, /device:TPU:0, one launch (start us, length us, event | category | flops | bytes accessed | tf_op | source)
XLA Modules:
  0.0 123.7 jit_solution(5809960628762524399)
XLA Ops:
  0.0 4.3 %shard_map.91 = (f32[12,128,256]{2,1,0:T(8,128)S(1)}, f32[16,256]{1,0:T(8,128)S(1)}, f32[12,128,128]{2,1,0:T(8,128)S(1)}, f32[24,128]{1,0:T(8,128)S(1)}, bf16[4,...) custom-call(s32[1,24]{1,0:T(1,128)} %bitcast.34, ...), custom_call_target="tpu_custom_call" | custom-call | tf_op jit(solution)/shard_map/pallas_call | solution.py:371
  4.3 5.1 %collective-permute-start.2 = (f32[24,128]{1,0:T(8,128)S(1)}, f32[24,128]{1,0:T(8,128)S(1)}, u32[]{:S(2)}, u32[]{:S(2)}) collective-permute-start(f32[24,128]{1,0:T(8,128)S(1)} %get-tuple-element.50), channel_id=1, source_target_pairs={{0,6},{1,7},{2,4},{3,5},{4,2},{5,3},{6,0},{7,1},{8,14},{9,15},{10,... | collective-permute-start | bytes 36872 | tf_op jit(solution)/shard_map/ppermute | solution.py:56
  11.1 2.9 %collective-permute-done.1 = f32[24,128]{1,0:T(8,128)S(1)} collective-permute-done((f32[24,128]{1,0:T(8,128)S(1)}, f32[24,128]{1,0:T(8,128)S(1)}, u32[]{:S(2)}, u32[]{:S(2)}) %collective-permute-start.1) | collective-permute-done | bytes 12320 | tf_op jit(solution)/shard_map/ppermute | solution.py:56
  16.7 2.0 %collective-permute-start.5 = (bf16[48,256]{1,0:T(8,128)(2,1)S(1)}, bf16[48,256]{1,0:T(8,128)(2,1)S(1)}, u32[]{:S(2)}, u32[]{:S(2)}) collective-permute-start(bf16[48,256]{1,0:T(8,128)(2,1)S(1)} %get-tuple-element.54), channel_id=1, source_target_pairs={{0,4},{1,5},{2,6},{3,7},{4,0},{5,1},{6,2},{7,3},{8,12},{9,13},{10,... | collective-permute-start | bytes 73736 | tf_op jit(solution)/shard_map/ppermute | solution.py:56
  18.7 2.4 %collective-permute-start.6 = (bf16[48,256]{1,0:T(8,128)(2,1)S(1)}, bf16[48,256]{1,0:T(8,128)(2,1)S(1)}, u32[]{:S(2)}, u32[]{:S(2)}) collective-permute-start(bf16[48,256]{1,0:T(8,128)(2,1)S(1)} %get-tuple-element.55), channel_id=1, source_target_pairs={{0,6},{1,7},{2,4},{3,5},{4,2},{5,3},{6,0},{7,1},{8,14},{9,15},{10,... | collective-permute-start | bytes 73736 | tf_op jit(solution)/shard_map/ppermute | solution.py:56
  21.5 2.9 %collective-permute-done.6.refs_3_ = bf16[48,256]{1,0:T(8,128)(2,1)S(1)} collective-permute-done((bf16[48,256]{1,0:T(8,128)(2,1)S(1)}, bf16[48,256]{1,0:T(8,128)(2,1)S(1)}, u32[]{:S(2)}, u32[]{:S(2)}) %collective-permute-start.6) | collective-permute-done | bytes 24608 | tf_op jit(solution)/shard_map/ppermute | solution.py:56
  24.4 2.4 %collective-permute-start.8 = (bf16[4,128,256]{2,1,0:T(8,128)(2,1)S(1)}, bf16[4,128,256]{2,1,0:T(8,128)(2,1)S(1)}, u32[]{:S(2)}, u32[]{:S(2)}) collective-permute-start(bf16[4,128,256]{2,1,0:T(8,128)(2,1)S(1)} %get-tuple-element.62), channel_id=1, source_target_pairs={{0,6},{1,7},{2,4},{3,5},{4,2},{5,3},{6,0},{7,1},{8,14},{9,15},{10,... | collective-permute-start | bytes 786440 | tf_op jit(solution)/shard_map/ppermute | solution.py:51
  31.6 3.8 %collective-permute-done.8.rest_0_ = bf16[4,128,256]{2,1,0:T(8,128)(2,1)S(1)} collective-permute-done((bf16[4,128,256]{2,1,0:T(8,128)(2,1)S(1)}, bf16[4,128,256]{2,1,0:T(8,128)(2,1)S(1)}, u32[]{:S(2)}, u32[]{:S(2)}) %collective-permute-start.8) | collective-permute-done | bytes 262176 | tf_op jit(solution)/shard_map/ppermute | solution.py:51
  35.5 2.4 %collective-permute-start.13 = (bf16[4,128,256]{2,1,0:T(8,128)(2,1)S(1)}, bf16[4,128,256]{2,1,0:T(8,128)(2,1)S(1)}, u32[]{:S(2)}, u32[]{:S(2)}) collective-permute-start(bf16[4,128,256]{2,1,0:T(8,128)(2,1)S(1)} %get-tuple-element.67), channel_id=1, source_target_pairs={{0,24},{8,16},{16,8},{24,0},{1,25},{9,17},{17,9},{25,1},{2,26},{10... | collective-permute-start | bytes 786440 | tf_op jit(solution)/shard_map/ppermute | solution.py:51
  37.9 3.2 %collective-permute-done.9.rest_1_ = bf16[4,128,256]{2,1,0:T(8,128)(2,1)S(1)} collective-permute-done((bf16[4,128,256]{2,1,0:T(8,128)(2,1)S(1)}, bf16[4,128,256]{2,1,0:T(8,128)(2,1)S(1)}, u32[]{:S(2)}, u32[]{:S(2)}) %collective-permute-start.9) | collective-permute-done | bytes 262176 | tf_op jit(solution)/shard_map/ppermute | solution.py:51
  41.1 4.7 %collective-permute-done.10.rest_2_ = bf16[4,128,256]{2,1,0:T(8,128)(2,1)S(1)} collective-permute-done((bf16[4,128,256]{2,1,0:T(8,128)(2,1)S(1)}, bf16[4,128,256]{2,1,0:T(8,128)(2,1)S(1)}, u32[]{:S(2)}, u32[]{:S(2)}) %collective-permute-start.10) | collective-permute-done | bytes 262176 | tf_op jit(solution)/shard_map/ppermute | solution.py:51
  45.9 4.6 %shard_map.95 = (bf16[12,128,256]{2,1,0:T(8,128)(2,1)S(1)}, bf16[4,128,256]{2,1,0:T(8,128)(2,1)S(1)}, bf16[4,128,256]{2,1,0:T(8,128)(2,1)S(1)}, bf16[4,128,256]{...) custom-call(s32[24]{0:T(128)S(1)} %bitcast.36, ...), custom_call_target="tpu_custom_call" | custom-call | tf_op jit(solution)/shard_map/pallas_call | solution.py:428
  55.5 6.0 %collective-permute-done.14.rest_0_ = bf16[4,128,256]{2,1,0:T(8,128)(2,1)S(1)} collective-permute-done((bf16[4,128,256]{2,1,0:T(8,128)(2,1)S(1)}, bf16[4,128,256]{2,1,0:T(8,128)(2,1)S(1)}, u32[]{:S(2)}, u32[]{:S(2)}) %collective-permute-start.14) | collective-permute-done | bytes 262176 | tf_op jit(solution)/shard_map/ppermute | solution.py:51
  61.5 2.4 %collective-permute-start.19 = (bf16[4,128,256]{2,1,0:T(8,128)(2,1)S(1)}, bf16[4,128,256]{2,1,0:T(8,128)(2,1)S(1)}, u32[]{:S(2)}, u32[]{:S(2)}) collective-permute-start(bf16[4,128,256]{2,1,0:T(8,128)(2,1)S(1)} %get-tuple-element.74), channel_id=1, source_target_pairs={{0,24},{8,16},{16,8},{24,0},{1,25},{9,17},{17,9},{25,1},{2,26},{10... | collective-permute-start | bytes 786440 | tf_op jit(solution)/shard_map/ppermute | solution.py:51
  64.0 2.4 %collective-permute-done.15.rest_1_ = bf16[4,128,256]{2,1,0:T(8,128)(2,1)S(1)} collective-permute-done((bf16[4,128,256]{2,1,0:T(8,128)(2,1)S(1)}, bf16[4,128,256]{2,1,0:T(8,128)(2,1)S(1)}, u32[]{:S(2)}, u32[]{:S(2)}) %collective-permute-start.15) | collective-permute-done | bytes 262176 | tf_op jit(solution)/shard_map/ppermute | solution.py:51
  66.3 5.1 %collective-permute-done.16.rest_2_ = bf16[4,128,256]{2,1,0:T(8,128)(2,1)S(1)} collective-permute-done((bf16[4,128,256]{2,1,0:T(8,128)(2,1)S(1)}, bf16[4,128,256]{2,1,0:T(8,128)(2,1)S(1)}, u32[]{:S(2)}, u32[]{:S(2)}) %collective-permute-start.16) | collective-permute-done | bytes 262176 | tf_op jit(solution)/shard_map/ppermute | solution.py:51
  71.5 2.2 %shard_map.96 = (f32[12,128,256]{2,1,0:T(8,128)S(1)}, f32[12,128,256]{2,1,0:T(8,128)S(1)}, f32[16,256]{1,0:T(8,128)S(1)}, bf16[4,128,256]{2,1,0:T(8,128)(2,1)S(1...) custom-call(s32[24]{0:T(128)S(1)} %bitcast.37, ...), custom_call_target="tpu_custom_call" | custom-call | tf_op jit(solution)/shard_map/pallas_call | solution.py:442
  73.7 2.9 %collective-permute-start.21 = (bf16[16,256]{1,0:T(8,128)(2,1)S(1)}, bf16[16,256]{1,0:T(8,128)(2,1)S(1)}, u32[]{:S(2)}, u32[]{:S(2)}) collective-permute-start(bf16[16,256]{1,0:T(8,128)(2,1)S(1)} %convert_element_type.8), channel_id=1, source_target_pairs={{0,4},{1,5},{2,6},{3,7},{4,0},{5,1},{6,2},{7,3},{8,12},{9,13},{10,... | collective-permute-start | bytes 24584 | tf_op jit(solution)/shard_map/ppermute | solution.py:56
  78.2 2.3 %collective-permute-start.24 = (bf16[4,128,256]{2,1,0:T(8,128)(2,1)S(1)}, bf16[4,128,256]{2,1,0:T(8,128)(2,1)S(1)}, u32[]{:S(2)}, u32[]{:S(2)}) collective-permute-start(bf16[4,128,256]{2,1,0:T(8,128)(2,1)S(1)} %get-tuple-element.80), channel_id=1, source_target_pairs={{0,6},{1,7},{2,4},{3,5},{4,2},{5,3},{6,0},{7,1},{8,14},{9,15},{10,... | collective-permute-start | bytes 786440 | tf_op jit(solution)/shard_map/ppermute | solution.py:51
  80.5 1.8 %collective-permute-done.22 = bf16[16,256]{1,0:T(8,128)(2,1)S(1)} collective-permute-done((bf16[16,256]{1,0:T(8,128)(2,1)S(1)}, bf16[16,256]{1,0:T(8,128)(2,1)S(1)}, u32[]{:S(2)}, u32[]{:S(2)}) %collective-permute-start.22) | collective-permute-done | bytes 8224 | tf_op jit(solution)/shard_map/ppermute | solution.py:56
  87.3 2.0 %collective-permute-done.24.rest_0_ = bf16[4,128,256]{2,1,0:T(8,128)(2,1)S(1)} collective-permute-done((bf16[4,128,256]{2,1,0:T(8,128)(2,1)S(1)}, bf16[4,128,256]{2,1,0:T(8,128)(2,1)S(1)}, u32[]{:S(2)}, u32[]{:S(2)}) %collective-permute-start.24) | collective-permute-done | bytes 262176 | tf_op jit(solution)/shard_map/ppermute | solution.py:51
  89.2 2.4 %collective-permute-start.29 = (bf16[4,128,256]{2,1,0:T(8,128)(2,1)S(1)}, bf16[4,128,256]{2,1,0:T(8,128)(2,1)S(1)}, u32[]{:S(2)}, u32[]{:S(2)}) collective-permute-start(bf16[4,128,256]{2,1,0:T(8,128)(2,1)S(1)} %get-tuple-element.85), channel_id=1, source_target_pairs={{0,24},{8,16},{16,8},{24,0},{1,25},{9,17},{17,9},{25,1},{2,26},{10... | collective-permute-start | bytes 786440 | tf_op jit(solution)/shard_map/ppermute | solution.py:51
  91.7 3.3 %collective-permute-done.25.rest_1_ = bf16[4,128,256]{2,1,0:T(8,128)(2,1)S(1)} collective-permute-done((bf16[4,128,256]{2,1,0:T(8,128)(2,1)S(1)}, bf16[4,128,256]{2,1,0:T(8,128)(2,1)S(1)}, u32[]{:S(2)}, u32[]{:S(2)}) %collective-permute-start.25) | collective-permute-done | bytes 262176 | tf_op jit(solution)/shard_map/ppermute | solution.py:51
  95.0 2.6 %collective-permute-done.26.rest_2_ = bf16[4,128,256]{2,1,0:T(8,128)(2,1)S(1)} collective-permute-done((bf16[4,128,256]{2,1,0:T(8,128)(2,1)S(1)}, bf16[4,128,256]{2,1,0:T(8,128)(2,1)S(1)}, u32[]{:S(2)}, u32[]{:S(2)}) %collective-permute-start.26) | collective-permute-done | bytes 262176 | tf_op jit(solution)/shard_map/ppermute | solution.py:51
  97.6 3.0 %collective-permute-done.29.rest_5_ = bf16[4,128,256]{2,1,0:T(8,128)(2,1)S(1)} collective-permute-done((bf16[4,128,256]{2,1,0:T(8,128)(2,1)S(1)}, bf16[4,128,256]{2,1,0:T(8,128)(2,1)S(1)}, u32[]{:S(2)}, u32[]{:S(2)}) %collective-permute-start.29) | collective-permute-done | bytes 262176 | tf_op jit(solution)/shard_map/ppermute | solution.py:51
  100.6 2.5 %shard_map.98 = (bf16[12,128,256]{2,1,0:T(8,128)(2,1)S(1)}, bf16[4,128,256]{2,1,0:T(8,128)(2,1)S(1)}, bf16[4,128,256]{2,1,0:T(8,128)(2,1)S(1)}, bf16[4,128,256]{...) custom-call(s32[24]{0:T(128)S(1)} %bitcast.39, ...), custom_call_target="tpu_custom_call" | custom-call | tf_op jit(solution)/shard_map/pallas_call | solution.py:428
  103.0 2.0 %collective-permute-start.30 = (bf16[4,128,256]{2,1,0:T(8,128)(2,1)S(1)}, bf16[4,128,256]{2,1,0:T(8,128)(2,1)S(1)}, u32[]{:S(2)}, u32[]{:S(2)}) collective-permute-start(bf16[4,128,256]{2,1,0:T(8,128)(2,1)S(1)} %get-tuple-element.87), channel_id=1, source_target_pairs={{0,6},{1,7},{2,4},{3,5},{4,2},{5,3},{6,0},{7,1},{8,14},{9,15},{10,... | collective-permute-start | bytes 786440 | tf_op jit(solution)/shard_map/ppermute | solution.py:51
  105.4 1.8 %collective-permute-start.33 = (bf16[4,128,256]{2,1,0:T(8,128)(2,1)S(1)}, bf16[4,128,256]{2,1,0:T(8,128)(2,1)S(1)}, u32[]{:S(2)}, u32[]{:S(2)}) collective-permute-start(bf16[4,128,256]{2,1,0:T(8,128)(2,1)S(1)} %get-tuple-element.90), channel_id=1, source_target_pairs={{0,1},{1,0},{2,3},{3,2},{4,5},{5,4},{6,7},{7,6},{8,9},{9,8},{10,11... | collective-permute-start | bytes 786440 | tf_op jit(solution)/shard_map/ppermute | solution.py:51
  108.7 5.5 %collective-permute-done.30.rest_0_ = bf16[4,128,256]{2,1,0:T(8,128)(2,1)S(1)} collective-permute-done((bf16[4,128,256]{2,1,0:T(8,128)(2,1)S(1)}, bf16[4,128,256]{2,1,0:T(8,128)(2,1)S(1)}, u32[]{:S(2)}, u32[]{:S(2)}) %collective-permute-start.30) | collective-permute-done | bytes 262176 | tf_op jit(solution)/shard_map/ppermute | solution.py:51
  115.5 3.8 %collective-permute-done.31.rest_1_ = bf16[4,128,256]{2,1,0:T(8,128)(2,1)S(1)} collective-permute-done((bf16[4,128,256]{2,1,0:T(8,128)(2,1)S(1)}, bf16[4,128,256]{2,1,0:T(8,128)(2,1)S(1)}, u32[]{:S(2)}, u32[]{:S(2)}) %collective-permute-start.31) | collective-permute-done | bytes 262176 | tf_op jit(solution)/shard_map/ppermute | solution.py:51
  119.3 2.4 %collective-permute-done.32.rest_2_ = bf16[4,128,256]{2,1,0:T(8,128)(2,1)S(1)} collective-permute-done((bf16[4,128,256]{2,1,0:T(8,128)(2,1)S(1)}, bf16[4,128,256]{2,1,0:T(8,128)(2,1)S(1)}, u32[]{:S(2)}, u32[]{:S(2)}) %collective-permute-start.32) | collective-permute-done | bytes 262176 | tf_op jit(solution)/shard_map/ppermute | solution.py:51
  121.7 2.0 %shard_map.99 = f32[12,128,256]{2,1,0:T(8,128)} custom-call(s32[12]{0:T(128)S(1)} %bitcast.44, f32[12,128,256]{2,1,0:T(8,128)S(1)} %get-tuple-element.75.mult, bf16[12,128,256]{2,1,0:T(8,128)(2,1)S(1)} %get-tuple-element.86.dual, bf16[4,128,256]{2,1,0:T(8,128)(2,1)S(1)} %collective-permute-done.30.rest_0_, ...), custom_call_target="tpu_custom_call" | custom-call | tf_op jit(solution)/shard_map/pallas_call | solution.py:450
  (77 shorter events, 24.4 us)
Async XLA Ops:
  4.3 6.8 %collective-permute-start.2 = (f32[24,128]{1,0:T(8,128)S(1)}, f32[24,128]{1,0:T(8,128)S(1)}, u32[]{:S(2)}, u32[]{:S(2)}) collective-permute-start(f32[24,128]{1,0:T(8,128)S(1)} %get-tuple-element.50), channel_id=1, source_target_pairs={{0,6},{1,7},{2,4},{3,5},{4,2},{5,3},{6,0},{7,1},{8,14},{9,15},{10,... | collective-permute-start | bytes 36872 | tf_op jit(solution)/shard_map/ppermute | solution.py:56
  9.5 4.6 %collective-permute-start.1 = (f32[24,128]{1,0:T(8,128)S(1)}, f32[24,128]{1,0:T(8,128)S(1)}, u32[]{:S(2)}, u32[]{:S(2)}) collective-permute-start(f32[24,128]{1,0:T(8,128)S(1)} %get-tuple-element.50), channel_id=1, source_target_pairs={{0,4},{1,5},{2,6},{3,7},{4,0},{5,1},{6,2},{7,3},{8,12},{9,13},{10,... | collective-permute-start | bytes 36872 | tf_op jit(solution)/shard_map/ppermute | solution.py:56
  9.5 4.6 %collective-permute-start = (f32[24,128]{1,0:T(8,128)S(1)}, f32[24,128]{1,0:T(8,128)S(1)}, u32[]{:S(2)}, u32[]{:S(2)}) collective-permute-start(f32[24,128]{1,0:T(8,128)S(1)} %get-tuple-element.50), channel_id=1, source_target_pairs={{0,2},{1,3},{2,0},{3,1},{4,6},{5,7},{6,4},{7,5},{8,10},{9,11},{10,... | collective-permute-start | bytes 36872 | tf_op jit(solution)/shard_map/ppermute | solution.py:56
  16.7 4.8 %collective-permute-start.5 = (bf16[48,256]{1,0:T(8,128)(2,1)S(1)}, bf16[48,256]{1,0:T(8,128)(2,1)S(1)}, u32[]{:S(2)}, u32[]{:S(2)}) collective-permute-start(bf16[48,256]{1,0:T(8,128)(2,1)S(1)} %get-tuple-element.54), channel_id=1, source_target_pairs={{0,4},{1,5},{2,6},{3,7},{4,0},{5,1},{6,2},{7,3},{8,12},{9,13},{10,... | collective-permute-start | bytes 73736 | tf_op jit(solution)/shard_map/ppermute | solution.py:56
  18.7 5.6 %collective-permute-start.6 = (bf16[48,256]{1,0:T(8,128)(2,1)S(1)}, bf16[48,256]{1,0:T(8,128)(2,1)S(1)}, u32[]{:S(2)}, u32[]{:S(2)}) collective-permute-start(bf16[48,256]{1,0:T(8,128)(2,1)S(1)} %get-tuple-element.55), channel_id=1, source_target_pairs={{0,6},{1,7},{2,4},{3,5},{4,2},{5,3},{6,0},{7,1},{8,14},{9,15},{10,... | collective-permute-start | bytes 73736 | tf_op jit(solution)/shard_map/ppermute | solution.py:56
  24.3 4.6 %collective-permute-start.7 = (bf16[5,16,256]{2,1,0:T(8,128)(2,1)S(1)}, bf16[5,16,256]{2,1,0:T(8,128)(2,1)S(1)}, u32[]{:S(2)}, u32[]{:S(2)}) collective-permute-start(bf16[5,16,256]{2,1,0:T(8,128)(2,1)S(1)} %get-tuple-element.56), channel_id=1, source_target_pairs={{0,1},{1,0},{2,3},{3,2},{4,5},{5,4},{6,7},{7,6},{8,9},{9,8},{10,11... | collective-permute-start | bytes 122888 | tf_op jit(solution)/shard_map/ppermute | solution.py:56
  24.4 11.1 %collective-permute-start.8 = (bf16[4,128,256]{2,1,0:T(8,128)(2,1)S(1)}, bf16[4,128,256]{2,1,0:T(8,128)(2,1)S(1)}, u32[]{:S(2)}, u32[]{:S(2)}) collective-permute-start(bf16[4,128,256]{2,1,0:T(8,128)(2,1)S(1)} %get-tuple-element.62), channel_id=1, source_target_pairs={{0,6},{1,7},{2,4},{3,5},{4,2},{5,3},{6,0},{7,1},{8,14},{9,15},{10,... | collective-permute-start | bytes 786440 | tf_op jit(solution)/shard_map/ppermute | solution.py:51
  26.8 14.3 %collective-permute-start.9 = (bf16[4,128,256]{2,1,0:T(8,128)(2,1)S(1)}, bf16[4,128,256]{2,1,0:T(8,128)(2,1)S(1)}, u32[]{:S(2)}, u32[]{:S(2)}) collective-permute-start(bf16[4,128,256]{2,1,0:T(8,128)(2,1)S(1)} %get-tuple-element.63), channel_id=1, source_target_pairs={{0,2},{1,3},{2,0},{3,1},{4,6},{5,7},{6,4},{7,5},{8,10},{9,11},{10,... | collective-permute-start | bytes 786440 | tf_op jit(solution)/shard_map/ppermute | solution.py:51
  26.8 19.0 %collective-permute-start.10 = (bf16[4,128,256]{2,1,0:T(8,128)(2,1)S(1)}, bf16[4,128,256]{2,1,0:T(8,128)(2,1)S(1)}, u32[]{:S(2)}, u32[]{:S(2)}) collective-permute-start(bf16[4,128,256]{2,1,0:T(8,128)(2,1)S(1)} %get-tuple-element.64), channel_id=1, source_target_pairs={{0,7},{1,2},{2,1},{3,4},{4,3},{5,6},{6,5},{7,0},{8,15},{9,10},{10,... | collective-permute-start | bytes 786440 | tf_op jit(solution)/shard_map/ppermute | solution.py:51
  28.1 17.7 %collective-permute-start.11 = (bf16[4,128,256]{2,1,0:T(8,128)(2,1)S(1)}, bf16[4,128,256]{2,1,0:T(8,128)(2,1)S(1)}, u32[]{:S(2)}, u32[]{:S(2)}) collective-permute-start(bf16[4,128,256]{2,1,0:T(8,128)(2,1)S(1)} %get-tuple-element.65), channel_id=1, source_target_pairs={{0,1},{1,0},{2,3},{3,2},{4,5},{5,4},{6,7},{7,6},{8,9},{9,8},{10,11... | collective-permute-start | bytes 786440 | tf_op jit(solution)/shard_map/ppermute | solution.py:51
  30.1 15.7 %collective-permute-start.12 = (bf16[4,128,256]{2,1,0:T(8,128)(2,1)S(1)}, bf16[4,128,256]{2,1,0:T(8,128)(2,1)S(1)}, u32[]{:S(2)}, u32[]{:S(2)}) collective-permute-start(bf16[4,128,256]{2,1,0:T(8,128)(2,1)S(1)} %get-tuple-element.66), channel_id=1, source_target_pairs={{0,8},{8,0},{16,24},{24,16},{1,9},{9,1},{17,25},{25,17},{2,10},{10... | collective-permute-start | bytes 786440 | tf_op jit(solution)/shard_map/ppermute | solution.py:51
  35.5 10.3 %collective-permute-start.13 = (bf16[4,128,256]{2,1,0:T(8,128)(2,1)S(1)}, bf16[4,128,256]{2,1,0:T(8,128)(2,1)S(1)}, u32[]{:S(2)}, u32[]{:S(2)}) collective-permute-start(bf16[4,128,256]{2,1,0:T(8,128)(2,1)S(1)} %get-tuple-element.67), channel_id=1, source_target_pairs={{0,24},{8,16},{16,8},{24,0},{1,25},{9,17},{17,9},{25,1},{2,26},{10... | collective-permute-start | bytes 786440 | tf_op jit(solution)/shard_map/ppermute | solution.py:51
  50.5 11.0 %collective-permute-start.14 = (bf16[4,128,256]{2,1,0:T(8,128)(2,1)S(1)}, bf16[4,128,256]{2,1,0:T(8,128)(2,1)S(1)}, u32[]{:S(2)}, u32[]{:S(2)}) collective-permute-start(bf16[4,128,256]{2,1,0:T(8,128)(2,1)S(1)} %get-tuple-element.69), channel_id=1, source_target_pairs={{0,6},{1,7},{2,4},{3,5},{4,2},{5,3},{6,0},{7,1},{8,14},{9,15},{10,... | collective-permute-start | bytes 786440 | tf_op jit(solution)/shard_map/ppermute | solution.py:51
  51.5 14.8 %collective-permute-start.15 = (bf16[4,128,256]{2,1,0:T(8,128)(2,1)S(1)}, bf16[4,128,256]{2,1,0:T(8,128)(2,1)S(1)}, u32[]{:S(2)}, u32[]{:S(2)}) collective-permute-start(bf16[4,128,256]{2,1,0:T(8,128)(2,1)S(1)} %get-tuple-element.70), channel_id=1, source_target_pairs={{0,2},{1,3},{2,0},{3,1},{4,6},{5,7},{6,4},{7,5},{8,10},{9,11},{10,... | collective-permute-start | bytes 786440 | tf_op jit(solution)/shard_map/ppermute | solution.py:51
  52.6 18.8 %collective-permute-start.16 = (bf16[4,128,256]{2,1,0:T(8,128)(2,1)S(1)}, bf16[4,128,256]{2,1,0:T(8,128)(2,1)S(1)}, u32[]{:S(2)}, u32[]{:S(2)}) collective-permute-start(bf16[4,128,256]{2,1,0:T(8,128)(2,1)S(1)} %get-tuple-element.71), channel_id=1, source_target_pairs={{0,7},{1,2},{2,1},{3,4},{4,3},{5,6},{6,5},{7,0},{8,15},{9,10},{10,... | collective-permute-start | bytes 786440 | tf_op jit(solution)/shard_map/ppermute | solution.py:51
  54.0 17.5 %collective-permute-start.17 = (bf16[4,128,256]{2,1,0:T(8,128)(2,1)S(1)}, bf16[4,128,256]{2,1,0:T(8,128)(2,1)S(1)}, u32[]{:S(2)}, u32[]{:S(2)}) collective-permute-start(bf16[4,128,256]{2,1,0:T(8,128)(2,1)S(1)} %get-tuple-element.72), channel_id=1, source_target_pairs={{0,1},{1,0},{2,3},{3,2},{4,5},{5,4},{6,7},{7,6},{8,9},{9,8},{10,11... | collective-permute-start | bytes 786440 | tf_op jit(solution)/shard_map/ppermute | solution.py:51
  54.0 17.5 %collective-permute-start.18 = (bf16[4,128,256]{2,1,0:T(8,128)(2,1)S(1)}, bf16[4,128,256]{2,1,0:T(8,128)(2,1)S(1)}, u32[]{:S(2)}, u32[]{:S(2)}) collective-permute-start(bf16[4,128,256]{2,1,0:T(8,128)(2,1)S(1)} %get-tuple-element.73), channel_id=1, source_target_pairs={{0,8},{8,0},{16,24},{24,16},{1,9},{9,1},{17,25},{25,17},{2,10},{10... | collective-permute-start | bytes 786440 | tf_op jit(solution)/shard_map/ppermute | solution.py:51
  61.5 10.0 %collective-permute-start.19 = (bf16[4,128,256]{2,1,0:T(8,128)(2,1)S(1)}, bf16[4,128,256]{2,1,0:T(8,128)(2,1)S(1)}, u32[]{:S(2)}, u32[]{:S(2)}) collective-permute-start(bf16[4,128,256]{2,1,0:T(8,128)(2,1)S(1)} %get-tuple-element.74), channel_id=1, source_target_pairs={{0,24},{8,16},{16,8},{24,0},{1,25},{9,17},{17,9},{25,1},{2,26},{10... | collective-permute-start | bytes 786440 | tf_op jit(solution)/shard_map/ppermute | solution.py:51
  73.7 6.8 %collective-permute-start.21 = (bf16[16,256]{1,0:T(8,128)(2,1)S(1)}, bf16[16,256]{1,0:T(8,128)(2,1)S(1)}, u32[]{:S(2)}, u32[]{:S(2)}) collective-permute-start(bf16[16,256]{1,0:T(8,128)(2,1)S(1)} %convert_element_type.8), channel_id=1, source_target_pairs={{0,4},{1,5},{2,6},{3,7},{4,0},{5,1},{6,2},{7,3},{8,12},{9,13},{10,... | collective-permute-start | bytes 24584 | tf_op jit(solution)/shard_map/ppermute | solution.py:56
  76.7 5.6 %collective-permute-start.22 = (bf16[16,256]{1,0:T(8,128)(2,1)S(1)}, bf16[16,256]{1,0:T(8,128)(2,1)S(1)}, u32[]{:S(2)}, u32[]{:S(2)}) collective-permute-start(bf16[16,256]{1,0:T(8,128)(2,1)S(1)} %convert_element_type.8), channel_id=1, source_target_pairs={{0,6},{1,7},{2,4},{3,5},{4,2},{5,3},{6,0},{7,1},{8,14},{9,15},{10,... | collective-permute-start | bytes 24584 | tf_op jit(solution)/shard_map/ppermute | solution.py:56
  78.2 11.0 %collective-permute-start.24 = (bf16[4,128,256]{2,1,0:T(8,128)(2,1)S(1)}, bf16[4,128,256]{2,1,0:T(8,128)(2,1)S(1)}, u32[]{:S(2)}, u32[]{:S(2)}) collective-permute-start(bf16[4,128,256]{2,1,0:T(8,128)(2,1)S(1)} %get-tuple-element.80), channel_id=1, source_target_pairs={{0,6},{1,7},{2,4},{3,5},{4,2},{5,3},{6,0},{7,1},{8,14},{9,15},{10,... | collective-permute-start | bytes 786440 | tf_op jit(solution)/shard_map/ppermute | solution.py:51
  82.4 12.5 %collective-permute-start.25 = (bf16[4,128,256]{2,1,0:T(8,128)(2,1)S(1)}, bf16[4,128,256]{2,1,0:T(8,128)(2,1)S(1)}, u32[]{:S(2)}, u32[]{:S(2)}) collective-permute-start(bf16[4,128,256]{2,1,0:T(8,128)(2,1)S(1)} %get-tuple-element.81), channel_id=1, source_target_pairs={{0,2},{1,3},{2,0},{3,1},{4,6},{5,7},{6,4},{7,5},{8,10},{9,11},{10,... | collective-permute-start | bytes 786440 | tf_op jit(solution)/shard_map/ppermute | solution.py:51
  82.6 15.0 %collective-permute-start.26 = (bf16[4,128,256]{2,1,0:T(8,128)(2,1)S(1)}, bf16[4,128,256]{2,1,0:T(8,128)(2,1)S(1)}, u32[]{:S(2)}, u32[]{:S(2)}) collective-permute-start(bf16[4,128,256]{2,1,0:T(8,128)(2,1)S(1)} %get-tuple-element.82), channel_id=1, source_target_pairs={{0,7},{1,2},{2,1},{3,4},{4,3},{5,6},{6,5},{7,0},{8,15},{9,10},{10,... | collective-permute-start | bytes 786440 | tf_op jit(solution)/shard_map/ppermute | solution.py:51
  84.0 13.6 %collective-permute-start.27 = (bf16[4,128,256]{2,1,0:T(8,128)(2,1)S(1)}, bf16[4,128,256]{2,1,0:T(8,128)(2,1)S(1)}, u32[]{:S(2)}, u32[]{:S(2)}) collective-permute-start(bf16[4,128,256]{2,1,0:T(8,128)(2,1)S(1)} %get-tuple-element.83), channel_id=1, source_target_pairs={{0,1},{1,0},{2,3},{3,2},{4,5},{5,4},{6,7},{7,6},{8,9},{9,8},{10,11... | collective-permute-start | bytes 786440 | tf_op jit(solution)/shard_map/ppermute | solution.py:51
  85.7 11.9 %collective-permute-start.28 = (bf16[4,128,256]{2,1,0:T(8,128)(2,1)S(1)}, bf16[4,128,256]{2,1,0:T(8,128)(2,1)S(1)}, u32[]{:S(2)}, u32[]{:S(2)}) collective-permute-start(bf16[4,128,256]{2,1,0:T(8,128)(2,1)S(1)} %get-tuple-element.84), channel_id=1, source_target_pairs={{0,8},{8,0},{16,24},{24,16},{1,9},{9,1},{17,25},{25,17},{2,10},{10... | collective-permute-start | bytes 786440 | tf_op jit(solution)/shard_map/ppermute | solution.py:51
  89.2 11.3 %collective-permute-start.29 = (bf16[4,128,256]{2,1,0:T(8,128)(2,1)S(1)}, bf16[4,128,256]{2,1,0:T(8,128)(2,1)S(1)}, u32[]{:S(2)}, u32[]{:S(2)}) collective-permute-start(bf16[4,128,256]{2,1,0:T(8,128)(2,1)S(1)} %get-tuple-element.85), channel_id=1, source_target_pairs={{0,24},{8,16},{16,8},{24,0},{1,25},{9,17},{17,9},{25,1},{2,26},{10... | collective-permute-start | bytes 786440 | tf_op jit(solution)/shard_map/ppermute | solution.py:51
  103.0 11.1 %collective-permute-start.30 = (bf16[4,128,256]{2,1,0:T(8,128)(2,1)S(1)}, bf16[4,128,256]{2,1,0:T(8,128)(2,1)S(1)}, u32[]{:S(2)}, u32[]{:S(2)}) collective-permute-start(bf16[4,128,256]{2,1,0:T(8,128)(2,1)S(1)} %get-tuple-element.87), channel_id=1, source_target_pairs={{0,6},{1,7},{2,4},{3,5},{4,2},{5,3},{6,0},{7,1},{8,14},{9,15},{10,... | collective-permute-start | bytes 786440 | tf_op jit(solution)/shard_map/ppermute | solution.py:51
  105.0 14.3 %collective-permute-start.31 = (bf16[4,128,256]{2,1,0:T(8,128)(2,1)S(1)}, bf16[4,128,256]{2,1,0:T(8,128)(2,1)S(1)}, u32[]{:S(2)}, u32[]{:S(2)}) collective-permute-start(bf16[4,128,256]{2,1,0:T(8,128)(2,1)S(1)} %get-tuple-element.88), channel_id=1, source_target_pairs={{0,2},{1,3},{2,0},{3,1},{4,6},{5,7},{6,4},{7,5},{8,10},{9,11},{10,... | collective-permute-start | bytes 786440 | tf_op jit(solution)/shard_map/ppermute | solution.py:51
  105.3 16.4 %collective-permute-start.32 = (bf16[4,128,256]{2,1,0:T(8,128)(2,1)S(1)}, bf16[4,128,256]{2,1,0:T(8,128)(2,1)S(1)}, u32[]{:S(2)}, u32[]{:S(2)}) collective-permute-start(bf16[4,128,256]{2,1,0:T(8,128)(2,1)S(1)} %get-tuple-element.89), channel_id=1, source_target_pairs={{0,7},{1,2},{2,1},{3,4},{4,3},{5,6},{6,5},{7,0},{8,15},{9,10},{10,... | collective-permute-start | bytes 786440 | tf_op jit(solution)/shard_map/ppermute | solution.py:51
  105.4 16.3 %collective-permute-start.33 = (bf16[4,128,256]{2,1,0:T(8,128)(2,1)S(1)}, bf16[4,128,256]{2,1,0:T(8,128)(2,1)S(1)}, u32[]{:S(2)}, u32[]{:S(2)}) collective-permute-start(bf16[4,128,256]{2,1,0:T(8,128)(2,1)S(1)} %get-tuple-element.90), channel_id=1, source_target_pairs={{0,1},{1,0},{2,3},{3,2},{4,5},{5,4},{6,7},{7,6},{8,9},{9,8},{10,11... | collective-permute-start | bytes 786440 | tf_op jit(solution)/shard_map/ppermute | solution.py:51
  107.2 14.5 %collective-permute-start.34 = (bf16[4,128,256]{2,1,0:T(8,128)(2,1)S(1)}, bf16[4,128,256]{2,1,0:T(8,128)(2,1)S(1)}, u32[]{:S(2)}, u32[]{:S(2)}) collective-permute-start(bf16[4,128,256]{2,1,0:T(8,128)(2,1)S(1)} %get-tuple-element.91), channel_id=1, source_target_pairs={{0,8},{8,0},{16,24},{24,16},{1,9},{9,1},{17,25},{25,17},{2,10},{10... | collective-permute-start | bytes 786440 | tf_op jit(solution)/shard_map/ppermute | solution.py:51
  114.1 7.6 %collective-permute-start.35 = (bf16[4,128,256]{2,1,0:T(8,128)(2,1)S(1)}, bf16[4,128,256]{2,1,0:T(8,128)(2,1)S(1)}, u32[]{:S(2)}, u32[]{:S(2)}) collective-permute-start(bf16[4,128,256]{2,1,0:T(8,128)(2,1)S(1)} %get-tuple-element.92), channel_id=1, source_target_pairs={{0,24},{8,16},{16,8},{24,0},{1,25},{9,17},{17,9},{25,1},{2,26},{10... | collective-permute-start | bytes 786440 | tf_op jit(solution)/shard_map/ppermute | solution.py:51
  (13 other events, 246.2 us)

commit v4 on v3

v4 whole, which is shorter than its diff:
```python
import functools

import jax
import jax.numpy as jnp
from jax import lax
from jax.experimental import pallas as pl
from jax.experimental.pallas import tpu as pltpu
from jax.sharding import PartitionSpec as P

BLK = 128
DIRS = 6
CAP = 4
NEAR = 4 * CAP
ITERS = 2
EARLY = 5
ROWS = 512
SHIFTS = {2: 2, 3: -2}
OFFSETS = (1, -1, 2, -2)
ORDER = (2, 1, 3, 0, 4, 5)
HIGHEST = lax.Precision.HIGHEST
VMEM = pl.BlockSpec(memory_space=pltpu.VMEM)
SMEM = pl.BlockSpec(memory_space=pltpu.SMEM)
HBM = pl.BlockSpec(memory_space=pltpu.HBM)
ANY = pl.BlockSpec(memory_space=pl.ANY)
MIB = 1024 * 1024
PARAMS = pltpu.CompilerParams(vmem_limit_bytes=20 * MIB)


def f32(*shape):
    return jax.ShapeDtypeStruct(shape, jnp.float32)


def bf16(*shape):
    return jax.ShapeDtypeStruct(shape, jnp.bfloat16)


def in_hbm(array):
    return pltpu.with_memory_space_constraint(array, pltpu.HBM)


def is_lower(way):
    return lax.axis_index("sub" if way < 2 else "group") % 2 == 0


def exchanged(slab, way):
    axis = "sub" if way < 4 else "group"
    count = lax.axis_size(axis)
    steps = [SHIFTS.get(way, 1 if i % 2 == way % 2 else -1) for i in range(count)]
    return lax.ppermute(slab, axis, [(i, (i + step) % count) for i, step in enumerate(steps)])


def swapped(value, mask):
    count = lax.axis_size("sub")
    return lax.ppermute(value, "sub", [(i, i ^ mask) for i in range(count)])


def to_chips(chunks):
    return [chunks[0]] + [swapped(chunk, 2 * p) for p, chunk in enumerate(chunks) if p]


def slot_block(send, way, j):
    direction = way if way in SHIFTS else jnp.where(is_lower(way), way, way ^ 1)
    return jnp.maximum(send[direction * CAP + j], 0)


def slot_read(read, b):
    code = read[b]
    way = code // CAP
    swap = jnp.where(way < 2, is_lower(0), (way > 3) & is_lower(4))
    return jnp.where(swap, code ^ CAP, code)


def pick_blocks(send, values, slabs, ways):
    for slab, way in zip(slabs, ways):
        for j in range(CAP):
            slab[j] = values[slot_block(send, way, j)]


def stack_slabs(arrived, received):
    for way, slab in zip(ORDER, arrived):
        for j in range(CAP):
            received[way * CAP + j] = slab[j]


def as_column(row):
    return jnp.broadcast_to(row, (BLK, BLK)).T


def column_parts(cases):
    return [slice(w * BLK, (w + 1) * BLK) for w in range(cases // BLK)]


def matrix_copies(matrix, held, sems):
    return [
        pltpu.make_async_copy(
            matrix.at[pl.ds(i * ROWS, ROWS)], held.at[pl.ds(i * ROWS, ROWS)], sems.at[i]
        )
        for i in range(held.shape[0] // ROWS)
    ]


def each_rows(copies, matrix, rhs, consume):
    per = ROWS // BLK
    for i in range(matrix.shape[0] // ROWS):
        if copies:
            copies[i].wait()
            if i + 2 < len(copies):
                copies[i + 2].start()
        part = jnp.dot(
            matrix[pl.ds(i * ROWS, ROWS), :], rhs[...], preferred_element_type=jnp.float32
        )
        for k in range(per):
            consume(i * per + k, part[k * BLK : (k + 1) * BLK])


def solve(copies, matrix, rhs, columns, disp, narrow, proj):
    blocks = disp.shape[0]

    def consume(b, mine):
        disp[b] = mine
        narrow[b] = mine.astype(jnp.bfloat16)
        for cols in column_parts(mine.shape[1]):
            proj[b : b + 1, cols] = jnp.sum(columns[b] * mine[:, cols], axis=0, keepdims=True)

    proj[blocks:, :] = jnp.zeros((proj.shape[0] - blocks, proj.shape[1]), jnp.float32)
    each_rows(copies, matrix, rhs, consume)


def tell(wide, coarse_map, send, basis, told):
    subs = lax.axis_size("sub")
    here = lax.axis_index("sub")
    blocks = basis.shape[0]
    tall = (told.shape[0] - NEAR) // 2
    place = lax.broadcasted_iota(jnp.int32, (tall, BLK), 0) * BLK + lax.broadcasted_iota(
        jnp.int32, (tall, BLK), 1
    )
    own = jnp.zeros((tall, BLK), jnp.int32)
    for b in range(blocks):
        own = jnp.where(place == here * wide + b, coarse_map[0, b] + 1, own)
    theirs = jnp.zeros((tall, BLK), jnp.int32)
    for k in range(NEAR):
        block = jnp.maximum(send[0, k], 0)
        reader = lax.rem(here + OFFSETS[k // CAP] + subs, subs)
        theirs = jnp.where(place == reader * wide + k, coarse_map[0, block] + 1, theirs)
        told[k : k + 1, :] = basis[block]
    told[NEAR : NEAR + tall, :] = own.astype(jnp.float32)
    told[NEAR + tall :, :] = theirs.astype(jnp.float32)


def first_solve_kernel(wide, send, coarse_map, matrix, load, basis, disp, proj, columns, told, *rest):
    slabs, (held, *rest) = rest[:EARLY], rest[EARLY:]
    rhs, narrow, send_held, map_held, basis_held, rows, sems, more_sems = rest
    blocks = disp.shape[0]
    copies = matrix_copies(matrix, held, sems)
    pairs = ((send, send_held), (coarse_map, map_held), (basis, basis_held), (load, rhs))
    small = [
        pltpu.make_async_copy(source, target, more_sems.at[i])
        for i, (source, target) in enumerate(pairs)
    ]
    for copy in small + copies[:2]:
        copy.start()
    for copy in small[:3]:
        copy.wait()
    for b in range(blocks):
        row = basis_held[:, b * BLK : (b + 1) * BLK]
        rows[b] = row
        columns[b] = as_column(row)
    tell(wide, map_held, send_held, rows, told)
    small[3].wait()
    solve(copies, held, rhs, columns, disp, narrow, proj)
    pick_blocks(send_held.at[0], narrow, slabs, range(EARLY))


def next_solve_kernel(send, read, matrix, load, columns, dual, *rest):
    arrived, (mult, disp, proj), rest = rest[:DIRS], rest[DIRS : DIRS + 3], rest[DIRS + 3 :]
    *slabs, received, rhs, narrow = rest
    stack_slabs(arrived, received)
    for b in range(disp.shape[0]):
        far = received[slot_read(read, b)]
        step = dual[b].astype(jnp.float32) - far.astype(jnp.float32)
        mult[b] = step
        rows = pl.ds(b * BLK, BLK)
        rhs[rows, :] = (load[rows, :].astype(jnp.float32) - step).astype(jnp.bfloat16)
    solve([], matrix, rhs, columns, disp, narrow, proj)
    pick_blocks(send, narrow, slabs, range(len(slabs)))


def coarse_kernel(wide, chips, bring, send, basis, near_basis, disp, columns, *rest):
    parts, tables, rest = rest[:chips], rest[chips : 2 * chips], rest[2 * chips :]
    if bring:
        matrix, *rest, sem = rest
    (corrected, near), slabs, (ordered, held) = rest[:2], rest[2:4], rest[-2:]
    if bring:
        copy = pltpu.make_async_copy(matrix, rest[4], sem)
        copy.start()
    here = lax.axis_index("sub")
    cases = disp.shape[2]
    for p, part in enumerate(parts):
        for e in range(2):
            at = pl.multiple_of((here ^ (2 * p + e)) * wide, wide)
            ordered[pl.ds(at, wide), :] = part[e * wide : (e + 1) * wide, :].astype(jnp.float32)
    total = sum(table[2 * wide :, :].astype(jnp.float32) for table in tables)
    rows = [0.0, 0.0]
    for q, kind, group, cols in pieces_of(ordered.shape[0], cases):
        rows[kind] += jnp.dot(
            total[group * wide : (group + 1) * wide, cols],
            ordered[q * BLK : (q + 1) * BLK, :],
            preferred_element_type=jnp.float32,
            precision=HIGHEST,
        )
    near[:, :cases] = rows[1]
    near[:, cases:] = near_basis[...]
    for b in range(disp.shape[0]):
        held[b, :, :cases] = rows[0][b : b + 1]
        held[b, :, cases:] = basis[:, b * BLK : (b + 1) * BLK]
    for j in range(CAP):
        slabs[0][j : j + 1, :] = held[slot_block(send, 4, j)]
    for b in range(disp.shape[0]):
        for cols in column_parts(cases):
            corrected[b, :, cols] = (
                disp[b, :, cols] + columns[b] * rows[0][b : b + 1, cols]
            ).astype(jnp.bfloat16)
    pick_blocks(send, corrected, slabs[1:], (5,))
    if bring:
        copy.wait()


def dirichlet_kernel(send, read, weights, matrix, corrected, near, far_rows, *rest):
    arrived, dual, rest = rest[:DIRS], rest[DIRS], rest[DIRS + 1 :]
    slabs, (received, rows, rhs) = rest[:DIRS], rest[DIRS:]
    blocks, _, cases = corrected.shape
    stack_slabs(arrived, received)
    for k in range(NEAR):
        rows[k] = near[k : k + 1, :]
    for k in range(NEAR, DIRS * CAP):
        j = k - NEAR
        rows[k] = far_rows[j : j + 1, :] if j < CAP else jnp.zeros_like(rows[k])
    for b in range(blocks):
        place, code = slot_read(read, b), read[b]
        row = jnp.where(code < NEAR, code, place)
        far_column = as_column(rows[row, :, cases:])
        for cols in column_parts(cases):
            far = received[place, :, cols].astype(jnp.float32) + far_column * rows[row, :, cols]
            far = far.astype(jnp.bfloat16).astype(jnp.float32)
            gap = corrected[b, :, cols].astype(jnp.float32) - far
            rhs[b * BLK : (b + 1) * BLK, cols] = (gap * weights[b]).astype(jnp.bfloat16)

    def consume(b, mine):
        dual[b] = (mine * weights[b]).astype(jnp.bfloat16)

    each_rows([], matrix, rhs, consume)
    pick_blocks(send, dual, slabs, range(DIRS))


def finish_kernel(read, mult, dual, *rest):
    arrived, (out, received, ready, sems) = rest[:DIRS], rest[DIRS:]
    stack_slabs(arrived, received)
    copies = []
    for b in range(out.shape[0]):
        far = received[slot_read(read, b)]
        ready[b] = mult[b] + (dual[b].astype(jnp.float32) - far.astype(jnp.float32))
        copies.append(pltpu.make_async_copy(ready.at[b], out.at[b], sems.at[b]))
        copies[b].start()
    for copy in copies:
        copy.wait()


def pieces_of(lanes, cases):
    across = cases // BLK
    return [
        (i // 2, i % 2, i // across, slice(i % across * BLK, (i % across + 1) * BLK))
        for i in range(2 * (lanes // BLK))
    ]


def share_kernel(wide, own_rows, mine, theirs, proj, *rest):
    near_basis, keep, give, held = rest[-4:]
    high, order = own_rows.shape
    subs, here = lax.axis_size("sub"), lax.axis_index("sub")
    chips = mine.shape[0]
    tall = (mine.shape[1] - NEAR) // 2
    sums = sum(names[p, NEAR:, :] for p in range(chips) for names in (mine, theirs))
    sums = sums.astype(jnp.int32) - 1

    def lanes_of(first):
        return jnp.concatenate([sums[first + r : first + r + 1] for r in range(tall)], axis=1)

    dofs, lanes = (lanes_of(0), lanes_of(tall)), subs * wide
    local = (lax.broadcasted_iota(jnp.int32, (high, lanes), 0) + here * high == dofs[0][:, :lanes])
    local = local.astype(jnp.float32).astype(jnp.bfloat16)
    source = own_rows[...].astype(jnp.bfloat16)
    for kind in range(2):
        pick = lax.broadcasted_iota(jnp.int32, (order, lanes), 0) == dofs[kind][:, :lanes]
        chosen = jnp.dot(
            source,
            pick.astype(jnp.float32).astype(jnp.bfloat16),
            preferred_element_type=jnp.float32,
        )
        held[kind] = lax.dot_general(
            chosen.astype(jnp.bfloat16),
            local,
            (((0,), (0,)), ((), ())),
            preferred_element_type=jnp.float32,
        )
    for e, target in enumerate((keep, give)):
        target[chips, : wide, :] = proj[...].astype(jnp.bfloat16)
        for p in range(chips):
            at = pl.ds(pl.multiple_of((here ^ (2 * p + e)) * wide, wide), wide)
            for q, kind, group, cols in pieces_of(lanes, target.shape[2]):
                target[p, group * wide : (group + 1) * wide, cols] = held[
                    kind, at, q * BLK : (q + 1) * BLK
                ].astype(jnp.bfloat16)
    for k in range(NEAR):
        sender = lax.rem(here - OFFSETS[k // CAP] + subs, subs) ^ here
        p, same = sender // 2, sender % 2 == 0
        near_basis[k : k + 1, :] = jnp.where(same, mine[p, k : k + 1], theirs[p, k : k + 1])


def merge_kernel(wide, chips, keep, got, *rest):
    for p, chunk in enumerate(rest[-chips:]):
        chunk[:wide, :] = keep[chips, :wide, :]
        chunk[wide : 2 * wide, :] = got[chips, :wide, :]
        chunk[2 * wide :, :] = keep[p] + got[p]


def on_device(
    load_cases,
    inv_schur,
    schur_blocks,
    coarse_basis,
    coarse_map,
    multiplicity,
    recv_code,
    send_blocks,
    coarse_inv,
):
    dofs = inv_schur.shape[2]
    cases = load_cases.shape[3]
    blocks = dofs // BLK
    subs = lax.axis_size("sub")
    chips = subs // 2
    wide = NEAR * -(-blocks // NEAR)
    lanes = subs * wide
    tall = 4 * -(-lanes // (4 * BLK))
    groups = -(-2 * (lanes // BLK) // (cases // BLK))
    solve_matrix = inv_schur[0, 0]
    dirichlet_matrix = schur_blocks[0, 0]
    load = load_cases[0, 0]
    read = recv_code[0, 0]
    send = send_blocks[0, 0]
    weights = 1.0 / multiplicity[0, 0].astype(jnp.float32)
    whole = f32(blocks, BLK, cases)
    halved = bf16(blocks, BLK, cases)
    slab = bf16(CAP, BLK, cases)
    block_columns = f32(blocks, BLK, BLK)
    received = pltpu.VMEM((DIRS * CAP, BLK, cases), jnp.bfloat16)
    narrow = pltpu.VMEM((blocks, BLK, cases), jnp.bfloat16)
    rhs = pltpu.VMEM((dofs, cases), jnp.bfloat16)
    steps = pltpu.SemaphoreType.DMA((dofs // ROWS,))
    resident = pltpu.VMEM((dofs, dofs), jnp.bfloat16)

    disp, proj, columns, told, *slabs, solve_matrix = pl.pallas_call(
        functools.partial(first_solve_kernel, wide),
        out_shape=[whole, f32(wide, cases), block_columns, f32(NEAR + 2 * tall, BLK)]
        + [slab] * EARLY
        + [resident],
        in_specs=[HBM] * 5,
        out_specs=[VMEM] * (5 + EARLY),
        scratch_shapes=[
            rhs,
            narrow,
            pltpu.SMEM((1, DIRS * CAP), jnp.int32),
            pltpu.SMEM((1, blocks), jnp.int32),
            pltpu.VMEM((1, dofs), jnp.float32),
            pltpu.VMEM((blocks, 1, BLK), jnp.float32),
            steps,
            pltpu.SemaphoreType.DMA((4,)),
        ],
        compiler_params=PARAMS,
    )(
        in_hbm(send_blocks[0]), in_hbm(coarse_map[0]), in_hbm(solve_matrix), in_hbm(load),
        in_hbm(coarse_basis[0]),
    )
    arrived = {way: exchanged(slabs[way], way) for way in ORDER if way < EARLY}
    mine = jnp.stack(to_chips([told] * chips))
    theirs = swapped(mine, 1)
    outgoing = bf16(chips + 1, groups * wide, cases)
    near_basis, keep, give = pl.pallas_call(
        functools.partial(share_kernel, wide),
        out_shape=[f32(NEAR, BLK), outgoing, outgoing],
        in_specs=[VMEM] * 4 + [ANY] * 1,
        out_specs=[VMEM] * 3,
        scratch_shapes=[pltpu.VMEM((2, lanes, lanes), jnp.float32)],
        compiler_params=PARAMS,
    )(coarse_inv[0], mine, theirs, proj, arrived[4])
    chunks = pl.pallas_call(
        functools.partial(merge_kernel, wide, chips),
        out_shape=[bf16((2 + groups) * wide, cases)] * chips,
        in_specs=[VMEM] * 2 + [ANY] * 0,
        out_specs=[VMEM] * chips,
        compiler_params=PARAMS,
    )(keep, swapped(give, 1))
    parts = tables = to_chips(chunks)

    for iteration in range(ITERS):
        bring = iteration == 0
        if iteration:
            arrived = {way: exchanged(slabs[way], way) for way in ORDER if way < EARLY}
            proj = proj.astype(jnp.bfloat16)
            parts = to_chips([jnp.concatenate([proj, swapped(proj, 1)])] * chips)
        corrected, near, *far = pl.pallas_call(
            functools.partial(coarse_kernel, wide, chips, bring),
            out_shape=[halved, f32(NEAR, cases + BLK), f32(CAP, cases + BLK), slab]
            + [resident] * bring,
            in_specs=[SMEM] + [VMEM] * (4 + 2 * chips) + [HBM] * bring,
            out_specs=[VMEM] * (4 + bring),
            scratch_shapes=[
                pltpu.VMEM((lanes, cases), jnp.float32),
                pltpu.VMEM((blocks, 1, cases + BLK), jnp.float32),
            ]
            + [pltpu.SemaphoreType.DMA] * bring,
            compiler_params=PARAMS,
        )(
            send, coarse_basis[0], near_basis, disp, columns, *parts, *tables,
            *[in_hbm(dirichlet_matrix)] * bring,
        )
        if bring:
            *far, dirichlet_matrix = far
        far_rows, arrived[5] = [exchanged(far[way - 4], way) for way in (4, 5)]
        dual, *slabs = pl.pallas_call(
            dirichlet_kernel,
            out_shape=[halved] + [slab] * DIRS,
            in_specs=[SMEM] * 3 + [VMEM] * (4 + DIRS),
            out_specs=[VMEM] * (1 + DIRS),
            scratch_shapes=[received, pltpu.VMEM((DIRS * CAP, 1, cases + BLK), jnp.float32), rhs],
            compiler_params=PARAMS,
        )(
            send, read, weights, dirichlet_matrix, corrected, near, far_rows,
            *[arrived[way] for way in ORDER],
        )
        arrived = [exchanged(slabs[way], way) for way in ORDER]
        if iteration + 1 < ITERS:
            mult, disp, proj, *slabs = pl.pallas_call(
                next_solve_kernel,
                out_shape=[whole, whole, f32(wide, cases)] + [slab] * EARLY,
                in_specs=[SMEM] * 2 + [VMEM] * (4 + DIRS),
                out_specs=[VMEM] * (3 + EARLY),
                scratch_shapes=[received, rhs, narrow],
                compiler_params=PARAMS,
            )(send, read, solve_matrix, load, columns, dual, *arrived)
    out = pl.pallas_call(
        finish_kernel,
        out_shape=whole,
        in_specs=[SMEM] + [VMEM] * (2 + DIRS),
        out_specs=HBM,
        scratch_shapes=[
            received,
            pltpu.VMEM((blocks, BLK, cases), jnp.float32),
            pltpu.SemaphoreType.DMA((blocks,)),
        ],
        compiler_params=PARAMS,
    )(read, mult, dual, *arrived)
    return out.reshape(1, 1, dofs, cases)


def solution(mesh):
    split = P("group", "sub")
    return jax.shard_map(
        on_device, mesh=mesh, in_specs=(split,) * 9, out_specs=split, check_vma=False
    )
```

time: 125 us -> 118 us (0.944); the launches traced: 124 us -> 118 us
  waiting for transfers between devices: 58 us -> 55.3 us
  starting transfers between devices: 46.4 us -> 44.7 us
    ppermute x24 -> x26, waiting for transfers between devices: 47.8 us -> 44 us  [exchanged(): lax.ppermute(slab, axis, [(i, (i + step) % count) for i, step in enumerat...]
    ppermute x12, starting transfers between devices: 14.9 us -> 13.5 us  [swapped(): return lax.ppermute(value, 'sub', [(i, i ^ mask) for i in range(count)])]
    ppermute x24 -> x26, starting transfers between devices: 31.6 us -> 31.2 us  [exchanged(): lax.ppermute(slab, axis, [(i, (i + step) % count) for i, step in enumerat...]
  transfers between devices with their start and end apart: 36 -> 38, of which waited for: 19 -> 19; matrix products, arithmetic and copies ran while one was open for 0% -> 0% of each run, Pallas kernels for 2% -> 4%
where the time goes in v4:
time: 118 us
  waiting for transfers between devices  55.3 us (47%)
  starting transfers between devices  44.7 us (38%)
  Pallas kernels  17.9 us (15%)
    ppermute x26, waiting for transfers between devices, exchanged(): lax.ppermute(slab, axis, [(i, (i + step) % count) for i, step in enumerat...  44 us
    ppermute x26, starting transfers between devices, exchanged(): lax.ppermute(slab, axis, [(i, (i + step) % count) for i, step in enumerat...  31.2 us
    ppermute x12, starting transfers between devices, swapped(): return lax.ppermute(value, 'sub', [(i, i ^ mask) for i in range(count)])  13.5 us
    ppermute x12, waiting for transfers between devices, swapped(): return lax.ppermute(value, 'sub', [(i, i ^ mask) for i in range(count)])  11.3 us
    pallas_call x2, Pallas kernels, on_device(): pl.pallas_call(dirichlet_kernel, out_shape=[halved] + [slab] * DIRS, in_s...  4.89 us
    pallas_call x1, Pallas kernels, on_device(): pl.pallas_call(functools.partial(first_solve_kernel, wide), out_shape=[wh...  4.35 us
    pallas_call x2, Pallas kernels, on_device(): pl.pallas_call(functools.partial(coarse_kernel, wide, chips, bring), out_...  3.91 us
  transfers between devices with their start and end apart: 38, of which 19 were waited for; matrix products, arithmetic and copies ran while one was open for 0% of the time, Pallas kernels for 4%

profile of v4, /device:TPU:0, one launch (start us, length us, event | category | flops | bytes accessed | tf_op | source)
XLA Modules:
  0.0 118.2 jit_solution(5652026124325577982)
XLA Ops:
  0.0 4.3 %shard_map.91 = (f32[12,128,256]{2,1,0:T(8,128)S(1)}, f32[16,256]{1,0:T(8,128)S(1)}, f32[12,128,128]{2,1,0:T(8,128)S(1)}, f32[24,128]{1,0:T(8,128)S(1)}, bf16[4,...) custom-call(s32[1,24]{1,0:T(1,128)} %bitcast.22, ...), custom_call_target="tpu_custom_call" | custom-call | tf_op jit(solution)/shard_map/pallas_call | solution.py:362
  4.4 3.0 %collective-permute-start.4 = (bf16[4,128,256]{2,1,0:T(8,128)(2,1)S(1)}, bf16[4,128,256]{2,1,0:T(8,128)(2,1)S(1)}, u32[]{:S(2)}, u32[]{:S(2)}) collective-permute-start(bf16[4,128,256]{2,1,0:T(8,128)(2,1)S(1)} %get-tuple-element.57), channel_id=1, source_target_pairs={{0,8},{8,0},{16,24},{24,16},{1,9},{9,1},{17,25},{25,17},{2,10},{10... | collective-permute-start | bytes 786440 | tf_op jit(solution)/shard_map/ppermute | solution.py:49
  7.4 3.6 %collective-permute-start.2 = (f32[24,128]{1,0:T(8,128)S(1)}, f32[24,128]{1,0:T(8,128)S(1)}, u32[]{:S(2)}, u32[]{:S(2)}) collective-permute-start(f32[24,128]{1,0:T(8,128)S(1)} %get-tuple-element.55), channel_id=1, source_target_pairs={{0,6},{1,7},{2,4},{3,5},{4,2},{5,3},{6,0},{7,1},{8,14},{9,15},{10,... | collective-permute-start | bytes 36872 | tf_op jit(solution)/shard_map/ppermute | solution.py:54
  13.0 4.2 %collective-permute-done.1 = f32[24,128]{1,0:T(8,128)S(1)} collective-permute-done((f32[24,128]{1,0:T(8,128)S(1)}, f32[24,128]{1,0:T(8,128)S(1)}, u32[]{:S(2)}, u32[]{:S(2)}) %collective-permute-start.1) | collective-permute-done | bytes 12320 | tf_op jit(solution)/shard_map/ppermute | solution.py:54
  21.2 3.8 %collective-permute-start.8 = (bf16[48,256]{1,0:T(8,128)(2,1)S(1)}, bf16[48,256]{1,0:T(8,128)(2,1)S(1)}, u32[]{:S(2)}, u32[]{:S(2)}) collective-permute-start(bf16[48,256]{1,0:T(8,128)(2,1)S(1)} %get-tuple-element.65), channel_id=1, source_target_pairs={{0,6},{1,7},{2,4},{3,5},{4,2},{5,3},{6,0},{7,1},{8,14},{9,15},{10,... | collective-permute-start | bytes 73736 | tf_op jit(solution)/shard_map/ppermute | solution.py:54
  25.4 3.3 %collective-permute-start.13 = (bf16[4,128,256]{2,1,0:T(8,128)(2,1)S(1)}, bf16[4,128,256]{2,1,0:T(8,128)(2,1)S(1)}, u32[]{:S(2)}, u32[]{:S(2)}) collective-permute-start(bf16[4,128,256]{2,1,0:T(8,128)(2,1)S(1)} %get-tuple-element.73), channel_id=1, source_target_pairs={{0,1},{1,0},{2,3},{3,2},{4,5},{5,4},{6,7},{7,6},{8,9},{9,8},{10,11... | collective-permute-start | bytes 786440 | tf_op jit(solution)/shard_map/ppermute | solution.py:49
  28.7 2.9 %shard_map.94 = (bf16[12,128,256]{2,1,0:T(8,128)(2,1)S(1)}, f32[16,384]{1,0:T(8,128)S(1)}, f32[4,384]{1,0:T(4,128)S(1)}, bf16[4,128,256]{2,1,0:T(8,128)(2,1)S(1)}, bf16[1536,1536]{1,0:T(8,128)(2,1)S(1)}) custom-call(s32[24]{0:T(128)S(1)} %bitcast.23, f32[1,1536]{1,0:T(1,128)S(1)} %bitcast.20, f32[16,128]{1,0:T(8,128)S(1)} %get-tuple-element.58.near_basis, ...), custom_call_target="tpu_custom_call" | custom-call | tf_op jit(solution)/shard_map/pallas_call | solution.py:411
  31.6 1.6 %collective-permute-start.14 = (bf16[4,128,256]{2,1,0:T(8,128)(2,1)S(1)}, bf16[4,128,256]{2,1,0:T(8,128)(2,1)S(1)}, u32[]{:S(2)}, u32[]{:S(2)}) collective-permute-start(bf16[4,128,256]{2,1,0:T(8,128)(2,1)S(1)} %get-tuple-element.74), channel_id=1, source_target_pairs={{0,24},{8,16},{16,8},{24,0},{1,25},{9,17},{17,9},{25,1},{2,26},{10... | collective-permute-start | bytes 786440 | tf_op jit(solution)/shard_map/ppermute | solution.py:49
  33.1 1.5 %collective-permute-start.9 = (f32[4,384]{1,0:T(4,128)S(1)}, f32[4,384]{1,0:T(4,128)S(1)}, u32[]{:S(2)}, u32[]{:S(2)}) collective-permute-start(f32[4,384]{1,0:T(4,128)S(1)} %get-tuple-element.69), channel_id=1, source_target_pairs={{0,8},{8,0},{16,24},{24,16},{1,9},{9,1},{17,25},{25,17},{2,10},{10... | collective-permute-start | bytes 18440 | tf_op jit(solution)/shard_map/ppermute | solution.py:49
  35.4 2.9 %collective-permute-done.12.rest_2_ = bf16[4,128,256]{2,1,0:T(8,128)(2,1)S(1)} collective-permute-done((bf16[4,128,256]{2,1,0:T(8,128)(2,1)S(1)}, bf16[4,128,256]{2,1,0:T(8,128)(2,1)S(1)}, u32[]{:S(2)}, u32[]{:S(2)}) %collective-permute-start.12) | collective-permute-done | bytes 262176 | tf_op jit(solution)/shard_map/ppermute | solution.py:49
  38.4 2.6 %collective-permute-done.9.far_rows = f32[4,384]{1,0:T(4,128)S(1)} collective-permute-done((f32[4,384]{1,0:T(4,128)S(1)}, f32[4,384]{1,0:T(4,128)S(1)}, u32[]{:S(2)}, u32[]{:S(2)}) %collective-permute-start.9) | collective-permute-done | bytes 6176 | tf_op jit(solution)/shard_map/ppermute | solution.py:49
  41.0 2.4 %shard_map.95 = (bf16[12,128,256]{2,1,0:T(8,128)(2,1)S(1)}, bf16[4,128,256]{2,1,0:T(8,128)(2,1)S(1)}, bf16[4,128,256]{2,1,0:T(8,128)(2,1)S(1)}, bf16[4,128,256]{...) custom-call(s32[24]{0:T(128)S(1)} %bitcast.24, ...), custom_call_target="tpu_custom_call" | custom-call | tf_op jit(solution)/shard_map/pallas_call | solution.py:430
  43.5 2.3 %collective-permute-start.16 = (bf16[4,128,256]{2,1,0:T(8,128)(2,1)S(1)}, bf16[4,128,256]{2,1,0:T(8,128)(2,1)S(1)}, u32[]{:S(2)}, u32[]{:S(2)}) collective-permute-start(bf16[4,128,256]{2,1,0:T(8,128)(2,1)S(1)} %get-tuple-element.77), channel_id=1, source_target_pairs={{0,7},{1,2},{2,1},{3,4},{4,3},{5,6},{6,5},{7,0},{8,15},{9,10},{10,... | collective-permute-start | bytes 786440 | tf_op jit(solution)/shard_map/ppermute | solution.py:49
  45.8 1.5 %collective-permute-start.17 = (bf16[4,128,256]{2,1,0:T(8,128)(2,1)S(1)}, bf16[4,128,256]{2,1,0:T(8,128)(2,1)S(1)}, u32[]{:S(2)}, u32[]{:S(2)}) collective-permute-start(bf16[4,128,256]{2,1,0:T(8,128)(2,1)S(1)} %get-tuple-element.78), channel_id=1, source_target_pairs={{0,6},{1,7},{2,0},{3,1},{4,2},{5,3},{6,4},{7,5},{8,14},{9,15},{10,... | collective-permute-start | bytes 786440 | tf_op jit(solution)/shard_map/ppermute | solution.py:49
  47.8 6.8 %collective-permute-done.15.rest_0_ = bf16[4,128,256]{2,1,0:T(8,128)(2,1)S(1)} collective-permute-done((bf16[4,128,256]{2,1,0:T(8,128)(2,1)S(1)}, bf16[4,128,256]{2,1,0:T(8,128)(2,1)S(1)}, u32[]{:S(2)}, u32[]{:S(2)}) %collective-permute-start.15) | collective-permute-done | bytes 262176 | tf_op jit(solution)/shard_map/ppermute | solution.py:49
  56.5 6.2 %collective-permute-done.17.rest_2_ = bf16[4,128,256]{2,1,0:T(8,128)(2,1)S(1)} collective-permute-done((bf16[4,128,256]{2,1,0:T(8,128)(2,1)S(1)}, bf16[4,128,256]{2,1,0:T(8,128)(2,1)S(1)}, u32[]{:S(2)}, u32[]{:S(2)}) %collective-permute-start.17) | collective-permute-done | bytes 262176 | tf_op jit(solution)/shard_map/ppermute | solution.py:49
  62.8 2.2 %shard_map.96 = (f32[12,128,256]{2,1,0:T(8,128)S(1)}, f32[12,128,256]{2,1,0:T(8,128)S(1)}, f32[16,256]{1,0:T(8,128)S(1)}, bf16[4,128,256]{2,1,0:T(8,128)(2,1)S(1...) custom-call(s32[24]{0:T(128)S(1)} %bitcast.25, ...), custom_call_target="tpu_custom_call" | custom-call | tf_op jit(solution)/shard_map/pallas_call | solution.py:443
  67.0 3.1 %collective-permute-start.24 = (bf16[32,256]{1,0:T(8,128)(2,1)S(1)}, bf16[32,256]{1,0:T(8,128)(2,1)S(1)}, u32[]{:S(2)}, u32[]{:S(2)}) collective-permute-start(bf16[32,256]{1,0:T(8,128)(2,1)S(1)} %pad_maximum_fusion.1.rest_0_), channel_id=1, source_target_pairs={{0,6},{1,7},{2,4},{3,5},{4,2},{5,3},{6,0},{7,1},{8,14},{9,15},{10,... | collective-permute-start | bytes 49160 | tf_op jit(solution)/shard_map/ppermute | solution.py:54
  71.4 2.6 %collective-permute-done.24.rest_3_ = bf16[32,256]{1,0:T(8,128)(2,1)S(1)} collective-permute-done((bf16[32,256]{1,0:T(8,128)(2,1)S(1)}, bf16[32,256]{1,0:T(8,128)(2,1)S(1)}, u32[]{:S(2)}, u32[]{:S(2)}) %collective-permute-start.24) | collective-permute-done | bytes 16416 | tf_op jit(solution)/shard_map/ppermute | solution.py:54
  77.8 2.2 %collective-permute-start.29 = (bf16[4,128,256]{2,1,0:T(8,128)(2,1)S(1)}, bf16[4,128,256]{2,1,0:T(8,128)(2,1)S(1)}, u32[]{:S(2)}, u32[]{:S(2)}) collective-permute-start(bf16[4,128,256]{2,1,0:T(8,128)(2,1)S(1)} %get-tuple-element.91), channel_id=1, source_target_pairs={{0,1},{1,0},{2,3},{3,2},{4,5},{5,4},{6,7},{7,6},{8,9},{9,8},{10,11... | collective-permute-start | bytes 786440 | tf_op jit(solution)/shard_map/ppermute | solution.py:49
  80.0 1.5 %collective-permute-start.30 = (bf16[4,128,256]{2,1,0:T(8,128)(2,1)S(1)}, bf16[4,128,256]{2,1,0:T(8,128)(2,1)S(1)}, u32[]{:S(2)}, u32[]{:S(2)}) collective-permute-start(bf16[4,128,256]{2,1,0:T(8,128)(2,1)S(1)} %get-tuple-element.92), channel_id=1, source_target_pairs={{0,8},{8,0},{16,24},{24,16},{1,9},{9,1},{17,25},{25,17},{2,10},{10... | collective-permute-start | bytes 786440 | tf_op jit(solution)/shard_map/ppermute | solution.py:49
  82.8 4.0 %collective-permute-done.27.rest_1_ = bf16[4,128,256]{2,1,0:T(8,128)(2,1)S(1)} collective-permute-done((bf16[4,128,256]{2,1,0:T(8,128)(2,1)S(1)}, bf16[4,128,256]{2,1,0:T(8,128)(2,1)S(1)}, u32[]{:S(2)}, u32[]{:S(2)}) %collective-permute-start.27) | collective-permute-done | bytes 262176 | tf_op jit(solution)/shard_map/ppermute | solution.py:49
  86.8 3.2 %collective-permute-done.28.rest_2_ = bf16[4,128,256]{2,1,0:T(8,128)(2,1)S(1)} collective-permute-done((bf16[4,128,256]{2,1,0:T(8,128)(2,1)S(1)}, bf16[4,128,256]{2,1,0:T(8,128)(2,1)S(1)}, u32[]{:S(2)}, u32[]{:S(2)}) %collective-permute-start.28) | collective-permute-done | bytes 262176 | tf_op jit(solution)/shard_map/ppermute | solution.py:49
  90.0 4.6 %collective-permute-done.31.rest_5_ = bf16[4,128,256]{2,1,0:T(8,128)(2,1)S(1)} collective-permute-done((bf16[4,128,256]{2,1,0:T(8,128)(2,1)S(1)}, bf16[4,128,256]{2,1,0:T(8,128)(2,1)S(1)}, u32[]{:S(2)}, u32[]{:S(2)}) %collective-permute-start.31) | collective-permute-done | bytes 262176 | tf_op jit(solution)/shard_map/ppermute | solution.py:49
  94.6 2.4 %shard_map.98 = (bf16[12,128,256]{2,1,0:T(8,128)(2,1)S(1)}, bf16[4,128,256]{2,1,0:T(8,128)(2,1)S(1)}, bf16[4,128,256]{2,1,0:T(8,128)(2,1)S(1)}, bf16[4,128,256]{...) custom-call(s32[24]{0:T(128)S(1)} %bitcast.27, ...), custom_call_target="tpu_custom_call" | custom-call | tf_op jit(solution)/shard_map/pallas_call | solution.py:430
  97.1 2.3 %collective-permute-start.33 = (bf16[4,128,256]{2,1,0:T(8,128)(2,1)S(1)}, bf16[4,128,256]{2,1,0:T(8,128)(2,1)S(1)}, u32[]{:S(2)}, u32[]{:S(2)}) collective-permute-start(bf16[4,128,256]{2,1,0:T(8,128)(2,1)S(1)} %get-tuple-element.96), channel_id=1, source_target_pairs={{0,7},{1,2},{2,1},{3,4},{4,3},{5,6},{6,5},{7,0},{8,15},{9,10},{10,... | collective-permute-start | bytes 786440 | tf_op jit(solution)/shard_map/ppermute | solution.py:49
  99.4 1.5 %collective-permute-start.34 = (bf16[4,128,256]{2,1,0:T(8,128)(2,1)S(1)}, bf16[4,128,256]{2,1,0:T(8,128)(2,1)S(1)}, u32[]{:S(2)}, u32[]{:S(2)}) collective-permute-start(bf16[4,128,256]{2,1,0:T(8,128)(2,1)S(1)} %get-tuple-element.97), channel_id=1, source_target_pairs={{0,6},{1,7},{2,0},{3,1},{4,2},{5,3},{6,4},{7,5},{8,14},{9,15},{10,... | collective-permute-start | bytes 786440 | tf_op jit(solution)/shard_map/ppermute | solution.py:49
  100.9 1.5 %collective-permute-start.36 = (bf16[4,128,256]{2,1,0:T(8,128)(2,1)S(1)}, bf16[4,128,256]{2,1,0:T(8,128)(2,1)S(1)}, u32[]{:S(2)}, u32[]{:S(2)}) collective-permute-start(bf16[4,128,256]{2,1,0:T(8,128)(2,1)S(1)} %get-tuple-element.99), channel_id=1, source_target_pairs={{0,8},{8,0},{16,24},{24,16},{1,9},{9,1},{17,25},{25,17},{2,10},{10... | collective-permute-start | bytes 786440 | tf_op jit(solution)/shard_map/ppermute | solution.py:49
  102.4 5.8 %collective-permute-done.32.rest_0_ = bf16[4,128,256]{2,1,0:T(8,128)(2,1)S(1)} collective-permute-done((bf16[4,128,256]{2,1,0:T(8,128)(2,1)S(1)}, bf16[4,128,256]{2,1,0:T(8,128)(2,1)S(1)}, u32[]{:S(2)}, u32[]{:S(2)}) %collective-permute-start.32) | collective-permute-done | bytes 262176 | tf_op jit(solution)/shard_map/ppermute | solution.py:49
  108.2 1.6 %collective-permute-start.37 = (bf16[4,128,256]{2,1,0:T(8,128)(2,1)S(1)}, bf16[4,128,256]{2,1,0:T(8,128)(2,1)S(1)}, u32[]{:S(2)}, u32[]{:S(2)}) collective-permute-start(bf16[4,128,256]{2,1,0:T(8,128)(2,1)S(1)} %get-tuple-element.100), channel_id=1, source_target_pairs={{0,24},{8,16},{16,8},{24,0},{1,25},{9,17},{17,9},{25,1},{2,26},{10... | collective-permute-start | bytes 786440 | tf_op jit(solution)/shard_map/ppermute | solution.py:49
  110.1 6.3 %collective-permute-done.34.rest_2_ = bf16[4,128,256]{2,1,0:T(8,128)(2,1)S(1)} collective-permute-done((bf16[4,128,256]{2,1,0:T(8,128)(2,1)S(1)}, bf16[4,128,256]{2,1,0:T(8,128)(2,1)S(1)}, u32[]{:S(2)}, u32[]{:S(2)}) %collective-permute-start.34) | collective-permute-done | bytes 262176 | tf_op jit(solution)/shard_map/ppermute | solution.py:49
  116.3 1.9 %shard_map.99 = f32[12,128,256]{2,1,0:T(8,128)} custom-call(s32[12]{0:T(128)S(1)} %bitcast.32, f32[12,128,256]{2,1,0:T(8,128)S(1)} %get-tuple-element.82.mult, bf16[12,128,256]{2,1,0:T(8,128)(2,1)S(1)} %get-tuple-element.94.dual, bf16[4,128,256]{2,1,0:T(8,128)(2,1)S(1)} %collective-permute-done.32.rest_0_, ...), custom_call_target="tpu_custom_call" | custom-call | tf_op jit(solution)/shard_map/pallas_call | solution.py:451
  (69 shorter events, 18.3 us)
Async XLA Ops:
  4.4 14.2 %collective-permute-start.4 = (bf16[4,128,256]{2,1,0:T(8,128)(2,1)S(1)}, bf16[4,128,256]{2,1,0:T(8,128)(2,1)S(1)}, u32[]{:S(2)}, u32[]{:S(2)}) collective-permute-start(bf16[4,128,256]{2,1,0:T(8,128)(2,1)S(1)} %get-tuple-element.57), channel_id=1, source_target_pairs={{0,8},{8,0},{16,24},{24,16},{1,9},{9,1},{17,25},{25,17},{2,10},{10... | collective-permute-start | bytes 786440 | tf_op jit(solution)/shard_map/ppermute | solution.py:49
  7.4 5.6 %collective-permute-start.2 = (f32[24,128]{1,0:T(8,128)S(1)}, f32[24,128]{1,0:T(8,128)S(1)}, u32[]{:S(2)}, u32[]{:S(2)}) collective-permute-start(f32[24,128]{1,0:T(8,128)S(1)} %get-tuple-element.55), channel_id=1, source_target_pairs={{0,6},{1,7},{2,4},{3,5},{4,2},{5,3},{6,0},{7,1},{8,14},{9,15},{10,... | collective-permute-start | bytes 36872 | tf_op jit(solution)/shard_map/ppermute | solution.py:54
  11.0 6.2 %collective-permute-start.1 = (f32[24,128]{1,0:T(8,128)S(1)}, f32[24,128]{1,0:T(8,128)S(1)}, u32[]{:S(2)}, u32[]{:S(2)}) collective-permute-start(f32[24,128]{1,0:T(8,128)S(1)} %get-tuple-element.55), channel_id=1, source_target_pairs={{0,4},{1,5},{2,6},{3,7},{4,0},{5,1},{6,2},{7,3},{8,12},{9,13},{10,... | collective-permute-start | bytes 36872 | tf_op jit(solution)/shard_map/ppermute | solution.py:54
  11.0 6.2 %collective-permute-start = (f32[24,128]{1,0:T(8,128)S(1)}, f32[24,128]{1,0:T(8,128)S(1)}, u32[]{:S(2)}, u32[]{:S(2)}) collective-permute-start(f32[24,128]{1,0:T(8,128)S(1)} %get-tuple-element.55), channel_id=1, source_target_pairs={{0,2},{1,3},{2,0},{3,1},{4,6},{5,7},{6,4},{7,5},{8,10},{9,11},{10,... | collective-permute-start | bytes 36872 | tf_op jit(solution)/shard_map/ppermute | solution.py:54
  11.8 21.4 %collective-permute-start.10 = (bf16[4,128,256]{2,1,0:T(8,128)(2,1)S(1)}, bf16[4,128,256]{2,1,0:T(8,128)(2,1)S(1)}, u32[]{:S(2)}, u32[]{:S(2)}) collective-permute-start(bf16[4,128,256]{2,1,0:T(8,128)(2,1)S(1)} %get-tuple-element.70), channel_id=1, source_target_pairs={{0,2},{1,3},{2,4},{3,5},{4,6},{5,7},{6,0},{7,1},{8,10},{9,11},{10,... | collective-permute-start | bytes 786440 | tf_op jit(solution)/shard_map/ppermute | solution.py:49
  20.6 4.8 %collective-permute-start.7 = (bf16[48,256]{1,0:T(8,128)(2,1)S(1)}, bf16[48,256]{1,0:T(8,128)(2,1)S(1)}, u32[]{:S(2)}, u32[]{:S(2)}) collective-permute-start(bf16[48,256]{1,0:T(8,128)(2,1)S(1)} %get-tuple-element.64), channel_id=1, source_target_pairs={{0,4},{1,5},{2,6},{3,7},{4,0},{5,1},{6,2},{7,3},{8,12},{9,13},{10,... | collective-permute-start | bytes 73736 | tf_op jit(solution)/shard_map/ppermute | solution.py:54
  21.2 7.5 %collective-permute-start.8 = (bf16[48,256]{1,0:T(8,128)(2,1)S(1)}, bf16[48,256]{1,0:T(8,128)(2,1)S(1)}, u32[]{:S(2)}, u32[]{:S(2)}) collective-permute-start(bf16[48,256]{1,0:T(8,128)(2,1)S(1)} %get-tuple-element.65), channel_id=1, source_target_pairs={{0,6},{1,7},{2,4},{3,5},{4,2},{5,3},{6,0},{7,1},{8,14},{9,15},{10,... | collective-permute-start | bytes 73736 | tf_op jit(solution)/shard_map/ppermute | solution.py:54
  25.0 10.5 %collective-permute-start.11 = (bf16[4,128,256]{2,1,0:T(8,128)(2,1)S(1)}, bf16[4,128,256]{2,1,0:T(8,128)(2,1)S(1)}, u32[]{:S(2)}, u32[]{:S(2)}) collective-permute-start(bf16[4,128,256]{2,1,0:T(8,128)(2,1)S(1)} %get-tuple-element.71), channel_id=1, source_target_pairs={{0,7},{1,2},{2,1},{3,4},{4,3},{5,6},{6,5},{7,0},{8,15},{9,10},{10,... | collective-permute-start | bytes 786440 | tf_op jit(solution)/shard_map/ppermute | solution.py:49
  25.0 13.4 %collective-permute-start.12 = (bf16[4,128,256]{2,1,0:T(8,128)(2,1)S(1)}, bf16[4,128,256]{2,1,0:T(8,128)(2,1)S(1)}, u32[]{:S(2)}, u32[]{:S(2)}) collective-permute-start(bf16[4,128,256]{2,1,0:T(8,128)(2,1)S(1)} %get-tuple-element.72), channel_id=1, source_target_pairs={{0,6},{1,7},{2,0},{3,1},{4,2},{5,3},{6,4},{7,5},{8,14},{9,15},{10,... | collective-permute-start | bytes 786440 | tf_op jit(solution)/shard_map/ppermute | solution.py:49
  25.4 13.0 %collective-permute-start.13 = (bf16[4,128,256]{2,1,0:T(8,128)(2,1)S(1)}, bf16[4,128,256]{2,1,0:T(8,128)(2,1)S(1)}, u32[]{:S(2)}, u32[]{:S(2)}) collective-permute-start(bf16[4,128,256]{2,1,0:T(8,128)(2,1)S(1)} %get-tuple-element.73), channel_id=1, source_target_pairs={{0,1},{1,0},{2,3},{3,2},{4,5},{5,4},{6,7},{7,6},{8,9},{9,8},{10,11... | collective-permute-start | bytes 786440 | tf_op jit(solution)/shard_map/ppermute | solution.py:49
  31.6 9.4 %collective-permute-start.14 = (bf16[4,128,256]{2,1,0:T(8,128)(2,1)S(1)}, bf16[4,128,256]{2,1,0:T(8,128)(2,1)S(1)}, u32[]{:S(2)}, u32[]{:S(2)}) collective-permute-start(bf16[4,128,256]{2,1,0:T(8,128)(2,1)S(1)} %get-tuple-element.74), channel_id=1, source_target_pairs={{0,24},{8,16},{16,8},{24,0},{1,25},{9,17},{17,9},{25,1},{2,26},{10... | collective-permute-start | bytes 786440 | tf_op jit(solution)/shard_map/ppermute | solution.py:49
  33.1 7.8 %collective-permute-start.9 = (f32[4,384]{1,0:T(4,128)S(1)}, f32[4,384]{1,0:T(4,128)S(1)}, u32[]{:S(2)}, u32[]{:S(2)}) collective-permute-start(f32[4,384]{1,0:T(4,128)S(1)} %get-tuple-element.69), channel_id=1, source_target_pairs={{0,8},{8,0},{16,24},{24,16},{1,9},{9,1},{17,25},{25,17},{2,10},{10... | collective-permute-start | bytes 18440 | tf_op jit(solution)/shard_map/ppermute | solution.py:49
  43.4 11.2 %collective-permute-start.15 = (bf16[4,128,256]{2,1,0:T(8,128)(2,1)S(1)}, bf16[4,128,256]{2,1,0:T(8,128)(2,1)S(1)}, u32[]{:S(2)}, u32[]{:S(2)}) collective-permute-start(bf16[4,128,256]{2,1,0:T(8,128)(2,1)S(1)} %get-tuple-element.76), channel_id=1, source_target_pairs={{0,2},{1,3},{2,4},{3,5},{4,6},{5,7},{6,0},{7,1},{8,10},{9,11},{10,... | collective-permute-start | bytes 786440 | tf_op jit(solution)/shard_map/ppermute | solution.py:49
  43.5 13.0 %collective-permute-start.16 = (bf16[4,128,256]{2,1,0:T(8,128)(2,1)S(1)}, bf16[4,128,256]{2,1,0:T(8,128)(2,1)S(1)}, u32[]{:S(2)}, u32[]{:S(2)}) collective-permute-start(bf16[4,128,256]{2,1,0:T(8,128)(2,1)S(1)} %get-tuple-element.77), channel_id=1, source_target_pairs={{0,7},{1,2},{2,1},{3,4},{4,3},{5,6},{6,5},{7,0},{8,15},{9,10},{10,... | collective-permute-start | bytes 786440 | tf_op jit(solution)/shard_map/ppermute | solution.py:49
  45.8 17.0 %collective-permute-start.17 = (bf16[4,128,256]{2,1,0:T(8,128)(2,1)S(1)}, bf16[4,128,256]{2,1,0:T(8,128)(2,1)S(1)}, u32[]{:S(2)}, u32[]{:S(2)}) collective-permute-start(bf16[4,128,256]{2,1,0:T(8,128)(2,1)S(1)} %get-tuple-element.78), channel_id=1, source_target_pairs={{0,6},{1,7},{2,0},{3,1},{4,2},{5,3},{6,4},{7,5},{8,14},{9,15},{10,... | collective-permute-start | bytes 786440 | tf_op jit(solution)/shard_map/ppermute | solution.py:49
  47.3 15.4 %collective-permute-start.18 = (bf16[4,128,256]{2,1,0:T(8,128)(2,1)S(1)}, bf16[4,128,256]{2,1,0:T(8,128)(2,1)S(1)}, u32[]{:S(2)}, u32[]{:S(2)}) collective-permute-start(bf16[4,128,256]{2,1,0:T(8,128)(2,1)S(1)} %get-tuple-element.79), channel_id=1, source_target_pairs={{0,1},{1,0},{2,3},{3,2},{4,5},{5,4},{6,7},{7,6},{8,9},{9,8},{10,11... | collective-permute-start | bytes 786440 | tf_op jit(solution)/shard_map/ppermute | solution.py:49
  47.3 15.4 %collective-permute-start.19 = (bf16[4,128,256]{2,1,0:T(8,128)(2,1)S(1)}, bf16[4,128,256]{2,1,0:T(8,128)(2,1)S(1)}, u32[]{:S(2)}, u32[]{:S(2)}) collective-permute-start(bf16[4,128,256]{2,1,0:T(8,128)(2,1)S(1)} %get-tuple-element.80), channel_id=1, source_target_pairs={{0,8},{8,0},{16,24},{24,16},{1,9},{9,1},{17,25},{25,17},{2,10},{10... | collective-permute-start | bytes 786440 | tf_op jit(solution)/shard_map/ppermute | solution.py:49
  54.6 8.1 %collective-permute-start.20 = (bf16[4,128,256]{2,1,0:T(8,128)(2,1)S(1)}, bf16[4,128,256]{2,1,0:T(8,128)(2,1)S(1)}, u32[]{:S(2)}, u32[]{:S(2)}) collective-permute-start(bf16[4,128,256]{2,1,0:T(8,128)(2,1)S(1)} %get-tuple-element.81), channel_id=1, source_target_pairs={{0,24},{8,16},{16,8},{24,0},{1,25},{9,17},{17,9},{25,1},{2,26},{10... | collective-permute-start | bytes 786440 | tf_op jit(solution)/shard_map/ppermute | solution.py:49
  65.0 16.5 %collective-permute-start.26 = (bf16[4,128,256]{2,1,0:T(8,128)(2,1)S(1)}, bf16[4,128,256]{2,1,0:T(8,128)(2,1)S(1)}, u32[]{:S(2)}, u32[]{:S(2)}) collective-permute-start(bf16[4,128,256]{2,1,0:T(8,128)(2,1)S(1)} %get-tuple-element.88), channel_id=1, source_target_pairs={{0,2},{1,3},{2,4},{3,5},{4,6},{5,7},{6,0},{7,1},{8,10},{9,11},{10,... | collective-permute-start | bytes 786440 | tf_op jit(solution)/shard_map/ppermute | solution.py:49
  67.0 7.0 %collective-permute-start.24 = (bf16[32,256]{1,0:T(8,128)(2,1)S(1)}, bf16[32,256]{1,0:T(8,128)(2,1)S(1)}, u32[]{:S(2)}, u32[]{:S(2)}) collective-permute-start(bf16[32,256]{1,0:T(8,128)(2,1)S(1)} %pad_maximum_fusion.1.rest_0_), channel_id=1, source_target_pairs={{0,6},{1,7},{2,4},{3,5},{4,2},{5,3},{6,0},{7,1},{8,14},{9,15},{10,... | collective-permute-start | bytes 49160 | tf_op jit(solution)/shard_map/ppermute | solution.py:54
  70.1 4.6 %collective-permute-start.23 = (bf16[32,256]{1,0:T(8,128)(2,1)S(1)}, bf16[32,256]{1,0:T(8,128)(2,1)S(1)}, u32[]{:S(2)}, u32[]{:S(2)}) collective-permute-start(bf16[32,256]{1,0:T(8,128)(2,1)S(1)} %pad_maximum_fusion.1.rest_0_), channel_id=1, source_target_pairs={{0,4},{1,5},{2,6},{3,7},{4,0},{5,1},{6,2},{7,3},{8,12},{9,13},{10,... | collective-permute-start | bytes 49160 | tf_op jit(solution)/shard_map/ppermute | solution.py:54
  76.3 10.5 %collective-permute-start.27 = (bf16[4,128,256]{2,1,0:T(8,128)(2,1)S(1)}, bf16[4,128,256]{2,1,0:T(8,128)(2,1)S(1)}, u32[]{:S(2)}, u32[]{:S(2)}) collective-permute-start(bf16[4,128,256]{2,1,0:T(8,128)(2,1)S(1)} %get-tuple-element.89), channel_id=1, source_target_pairs={{0,7},{1,2},{2,1},{3,4},{4,3},{5,6},{6,5},{7,0},{8,15},{9,10},{10,... | collective-permute-start | bytes 786440 | tf_op jit(solution)/shard_map/ppermute | solution.py:49
  76.3 13.7 %collective-permute-start.28 = (bf16[4,128,256]{2,1,0:T(8,128)(2,1)S(1)}, bf16[4,128,256]{2,1,0:T(8,128)(2,1)S(1)}, u32[]{:S(2)}, u32[]{:S(2)}) collective-permute-start(bf16[4,128,256]{2,1,0:T(8,128)(2,1)S(1)} %get-tuple-element.90), channel_id=1, source_target_pairs={{0,6},{1,7},{2,0},{3,1},{4,2},{5,3},{6,4},{7,5},{8,14},{9,15},{10,... | collective-permute-start | bytes 786440 | tf_op jit(solution)/shard_map/ppermute | solution.py:49
  77.8 12.2 %collective-permute-start.29 = (bf16[4,128,256]{2,1,0:T(8,128)(2,1)S(1)}, bf16[4,128,256]{2,1,0:T(8,128)(2,1)S(1)}, u32[]{:S(2)}, u32[]{:S(2)}) collective-permute-start(bf16[4,128,256]{2,1,0:T(8,128)(2,1)S(1)} %get-tuple-element.91), channel_id=1, source_target_pairs={{0,1},{1,0},{2,3},{3,2},{4,5},{5,4},{6,7},{7,6},{8,9},{9,8},{10,11... | collective-permute-start | bytes 786440 | tf_op jit(solution)/shard_map/ppermute | solution.py:49
  80.0 10.0 %collective-permute-start.30 = (bf16[4,128,256]{2,1,0:T(8,128)(2,1)S(1)}, bf16[4,128,256]{2,1,0:T(8,128)(2,1)S(1)}, u32[]{:S(2)}, u32[]{:S(2)}) collective-permute-start(bf16[4,128,256]{2,1,0:T(8,128)(2,1)S(1)} %get-tuple-element.92), channel_id=1, source_target_pairs={{0,8},{8,0},{16,24},{24,16},{1,9},{9,1},{17,25},{25,17},{2,10},{10... | collective-permute-start | bytes 786440 | tf_op jit(solution)/shard_map/ppermute | solution.py:49
  81.5 13.1 %collective-permute-start.31 = (bf16[4,128,256]{2,1,0:T(8,128)(2,1)S(1)}, bf16[4,128,256]{2,1,0:T(8,128)(2,1)S(1)}, u32[]{:S(2)}, u32[]{:S(2)}) collective-permute-start(bf16[4,128,256]{2,1,0:T(8,128)(2,1)S(1)} %get-tuple-element.93), channel_id=1, source_target_pairs={{0,24},{8,16},{16,8},{24,0},{1,25},{9,17},{17,9},{25,1},{2,26},{10... | collective-permute-start | bytes 786440 | tf_op jit(solution)/shard_map/ppermute | solution.py:49
  97.0 11.2 %collective-permute-start.32 = (bf16[4,128,256]{2,1,0:T(8,128)(2,1)S(1)}, bf16[4,128,256]{2,1,0:T(8,128)(2,1)S(1)}, u32[]{:S(2)}, u32[]{:S(2)}) collective-permute-start(bf16[4,128,256]{2,1,0:T(8,128)(2,1)S(1)} %get-tuple-element.95), channel_id=1, source_target_pairs={{0,2},{1,3},{2,4},{3,5},{4,6},{5,7},{6,0},{7,1},{8,10},{9,11},{10,... | collective-permute-start | bytes 786440 | tf_op jit(solution)/shard_map/ppermute | solution.py:49
  97.1 13.0 %collective-permute-start.33 = (bf16[4,128,256]{2,1,0:T(8,128)(2,1)S(1)}, bf16[4,128,256]{2,1,0:T(8,128)(2,1)S(1)}, u32[]{:S(2)}, u32[]{:S(2)}) collective-permute-start(bf16[4,128,256]{2,1,0:T(8,128)(2,1)S(1)} %get-tuple-element.96), channel_id=1, source_target_pairs={{0,7},{1,2},{2,1},{3,4},{4,3},{5,6},{6,5},{7,0},{8,15},{9,10},{10,... | collective-permute-start | bytes 786440 | tf_op jit(solution)/shard_map/ppermute | solution.py:49
  99.4 17.0 %collective-permute-start.34 = (bf16[4,128,256]{2,1,0:T(8,128)(2,1)S(1)}, bf16[4,128,256]{2,1,0:T(8,128)(2,1)S(1)}, u32[]{:S(2)}, u32[]{:S(2)}) collective-permute-start(bf16[4,128,256]{2,1,0:T(8,128)(2,1)S(1)} %get-tuple-element.97), channel_id=1, source_target_pairs={{0,6},{1,7},{2,0},{3,1},{4,2},{5,3},{6,4},{7,5},{8,14},{9,15},{10,... | collective-permute-start | bytes 786440 | tf_op jit(solution)/shard_map/ppermute | solution.py:49
  100.9 15.4 %collective-permute-start.35 = (bf16[4,128,256]{2,1,0:T(8,128)(2,1)S(1)}, bf16[4,128,256]{2,1,0:T(8,128)(2,1)S(1)}, u32[]{:S(2)}, u32[]{:S(2)}) collective-permute-start(bf16[4,128,256]{2,1,0:T(8,128)(2,1)S(1)} %get-tuple-element.98), channel_id=1, source_target_pairs={{0,1},{1,0},{2,3},{3,2},{4,5},{5,4},{6,7},{7,6},{8,9},{9,8},{10,11... | collective-permute-start | bytes 786440 | tf_op jit(solution)/shard_map/ppermute | solution.py:49
  100.9 15.4 %collective-permute-start.36 = (bf16[4,128,256]{2,1,0:T(8,128)(2,1)S(1)}, bf16[4,128,256]{2,1,0:T(8,128)(2,1)S(1)}, u32[]{:S(2)}, u32[]{:S(2)}) collective-permute-start(bf16[4,128,256]{2,1,0:T(8,128)(2,1)S(1)} %get-tuple-element.99), channel_id=1, source_target_pairs={{0,8},{8,0},{16,24},{24,16},{1,9},{9,1},{17,25},{25,17},{2,10},{10... | collective-permute-start | bytes 786440 | tf_op jit(solution)/shard_map/ppermute | solution.py:49
  108.2 8.1 %collective-permute-start.37 = (bf16[4,128,256]{2,1,0:T(8,128)(2,1)S(1)}, bf16[4,128,256]{2,1,0:T(8,128)(2,1)S(1)}, u32[]{:S(2)}, u32[]{:S(2)}) collective-permute-start(bf16[4,128,256]{2,1,0:T(8,128)(2,1)S(1)} %get-tuple-element.100), channel_id=1, source_target_pairs={{0,24},{8,16},{16,8},{24,0},{1,25},{9,17},{17,9},{25,1},{2,26},{10... | collective-permute-start | bytes 786440 | tf_op jit(solution)/shard_map/ppermute | solution.py:49
  (12 other events, 191.0 us)

commit v5 on v4

--- a/solution.py
+++ b/solution.py
@@ -12,7 +12,7 @@
 CAP = 4
 NEAR = 4 * CAP
 ITERS = 2
-EARLY = 5
+EARLY = (5, 5)
 ROWS = 512
 SHIFTS = {2: 2, 3: -2}
 OFFSETS = (1, -1, 2, -2)
@@ -148,7 +148,7 @@
 
 
 def first_solve_kernel(wide, send, coarse_map, matrix, load, basis, disp, proj, columns, told, *rest):
-    slabs, (held, *rest) = rest[:EARLY], rest[EARLY:]
+    slabs, (held, *rest) = rest[: EARLY[0]], rest[EARLY[0] :]
     rhs, narrow, send_held, map_held, basis_held, rows, sems, more_sems = rest
     blocks = disp.shape[0]
     copies = matrix_copies(matrix, held, sems)
@@ -168,7 +168,7 @@
     tell(wide, map_held, send_held, rows, told)
     small[3].wait()
     solve(copies, held, rhs, columns, disp, narrow, proj)
-    pick_blocks(send_held.at[0], narrow, slabs, range(EARLY))
+    pick_blocks(send_held.at[0], narrow, slabs, range(EARLY[0]))
 
 
 def next_solve_kernel(send, read, matrix, load, columns, dual, *rest):
@@ -185,7 +185,8 @@
     pick_blocks(send, narrow, slabs, range(len(slabs)))
 
 
-def coarse_kernel(wide, chips, bring, send, basis, near_basis, disp, columns, *rest):
+def coarse_kernel(wide, chips, early, bring, ties, send, basis, near_basis, disp, columns, *rest):
+    rest = rest[ties:]
     parts, tables, rest = rest[:chips], rest[chips : 2 * chips], rest[2 * chips :]
     if bring:
         matrix, *rest, sem = rest
@@ -210,22 +211,24 @@
         )
     near[:, :cases] = rows[1]
     near[:, cases:] = near_basis[...]
-    for b in range(disp.shape[0]):
-        held[b, :, :cases] = rows[0][b : b + 1]
-        held[b, :, cases:] = basis[:, b * BLK : (b + 1) * BLK]
-    for j in range(CAP):
-        slabs[0][j : j + 1, :] = held[slot_block(send, 4, j)]
+    if early > 4:
+        for b in range(disp.shape[0]):
+            held[b, :, :cases] = rows[0][b : b + 1]
+            held[b, :, cases:] = basis[:, b * BLK : (b + 1) * BLK]
+        for j in range(CAP):
+            slabs[0][j : j + 1, :] = held[slot_block(send, 4, j)]
     for b in range(disp.shape[0]):
         for cols in column_parts(cases):
             corrected[b, :, cols] = (
                 disp[b, :, cols] + columns[b] * rows[0][b : b + 1, cols]
             ).astype(jnp.bfloat16)
-    pick_blocks(send, corrected, slabs[1:], (5,))
+    pick_blocks(send, corrected, slabs[early - 4 :], range(early, DIRS))
     if bring:
         copy.wait()
 
 
-def dirichlet_kernel(send, read, weights, matrix, corrected, near, far_rows, *rest):
+def dirichlet_kernel(early, send, read, weights, matrix, corrected, near, *rest):
+    far_rows, rest = rest[: early - 4], rest[early - 4 :]
     arrived, dual, rest = rest[:DIRS], rest[DIRS], rest[DIRS + 1 :]
     slabs, (received, rows, rhs) = rest[:DIRS], rest[DIRS:]
     blocks, _, cases = corrected.shape
@@ -234,7 +237,7 @@
         rows[k] = near[k : k + 1, :]
     for k in range(NEAR, DIRS * CAP):
         j = k - NEAR
-        rows[k] = far_rows[j : j + 1, :] if j < CAP else jnp.zeros_like(rows[k])
+        rows[k] = far_rows[0][j : j + 1, :] if far_rows and j < CAP else jnp.zeros_like(rows[k])
     for b in range(blocks):
         place, code = slot_read(read, b), read[b]
         row = jnp.where(code < NEAR, code, place)
@@ -362,10 +365,10 @@
     disp, proj, columns, told, *slabs, solve_matrix = pl.pallas_call(
         functools.partial(first_solve_kernel, wide),
         out_shape=[whole, f32(wide, cases), block_columns, f32(NEAR + 2 * tall, BLK)]
-        + [slab] * EARLY
+        + [slab] * EARLY[0]
         + [resident],
         in_specs=[HBM] * 5,
-        out_specs=[VMEM] * (5 + EARLY),
+        out_specs=[VMEM] * (5 + EARLY[0]),
         scratch_shapes=[
             rhs,
             narrow,
@@ -381,7 +384,7 @@
         in_hbm(send_blocks[0]), in_hbm(coarse_map[0]), in_hbm(solve_matrix), in_hbm(load),
         in_hbm(coarse_basis[0]),
     )
-    arrived = {way: exchanged(slabs[way], way) for way in ORDER if way < EARLY}
+    arrived = {way: exchanged(slabs[way], way) for way in ORDER if way < EARLY[0]}
     mine = jnp.stack(to_chips([told] * chips))
     theirs = swapped(mine, 1)
     outgoing = bf16(chips + 1, groups * wide, cases)
@@ -404,15 +407,17 @@
 
     for iteration in range(ITERS):
         bring = iteration == 0
+        early = EARLY[iteration]
         if iteration:
-            arrived = {way: exchanged(slabs[way], way) for way in ORDER if way < EARLY}
+            arrived = {way: exchanged(slabs[way], way) for way in ORDER if way < early}
             proj = proj.astype(jnp.bfloat16)
             parts = to_chips([jnp.concatenate([proj, swapped(proj, 1)])] * chips)
+        ties = [arrived[way] for way in (() if bring else (4, ))]
         corrected, near, *far = pl.pallas_call(
-            functools.partial(coarse_kernel, wide, chips, bring),
-            out_shape=[halved, f32(NEAR, cases + BLK), f32(CAP, cases + BLK), slab]
+            functools.partial(coarse_kernel, wide, chips, early, bring, len(ties)),
+            out_shape=[halved, f32(NEAR, cases + BLK), f32(CAP, cases + BLK) if early > 4 else slab, slab]
             + [resident] * bring,
-            in_specs=[SMEM] + [VMEM] * (4 + 2 * chips) + [HBM] * bring,
+            in_specs=[SMEM] + [VMEM] * 4 + [ANY] * len(ties) + [VMEM] * (2 * chips) + [HBM] * bring,
             out_specs=[VMEM] * (4 + bring),
             scratch_shapes=[
                 pltpu.VMEM((lanes, cases), jnp.float32),
@@ -421,30 +426,34 @@
             + [pltpu.SemaphoreType.DMA] * bring,
             compiler_params=PARAMS,
         )(
-            send, coarse_basis[0], near_basis, disp, columns, *parts, *tables,
+            send, coarse_basis[0], near_basis, disp, columns, *ties, *parts, *tables,
             *[in_hbm(dirichlet_matrix)] * bring,
         )
         if bring:
             *far, dirichlet_matrix = far
-        far_rows, arrived[5] = [exchanged(far[way - 4], way) for way in (4, 5)]
+        arrived[5] = exchanged(far[1], 5)
+        moved = exchanged(far[0], 4)
+        if early == 4:
+            arrived[4] = moved
+        far_rows = [moved] * (early - 4)
         dual, *slabs = pl.pallas_call(
-            dirichlet_kernel,
+            functools.partial(dirichlet_kernel, early),
             out_shape=[halved] + [slab] * DIRS,
-            in_specs=[SMEM] * 3 + [VMEM] * (4 + DIRS),
+            in_specs=[SMEM] * 3 + [VMEM] * (early - 1 + DIRS),
             out_specs=[VMEM] * (1 + DIRS),
             scratch_shapes=[received, pltpu.VMEM((DIRS * CAP, 1, cases + BLK), jnp.float32), rhs],
             compiler_params=PARAMS,
         )(
-            send, read, weights, dirichlet_matrix, corrected, near, far_rows,
+            send, read, weights, dirichlet_matrix, corrected, near, *far_rows,
             *[arrived[way] for way in ORDER],
         )
         arrived = [exchanged(slabs[way], way) for way in ORDER]
         if iteration + 1 < ITERS:
             mult, disp, proj, *slabs = pl.pallas_call(
                 next_solve_kernel,
-                out_shape=[whole, whole, f32(wide, cases)] + [slab] * EARLY,
+                out_shape=[whole, whole, f32(wide, cases)] + [slab] * EARLY[iteration + 1],
                 in_specs=[SMEM] * 2 + [VMEM] * (4 + DIRS),
-                out_specs=[VMEM] * (3 + EARLY),
+                out_specs=[VMEM] * (3 + EARLY[iteration + 1]),
                 scratch_shapes=[received, rhs, narrow],
                 compiler_params=PARAMS,
             )(send, read, solve_matrix, load, columns, dual, *arrived)

time: 118 us -> 115 us (0.975)
  waiting for transfers between devices: 55.3 us -> 50.4 us
  starting transfers between devices: 44.7 us -> 46.2 us
    ppermute x26, waiting for transfers between devices: 44 us -> 41.3 us  [exchanged(): lax.ppermute(slab, axis, [(i, (i + step) % count) for i, step in enumerat...]
    ppermute x12, waiting for transfers between devices: 11.3 us -> 9.14 us  [swapped(): return lax.ppermute(value, 'sub', [(i, i ^ mask) for i in range(count)])]
    ppermute x26, starting transfers between devices: 31.2 us -> 32.7 us  [exchanged(): lax.ppermute(slab, axis, [(i, (i + step) % count) for i, step in enumerat...]
  transfers between devices with their start and end apart: 38 -> 38, of which waited for: 19 -> 17; matrix products, arithmetic and copies ran while one was open for 0% -> 0% of each run, Pallas kernels for 4% -> 4%
where the time goes in v5:
time: 115 us
  waiting for transfers between devices  50.4 us (44%)
  starting transfers between devices  46.2 us (40%)
  Pallas kernels  18 us (16%)
    ppermute x26, waiting for transfers between devices, exchanged(): lax.ppermute(slab, axis, [(i, (i + step) % count) for i, step in enumerat...  41.3 us
    ppermute x26, starting transfers between devices, exchanged(): lax.ppermute(slab, axis, [(i, (i + step) % count) for i, step in enumerat...  32.7 us
    ppermute x12, starting transfers between devices, swapped(): return lax.ppermute(value, 'sub', [(i, i ^ mask) for i in range(count)])  13.5 us
    ppermute x12, waiting for transfers between devices, swapped(): return lax.ppermute(value, 'sub', [(i, i ^ mask) for i in range(count)])  9.14 us
    pallas_call x2, Pallas kernels, on_device(): pl.pallas_call(functools.partial(dirichlet_kernel, early), out_shape=[hal...  4.93 us
    pallas_call x1, Pallas kernels, on_device(): pl.pallas_call(functools.partial(first_solve_kernel, wide), out_shape=[wh...  4.35 us
    pallas_call x2, Pallas kernels, on_device(): pl.pallas_call(functools.partial(coarse_kernel, wide, chips, early, bring...  3.93 us
  transfers between devices with their start and end apart: 38, of which 17 were waited for; matrix products, arithmetic and copies ran while one was open for 0% of the time, Pallas kernels for 4%

profile of v5, /device:TPU:0, one launch (start us, length us, event | category | flops | bytes accessed | tf_op | source)
XLA Modules:
  0.0 114.9 jit_solution(14931226318187951734)
XLA Ops:
  0.0 4.3 %shard_map.91 = (f32[12,128,256]{2,1,0:T(8,128)S(1)}, f32[16,256]{1,0:T(8,128)S(1)}, f32[12,128,128]{2,1,0:T(8,128)S(1)}, f32[24,128]{1,0:T(8,128)S(1)}, bf16[4,...) custom-call(s32[1,24]{1,0:T(1,128)} %bitcast.22, ...), custom_call_target="tpu_custom_call" | custom-call | tf_op jit(solution)/shard_map/pallas_call | solution.py:365
  4.4 3.0 %collective-permute-start.4 = (bf16[4,128,256]{2,1,0:T(8,128)(2,1)S(1)}, bf16[4,128,256]{2,1,0:T(8,128)(2,1)S(1)}, u32[]{:S(2)}, u32[]{:S(2)}) collective-permute-start(bf16[4,128,256]{2,1,0:T(8,128)(2,1)S(1)} %get-tuple-element.57), channel_id=1, source_target_pairs={{0,8},{8,0},{16,24},{24,16},{1,9},{9,1},{17,25},{25,17},{2,10},{10... | collective-permute-start | bytes 786440 | tf_op jit(solution)/shard_map/ppermute | solution.py:49
  7.4 3.6 %collective-permute-start.2 = (f32[24,128]{1,0:T(8,128)S(1)}, f32[24,128]{1,0:T(8,128)S(1)}, u32[]{:S(2)}, u32[]{:S(2)}) collective-permute-start(f32[24,128]{1,0:T(8,128)S(1)} %get-tuple-element.55), channel_id=1, source_target_pairs={{0,6},{1,7},{2,4},{3,5},{4,2},{5,3},{6,0},{7,1},{8,14},{9,15},{10,... | collective-permute-start | bytes 36872 | tf_op jit(solution)/shard_map/ppermute | solution.py:54
  13.0 4.2 %collective-permute-done.1 = f32[24,128]{1,0:T(8,128)S(1)} collective-permute-done((f32[24,128]{1,0:T(8,128)S(1)}, f32[24,128]{1,0:T(8,128)S(1)}, u32[]{:S(2)}, u32[]{:S(2)}) %collective-permute-start.1) | collective-permute-done | bytes 12320 | tf_op jit(solution)/shard_map/ppermute | solution.py:54
  21.2 3.8 %collective-permute-start.8 = (bf16[48,256]{1,0:T(8,128)(2,1)S(1)}, bf16[48,256]{1,0:T(8,128)(2,1)S(1)}, u32[]{:S(2)}, u32[]{:S(2)}) collective-permute-start(bf16[48,256]{1,0:T(8,128)(2,1)S(1)} %get-tuple-element.65), channel_id=1, source_target_pairs={{0,6},{1,7},{2,4},{3,5},{4,2},{5,3},{6,0},{7,1},{8,14},{9,15},{10,... | collective-permute-start | bytes 73736 | tf_op jit(solution)/shard_map/ppermute | solution.py:54
  25.4 3.3 %collective-permute-start.13 = (bf16[4,128,256]{2,1,0:T(8,128)(2,1)S(1)}, bf16[4,128,256]{2,1,0:T(8,128)(2,1)S(1)}, u32[]{:S(2)}, u32[]{:S(2)}) collective-permute-start(bf16[4,128,256]{2,1,0:T(8,128)(2,1)S(1)} %get-tuple-element.73), channel_id=1, source_target_pairs={{0,1},{1,0},{2,3},{3,2},{4,5},{5,4},{6,7},{7,6},{8,9},{9,8},{10,11... | collective-permute-start | bytes 786440 | tf_op jit(solution)/shard_map/ppermute | solution.py:49
  28.7 2.9 %shard_map.94 = (bf16[12,128,256]{2,1,0:T(8,128)(2,1)S(1)}, f32[16,384]{1,0:T(8,128)S(1)}, f32[4,384]{1,0:T(4,128)S(1)}, bf16[4,128,256]{2,1,0:T(8,128)(2,1)S(1)}, bf16[1536,1536]{1,0:T(8,128)(2,1)S(1)}) custom-call(s32[24]{0:T(128)S(1)} %bitcast.23, f32[1,1536]{1,0:T(1,128)S(1)} %bitcast.20, f32[16,128]{1,0:T(8,128)S(1)} %get-tuple-element.58.near_basis, ...), custom_call_target="tpu_custom_call" | custom-call | tf_op jit(solution)/shard_map/pallas_call | solution.py:416
  31.6 1.6 %collective-permute-start.14 = (bf16[4,128,256]{2,1,0:T(8,128)(2,1)S(1)}, bf16[4,128,256]{2,1,0:T(8,128)(2,1)S(1)}, u32[]{:S(2)}, u32[]{:S(2)}) collective-permute-start(bf16[4,128,256]{2,1,0:T(8,128)(2,1)S(1)} %get-tuple-element.74), channel_id=1, source_target_pairs={{0,24},{8,16},{16,8},{24,0},{1,25},{9,17},{17,9},{25,1},{2,26},{10... | collective-permute-start | bytes 786440 | tf_op jit(solution)/shard_map/ppermute | solution.py:49
  33.1 1.5 %collective-permute-start.9 = (f32[4,384]{1,0:T(4,128)S(1)}, f32[4,384]{1,0:T(4,128)S(1)}, u32[]{:S(2)}, u32[]{:S(2)}) collective-permute-start(f32[4,384]{1,0:T(4,128)S(1)} %get-tuple-element.69), channel_id=1, source_target_pairs={{0,8},{8,0},{16,24},{24,16},{1,9},{9,1},{17,25},{25,17},{2,10},{10... | collective-permute-start | bytes 18440 | tf_op jit(solution)/shard_map/ppermute | solution.py:49
  35.4 2.9 %collective-permute-done.12.rest_3_ = bf16[4,128,256]{2,1,0:T(8,128)(2,1)S(1)} collective-permute-done((bf16[4,128,256]{2,1,0:T(8,128)(2,1)S(1)}, bf16[4,128,256]{2,1,0:T(8,128)(2,1)S(1)}, u32[]{:S(2)}, u32[]{:S(2)}) %collective-permute-start.12) | collective-permute-done | bytes 262176 | tf_op jit(solution)/shard_map/ppermute | solution.py:49
  38.4 2.6 %collective-permute-done.9.rest_0_ = f32[4,384]{1,0:T(4,128)S(1)} collective-permute-done((f32[4,384]{1,0:T(4,128)S(1)}, f32[4,384]{1,0:T(4,128)S(1)}, u32[]{:S(2)}, u32[]{:S(2)}) %collective-permute-start.9) | collective-permute-done | bytes 6176 | tf_op jit(solution)/shard_map/ppermute | solution.py:49
  41.0 2.4 %shard_map.95 = (bf16[12,128,256]{2,1,0:T(8,128)(2,1)S(1)}, bf16[4,128,256]{2,1,0:T(8,128)(2,1)S(1)}, bf16[4,128,256]{2,1,0:T(8,128)(2,1)S(1)}, bf16[4,128,256]{...) custom-call(s32[24]{0:T(128)S(1)} %bitcast.24, ...), custom_call_target="tpu_custom_call" | custom-call | tf_op jit(solution)/shard_map/pallas_call | solution.py:439
  43.5 2.3 %collective-permute-start.16 = (bf16[4,128,256]{2,1,0:T(8,128)(2,1)S(1)}, bf16[4,128,256]{2,1,0:T(8,128)(2,1)S(1)}, u32[]{:S(2)}, u32[]{:S(2)}) collective-permute-start(bf16[4,128,256]{2,1,0:T(8,128)(2,1)S(1)} %get-tuple-element.77), channel_id=1, source_target_pairs={{0,7},{1,2},{2,1},{3,4},{4,3},{5,6},{6,5},{7,0},{8,15},{9,10},{10,... | collective-permute-start | bytes 786440 | tf_op jit(solution)/shard_map/ppermute | solution.py:49
  45.8 1.5 %collective-permute-start.17 = (bf16[4,128,256]{2,1,0:T(8,128)(2,1)S(1)}, bf16[4,128,256]{2,1,0:T(8,128)(2,1)S(1)}, u32[]{:S(2)}, u32[]{:S(2)}) collective-permute-start(bf16[4,128,256]{2,1,0:T(8,128)(2,1)S(1)} %get-tuple-element.78), channel_id=1, source_target_pairs={{0,6},{1,7},{2,0},{3,1},{4,2},{5,3},{6,4},{7,5},{8,14},{9,15},{10,... | collective-permute-start | bytes 786440 | tf_op jit(solution)/shard_map/ppermute | solution.py:49
  47.8 6.8 %collective-permute-done.15.rest_0_ = bf16[4,128,256]{2,1,0:T(8,128)(2,1)S(1)} collective-permute-done((bf16[4,128,256]{2,1,0:T(8,128)(2,1)S(1)}, bf16[4,128,256]{2,1,0:T(8,128)(2,1)S(1)}, u32[]{:S(2)}, u32[]{:S(2)}) %collective-permute-start.15) | collective-permute-done | bytes 262176 | tf_op jit(solution)/shard_map/ppermute | solution.py:49
  54.6 1.4 %collective-permute-start.20 = (bf16[4,128,256]{2,1,0:T(8,128)(2,1)S(1)}, bf16[4,128,256]{2,1,0:T(8,128)(2,1)S(1)}, u32[]{:S(2)}, u32[]{:S(2)}) collective-permute-start(bf16[4,128,256]{2,1,0:T(8,128)(2,1)S(1)} %get-tuple-element.81), channel_id=1, source_target_pairs={{0,24},{8,16},{16,8},{24,0},{1,25},{9,17},{17,9},{25,1},{2,26},{10... | collective-permute-start | bytes 786440 | tf_op jit(solution)/shard_map/ppermute | solution.py:49
  56.5 6.2 %collective-permute-done.17.rest_2_ = bf16[4,128,256]{2,1,0:T(8,128)(2,1)S(1)} collective-permute-done((bf16[4,128,256]{2,1,0:T(8,128)(2,1)S(1)}, bf16[4,128,256]{2,1,0:T(8,128)(2,1)S(1)}, u32[]{:S(2)}, u32[]{:S(2)}) %collective-permute-start.17) | collective-permute-done | bytes 262176 | tf_op jit(solution)/shard_map/ppermute | solution.py:49
  62.8 2.2 %shard_map.96 = (f32[12,128,256]{2,1,0:T(8,128)S(1)}, f32[12,128,256]{2,1,0:T(8,128)S(1)}, f32[16,256]{1,0:T(8,128)S(1)}, bf16[4,128,256]{2,1,0:T(8,128)(2,1)S(1...) custom-call(s32[24]{0:T(128)S(1)} %bitcast.25, ...), custom_call_target="tpu_custom_call" | custom-call | tf_op jit(solution)/shard_map/pallas_call | solution.py:452
  66.8 1.4 %collective-permute-start.25 = (bf16[32,256]{1,0:T(8,128)(2,1)S(1)}, bf16[32,256]{1,0:T(8,128)(2,1)S(1)}, u32[]{:S(2)}, u32[]{:S(2)}) collective-permute-start(bf16[32,256]{1,0:T(8,128)(2,1)S(1)} %pad_maximum_fusion.1.rest_1_), channel_id=1, source_target_pairs={{0,6},{1,7},{2,4},{3,5},{4,2},{5,3},{6,0},{7,1},{8,14},{9,15},{10,... | collective-permute-start | bytes 49160 | tf_op jit(solution)/shard_map/ppermute | solution.py:54
  69.0 2.2 %collective-permute-start.23 = (bf16[32,256]{1,0:T(8,128)(2,1)S(1)}, bf16[32,256]{1,0:T(8,128)(2,1)S(1)}, u32[]{:S(2)}, u32[]{:S(2)}) collective-permute-start(bf16[32,256]{1,0:T(8,128)(2,1)S(1)} %pad_maximum_fusion.1.rest_1_), channel_id=1, source_target_pairs={{0,2},{1,3},{2,0},{3,1},{4,6},{5,7},{6,4},{7,5},{8,10},{9,11},{10,... | collective-permute-start | bytes 49160 | tf_op jit(solution)/shard_map/ppermute | solution.py:54
  73.7 1.8 %collective-permute-start.29 = (bf16[4,128,256]{2,1,0:T(8,128)(2,1)S(1)}, bf16[4,128,256]{2,1,0:T(8,128)(2,1)S(1)}, u32[]{:S(2)}, u32[]{:S(2)}) collective-permute-start(bf16[4,128,256]{2,1,0:T(8,128)(2,1)S(1)} %get-tuple-element.91), channel_id=1, source_target_pairs={{0,6},{1,7},{2,0},{3,1},{4,2},{5,3},{6,4},{7,5},{8,14},{9,15},{10,... | collective-permute-start | bytes 786440 | tf_op jit(solution)/shard_map/ppermute | solution.py:49
  77.0 2.3 %collective-permute-start.31 = (bf16[4,128,256]{2,1,0:T(8,128)(2,1)S(1)}, bf16[4,128,256]{2,1,0:T(8,128)(2,1)S(1)}, u32[]{:S(2)}, u32[]{:S(2)}) collective-permute-start(bf16[4,128,256]{2,1,0:T(8,128)(2,1)S(1)} %get-tuple-element.93), channel_id=1, source_target_pairs={{0,24},{8,16},{16,8},{24,0},{1,25},{9,17},{17,9},{25,1},{2,26},{10... | collective-permute-start | bytes 786440 | tf_op jit(solution)/shard_map/ppermute | solution.py:49
  79.3 3.0 %collective-permute-done.27.rest_1_ = bf16[4,128,256]{2,1,0:T(8,128)(2,1)S(1)} collective-permute-done((bf16[4,128,256]{2,1,0:T(8,128)(2,1)S(1)}, bf16[4,128,256]{2,1,0:T(8,128)(2,1)S(1)}, u32[]{:S(2)}, u32[]{:S(2)}) %collective-permute-start.27) | collective-permute-done | bytes 262176 | tf_op jit(solution)/shard_map/ppermute | solution.py:49
  82.3 1.5 %collective-permute-start.26 = (f32[4,384]{1,0:T(4,128)S(1)}, f32[4,384]{1,0:T(4,128)S(1)}, u32[]{:S(2)}, u32[]{:S(2)}) collective-permute-start(f32[4,384]{1,0:T(4,128)S(1)} %get-tuple-element.88), channel_id=1, source_target_pairs={{0,8},{8,0},{16,24},{24,16},{1,9},{9,1},{17,25},{25,17},{2,10},{10... | collective-permute-start | bytes 18440 | tf_op jit(solution)/shard_map/ppermute | solution.py:49
  84.5 6.9 %collective-permute-done.29.rest_3_ = bf16[4,128,256]{2,1,0:T(8,128)(2,1)S(1)} collective-permute-done((bf16[4,128,256]{2,1,0:T(8,128)(2,1)S(1)}, bf16[4,128,256]{2,1,0:T(8,128)(2,1)S(1)}, u32[]{:S(2)}, u32[]{:S(2)}) %collective-permute-start.29) | collective-permute-done | bytes 262176 | tf_op jit(solution)/shard_map/ppermute | solution.py:49
  91.4 2.5 %shard_map.98 = (bf16[12,128,256]{2,1,0:T(8,128)(2,1)S(1)}, bf16[4,128,256]{2,1,0:T(8,128)(2,1)S(1)}, bf16[4,128,256]{2,1,0:T(8,128)(2,1)S(1)}, bf16[4,128,256]{...) custom-call(s32[24]{0:T(128)S(1)} %bitcast.27, ...), custom_call_target="tpu_custom_call" | custom-call | tf_op jit(solution)/shard_map/pallas_call | solution.py:439
  94.9 2.9 %collective-permute-start.34 = (bf16[4,128,256]{2,1,0:T(8,128)(2,1)S(1)}, bf16[4,128,256]{2,1,0:T(8,128)(2,1)S(1)}, u32[]{:S(2)}, u32[]{:S(2)}) collective-permute-start(bf16[4,128,256]{2,1,0:T(8,128)(2,1)S(1)} %get-tuple-element.97), channel_id=1, source_target_pairs={{0,6},{1,7},{2,0},{3,1},{4,2},{5,3},{6,4},{7,5},{8,14},{9,15},{10,... | collective-permute-start | bytes 786440 | tf_op jit(solution)/shard_map/ppermute | solution.py:49
  98.4 1.5 %collective-permute-start.36 = (bf16[4,128,256]{2,1,0:T(8,128)(2,1)S(1)}, bf16[4,128,256]{2,1,0:T(8,128)(2,1)S(1)}, u32[]{:S(2)}, u32[]{:S(2)}) collective-permute-start(bf16[4,128,256]{2,1,0:T(8,128)(2,1)S(1)} %get-tuple-element.99), channel_id=1, source_target_pairs={{0,8},{8,0},{16,24},{24,16},{1,9},{9,1},{17,25},{25,17},{2,10},{10... | collective-permute-start | bytes 786440 | tf_op jit(solution)/shard_map/ppermute | solution.py:49
  99.9 5.0 %collective-permute-done.32.rest_0_ = bf16[4,128,256]{2,1,0:T(8,128)(2,1)S(1)} collective-permute-done((bf16[4,128,256]{2,1,0:T(8,128)(2,1)S(1)}, bf16[4,128,256]{2,1,0:T(8,128)(2,1)S(1)}, u32[]{:S(2)}, u32[]{:S(2)}) %collective-permute-start.32) | collective-permute-done | bytes 262176 | tf_op jit(solution)/shard_map/ppermute | solution.py:49
  104.8 2.2 %collective-permute-start.37 = (bf16[4,128,256]{2,1,0:T(8,128)(2,1)S(1)}, bf16[4,128,256]{2,1,0:T(8,128)(2,1)S(1)}, u32[]{:S(2)}, u32[]{:S(2)}) collective-permute-start(bf16[4,128,256]{2,1,0:T(8,128)(2,1)S(1)} %get-tuple-element.100), channel_id=1, source_target_pairs={{0,24},{8,16},{16,8},{24,0},{1,25},{9,17},{17,9},{25,1},{2,26},{10... | collective-permute-start | bytes 786440 | tf_op jit(solution)/shard_map/ppermute | solution.py:49
  107.1 5.9 %collective-permute-done.34.rest_2_ = bf16[4,128,256]{2,1,0:T(8,128)(2,1)S(1)} collective-permute-done((bf16[4,128,256]{2,1,0:T(8,128)(2,1)S(1)}, bf16[4,128,256]{2,1,0:T(8,128)(2,1)S(1)}, u32[]{:S(2)}, u32[]{:S(2)}) %collective-permute-start.34) | collective-permute-done | bytes 262176 | tf_op jit(solution)/shard_map/ppermute | solution.py:49
  113.0 1.9 %shard_map.99 = f32[12,128,256]{2,1,0:T(8,128)} custom-call(s32[12]{0:T(128)S(1)} %bitcast.32, f32[12,128,256]{2,1,0:T(8,128)S(1)} %get-tuple-element.82.mult, bf16[12,128,256]{2,1,0:T(8,128)(2,1)S(1)} %get-tuple-element.94.dual, bf16[4,128,256]{2,1,0:T(8,128)(2,1)S(1)} %collective-permute-done.32.rest_0_, ...), custom_call_target="tpu_custom_call" | custom-call | tf_op jit(solution)/shard_map/pallas_call | solution.py:460
  (69 shorter events, 17.2 us)
Async XLA Ops:
  4.4 14.2 %collective-permute-start.4 = (bf16[4,128,256]{2,1,0:T(8,128)(2,1)S(1)}, bf16[4,128,256]{2,1,0:T(8,128)(2,1)S(1)}, u32[]{:S(2)}, u32[]{:S(2)}) collective-permute-start(bf16[4,128,256]{2,1,0:T(8,128)(2,1)S(1)} %get-tuple-element.57), channel_id=1, source_target_pairs={{0,8},{8,0},{16,24},{24,16},{1,9},{9,1},{17,25},{25,17},{2,10},{10... | collective-permute-start | bytes 786440 | tf_op jit(solution)/shard_map/ppermute | solution.py:49
  7.4 5.6 %collective-permute-start.2 = (f32[24,128]{1,0:T(8,128)S(1)}, f32[24,128]{1,0:T(8,128)S(1)}, u32[]{:S(2)}, u32[]{:S(2)}) collective-permute-start(f32[24,128]{1,0:T(8,128)S(1)} %get-tuple-element.55), channel_id=1, source_target_pairs={{0,6},{1,7},{2,4},{3,5},{4,2},{5,3},{6,0},{7,1},{8,14},{9,15},{10,... | collective-permute-start | bytes 36872 | tf_op jit(solution)/shard_map/ppermute | solution.py:54
  11.0 6.2 %collective-permute-start.1 = (f32[24,128]{1,0:T(8,128)S(1)}, f32[24,128]{1,0:T(8,128)S(1)}, u32[]{:S(2)}, u32[]{:S(2)}) collective-permute-start(f32[24,128]{1,0:T(8,128)S(1)} %get-tuple-element.55), channel_id=1, source_target_pairs={{0,4},{1,5},{2,6},{3,7},{4,0},{5,1},{6,2},{7,3},{8,12},{9,13},{10,... | collective-permute-start | bytes 36872 | tf_op jit(solution)/shard_map/ppermute | solution.py:54
  11.0 6.2 %collective-permute-start = (f32[24,128]{1,0:T(8,128)S(1)}, f32[24,128]{1,0:T(8,128)S(1)}, u32[]{:S(2)}, u32[]{:S(2)}) collective-permute-start(f32[24,128]{1,0:T(8,128)S(1)} %get-tuple-element.55), channel_id=1, source_target_pairs={{0,2},{1,3},{2,0},{3,1},{4,6},{5,7},{6,4},{7,5},{8,10},{9,11},{10,... | collective-permute-start | bytes 36872 | tf_op jit(solution)/shard_map/ppermute | solution.py:54
  11.8 21.4 %collective-permute-start.10 = (bf16[4,128,256]{2,1,0:T(8,128)(2,1)S(1)}, bf16[4,128,256]{2,1,0:T(8,128)(2,1)S(1)}, u32[]{:S(2)}, u32[]{:S(2)}) collective-permute-start(bf16[4,128,256]{2,1,0:T(8,128)(2,1)S(1)} %get-tuple-element.70), channel_id=1, source_target_pairs={{0,2},{1,3},{2,4},{3,5},{4,6},{5,7},{6,0},{7,1},{8,10},{9,11},{10,... | collective-permute-start | bytes 786440 | tf_op jit(solution)/shard_map/ppermute | solution.py:49
  21.2 7.5 %collective-permute-start.8 = (bf16[48,256]{1,0:T(8,128)(2,1)S(1)}, bf16[48,256]{1,0:T(8,128)(2,1)S(1)}, u32[]{:S(2)}, u32[]{:S(2)}) collective-permute-start(bf16[48,256]{1,0:T(8,128)(2,1)S(1)} %get-tuple-element.65), channel_id=1, source_target_pairs={{0,6},{1,7},{2,4},{3,5},{4,2},{5,3},{6,0},{7,1},{8,14},{9,15},{10,... | collective-permute-start | bytes 73736 | tf_op jit(solution)/shard_map/ppermute | solution.py:54
  25.0 10.5 %collective-permute-start.11 = (bf16[4,128,256]{2,1,0:T(8,128)(2,1)S(1)}, bf16[4,128,256]{2,1,0:T(8,128)(2,1)S(1)}, u32[]{:S(2)}, u32[]{:S(2)}) collective-permute-start(bf16[4,128,256]{2,1,0:T(8,128)(2,1)S(1)} %get-tuple-element.71), channel_id=1, source_target_pairs={{0,7},{1,2},{2,1},{3,4},{4,3},{5,6},{6,5},{7,0},{8,15},{9,10},{10,... | collective-permute-start | bytes 786440 | tf_op jit(solution)/shard_map/ppermute | solution.py:49
  25.0 13.4 %collective-permute-start.12 = (bf16[4,128,256]{2,1,0:T(8,128)(2,1)S(1)}, bf16[4,128,256]{2,1,0:T(8,128)(2,1)S(1)}, u32[]{:S(2)}, u32[]{:S(2)}) collective-permute-start(bf16[4,128,256]{2,1,0:T(8,128)(2,1)S(1)} %get-tuple-element.72), channel_id=1, source_target_pairs={{0,6},{1,7},{2,0},{3,1},{4,2},{5,3},{6,4},{7,5},{8,14},{9,15},{10,... | collective-permute-start | bytes 786440 | tf_op jit(solution)/shard_map/ppermute | solution.py:49
  25.4 13.0 %collective-permute-start.13 = (bf16[4,128,256]{2,1,0:T(8,128)(2,1)S(1)}, bf16[4,128,256]{2,1,0:T(8,128)(2,1)S(1)}, u32[]{:S(2)}, u32[]{:S(2)}) collective-permute-start(bf16[4,128,256]{2,1,0:T(8,128)(2,1)S(1)} %get-tuple-element.73), channel_id=1, source_target_pairs={{0,1},{1,0},{2,3},{3,2},{4,5},{5,4},{6,7},{7,6},{8,9},{9,8},{10,11... | collective-permute-start | bytes 786440 | tf_op jit(solution)/shard_map/ppermute | solution.py:49
  31.6 9.4 %collective-permute-start.14 = (bf16[4,128,256]{2,1,0:T(8,128)(2,1)S(1)}, bf16[4,128,256]{2,1,0:T(8,128)(2,1)S(1)}, u32[]{:S(2)}, u32[]{:S(2)}) collective-permute-start(bf16[4,128,256]{2,1,0:T(8,128)(2,1)S(1)} %get-tuple-element.74), channel_id=1, source_target_pairs={{0,24},{8,16},{16,8},{24,0},{1,25},{9,17},{17,9},{25,1},{2,26},{10... | collective-permute-start | bytes 786440 | tf_op jit(solution)/shard_map/ppermute | solution.py:49
  33.1 7.8 %collective-permute-start.9 = (f32[4,384]{1,0:T(4,128)S(1)}, f32[4,384]{1,0:T(4,128)S(1)}, u32[]{:S(2)}, u32[]{:S(2)}) collective-permute-start(f32[4,384]{1,0:T(4,128)S(1)} %get-tuple-element.69), channel_id=1, source_target_pairs={{0,8},{8,0},{16,24},{24,16},{1,9},{9,1},{17,25},{25,17},{2,10},{10... | collective-permute-start | bytes 18440 | tf_op jit(solution)/shard_map/ppermute | solution.py:49
  43.4 11.2 %collective-permute-start.15 = (bf16[4,128,256]{2,1,0:T(8,128)(2,1)S(1)}, bf16[4,128,256]{2,1,0:T(8,128)(2,1)S(1)}, u32[]{:S(2)}, u32[]{:S(2)}) collective-permute-start(bf16[4,128,256]{2,1,0:T(8,128)(2,1)S(1)} %get-tuple-element.76), channel_id=1, source_target_pairs={{0,2},{1,3},{2,4},{3,5},{4,6},{5,7},{6,0},{7,1},{8,10},{9,11},{10,... | collective-permute-start | bytes 786440 | tf_op jit(solution)/shard_map/ppermute | solution.py:49
  43.5 13.0 %collective-permute-start.16 = (bf16[4,128,256]{2,1,0:T(8,128)(2,1)S(1)}, bf16[4,128,256]{2,1,0:T(8,128)(2,1)S(1)}, u32[]{:S(2)}, u32[]{:S(2)}) collective-permute-start(bf16[4,128,256]{2,1,0:T(8,128)(2,1)S(1)} %get-tuple-element.77), channel_id=1, source_target_pairs={{0,7},{1,2},{2,1},{3,4},{4,3},{5,6},{6,5},{7,0},{8,15},{9,10},{10,... | collective-permute-start | bytes 786440 | tf_op jit(solution)/shard_map/ppermute | solution.py:49
  45.8 17.0 %collective-permute-start.17 = (bf16[4,128,256]{2,1,0:T(8,128)(2,1)S(1)}, bf16[4,128,256]{2,1,0:T(8,128)(2,1)S(1)}, u32[]{:S(2)}, u32[]{:S(2)}) collective-permute-start(bf16[4,128,256]{2,1,0:T(8,128)(2,1)S(1)} %get-tuple-element.78), channel_id=1, source_target_pairs={{0,6},{1,7},{2,0},{3,1},{4,2},{5,3},{6,4},{7,5},{8,14},{9,15},{10,... | collective-permute-start | bytes 786440 | tf_op jit(solution)/shard_map/ppermute | solution.py:49
  47.3 15.4 %collective-permute-start.18 = (bf16[4,128,256]{2,1,0:T(8,128)(2,1)S(1)}, bf16[4,128,256]{2,1,0:T(8,128)(2,1)S(1)}, u32[]{:S(2)}, u32[]{:S(2)}) collective-permute-start(bf16[4,128,256]{2,1,0:T(8,128)(2,1)S(1)} %get-tuple-element.79), channel_id=1, source_target_pairs={{0,1},{1,0},{2,3},{3,2},{4,5},{5,4},{6,7},{7,6},{8,9},{9,8},{10,11... | collective-permute-start | bytes 786440 | tf_op jit(solution)/shard_map/ppermute | solution.py:49
  47.3 15.4 %collective-permute-start.19 = (bf16[4,128,256]{2,1,0:T(8,128)(2,1)S(1)}, bf16[4,128,256]{2,1,0:T(8,128)(2,1)S(1)}, u32[]{:S(2)}, u32[]{:S(2)}) collective-permute-start(bf16[4,128,256]{2,1,0:T(8,128)(2,1)S(1)} %get-tuple-element.80), channel_id=1, source_target_pairs={{0,8},{8,0},{16,24},{24,16},{1,9},{9,1},{17,25},{25,17},{2,10},{10... | collective-permute-start | bytes 786440 | tf_op jit(solution)/shard_map/ppermute | solution.py:49
  54.6 8.1 %collective-permute-start.20 = (bf16[4,128,256]{2,1,0:T(8,128)(2,1)S(1)}, bf16[4,128,256]{2,1,0:T(8,128)(2,1)S(1)}, u32[]{:S(2)}, u32[]{:S(2)}) collective-permute-start(bf16[4,128,256]{2,1,0:T(8,128)(2,1)S(1)} %get-tuple-element.81), channel_id=1, source_target_pairs={{0,24},{8,16},{16,8},{24,0},{1,25},{9,17},{17,9},{25,1},{2,26},{10... | collective-permute-start | bytes 786440 | tf_op jit(solution)/shard_map/ppermute | solution.py:49
  65.0 11.0 %collective-permute-start.21 = (bf16[4,128,256]{2,1,0:T(8,128)(2,1)S(1)}, bf16[4,128,256]{2,1,0:T(8,128)(2,1)S(1)}, u32[]{:S(2)}, u32[]{:S(2)}) collective-permute-start(bf16[4,128,256]{2,1,0:T(8,128)(2,1)S(1)} %get-tuple-element.84), channel_id=1, source_target_pairs={{0,8},{8,0},{16,24},{24,16},{1,9},{9,1},{17,25},{25,17},{2,10},{10... | collective-permute-start | bytes 786440 | tf_op jit(solution)/shard_map/ppermute | solution.py:49
  66.8 5.5 %collective-permute-start.25 = (bf16[32,256]{1,0:T(8,128)(2,1)S(1)}, bf16[32,256]{1,0:T(8,128)(2,1)S(1)}, u32[]{:S(2)}, u32[]{:S(2)}) collective-permute-start(bf16[32,256]{1,0:T(8,128)(2,1)S(1)} %pad_maximum_fusion.1.rest_1_), channel_id=1, source_target_pairs={{0,6},{1,7},{2,4},{3,5},{4,2},{5,3},{6,0},{7,1},{8,14},{9,15},{10,... | collective-permute-start | bytes 49160 | tf_op jit(solution)/shard_map/ppermute | solution.py:54
  69.0 6.4 %collective-permute-start.23 = (bf16[32,256]{1,0:T(8,128)(2,1)S(1)}, bf16[32,256]{1,0:T(8,128)(2,1)S(1)}, u32[]{:S(2)}, u32[]{:S(2)}) collective-permute-start(bf16[32,256]{1,0:T(8,128)(2,1)S(1)} %pad_maximum_fusion.1.rest_1_), channel_id=1, source_target_pairs={{0,2},{1,3},{2,0},{3,1},{4,6},{5,7},{6,4},{7,5},{8,10},{9,11},{10,... | collective-permute-start | bytes 49160 | tf_op jit(solution)/shard_map/ppermute | solution.py:54
  71.2 11.2 %collective-permute-start.27 = (bf16[4,128,256]{2,1,0:T(8,128)(2,1)S(1)}, bf16[4,128,256]{2,1,0:T(8,128)(2,1)S(1)}, u32[]{:S(2)}, u32[]{:S(2)}) collective-permute-start(bf16[4,128,256]{2,1,0:T(8,128)(2,1)S(1)} %get-tuple-element.89), channel_id=1, source_target_pairs={{0,2},{1,3},{2,4},{3,5},{4,6},{5,7},{6,0},{7,1},{8,10},{9,11},{10,... | collective-permute-start | bytes 786440 | tf_op jit(solution)/shard_map/ppermute | solution.py:49
  72.3 12.2 %collective-permute-start.28 = (bf16[4,128,256]{2,1,0:T(8,128)(2,1)S(1)}, bf16[4,128,256]{2,1,0:T(8,128)(2,1)S(1)}, u32[]{:S(2)}, u32[]{:S(2)}) collective-permute-start(bf16[4,128,256]{2,1,0:T(8,128)(2,1)S(1)} %get-tuple-element.90), channel_id=1, source_target_pairs={{0,7},{1,2},{2,1},{3,4},{4,3},{5,6},{6,5},{7,0},{8,15},{9,10},{10,... | collective-permute-start | bytes 786440 | tf_op jit(solution)/shard_map/ppermute | solution.py:49
  73.7 17.7 %collective-permute-start.29 = (bf16[4,128,256]{2,1,0:T(8,128)(2,1)S(1)}, bf16[4,128,256]{2,1,0:T(8,128)(2,1)S(1)}, u32[]{:S(2)}, u32[]{:S(2)}) collective-permute-start(bf16[4,128,256]{2,1,0:T(8,128)(2,1)S(1)} %get-tuple-element.91), channel_id=1, source_target_pairs={{0,6},{1,7},{2,0},{3,1},{4,2},{5,3},{6,4},{7,5},{8,14},{9,15},{10,... | collective-permute-start | bytes 786440 | tf_op jit(solution)/shard_map/ppermute | solution.py:49
  75.4 15.9 %collective-permute-start.30 = (bf16[4,128,256]{2,1,0:T(8,128)(2,1)S(1)}, bf16[4,128,256]{2,1,0:T(8,128)(2,1)S(1)}, u32[]{:S(2)}, u32[]{:S(2)}) collective-permute-start(bf16[4,128,256]{2,1,0:T(8,128)(2,1)S(1)} %get-tuple-element.92), channel_id=1, source_target_pairs={{0,1},{1,0},{2,3},{3,2},{4,5},{5,4},{6,7},{7,6},{8,9},{9,8},{10,11... | collective-permute-start | bytes 786440 | tf_op jit(solution)/shard_map/ppermute | solution.py:49
  77.0 14.4 %collective-permute-start.31 = (bf16[4,128,256]{2,1,0:T(8,128)(2,1)S(1)}, bf16[4,128,256]{2,1,0:T(8,128)(2,1)S(1)}, u32[]{:S(2)}, u32[]{:S(2)}) collective-permute-start(bf16[4,128,256]{2,1,0:T(8,128)(2,1)S(1)} %get-tuple-element.93), channel_id=1, source_target_pairs={{0,24},{8,16},{16,8},{24,0},{1,25},{9,17},{17,9},{25,1},{2,26},{10... | collective-permute-start | bytes 786440 | tf_op jit(solution)/shard_map/ppermute | solution.py:49
  82.3 9.0 %collective-permute-start.26 = (f32[4,384]{1,0:T(4,128)S(1)}, f32[4,384]{1,0:T(4,128)S(1)}, u32[]{:S(2)}, u32[]{:S(2)}) collective-permute-start(f32[4,384]{1,0:T(4,128)S(1)} %get-tuple-element.88), channel_id=1, source_target_pairs={{0,8},{8,0},{16,24},{24,16},{1,9},{9,1},{17,25},{25,17},{2,10},{10... | collective-permute-start | bytes 18440 | tf_op jit(solution)/shard_map/ppermute | solution.py:49
  93.9 11.0 %collective-permute-start.32 = (bf16[4,128,256]{2,1,0:T(8,128)(2,1)S(1)}, bf16[4,128,256]{2,1,0:T(8,128)(2,1)S(1)}, u32[]{:S(2)}, u32[]{:S(2)}) collective-permute-start(bf16[4,128,256]{2,1,0:T(8,128)(2,1)S(1)} %get-tuple-element.95), channel_id=1, source_target_pairs={{0,2},{1,3},{2,4},{3,5},{4,6},{5,7},{6,0},{7,1},{8,10},{9,11},{10,... | collective-permute-start | bytes 786440 | tf_op jit(solution)/shard_map/ppermute | solution.py:49
  94.7 12.4 %collective-permute-start.33 = (bf16[4,128,256]{2,1,0:T(8,128)(2,1)S(1)}, bf16[4,128,256]{2,1,0:T(8,128)(2,1)S(1)}, u32[]{:S(2)}, u32[]{:S(2)}) collective-permute-start(bf16[4,128,256]{2,1,0:T(8,128)(2,1)S(1)} %get-tuple-element.96), channel_id=1, source_target_pairs={{0,7},{1,2},{2,1},{3,4},{4,3},{5,6},{6,5},{7,0},{8,15},{9,10},{10,... | collective-permute-start | bytes 786440 | tf_op jit(solution)/shard_map/ppermute | solution.py:49
  94.9 18.1 %collective-permute-start.34 = (bf16[4,128,256]{2,1,0:T(8,128)(2,1)S(1)}, bf16[4,128,256]{2,1,0:T(8,128)(2,1)S(1)}, u32[]{:S(2)}, u32[]{:S(2)}) collective-permute-start(bf16[4,128,256]{2,1,0:T(8,128)(2,1)S(1)} %get-tuple-element.97), channel_id=1, source_target_pairs={{0,6},{1,7},{2,0},{3,1},{4,2},{5,3},{6,4},{7,5},{8,14},{9,15},{10,... | collective-permute-start | bytes 786440 | tf_op jit(solution)/shard_map/ppermute | solution.py:49
  97.8 15.2 %collective-permute-start.35 = (bf16[4,128,256]{2,1,0:T(8,128)(2,1)S(1)}, bf16[4,128,256]{2,1,0:T(8,128)(2,1)S(1)}, u32[]{:S(2)}, u32[]{:S(2)}) collective-permute-start(bf16[4,128,256]{2,1,0:T(8,128)(2,1)S(1)} %get-tuple-element.98), channel_id=1, source_target_pairs={{0,1},{1,0},{2,3},{3,2},{4,5},{5,4},{6,7},{7,6},{8,9},{9,8},{10,11... | collective-permute-start | bytes 786440 | tf_op jit(solution)/shard_map/ppermute | solution.py:49
  98.4 14.6 %collective-permute-start.36 = (bf16[4,128,256]{2,1,0:T(8,128)(2,1)S(1)}, bf16[4,128,256]{2,1,0:T(8,128)(2,1)S(1)}, u32[]{:S(2)}, u32[]{:S(2)}) collective-permute-start(bf16[4,128,256]{2,1,0:T(8,128)(2,1)S(1)} %get-tuple-element.99), channel_id=1, source_target_pairs={{0,8},{8,0},{16,24},{24,16},{1,9},{9,1},{17,25},{25,17},{2,10},{10... | collective-permute-start | bytes 786440 | tf_op jit(solution)/shard_map/ppermute | solution.py:49
  104.8 8.1 %collective-permute-start.37 = (bf16[4,128,256]{2,1,0:T(8,128)(2,1)S(1)}, bf16[4,128,256]{2,1,0:T(8,128)(2,1)S(1)}, u32[]{:S(2)}, u32[]{:S(2)}) collective-permute-start(bf16[4,128,256]{2,1,0:T(8,128)(2,1)S(1)} %get-tuple-element.100), channel_id=1, source_target_pairs={{0,24},{8,16},{16,8},{24,0},{1,25},{9,17},{17,9},{25,1},{2,26},{10... | collective-permute-start | bytes 786440 | tf_op jit(solution)/shard_map/ppermute | solution.py:49
  (12 other events, 192.4 us)

commit v6 on v5

--- a/solution.py
+++ b/solution.py
@@ -185,15 +185,10 @@
     pick_blocks(send, narrow, slabs, range(len(slabs)))
 
 
-def coarse_kernel(wide, chips, early, bring, ties, send, basis, near_basis, disp, columns, *rest):
+def coarse_kernel(wide, chips, early, ties, send, basis, near_basis, disp, columns, *rest):
     rest = rest[ties:]
     parts, tables, rest = rest[:chips], rest[chips : 2 * chips], rest[2 * chips :]
-    if bring:
-        matrix, *rest, sem = rest
-    (corrected, near), slabs, (ordered, held) = rest[:2], rest[2:4], rest[-2:]
-    if bring:
-        copy = pltpu.make_async_copy(matrix, rest[4], sem)
-        copy.start()
+    corrected, near, *slabs, ordered, held = rest
     here = lax.axis_index("sub")
     cases = disp.shape[2]
     for p, part in enumerate(parts):
@@ -223,8 +218,6 @@
                 disp[b, :, cols] + columns[b] * rows[0][b : b + 1, cols]
             ).astype(jnp.bfloat16)
     pick_blocks(send, corrected, slabs[early - 4 :], range(early, DIRS))
-    if bring:
-        copy.wait()
 
 
 def dirichlet_kernel(early, send, read, weights, matrix, corrected, near, *rest):
@@ -274,6 +267,12 @@
         (i // 2, i % 2, i // across, slice(i % across * BLK, (i % across + 1) * BLK))
         for i in range(2 * (lanes // BLK))
     ]
+
+
+def bring_kernel(matrix, after, held, sem):
+    copy = pltpu.make_async_copy(matrix, held, sem)
+    copy.start()
+    copy.wait()
 
 
 def share_kernel(wide, own_rows, mine, theirs, proj, *rest):
@@ -405,32 +404,35 @@
     )(keep, swapped(give, 1))
     parts = tables = to_chips(chunks)
 
+    dirichlet_matrix = pl.pallas_call(
+        bring_kernel,
+        out_shape=resident,
+        in_specs=[HBM, ANY],
+        out_specs=VMEM,
+        scratch_shapes=[pltpu.SemaphoreType.DMA],
+        compiler_params=PARAMS,
+    )(in_hbm(dirichlet_matrix), proj)
+
     for iteration in range(ITERS):
-        bring = iteration == 0
         early = EARLY[iteration]
         if iteration:
             arrived = {way: exchanged(slabs[way], way) for way in ORDER if way < early}
             proj = proj.astype(jnp.bfloat16)
             parts = to_chips([jnp.concatenate([proj, swapped(proj, 1)])] * chips)
-        ties = [arrived[way] for way in (() if bring else (4, ))]
+        ties = [arrived[way] for way in (() if iteration == 0 else (4, 2, ))]
         corrected, near, *far = pl.pallas_call(
-            functools.partial(coarse_kernel, wide, chips, early, bring, len(ties)),
-            out_shape=[halved, f32(NEAR, cases + BLK), f32(CAP, cases + BLK) if early > 4 else slab, slab]
-            + [resident] * bring,
-            in_specs=[SMEM] + [VMEM] * 4 + [ANY] * len(ties) + [VMEM] * (2 * chips) + [HBM] * bring,
-            out_specs=[VMEM] * (4 + bring),
+            functools.partial(coarse_kernel, wide, chips, early, len(ties)),
+            out_shape=[halved, f32(NEAR, cases + BLK), f32(CAP, cases + BLK) if early > 4 else slab, slab],
+            in_specs=[SMEM] + [VMEM] * 4 + [ANY] * len(ties) + [VMEM] * (2 * chips),
+            out_specs=[VMEM] * 4,
             scratch_shapes=[
                 pltpu.VMEM((lanes, cases), jnp.float32),
                 pltpu.VMEM((blocks, 1, cases + BLK), jnp.float32),
-            ]
-            + [pltpu.SemaphoreType.DMA] * bring,
+            ],
             compiler_params=PARAMS,
         )(
             send, coarse_basis[0], near_basis, disp, columns, *ties, *parts, *tables,
-            *[in_hbm(dirichlet_matrix)] * bring,
-        )
-        if bring:
-            *far, dirichlet_matrix = far
+        )
         arrived[5] = exchanged(far[1], 5)
         moved = exchanged(far[0], 4)
         if early == 4:

time: 115 us -> 111 us (0.965)
  waiting for transfers between devices: 50.4 us -> 45 us
    ppermute x26, waiting for transfers between devices: 41.3 us -> 35 us  [exchanged(): lax.ppermute(slab, axis, [(i, (i + step) % count) for i, step in enumerat...]
    pallas_call x2 -> x3, Pallas kernels: 3.93 us -> 4.4 us  [the longest x1 2.36 us: on_device(): pl.pallas_call(bring_kernel, out_shape=resident, in_specs=[HBM, ANY], out...]
  transfers between devices with their start and end apart: 38 -> 38, of which waited for: 17 -> 20; matrix products, arithmetic and copies ran while one was open for 0% -> 0% of each run, Pallas kernels for 4% -> 5%
where the time goes in v6:
time: 111 us
  starting transfers between devices  47 us (42%)
  waiting for transfers between devices  45 us (41%)
  Pallas kernels  18.4 us (17%)
    ppermute x26, waiting for transfers between devices, exchanged(): lax.ppermute(slab, axis, [(i, (i + step) % count) for i, step in enumerat...  35 us
    ppermute x26, starting transfers between devices, exchanged(): lax.ppermute(slab, axis, [(i, (i + step) % count) for i, step in enumerat...  33.4 us
    ppermute x12, starting transfers between devices, swapped(): return lax.ppermute(value, 'sub', [(i, i ^ mask) for i in range(count)])  13.5 us
    ppermute x12, waiting for transfers between devices, swapped(): return lax.ppermute(value, 'sub', [(i, i ^ mask) for i in range(count)])  10 us
    pallas_call x2, Pallas kernels, on_device(): pl.pallas_call(functools.partial(dirichlet_kernel, early), out_shape=[hal...  4.89 us
    pallas_call x1, Pallas kernels, on_device(): pl.pallas_call(functools.partial(first_solve_kernel, wide), out_shape=[wh...  4.35 us
    pallas_call x1, Pallas kernels, on_device(): pl.pallas_call(bring_kernel, out_shape=resident, in_specs=[HBM, ANY], out...  2.36 us
    pallas_call x1, Pallas kernels, on_device(): pl.pallas_call(next_solve_kernel, out_shape=[whole, whole, f32(wide, case...  2.24 us
  transfers between devices with their start and end apart: 38, of which 20 were waited for; matrix products, arithmetic and copies ran while one was open for 0% of the time, Pallas kernels for 5%

profile of v6, /device:TPU:0, one launch (start us, length us, event | category | flops | bytes accessed | tf_op | source)
XLA Modules:
  0.0 110.6 jit_solution(10852765975007263294)
XLA Ops:
  0.0 4.3 %shard_map.91 = (f32[12,128,256]{2,1,0:T(8,128)S(1)}, f32[16,256]{1,0:T(8,128)S(1)}, f32[12,128,128]{2,1,0:T(8,128)S(1)}, f32[24,128]{1,0:T(8,128)S(1)}, bf16[4,...) custom-call(s32[1,24]{1,0:T(1,128)} %bitcast.22, ...), custom_call_target="tpu_custom_call" | custom-call | tf_op jit(solution)/shard_map/pallas_call | solution.py:364
  4.4 3.0 %collective-permute-start.4 = (bf16[4,128,256]{2,1,0:T(8,128)(2,1)S(1)}, bf16[4,128,256]{2,1,0:T(8,128)(2,1)S(1)}, u32[]{:S(2)}, u32[]{:S(2)}) collective-permute-start(bf16[4,128,256]{2,1,0:T(8,128)(2,1)S(1)} %get-tuple-element.56), channel_id=1, source_target_pairs={{0,8},{8,0},{16,24},{24,16},{1,9},{9,1},{17,25},{25,17},{2,10},{10... | collective-permute-start | bytes 786440 | tf_op jit(solution)/shard_map/ppermute | solution.py:49
  7.4 3.6 %collective-permute-start.2 = (f32[24,128]{1,0:T(8,128)S(1)}, f32[24,128]{1,0:T(8,128)S(1)}, u32[]{:S(2)}, u32[]{:S(2)}) collective-permute-start(f32[24,128]{1,0:T(8,128)S(1)} %get-tuple-element.55), channel_id=1, source_target_pairs={{0,6},{1,7},{2,4},{3,5},{4,2},{5,3},{6,0},{7,1},{8,14},{9,15},{10,... | collective-permute-start | bytes 36872 | tf_op jit(solution)/shard_map/ppermute | solution.py:54
  13.0 4.2 %collective-permute-done.1 = f32[24,128]{1,0:T(8,128)S(1)} collective-permute-done((f32[24,128]{1,0:T(8,128)S(1)}, f32[24,128]{1,0:T(8,128)S(1)}, u32[]{:S(2)}, u32[]{:S(2)}) %collective-permute-start.1) | collective-permute-done | bytes 12320 | tf_op jit(solution)/shard_map/ppermute | solution.py:54
  21.1 3.8 %collective-permute-start.8 = (bf16[48,256]{1,0:T(8,128)(2,1)S(1)}, bf16[48,256]{1,0:T(8,128)(2,1)S(1)}, u32[]{:S(2)}, u32[]{:S(2)}) collective-permute-start(bf16[48,256]{1,0:T(8,128)(2,1)S(1)} %get-tuple-element.64), channel_id=1, source_target_pairs={{0,6},{1,7},{2,4},{3,5},{4,2},{5,3},{6,0},{7,1},{8,14},{9,15},{10,... | collective-permute-start | bytes 73736 | tf_op jit(solution)/shard_map/ppermute | solution.py:54
  25.4 3.3 %collective-permute-start.13 = (bf16[4,128,256]{2,1,0:T(8,128)(2,1)S(1)}, bf16[4,128,256]{2,1,0:T(8,128)(2,1)S(1)}, u32[]{:S(2)}, u32[]{:S(2)}) collective-permute-start(bf16[4,128,256]{2,1,0:T(8,128)(2,1)S(1)} %get-tuple-element.71), channel_id=1, source_target_pairs={{0,1},{1,0},{2,3},{3,2},{4,5},{5,4},{6,7},{7,6},{8,9},{9,8},{10,11... | collective-permute-start | bytes 786440 | tf_op jit(solution)/shard_map/ppermute | solution.py:49
  29.7 1.6 %collective-permute-start.14 = (bf16[4,128,256]{2,1,0:T(8,128)(2,1)S(1)}, bf16[4,128,256]{2,1,0:T(8,128)(2,1)S(1)}, u32[]{:S(2)}, u32[]{:S(2)}) collective-permute-start(bf16[4,128,256]{2,1,0:T(8,128)(2,1)S(1)} %get-tuple-element.72), channel_id=1, source_target_pairs={{0,24},{8,16},{16,8},{24,0},{1,25},{9,17},{17,9},{25,1},{2,26},{10... | collective-permute-start | bytes 786440 | tf_op jit(solution)/shard_map/ppermute | solution.py:49
  31.2 1.5 %collective-permute-start.9 = (f32[4,384]{1,0:T(4,128)S(1)}, f32[4,384]{1,0:T(4,128)S(1)}, u32[]{:S(2)}, u32[]{:S(2)}) collective-permute-start(f32[4,384]{1,0:T(4,128)S(1)} %get-tuple-element.67), channel_id=1, source_target_pairs={{0,8},{8,0},{16,24},{24,16},{1,9},{9,1},{17,25},{25,17},{2,10},{10... | collective-permute-start | bytes 18440 | tf_op jit(solution)/shard_map/ppermute | solution.py:49
  32.7 2.4 %shard_map.92.matrix = bf16[1536,1536]{1,0:T(8,128)(2,1)S(1)} custom-call(bf16[1536,1536]{1,0:T(8,128)(2,1)} %bitcast.34, f32[16,256]{1,0:T(8,128)S(1)} %get-tuple-element.54.after.proj), custom_call_target="tpu_custom_call" | custom-call | tf_op jit(solution)/shard_map/pallas_call | solution.py:407
  35.4 2.9 %collective-permute-done.12.rest_3_ = bf16[4,128,256]{2,1,0:T(8,128)(2,1)S(1)} collective-permute-done((bf16[4,128,256]{2,1,0:T(8,128)(2,1)S(1)}, bf16[4,128,256]{2,1,0:T(8,128)(2,1)S(1)}, u32[]{:S(2)}, u32[]{:S(2)}) %collective-permute-start.12) | collective-permute-done | bytes 262176 | tf_op jit(solution)/shard_map/ppermute | solution.py:49
  39.1 2.4 %shard_map.96 = (bf16[12,128,256]{2,1,0:T(8,128)(2,1)S(1)}, bf16[4,128,256]{2,1,0:T(8,128)(2,1)S(1)}, bf16[4,128,256]{2,1,0:T(8,128)(2,1)S(1)}, bf16[4,128,256]{...) custom-call(s32[24]{0:T(128)S(1)} %bitcast.24, ...), custom_call_target="tpu_custom_call" | custom-call | tf_op jit(solution)/shard_map/pallas_call | solution.py:441
  41.6 2.3 %collective-permute-start.16 = (bf16[4,128,256]{2,1,0:T(8,128)(2,1)S(1)}, bf16[4,128,256]{2,1,0:T(8,128)(2,1)S(1)}, u32[]{:S(2)}, u32[]{:S(2)}) collective-permute-start(bf16[4,128,256]{2,1,0:T(8,128)(2,1)S(1)} %get-tuple-element.75), channel_id=1, source_target_pairs={{0,7},{1,2},{2,1},{3,4},{4,3},{5,6},{6,5},{7,0},{8,15},{9,10},{10,... | collective-permute-start | bytes 786440 | tf_op jit(solution)/shard_map/ppermute | solution.py:49
  43.9 1.5 %collective-permute-start.17 = (bf16[4,128,256]{2,1,0:T(8,128)(2,1)S(1)}, bf16[4,128,256]{2,1,0:T(8,128)(2,1)S(1)}, u32[]{:S(2)}, u32[]{:S(2)}) collective-permute-start(bf16[4,128,256]{2,1,0:T(8,128)(2,1)S(1)} %get-tuple-element.76), channel_id=1, source_target_pairs={{0,6},{1,7},{2,0},{3,1},{4,2},{5,3},{6,4},{7,5},{8,14},{9,15},{10,... | collective-permute-start | bytes 786440 | tf_op jit(solution)/shard_map/ppermute | solution.py:49
  45.9 6.8 %collective-permute-done.15.rest_0_ = bf16[4,128,256]{2,1,0:T(8,128)(2,1)S(1)} collective-permute-done((bf16[4,128,256]{2,1,0:T(8,128)(2,1)S(1)}, bf16[4,128,256]{2,1,0:T(8,128)(2,1)S(1)}, u32[]{:S(2)}, u32[]{:S(2)}) %collective-permute-start.15) | collective-permute-done | bytes 262176 | tf_op jit(solution)/shard_map/ppermute | solution.py:49
  54.5 6.3 %collective-permute-done.17.rest_2_ = bf16[4,128,256]{2,1,0:T(8,128)(2,1)S(1)} collective-permute-done((bf16[4,128,256]{2,1,0:T(8,128)(2,1)S(1)}, bf16[4,128,256]{2,1,0:T(8,128)(2,1)S(1)}, u32[]{:S(2)}, u32[]{:S(2)}) %collective-permute-start.17) | collective-permute-done | bytes 262176 | tf_op jit(solution)/shard_map/ppermute | solution.py:49
  60.9 2.2 %shard_map.97 = (f32[12,128,256]{2,1,0:T(8,128)S(1)}, f32[12,128,256]{2,1,0:T(8,128)S(1)}, f32[16,256]{1,0:T(8,128)S(1)}, bf16[4,128,256]{2,1,0:T(8,128)(2,1)S(1...) custom-call(s32[24]{0:T(128)S(1)} %bitcast.25, ...), custom_call_target="tpu_custom_call" | custom-call | tf_op jit(solution)/shard_map/pallas_call | solution.py:454
  63.7 1.7 %collective-permute-start.22 = (bf16[4,128,256]{2,1,0:T(8,128)(2,1)S(1)}, bf16[4,128,256]{2,1,0:T(8,128)(2,1)S(1)}, u32[]{:S(2)}, u32[]{:S(2)}) collective-permute-start(bf16[4,128,256]{2,1,0:T(8,128)(2,1)S(1)} %get-tuple-element.83), channel_id=1, source_target_pairs={{0,2},{1,3},{2,4},{3,5},{4,6},{5,7},{6,0},{7,1},{8,10},{9,11},{10,... | collective-permute-start | bytes 786440 | tf_op jit(solution)/shard_map/ppermute | solution.py:49
  66.6 2.1 %collective-permute-start.26 = (bf16[32,256]{1,0:T(8,128)(2,1)S(1)}, bf16[32,256]{1,0:T(8,128)(2,1)S(1)}, u32[]{:S(2)}, u32[]{:S(2)}) collective-permute-start(bf16[32,256]{1,0:T(8,128)(2,1)S(1)} %pad_maximum_fusion.1.rest_2_), channel_id=1, source_target_pairs={{0,6},{1,7},{2,4},{3,5},{4,2},{5,3},{6,0},{7,1},{8,14},{9,15},{10,... | collective-permute-start | bytes 49160 | tf_op jit(solution)/shard_map/ppermute | solution.py:54
  68.7 2.3 %collective-permute-start.24 = (bf16[32,256]{1,0:T(8,128)(2,1)S(1)}, bf16[32,256]{1,0:T(8,128)(2,1)S(1)}, u32[]{:S(2)}, u32[]{:S(2)}) collective-permute-start(bf16[32,256]{1,0:T(8,128)(2,1)S(1)} %pad_maximum_fusion.1.rest_2_), channel_id=1, source_target_pairs={{0,2},{1,3},{2,0},{3,1},{4,6},{5,7},{6,4},{7,5},{8,10},{9,11},{10,... | collective-permute-start | bytes 49160 | tf_op jit(solution)/shard_map/ppermute | solution.py:54
  71.0 1.7 %collective-permute-done.26.rest_5_ = bf16[32,256]{1,0:T(8,128)(2,1)S(1)} collective-permute-done((bf16[32,256]{1,0:T(8,128)(2,1)S(1)}, bf16[32,256]{1,0:T(8,128)(2,1)S(1)}, u32[]{:S(2)}, u32[]{:S(2)}) %collective-permute-start.26) | collective-permute-done | bytes 16416 | tf_op jit(solution)/shard_map/ppermute | solution.py:54
  73.4 1.6 %collective-permute-start.29 = (bf16[4,128,256]{2,1,0:T(8,128)(2,1)S(1)}, bf16[4,128,256]{2,1,0:T(8,128)(2,1)S(1)}, u32[]{:S(2)}, u32[]{:S(2)}) collective-permute-start(bf16[4,128,256]{2,1,0:T(8,128)(2,1)S(1)} %get-tuple-element.89), channel_id=1, source_target_pairs={{0,6},{1,7},{2,0},{3,1},{4,2},{5,3},{6,4},{7,5},{8,14},{9,15},{10,... | collective-permute-start | bytes 786440 | tf_op jit(solution)/shard_map/ppermute | solution.py:49
  77.4 2.3 %collective-permute-start.31 = (bf16[4,128,256]{2,1,0:T(8,128)(2,1)S(1)}, bf16[4,128,256]{2,1,0:T(8,128)(2,1)S(1)}, u32[]{:S(2)}, u32[]{:S(2)}) collective-permute-start(bf16[4,128,256]{2,1,0:T(8,128)(2,1)S(1)} %get-tuple-element.91), channel_id=1, source_target_pairs={{0,24},{8,16},{16,8},{24,0},{1,25},{9,17},{17,9},{25,1},{2,26},{10... | collective-permute-start | bytes 786440 | tf_op jit(solution)/shard_map/ppermute | solution.py:49
  80.2 2.9 %collective-permute-done.28.rest_2_ = bf16[4,128,256]{2,1,0:T(8,128)(2,1)S(1)} collective-permute-done((bf16[4,128,256]{2,1,0:T(8,128)(2,1)S(1)}, bf16[4,128,256]{2,1,0:T(8,128)(2,1)S(1)}, u32[]{:S(2)}, u32[]{:S(2)}) %collective-permute-start.28) | collective-permute-done | bytes 262176 | tf_op jit(solution)/shard_map/ppermute | solution.py:49
  83.1 3.4 %collective-permute-done.29.rest_3_ = bf16[4,128,256]{2,1,0:T(8,128)(2,1)S(1)} collective-permute-done((bf16[4,128,256]{2,1,0:T(8,128)(2,1)S(1)}, bf16[4,128,256]{2,1,0:T(8,128)(2,1)S(1)}, u32[]{:S(2)}, u32[]{:S(2)}) %collective-permute-start.29) | collective-permute-done | bytes 262176 | tf_op jit(solution)/shard_map/ppermute | solution.py:49
  86.6 2.4 %shard_map.99 = (bf16[12,128,256]{2,1,0:T(8,128)(2,1)S(1)}, bf16[4,128,256]{2,1,0:T(8,128)(2,1)S(1)}, bf16[4,128,256]{2,1,0:T(8,128)(2,1)S(1)}, bf16[4,128,256]{...) custom-call(s32[24]{0:T(128)S(1)} %bitcast.27, ...), custom_call_target="tpu_custom_call" | custom-call | tf_op jit(solution)/shard_map/pallas_call | solution.py:441
  90.1 1.9 %collective-permute-start.33 = (bf16[4,128,256]{2,1,0:T(8,128)(2,1)S(1)}, bf16[4,128,256]{2,1,0:T(8,128)(2,1)S(1)}, u32[]{:S(2)}, u32[]{:S(2)}) collective-permute-start(bf16[4,128,256]{2,1,0:T(8,128)(2,1)S(1)} %get-tuple-element.94), channel_id=1, source_target_pairs={{0,7},{1,2},{2,1},{3,4},{4,3},{5,6},{6,5},{7,0},{8,15},{9,10},{10,... | collective-permute-start | bytes 786440 | tf_op jit(solution)/shard_map/ppermute | solution.py:49
  92.0 1.7 %collective-permute-start.34 = (bf16[4,128,256]{2,1,0:T(8,128)(2,1)S(1)}, bf16[4,128,256]{2,1,0:T(8,128)(2,1)S(1)}, u32[]{:S(2)}, u32[]{:S(2)}) collective-permute-start(bf16[4,128,256]{2,1,0:T(8,128)(2,1)S(1)} %get-tuple-element.95), channel_id=1, source_target_pairs={{0,6},{1,7},{2,0},{3,1},{4,2},{5,3},{6,4},{7,5},{8,14},{9,15},{10,... | collective-permute-start | bytes 786440 | tf_op jit(solution)/shard_map/ppermute | solution.py:49
  93.8 1.6 %collective-permute-start.36 = (bf16[4,128,256]{2,1,0:T(8,128)(2,1)S(1)}, bf16[4,128,256]{2,1,0:T(8,128)(2,1)S(1)}, u32[]{:S(2)}, u32[]{:S(2)}) collective-permute-start(bf16[4,128,256]{2,1,0:T(8,128)(2,1)S(1)} %get-tuple-element.97), channel_id=1, source_target_pairs={{0,8},{8,0},{16,24},{24,16},{1,9},{9,1},{17,25},{25,17},{2,10},{10... | collective-permute-start | bytes 786440 | tf_op jit(solution)/shard_map/ppermute | solution.py:49
  95.3 5.0 %collective-permute-done.32.rest_0_ = bf16[4,128,256]{2,1,0:T(8,128)(2,1)S(1)} collective-permute-done((bf16[4,128,256]{2,1,0:T(8,128)(2,1)S(1)}, bf16[4,128,256]{2,1,0:T(8,128)(2,1)S(1)}, u32[]{:S(2)}, u32[]{:S(2)}) %collective-permute-start.32) | collective-permute-done | bytes 262176 | tf_op jit(solution)/shard_map/ppermute | solution.py:49
  100.3 2.3 %collective-permute-start.37 = (bf16[4,128,256]{2,1,0:T(8,128)(2,1)S(1)}, bf16[4,128,256]{2,1,0:T(8,128)(2,1)S(1)}, u32[]{:S(2)}, u32[]{:S(2)}) collective-permute-start(bf16[4,128,256]{2,1,0:T(8,128)(2,1)S(1)} %get-tuple-element.98), channel_id=1, source_target_pairs={{0,24},{8,16},{16,8},{24,0},{1,25},{9,17},{17,9},{25,1},{2,26},{10... | collective-permute-start | bytes 786440 | tf_op jit(solution)/shard_map/ppermute | solution.py:49
  103.1 5.5 %collective-permute-done.34.rest_2_ = bf16[4,128,256]{2,1,0:T(8,128)(2,1)S(1)} collective-permute-done((bf16[4,128,256]{2,1,0:T(8,128)(2,1)S(1)}, bf16[4,128,256]{2,1,0:T(8,128)(2,1)S(1)}, u32[]{:S(2)}, u32[]{:S(2)}) %collective-permute-start.34) | collective-permute-done | bytes 262176 | tf_op jit(solution)/shard_map/ppermute | solution.py:49
  108.7 1.9 %shard_map.100 = f32[12,128,256]{2,1,0:T(8,128)} custom-call(s32[12]{0:T(128)S(1)} %bitcast.32, f32[12,128,256]{2,1,0:T(8,128)S(1)} %get-tuple-element.80.mult, bf16[12,128,256]{2,1,0:T(8,128)(2,1)S(1)} %get-tuple-element.92.dual, bf16[4,128,256]{2,1,0:T(8,128)(2,1)S(1)} %collective-permute-done.32.rest_0_, ...), custom_call_target="tpu_custom_call" | custom-call | tf_op jit(solution)/shard_map/pallas_call | solution.py:462
  (70 shorter events, 18.1 us)
Async XLA Ops:
  4.4 14.2 %collective-permute-start.4 = (bf16[4,128,256]{2,1,0:T(8,128)(2,1)S(1)}, bf16[4,128,256]{2,1,0:T(8,128)(2,1)S(1)}, u32[]{:S(2)}, u32[]{:S(2)}) collective-permute-start(bf16[4,128,256]{2,1,0:T(8,128)(2,1)S(1)} %get-tuple-element.56), channel_id=1, source_target_pairs={{0,8},{8,0},{16,24},{24,16},{1,9},{9,1},{17,25},{25,17},{2,10},{10... | collective-permute-start | bytes 786440 | tf_op jit(solution)/shard_map/ppermute | solution.py:49
  7.4 5.6 %collective-permute-start.2 = (f32[24,128]{1,0:T(8,128)S(1)}, f32[24,128]{1,0:T(8,128)S(1)}, u32[]{:S(2)}, u32[]{:S(2)}) collective-permute-start(f32[24,128]{1,0:T(8,128)S(1)} %get-tuple-element.55), channel_id=1, source_target_pairs={{0,6},{1,7},{2,4},{3,5},{4,2},{5,3},{6,0},{7,1},{8,14},{9,15},{10,... | collective-permute-start | bytes 36872 | tf_op jit(solution)/shard_map/ppermute | solution.py:54
  11.0 6.2 %collective-permute-start.1 = (f32[24,128]{1,0:T(8,128)S(1)}, f32[24,128]{1,0:T(8,128)S(1)}, u32[]{:S(2)}, u32[]{:S(2)}) collective-permute-start(f32[24,128]{1,0:T(8,128)S(1)} %get-tuple-element.55), channel_id=1, source_target_pairs={{0,4},{1,5},{2,6},{3,7},{4,0},{5,1},{6,2},{7,3},{8,12},{9,13},{10,... | collective-permute-start | bytes 36872 | tf_op jit(solution)/shard_map/ppermute | solution.py:54
  11.0 6.2 %collective-permute-start = (f32[24,128]{1,0:T(8,128)S(1)}, f32[24,128]{1,0:T(8,128)S(1)}, u32[]{:S(2)}, u32[]{:S(2)}) collective-permute-start(f32[24,128]{1,0:T(8,128)S(1)} %get-tuple-element.55), channel_id=1, source_target_pairs={{0,2},{1,3},{2,0},{3,1},{4,6},{5,7},{6,4},{7,5},{8,10},{9,11},{10,... | collective-permute-start | bytes 36872 | tf_op jit(solution)/shard_map/ppermute | solution.py:54
  11.8 19.4 %collective-permute-start.10 = (bf16[4,128,256]{2,1,0:T(8,128)(2,1)S(1)}, bf16[4,128,256]{2,1,0:T(8,128)(2,1)S(1)}, u32[]{:S(2)}, u32[]{:S(2)}) collective-permute-start(bf16[4,128,256]{2,1,0:T(8,128)(2,1)S(1)} %get-tuple-element.68), channel_id=1, source_target_pairs={{0,2},{1,3},{2,4},{3,5},{4,6},{5,7},{6,0},{7,1},{8,10},{9,11},{10,... | collective-permute-start | bytes 786440 | tf_op jit(solution)/shard_map/ppermute | solution.py:49
  21.1 7.5 %collective-permute-start.8 = (bf16[48,256]{1,0:T(8,128)(2,1)S(1)}, bf16[48,256]{1,0:T(8,128)(2,1)S(1)}, u32[]{:S(2)}, u32[]{:S(2)}) collective-permute-start(bf16[48,256]{1,0:T(8,128)(2,1)S(1)} %get-tuple-element.64), channel_id=1, source_target_pairs={{0,6},{1,7},{2,4},{3,5},{4,2},{5,3},{6,0},{7,1},{8,14},{9,15},{10,... | collective-permute-start | bytes 73736 | tf_op jit(solution)/shard_map/ppermute | solution.py:54
  25.0 10.5 %collective-permute-start.11 = (bf16[4,128,256]{2,1,0:T(8,128)(2,1)S(1)}, bf16[4,128,256]{2,1,0:T(8,128)(2,1)S(1)}, u32[]{:S(2)}, u32[]{:S(2)}) collective-permute-start(bf16[4,128,256]{2,1,0:T(8,128)(2,1)S(1)} %get-tuple-element.69), channel_id=1, source_target_pairs={{0,7},{1,2},{2,1},{3,4},{4,3},{5,6},{6,5},{7,0},{8,15},{9,10},{10,... | collective-permute-start | bytes 786440 | tf_op jit(solution)/shard_map/ppermute | solution.py:49
  25.0 13.4 %collective-permute-start.12 = (bf16[4,128,256]{2,1,0:T(8,128)(2,1)S(1)}, bf16[4,128,256]{2,1,0:T(8,128)(2,1)S(1)}, u32[]{:S(2)}, u32[]{:S(2)}) collective-permute-start(bf16[4,128,256]{2,1,0:T(8,128)(2,1)S(1)} %get-tuple-element.70), channel_id=1, source_target_pairs={{0,6},{1,7},{2,0},{3,1},{4,2},{5,3},{6,4},{7,5},{8,14},{9,15},{10,... | collective-permute-start | bytes 786440 | tf_op jit(solution)/shard_map/ppermute | solution.py:49
  25.4 13.0 %collective-permute-start.13 = (bf16[4,128,256]{2,1,0:T(8,128)(2,1)S(1)}, bf16[4,128,256]{2,1,0:T(8,128)(2,1)S(1)}, u32[]{:S(2)}, u32[]{:S(2)}) collective-permute-start(bf16[4,128,256]{2,1,0:T(8,128)(2,1)S(1)} %get-tuple-element.71), channel_id=1, source_target_pairs={{0,1},{1,0},{2,3},{3,2},{4,5},{5,4},{6,7},{7,6},{8,9},{9,8},{10,11... | collective-permute-start | bytes 786440 | tf_op jit(solution)/shard_map/ppermute | solution.py:49
  29.7 9.4 %collective-permute-start.14 = (bf16[4,128,256]{2,1,0:T(8,128)(2,1)S(1)}, bf16[4,128,256]{2,1,0:T(8,128)(2,1)S(1)}, u32[]{:S(2)}, u32[]{:S(2)}) collective-permute-start(bf16[4,128,256]{2,1,0:T(8,128)(2,1)S(1)} %get-tuple-element.72), channel_id=1, source_target_pairs={{0,24},{8,16},{16,8},{24,0},{1,25},{9,17},{17,9},{25,1},{2,26},{10... | collective-permute-start | bytes 786440 | tf_op jit(solution)/shard_map/ppermute | solution.py:49
  31.2 7.8 %collective-permute-start.9 = (f32[4,384]{1,0:T(4,128)S(1)}, f32[4,384]{1,0:T(4,128)S(1)}, u32[]{:S(2)}, u32[]{:S(2)}) collective-permute-start(f32[4,384]{1,0:T(4,128)S(1)} %get-tuple-element.67), channel_id=1, source_target_pairs={{0,8},{8,0},{16,24},{24,16},{1,9},{9,1},{17,25},{25,17},{2,10},{10... | collective-permute-start | bytes 18440 | tf_op jit(solution)/shard_map/ppermute | solution.py:49
  41.5 11.2 %collective-permute-start.15 = (bf16[4,128,256]{2,1,0:T(8,128)(2,1)S(1)}, bf16[4,128,256]{2,1,0:T(8,128)(2,1)S(1)}, u32[]{:S(2)}, u32[]{:S(2)}) collective-permute-start(bf16[4,128,256]{2,1,0:T(8,128)(2,1)S(1)} %get-tuple-element.74), channel_id=1, source_target_pairs={{0,2},{1,3},{2,4},{3,5},{4,6},{5,7},{6,0},{7,1},{8,10},{9,11},{10,... | collective-permute-start | bytes 786440 | tf_op jit(solution)/shard_map/ppermute | solution.py:49
  41.6 13.0 %collective-permute-start.16 = (bf16[4,128,256]{2,1,0:T(8,128)(2,1)S(1)}, bf16[4,128,256]{2,1,0:T(8,128)(2,1)S(1)}, u32[]{:S(2)}, u32[]{:S(2)}) collective-permute-start(bf16[4,128,256]{2,1,0:T(8,128)(2,1)S(1)} %get-tuple-element.75), channel_id=1, source_target_pairs={{0,7},{1,2},{2,1},{3,4},{4,3},{5,6},{6,5},{7,0},{8,15},{9,10},{10,... | collective-permute-start | bytes 786440 | tf_op jit(solution)/shard_map/ppermute | solution.py:49
  43.9 17.0 %collective-permute-start.17 = (bf16[4,128,256]{2,1,0:T(8,128)(2,1)S(1)}, bf16[4,128,256]{2,1,0:T(8,128)(2,1)S(1)}, u32[]{:S(2)}, u32[]{:S(2)}) collective-permute-start(bf16[4,128,256]{2,1,0:T(8,128)(2,1)S(1)} %get-tuple-element.76), channel_id=1, source_target_pairs={{0,6},{1,7},{2,0},{3,1},{4,2},{5,3},{6,4},{7,5},{8,14},{9,15},{10,... | collective-permute-start | bytes 786440 | tf_op jit(solution)/shard_map/ppermute | solution.py:49
  45.4 15.4 %collective-permute-start.18 = (bf16[4,128,256]{2,1,0:T(8,128)(2,1)S(1)}, bf16[4,128,256]{2,1,0:T(8,128)(2,1)S(1)}, u32[]{:S(2)}, u32[]{:S(2)}) collective-permute-start(bf16[4,128,256]{2,1,0:T(8,128)(2,1)S(1)} %get-tuple-element.77), channel_id=1, source_target_pairs={{0,1},{1,0},{2,3},{3,2},{4,5},{5,4},{6,7},{7,6},{8,9},{9,8},{10,11... | collective-permute-start | bytes 786440 | tf_op jit(solution)/shard_map/ppermute | solution.py:49
  45.4 15.4 %collective-permute-start.19 = (bf16[4,128,256]{2,1,0:T(8,128)(2,1)S(1)}, bf16[4,128,256]{2,1,0:T(8,128)(2,1)S(1)}, u32[]{:S(2)}, u32[]{:S(2)}) collective-permute-start(bf16[4,128,256]{2,1,0:T(8,128)(2,1)S(1)} %get-tuple-element.78), channel_id=1, source_target_pairs={{0,8},{8,0},{16,24},{24,16},{1,9},{9,1},{17,25},{25,17},{2,10},{10... | collective-permute-start | bytes 786440 | tf_op jit(solution)/shard_map/ppermute | solution.py:49
  52.7 8.1 %collective-permute-start.20 = (bf16[4,128,256]{2,1,0:T(8,128)(2,1)S(1)}, bf16[4,128,256]{2,1,0:T(8,128)(2,1)S(1)}, u32[]{:S(2)}, u32[]{:S(2)}) collective-permute-start(bf16[4,128,256]{2,1,0:T(8,128)(2,1)S(1)} %get-tuple-element.79), channel_id=1, source_target_pairs={{0,24},{8,16},{16,8},{24,0},{1,25},{9,17},{17,9},{25,1},{2,26},{10... | collective-permute-start | bytes 786440 | tf_op jit(solution)/shard_map/ppermute | solution.py:49
  63.1 13.2 %collective-permute-start.21 = (bf16[4,128,256]{2,1,0:T(8,128)(2,1)S(1)}, bf16[4,128,256]{2,1,0:T(8,128)(2,1)S(1)}, u32[]{:S(2)}, u32[]{:S(2)}) collective-permute-start(bf16[4,128,256]{2,1,0:T(8,128)(2,1)S(1)} %get-tuple-element.82), channel_id=1, source_target_pairs={{0,8},{8,0},{16,24},{24,16},{1,9},{9,1},{17,25},{25,17},{2,10},{10... | collective-permute-start | bytes 786440 | tf_op jit(solution)/shard_map/ppermute | solution.py:49
  63.7 12.6 %collective-permute-start.22 = (bf16[4,128,256]{2,1,0:T(8,128)(2,1)S(1)}, bf16[4,128,256]{2,1,0:T(8,128)(2,1)S(1)}, u32[]{:S(2)}, u32[]{:S(2)}) collective-permute-start(bf16[4,128,256]{2,1,0:T(8,128)(2,1)S(1)} %get-tuple-element.83), channel_id=1, source_target_pairs={{0,2},{1,3},{2,4},{3,5},{4,6},{5,7},{6,0},{7,1},{8,10},{9,11},{10,... | collective-permute-start | bytes 786440 | tf_op jit(solution)/shard_map/ppermute | solution.py:49
  66.6 6.1 %collective-permute-start.26 = (bf16[32,256]{1,0:T(8,128)(2,1)S(1)}, bf16[32,256]{1,0:T(8,128)(2,1)S(1)}, u32[]{:S(2)}, u32[]{:S(2)}) collective-permute-start(bf16[32,256]{1,0:T(8,128)(2,1)S(1)} %pad_maximum_fusion.1.rest_2_), channel_id=1, source_target_pairs={{0,6},{1,7},{2,4},{3,5},{4,2},{5,3},{6,0},{7,1},{8,14},{9,15},{10,... | collective-permute-start | bytes 49160 | tf_op jit(solution)/shard_map/ppermute | solution.py:54
  68.7 6.3 %collective-permute-start.24 = (bf16[32,256]{1,0:T(8,128)(2,1)S(1)}, bf16[32,256]{1,0:T(8,128)(2,1)S(1)}, u32[]{:S(2)}, u32[]{:S(2)}) collective-permute-start(bf16[32,256]{1,0:T(8,128)(2,1)S(1)} %pad_maximum_fusion.1.rest_2_), channel_id=1, source_target_pairs={{0,2},{1,3},{2,0},{3,1},{4,6},{5,7},{6,4},{7,5},{8,10},{9,11},{10,... | collective-permute-start | bytes 49160 | tf_op jit(solution)/shard_map/ppermute | solution.py:54
  72.7 10.5 %collective-permute-start.28 = (bf16[4,128,256]{2,1,0:T(8,128)(2,1)S(1)}, bf16[4,128,256]{2,1,0:T(8,128)(2,1)S(1)}, u32[]{:S(2)}, u32[]{:S(2)}) collective-permute-start(bf16[4,128,256]{2,1,0:T(8,128)(2,1)S(1)} %get-tuple-element.88), channel_id=1, source_target_pairs={{0,7},{1,2},{2,1},{3,4},{4,3},{5,6},{6,5},{7,0},{8,15},{9,10},{10,... | collective-permute-start | bytes 786440 | tf_op jit(solution)/shard_map/ppermute | solution.py:49
  73.4 13.1 %collective-permute-start.29 = (bf16[4,128,256]{2,1,0:T(8,128)(2,1)S(1)}, bf16[4,128,256]{2,1,0:T(8,128)(2,1)S(1)}, u32[]{:S(2)}, u32[]{:S(2)}) collective-permute-start(bf16[4,128,256]{2,1,0:T(8,128)(2,1)S(1)} %get-tuple-element.89), channel_id=1, source_target_pairs={{0,6},{1,7},{2,0},{3,1},{4,2},{5,3},{6,4},{7,5},{8,14},{9,15},{10,... | collective-permute-start | bytes 786440 | tf_op jit(solution)/shard_map/ppermute | solution.py:49
  75.1 11.4 %collective-permute-start.30 = (bf16[4,128,256]{2,1,0:T(8,128)(2,1)S(1)}, bf16[4,128,256]{2,1,0:T(8,128)(2,1)S(1)}, u32[]{:S(2)}, u32[]{:S(2)}) collective-permute-start(bf16[4,128,256]{2,1,0:T(8,128)(2,1)S(1)} %get-tuple-element.90), channel_id=1, source_target_pairs={{0,1},{1,0},{2,3},{3,2},{4,5},{5,4},{6,7},{7,6},{8,9},{9,8},{10,11... | collective-permute-start | bytes 786440 | tf_op jit(solution)/shard_map/ppermute | solution.py:49
  77.4 9.3 %collective-permute-start.31 = (bf16[4,128,256]{2,1,0:T(8,128)(2,1)S(1)}, bf16[4,128,256]{2,1,0:T(8,128)(2,1)S(1)}, u32[]{:S(2)}, u32[]{:S(2)}) collective-permute-start(bf16[4,128,256]{2,1,0:T(8,128)(2,1)S(1)} %get-tuple-element.91), channel_id=1, source_target_pairs={{0,24},{8,16},{16,8},{24,0},{1,25},{9,17},{17,9},{25,1},{2,26},{10... | collective-permute-start | bytes 786440 | tf_op jit(solution)/shard_map/ppermute | solution.py:49
  79.7 6.9 %collective-permute-start.27 = (f32[4,384]{1,0:T(4,128)S(1)}, f32[4,384]{1,0:T(4,128)S(1)}, u32[]{:S(2)}, u32[]{:S(2)}) collective-permute-start(f32[4,384]{1,0:T(4,128)S(1)} %get-tuple-element.87), channel_id=1, source_target_pairs={{0,8},{8,0},{16,24},{24,16},{1,9},{9,1},{17,25},{25,17},{2,10},{10... | collective-permute-start | bytes 18440 | tf_op jit(solution)/shard_map/ppermute | solution.py:49
  89.1 11.3 %collective-permute-start.32 = (bf16[4,128,256]{2,1,0:T(8,128)(2,1)S(1)}, bf16[4,128,256]{2,1,0:T(8,128)(2,1)S(1)}, u32[]{:S(2)}, u32[]{:S(2)}) collective-permute-start(bf16[4,128,256]{2,1,0:T(8,128)(2,1)S(1)} %get-tuple-element.93), channel_id=1, source_target_pairs={{0,2},{1,3},{2,4},{3,5},{4,6},{5,7},{6,0},{7,1},{8,10},{9,11},{10,... | collective-permute-start | bytes 786440 | tf_op jit(solution)/shard_map/ppermute | solution.py:49
  90.1 13.0 %collective-permute-start.33 = (bf16[4,128,256]{2,1,0:T(8,128)(2,1)S(1)}, bf16[4,128,256]{2,1,0:T(8,128)(2,1)S(1)}, u32[]{:S(2)}, u32[]{:S(2)}) collective-permute-start(bf16[4,128,256]{2,1,0:T(8,128)(2,1)S(1)} %get-tuple-element.94), channel_id=1, source_target_pairs={{0,7},{1,2},{2,1},{3,4},{4,3},{5,6},{6,5},{7,0},{8,15},{9,10},{10,... | collective-permute-start | bytes 786440 | tf_op jit(solution)/shard_map/ppermute | solution.py:49
  92.0 16.6 %collective-permute-start.34 = (bf16[4,128,256]{2,1,0:T(8,128)(2,1)S(1)}, bf16[4,128,256]{2,1,0:T(8,128)(2,1)S(1)}, u32[]{:S(2)}, u32[]{:S(2)}) collective-permute-start(bf16[4,128,256]{2,1,0:T(8,128)(2,1)S(1)} %get-tuple-element.95), channel_id=1, source_target_pairs={{0,6},{1,7},{2,0},{3,1},{4,2},{5,3},{6,4},{7,5},{8,14},{9,15},{10,... | collective-permute-start | bytes 786440 | tf_op jit(solution)/shard_map/ppermute | solution.py:49
  93.7 14.9 %collective-permute-start.35 = (bf16[4,128,256]{2,1,0:T(8,128)(2,1)S(1)}, bf16[4,128,256]{2,1,0:T(8,128)(2,1)S(1)}, u32[]{:S(2)}, u32[]{:S(2)}) collective-permute-start(bf16[4,128,256]{2,1,0:T(8,128)(2,1)S(1)} %get-tuple-element.96), channel_id=1, source_target_pairs={{0,1},{1,0},{2,3},{3,2},{4,5},{5,4},{6,7},{7,6},{8,9},{9,8},{10,11... | collective-permute-start | bytes 786440 | tf_op jit(solution)/shard_map/ppermute | solution.py:49
  93.8 14.8 %collective-permute-start.36 = (bf16[4,128,256]{2,1,0:T(8,128)(2,1)S(1)}, bf16[4,128,256]{2,1,0:T(8,128)(2,1)S(1)}, u32[]{:S(2)}, u32[]{:S(2)}) collective-permute-start(bf16[4,128,256]{2,1,0:T(8,128)(2,1)S(1)} %get-tuple-element.97), channel_id=1, source_target_pairs={{0,8},{8,0},{16,24},{24,16},{1,9},{9,1},{17,25},{25,17},{2,10},{10... | collective-permute-start | bytes 786440 | tf_op jit(solution)/shard_map/ppermute | solution.py:49
  100.3 8.4 %collective-permute-start.37 = (bf16[4,128,256]{2,1,0:T(8,128)(2,1)S(1)}, bf16[4,128,256]{2,1,0:T(8,128)(2,1)S(1)}, u32[]{:S(2)}, u32[]{:S(2)}) collective-permute-start(bf16[4,128,256]{2,1,0:T(8,128)(2,1)S(1)} %get-tuple-element.98), channel_id=1, source_target_pairs={{0,24},{8,16},{16,8},{24,0},{1,25},{9,17},{17,9},{25,1},{2,26},{10... | collective-permute-start | bytes 786440 | tf_op jit(solution)/shard_map/ppermute | solution.py:49
  (12 other events, 158.3 us)

commit v7 on v6

--- a/solution.py
+++ b/solution.py
@@ -17,6 +17,7 @@
 SHIFTS = {2: 2, 3: -2}
 OFFSETS = (1, -1, 2, -2)
 ORDER = (2, 1, 3, 0, 4, 5)
+SECOND = (2, 1, 3, 4, 5, 0)
 HIGHEST = lax.Precision.HIGHEST
 VMEM = pl.BlockSpec(memory_space=pltpu.VMEM)
 SMEM = pl.BlockSpec(memory_space=pltpu.SMEM)
@@ -76,8 +77,8 @@
             slab[j] = values[slot_block(send, way, j)]
 
 
-def stack_slabs(arrived, received):
-    for way, slab in zip(ORDER, arrived):
+def stack_slabs(arrived, received, order):
+    for way, slab in zip(order, arrived):
         for j in range(CAP):
             received[way * CAP + j] = slab[j]
 
@@ -165,16 +166,16 @@
         row = basis_held[:, b * BLK : (b + 1) * BLK]
         rows[b] = row
         columns[b] = as_column(row)
-    tell(wide, map_held, send_held, rows, told)
     small[3].wait()
     solve(copies, held, rhs, columns, disp, narrow, proj)
+    tell(wide, map_held, send_held, rows, told)
     pick_blocks(send_held.at[0], narrow, slabs, range(EARLY[0]))
 
 
 def next_solve_kernel(send, read, matrix, load, columns, dual, *rest):
     arrived, (mult, disp, proj), rest = rest[:DIRS], rest[DIRS : DIRS + 3], rest[DIRS + 3 :]
     *slabs, received, rhs, narrow = rest
-    stack_slabs(arrived, received)
+    stack_slabs(arrived, received, SECOND)
     for b in range(disp.shape[0]):
         far = received[slot_read(read, b)]
         step = dual[b].astype(jnp.float32) - far.astype(jnp.float32)
@@ -225,7 +226,7 @@
     arrived, dual, rest = rest[:DIRS], rest[DIRS], rest[DIRS + 1 :]
     slabs, (received, rows, rhs) = rest[:DIRS], rest[DIRS:]
     blocks, _, cases = corrected.shape
-    stack_slabs(arrived, received)
+    stack_slabs(arrived, received, ORDER)
     for k in range(NEAR):
         rows[k] = near[k : k + 1, :]
     for k in range(NEAR, DIRS * CAP):
@@ -250,7 +251,7 @@
 
 def finish_kernel(read, mult, dual, *rest):
     arrived, (out, received, ready, sems) = rest[:DIRS], rest[DIRS:]
-    stack_slabs(arrived, received)
+    stack_slabs(arrived, received, SECOND)
     copies = []
     for b in range(out.shape[0]):
         far = received[slot_read(read, b)]
@@ -449,7 +450,7 @@
             send, read, weights, dirichlet_matrix, corrected, near, *far_rows,
             *[arrived[way] for way in ORDER],
         )
-        arrived = [exchanged(slabs[way], way) for way in ORDER]
+        arrived = [exchanged(slabs[way], way) for way in SECOND]
         if iteration + 1 < ITERS:
             mult, disp, proj, *slabs = pl.pallas_call(
                 next_solve_kernel,

time: 111 us -> 111 us (level)
  transfers between devices with their start and end apart: 38 -> 38, of which waited for: 20 -> 19; matrix products, arithmetic and copies ran while one was open for 0% -> 0% of each run, Pallas kernels for 5% -> 5%
where the time goes in v7:
time: 111 us
  starting transfers between devices  46.7 us (42%)
  waiting for transfers between devices  45.1 us (41%)
  Pallas kernels  18.4 us (17%)
    ppermute x26, waiting for transfers between devices, exchanged(): lax.ppermute(slab, axis, [(i, (i + step) % count) for i, step in enumerat...  35.1 us
    ppermute x26, starting transfers between devices, exchanged(): lax.ppermute(slab, axis, [(i, (i + step) % count) for i, step in enumerat...  33.2 us
    ppermute x12, starting transfers between devices, swapped(): return lax.ppermute(value, 'sub', [(i, i ^ mask) for i in range(count)])  13.5 us
    ppermute x12, waiting for transfers between devices, swapped(): return lax.ppermute(value, 'sub', [(i, i ^ mask) for i in range(count)])  10 us
    pallas_call x2, Pallas kernels, on_device(): pl.pallas_call(functools.partial(dirichlet_kernel, early), out_shape=[hal...  4.88 us
    pallas_call x1, Pallas kernels, on_device(): pl.pallas_call(functools.partial(first_solve_kernel, wide), out_shape=[wh...  4.35 us
    pallas_call x1, Pallas kernels, on_device(): pl.pallas_call(bring_kernel, out_shape=resident, in_specs=[HBM, ANY], out...  2.36 us
    pallas_call x1, Pallas kernels, on_device(): pl.pallas_call(next_solve_kernel, out_shape=[whole, whole, f32(wide, case...  2.24 us
  transfers between devices with their start and end apart: 38, of which 19 were waited for; matrix products, arithmetic and copies ran while one was open for 0% of the time, Pallas kernels for 5%

profile of v7, /device:TPU:0, one launch (start us, length us, event | category | flops | bytes accessed | tf_op | source)
XLA Modules:
  0.0 110.5 jit_solution(4659305121098042515)
XLA Ops:
  0.0 4.3 %shard_map.91 = (f32[12,128,256]{2,1,0:T(8,128)S(1)}, f32[16,256]{1,0:T(8,128)S(1)}, f32[12,128,128]{2,1,0:T(8,128)S(1)}, f32[24,128]{1,0:T(8,128)S(1)}, bf16[4,...) custom-call(s32[1,24]{1,0:T(1,128)} %bitcast.22, ...), custom_call_target="tpu_custom_call" | custom-call | tf_op jit(solution)/shard_map/pallas_call | solution.py:365
  4.4 3.0 %collective-permute-start.4 = (bf16[4,128,256]{2,1,0:T(8,128)(2,1)S(1)}, bf16[4,128,256]{2,1,0:T(8,128)(2,1)S(1)}, u32[]{:S(2)}, u32[]{:S(2)}) collective-permute-start(bf16[4,128,256]{2,1,0:T(8,128)(2,1)S(1)} %get-tuple-element.56), channel_id=1, source_target_pairs={{0,8},{8,0},{16,24},{24,16},{1,9},{9,1},{17,25},{25,17},{2,10},{10... | collective-permute-start | bytes 786440 | tf_op jit(solution)/shard_map/ppermute | solution.py:50
  7.4 3.6 %collective-permute-start.2 = (f32[24,128]{1,0:T(8,128)S(1)}, f32[24,128]{1,0:T(8,128)S(1)}, u32[]{:S(2)}, u32[]{:S(2)}) collective-permute-start(f32[24,128]{1,0:T(8,128)S(1)} %get-tuple-element.55), channel_id=1, source_target_pairs={{0,6},{1,7},{2,4},{3,5},{4,2},{5,3},{6,0},{7,1},{8,14},{9,15},{10,... | collective-permute-start | bytes 36872 | tf_op jit(solution)/shard_map/ppermute | solution.py:55
  13.0 4.2 %collective-permute-done.1 = f32[24,128]{1,0:T(8,128)S(1)} collective-permute-done((f32[24,128]{1,0:T(8,128)S(1)}, f32[24,128]{1,0:T(8,128)S(1)}, u32[]{:S(2)}, u32[]{:S(2)}) %collective-permute-start.1) | collective-permute-done | bytes 12320 | tf_op jit(solution)/shard_map/ppermute | solution.py:55
  21.2 3.8 %collective-permute-start.8 = (bf16[48,256]{1,0:T(8,128)(2,1)S(1)}, bf16[48,256]{1,0:T(8,128)(2,1)S(1)}, u32[]{:S(2)}, u32[]{:S(2)}) collective-permute-start(bf16[48,256]{1,0:T(8,128)(2,1)S(1)} %get-tuple-element.64), channel_id=1, source_target_pairs={{0,6},{1,7},{2,4},{3,5},{4,2},{5,3},{6,0},{7,1},{8,14},{9,15},{10,... | collective-permute-start | bytes 73736 | tf_op jit(solution)/shard_map/ppermute | solution.py:55
  25.4 3.3 %collective-permute-start.13 = (bf16[4,128,256]{2,1,0:T(8,128)(2,1)S(1)}, bf16[4,128,256]{2,1,0:T(8,128)(2,1)S(1)}, u32[]{:S(2)}, u32[]{:S(2)}) collective-permute-start(bf16[4,128,256]{2,1,0:T(8,128)(2,1)S(1)} %get-tuple-element.71), channel_id=1, source_target_pairs={{0,1},{1,0},{2,3},{3,2},{4,5},{5,4},{6,7},{7,6},{8,9},{9,8},{10,11... | collective-permute-start | bytes 786440 | tf_op jit(solution)/shard_map/ppermute | solution.py:50
  29.7 1.6 %collective-permute-start.14 = (bf16[4,128,256]{2,1,0:T(8,128)(2,1)S(1)}, bf16[4,128,256]{2,1,0:T(8,128)(2,1)S(1)}, u32[]{:S(2)}, u32[]{:S(2)}) collective-permute-start(bf16[4,128,256]{2,1,0:T(8,128)(2,1)S(1)} %get-tuple-element.72), channel_id=1, source_target_pairs={{0,24},{8,16},{16,8},{24,0},{1,25},{9,17},{17,9},{25,1},{2,26},{10... | collective-permute-start | bytes 786440 | tf_op jit(solution)/shard_map/ppermute | solution.py:50
  32.7 2.4 %shard_map.92.matrix = bf16[1536,1536]{1,0:T(8,128)(2,1)S(1)} custom-call(bf16[1536,1536]{1,0:T(8,128)(2,1)} %bitcast.34, f32[16,256]{1,0:T(8,128)S(1)} %get-tuple-element.54.after.proj), custom_call_target="tpu_custom_call" | custom-call | tf_op jit(solution)/shard_map/pallas_call | solution.py:408
  35.4 2.9 %collective-permute-done.12.rest_3_ = bf16[4,128,256]{2,1,0:T(8,128)(2,1)S(1)} collective-permute-done((bf16[4,128,256]{2,1,0:T(8,128)(2,1)S(1)}, bf16[4,128,256]{2,1,0:T(8,128)(2,1)S(1)}, u32[]{:S(2)}, u32[]{:S(2)}) %collective-permute-start.12) | collective-permute-done | bytes 262176 | tf_op jit(solution)/shard_map/ppermute | solution.py:50
  39.1 2.4 %shard_map.96 = (bf16[12,128,256]{2,1,0:T(8,128)(2,1)S(1)}, bf16[4,128,256]{2,1,0:T(8,128)(2,1)S(1)}, bf16[4,128,256]{2,1,0:T(8,128)(2,1)S(1)}, bf16[4,128,256]{...) custom-call(s32[24]{0:T(128)S(1)} %bitcast.24, ...), custom_call_target="tpu_custom_call" | custom-call | tf_op jit(solution)/shard_map/pallas_call | solution.py:442
  41.6 2.3 %collective-permute-start.16 = (bf16[4,128,256]{2,1,0:T(8,128)(2,1)S(1)}, bf16[4,128,256]{2,1,0:T(8,128)(2,1)S(1)}, u32[]{:S(2)}, u32[]{:S(2)}) collective-permute-start(bf16[4,128,256]{2,1,0:T(8,128)(2,1)S(1)} %get-tuple-element.75), channel_id=1, source_target_pairs={{0,7},{1,2},{2,1},{3,4},{4,3},{5,6},{6,5},{7,0},{8,15},{9,10},{10,... | collective-permute-start | bytes 786440 | tf_op jit(solution)/shard_map/ppermute | solution.py:50
  45.9 2.3 %collective-permute-start.19 = (bf16[4,128,256]{2,1,0:T(8,128)(2,1)S(1)}, bf16[4,128,256]{2,1,0:T(8,128)(2,1)S(1)}, u32[]{:S(2)}, u32[]{:S(2)}) collective-permute-start(bf16[4,128,256]{2,1,0:T(8,128)(2,1)S(1)} %get-tuple-element.78), channel_id=1, source_target_pairs={{0,24},{8,16},{16,8},{24,0},{1,25},{9,17},{17,9},{25,1},{2,26},{10... | collective-permute-start | bytes 786440 | tf_op jit(solution)/shard_map/ppermute | solution.py:50
  48.2 4.5 %collective-permute-done.15.rest_0_ = bf16[4,128,256]{2,1,0:T(8,128)(2,1)S(1)} collective-permute-done((bf16[4,128,256]{2,1,0:T(8,128)(2,1)S(1)}, bf16[4,128,256]{2,1,0:T(8,128)(2,1)S(1)}, u32[]{:S(2)}, u32[]{:S(2)}) %collective-permute-start.15) | collective-permute-done | bytes 262176 | tf_op jit(solution)/shard_map/ppermute | solution.py:50
  52.7 1.8 %collective-permute-done.16.rest_1_ = bf16[4,128,256]{2,1,0:T(8,128)(2,1)S(1)} collective-permute-done((bf16[4,128,256]{2,1,0:T(8,128)(2,1)S(1)}, bf16[4,128,256]{2,1,0:T(8,128)(2,1)S(1)}, u32[]{:S(2)}, u32[]{:S(2)}) %collective-permute-start.16) | collective-permute-done | bytes 262176 | tf_op jit(solution)/shard_map/ppermute | solution.py:50
  54.5 6.3 %collective-permute-done.17.rest_2_ = bf16[4,128,256]{2,1,0:T(8,128)(2,1)S(1)} collective-permute-done((bf16[4,128,256]{2,1,0:T(8,128)(2,1)S(1)}, bf16[4,128,256]{2,1,0:T(8,128)(2,1)S(1)}, u32[]{:S(2)}, u32[]{:S(2)}) %collective-permute-start.17) | collective-permute-done | bytes 262176 | tf_op jit(solution)/shard_map/ppermute | solution.py:50
  60.9 2.2 %shard_map.97 = (f32[12,128,256]{2,1,0:T(8,128)S(1)}, f32[12,128,256]{2,1,0:T(8,128)S(1)}, f32[16,256]{1,0:T(8,128)S(1)}, bf16[4,128,256]{2,1,0:T(8,128)(2,1)S(1...) custom-call(s32[24]{0:T(128)S(1)} %bitcast.25, ...), custom_call_target="tpu_custom_call" | custom-call | tf_op jit(solution)/shard_map/pallas_call | solution.py:455
  63.7 1.7 %collective-permute-start.22 = (bf16[4,128,256]{2,1,0:T(8,128)(2,1)S(1)}, bf16[4,128,256]{2,1,0:T(8,128)(2,1)S(1)}, u32[]{:S(2)}, u32[]{:S(2)}) collective-permute-start(bf16[4,128,256]{2,1,0:T(8,128)(2,1)S(1)} %get-tuple-element.83), channel_id=1, source_target_pairs={{0,2},{1,3},{2,4},{3,5},{4,6},{5,7},{6,0},{7,1},{8,10},{9,11},{10,... | collective-permute-start | bytes 786440 | tf_op jit(solution)/shard_map/ppermute | solution.py:50
  66.6 2.1 %collective-permute-start.26 = (bf16[32,256]{1,0:T(8,128)(2,1)S(1)}, bf16[32,256]{1,0:T(8,128)(2,1)S(1)}, u32[]{:S(2)}, u32[]{:S(2)}) collective-permute-start(bf16[32,256]{1,0:T(8,128)(2,1)S(1)} %pad_maximum_fusion.1.rest_2_), channel_id=1, source_target_pairs={{0,6},{1,7},{2,4},{3,5},{4,2},{5,3},{6,0},{7,1},{8,14},{9,15},{10,... | collective-permute-start | bytes 49160 | tf_op jit(solution)/shard_map/ppermute | solution.py:55
  68.7 2.3 %collective-permute-start.24 = (bf16[32,256]{1,0:T(8,128)(2,1)S(1)}, bf16[32,256]{1,0:T(8,128)(2,1)S(1)}, u32[]{:S(2)}, u32[]{:S(2)}) collective-permute-start(bf16[32,256]{1,0:T(8,128)(2,1)S(1)} %pad_maximum_fusion.1.rest_2_), channel_id=1, source_target_pairs={{0,2},{1,3},{2,0},{3,1},{4,6},{5,7},{6,4},{7,5},{8,10},{9,11},{10,... | collective-permute-start | bytes 49160 | tf_op jit(solution)/shard_map/ppermute | solution.py:55
  71.0 1.7 %collective-permute-done.26.rest_5_ = bf16[32,256]{1,0:T(8,128)(2,1)S(1)} collective-permute-done((bf16[32,256]{1,0:T(8,128)(2,1)S(1)}, bf16[32,256]{1,0:T(8,128)(2,1)S(1)}, u32[]{:S(2)}, u32[]{:S(2)}) %collective-permute-start.26) | collective-permute-done | bytes 16416 | tf_op jit(solution)/shard_map/ppermute | solution.py:55
  73.4 1.6 %collective-permute-start.29 = (bf16[4,128,256]{2,1,0:T(8,128)(2,1)S(1)}, bf16[4,128,256]{2,1,0:T(8,128)(2,1)S(1)}, u32[]{:S(2)}, u32[]{:S(2)}) collective-permute-start(bf16[4,128,256]{2,1,0:T(8,128)(2,1)S(1)} %get-tuple-element.89), channel_id=1, source_target_pairs={{0,6},{1,7},{2,0},{3,1},{4,2},{5,3},{6,4},{7,5},{8,14},{9,15},{10,... | collective-permute-start | bytes 786440 | tf_op jit(solution)/shard_map/ppermute | solution.py:50
  77.4 2.3 %collective-permute-start.31 = (bf16[4,128,256]{2,1,0:T(8,128)(2,1)S(1)}, bf16[4,128,256]{2,1,0:T(8,128)(2,1)S(1)}, u32[]{:S(2)}, u32[]{:S(2)}) collective-permute-start(bf16[4,128,256]{2,1,0:T(8,128)(2,1)S(1)} %get-tuple-element.91), channel_id=1, source_target_pairs={{0,24},{8,16},{16,8},{24,0},{1,25},{9,17},{17,9},{25,1},{2,26},{10... | collective-permute-start | bytes 786440 | tf_op jit(solution)/shard_map/ppermute | solution.py:50
  80.2 2.9 %collective-permute-done.28.rest_2_ = bf16[4,128,256]{2,1,0:T(8,128)(2,1)S(1)} collective-permute-done((bf16[4,128,256]{2,1,0:T(8,128)(2,1)S(1)}, bf16[4,128,256]{2,1,0:T(8,128)(2,1)S(1)}, u32[]{:S(2)}, u32[]{:S(2)}) %collective-permute-start.28) | collective-permute-done | bytes 262176 | tf_op jit(solution)/shard_map/ppermute | solution.py:50
  83.1 3.4 %collective-permute-done.29.rest_3_ = bf16[4,128,256]{2,1,0:T(8,128)(2,1)S(1)} collective-permute-done((bf16[4,128,256]{2,1,0:T(8,128)(2,1)S(1)}, bf16[4,128,256]{2,1,0:T(8,128)(2,1)S(1)}, u32[]{:S(2)}, u32[]{:S(2)}) %collective-permute-start.29) | collective-permute-done | bytes 262176 | tf_op jit(solution)/shard_map/ppermute | solution.py:50
  86.6 2.4 %shard_map.99 = (bf16[12,128,256]{2,1,0:T(8,128)(2,1)S(1)}, bf16[4,128,256]{2,1,0:T(8,128)(2,1)S(1)}, bf16[4,128,256]{2,1,0:T(8,128)(2,1)S(1)}, bf16[4,128,256]{...) custom-call(s32[24]{0:T(128)S(1)} %bitcast.27, ...), custom_call_target="tpu_custom_call" | custom-call | tf_op jit(solution)/shard_map/pallas_call | solution.py:442
  90.1 1.9 %collective-permute-start.33 = (bf16[4,128,256]{2,1,0:T(8,128)(2,1)S(1)}, bf16[4,128,256]{2,1,0:T(8,128)(2,1)S(1)}, u32[]{:S(2)}, u32[]{:S(2)}) collective-permute-start(bf16[4,128,256]{2,1,0:T(8,128)(2,1)S(1)} %get-tuple-element.94), channel_id=1, source_target_pairs={{0,7},{1,2},{2,1},{3,4},{4,3},{5,6},{6,5},{7,0},{8,15},{9,10},{10,... | collective-permute-start | bytes 786440 | tf_op jit(solution)/shard_map/ppermute | solution.py:50
  92.0 1.7 %collective-permute-start.34 = (bf16[4,128,256]{2,1,0:T(8,128)(2,1)S(1)}, bf16[4,128,256]{2,1,0:T(8,128)(2,1)S(1)}, u32[]{:S(2)}, u32[]{:S(2)}) collective-permute-start(bf16[4,128,256]{2,1,0:T(8,128)(2,1)S(1)} %get-tuple-element.95), channel_id=1, source_target_pairs={{0,6},{1,7},{2,0},{3,1},{4,2},{5,3},{6,4},{7,5},{8,14},{9,15},{10,... | collective-permute-start | bytes 786440 | tf_op jit(solution)/shard_map/ppermute | solution.py:50
  93.7 1.5 %collective-permute-start.35 = (bf16[4,128,256]{2,1,0:T(8,128)(2,1)S(1)}, bf16[4,128,256]{2,1,0:T(8,128)(2,1)S(1)}, u32[]{:S(2)}, u32[]{:S(2)}) collective-permute-start(bf16[4,128,256]{2,1,0:T(8,128)(2,1)S(1)} %get-tuple-element.96), channel_id=1, source_target_pairs={{0,8},{8,0},{16,24},{24,16},{1,9},{9,1},{17,25},{25,17},{2,10},{10... | collective-permute-start | bytes 786440 | tf_op jit(solution)/shard_map/ppermute | solution.py:50
  96.4 3.9 %collective-permute-done.32.rest_0_ = bf16[4,128,256]{2,1,0:T(8,128)(2,1)S(1)} collective-permute-done((bf16[4,128,256]{2,1,0:T(8,128)(2,1)S(1)}, bf16[4,128,256]{2,1,0:T(8,128)(2,1)S(1)}, u32[]{:S(2)}, u32[]{:S(2)}) %collective-permute-start.32) | collective-permute-done | bytes 262176 | tf_op jit(solution)/shard_map/ppermute | solution.py:50
  100.3 2.8 %collective-permute-done.33.rest_1_ = bf16[4,128,256]{2,1,0:T(8,128)(2,1)S(1)} collective-permute-done((bf16[4,128,256]{2,1,0:T(8,128)(2,1)S(1)}, bf16[4,128,256]{2,1,0:T(8,128)(2,1)S(1)}, u32[]{:S(2)}, u32[]{:S(2)}) %collective-permute-start.33) | collective-permute-done | bytes 262176 | tf_op jit(solution)/shard_map/ppermute | solution.py:50
  103.1 5.5 %collective-permute-done.34.rest_2_ = bf16[4,128,256]{2,1,0:T(8,128)(2,1)S(1)} collective-permute-done((bf16[4,128,256]{2,1,0:T(8,128)(2,1)S(1)}, bf16[4,128,256]{2,1,0:T(8,128)(2,1)S(1)}, u32[]{:S(2)}, u32[]{:S(2)}) %collective-permute-start.34) | collective-permute-done | bytes 262176 | tf_op jit(solution)/shard_map/ppermute | solution.py:50
  108.6 1.9 %shard_map.100 = f32[12,128,256]{2,1,0:T(8,128)} custom-call(s32[12]{0:T(128)S(1)} %bitcast.32, f32[12,128,256]{2,1,0:T(8,128)S(1)} %get-tuple-element.80.mult, bf16[12,128,256]{2,1,0:T(8,128)(2,1)S(1)} %get-tuple-element.92.dual, bf16[4,128,256]{2,1,0:T(8,128)(2,1)S(1)} %collective-permute-done.32.rest_0_, ...), custom_call_target="tpu_custom_call" | custom-call | tf_op jit(solution)/shard_map/pallas_call | solution.py:463
  (70 shorter events, 19.8 us)
Async XLA Ops:
  4.4 14.2 %collective-permute-start.4 = (bf16[4,128,256]{2,1,0:T(8,128)(2,1)S(1)}, bf16[4,128,256]{2,1,0:T(8,128)(2,1)S(1)}, u32[]{:S(2)}, u32[]{:S(2)}) collective-permute-start(bf16[4,128,256]{2,1,0:T(8,128)(2,1)S(1)} %get-tuple-element.56), channel_id=1, source_target_pairs={{0,8},{8,0},{16,24},{24,16},{1,9},{9,1},{17,25},{25,17},{2,10},{10... | collective-permute-start | bytes 786440 | tf_op jit(solution)/shard_map/ppermute | solution.py:50
  7.4 5.6 %collective-permute-start.2 = (f32[24,128]{1,0:T(8,128)S(1)}, f32[24,128]{1,0:T(8,128)S(1)}, u32[]{:S(2)}, u32[]{:S(2)}) collective-permute-start(f32[24,128]{1,0:T(8,128)S(1)} %get-tuple-element.55), channel_id=1, source_target_pairs={{0,6},{1,7},{2,4},{3,5},{4,2},{5,3},{6,0},{7,1},{8,14},{9,15},{10,... | collective-permute-start | bytes 36872 | tf_op jit(solution)/shard_map/ppermute | solution.py:55
  11.0 6.2 %collective-permute-start.1 = (f32[24,128]{1,0:T(8,128)S(1)}, f32[24,128]{1,0:T(8,128)S(1)}, u32[]{:S(2)}, u32[]{:S(2)}) collective-permute-start(f32[24,128]{1,0:T(8,128)S(1)} %get-tuple-element.55), channel_id=1, source_target_pairs={{0,4},{1,5},{2,6},{3,7},{4,0},{5,1},{6,2},{7,3},{8,12},{9,13},{10,... | collective-permute-start | bytes 36872 | tf_op jit(solution)/shard_map/ppermute | solution.py:55
  11.0 6.2 %collective-permute-start = (f32[24,128]{1,0:T(8,128)S(1)}, f32[24,128]{1,0:T(8,128)S(1)}, u32[]{:S(2)}, u32[]{:S(2)}) collective-permute-start(f32[24,128]{1,0:T(8,128)S(1)} %get-tuple-element.55), channel_id=1, source_target_pairs={{0,2},{1,3},{2,0},{3,1},{4,6},{5,7},{6,4},{7,5},{8,10},{9,11},{10,... | collective-permute-start | bytes 36872 | tf_op jit(solution)/shard_map/ppermute | solution.py:55
  11.8 19.4 %collective-permute-start.10 = (bf16[4,128,256]{2,1,0:T(8,128)(2,1)S(1)}, bf16[4,128,256]{2,1,0:T(8,128)(2,1)S(1)}, u32[]{:S(2)}, u32[]{:S(2)}) collective-permute-start(bf16[4,128,256]{2,1,0:T(8,128)(2,1)S(1)} %get-tuple-element.68), channel_id=1, source_target_pairs={{0,2},{1,3},{2,4},{3,5},{4,6},{5,7},{6,0},{7,1},{8,10},{9,11},{10,... | collective-permute-start | bytes 786440 | tf_op jit(solution)/shard_map/ppermute | solution.py:50
  21.2 7.5 %collective-permute-start.8 = (bf16[48,256]{1,0:T(8,128)(2,1)S(1)}, bf16[48,256]{1,0:T(8,128)(2,1)S(1)}, u32[]{:S(2)}, u32[]{:S(2)}) collective-permute-start(bf16[48,256]{1,0:T(8,128)(2,1)S(1)} %get-tuple-element.64), channel_id=1, source_target_pairs={{0,6},{1,7},{2,4},{3,5},{4,2},{5,3},{6,0},{7,1},{8,14},{9,15},{10,... | collective-permute-start | bytes 73736 | tf_op jit(solution)/shard_map/ppermute | solution.py:55
  25.0 10.5 %collective-permute-start.11 = (bf16[4,128,256]{2,1,0:T(8,128)(2,1)S(1)}, bf16[4,128,256]{2,1,0:T(8,128)(2,1)S(1)}, u32[]{:S(2)}, u32[]{:S(2)}) collective-permute-start(bf16[4,128,256]{2,1,0:T(8,128)(2,1)S(1)} %get-tuple-element.69), channel_id=1, source_target_pairs={{0,7},{1,2},{2,1},{3,4},{4,3},{5,6},{6,5},{7,0},{8,15},{9,10},{10,... | collective-permute-start | bytes 786440 | tf_op jit(solution)/shard_map/ppermute | solution.py:50
  25.0 13.4 %collective-permute-start.12 = (bf16[4,128,256]{2,1,0:T(8,128)(2,1)S(1)}, bf16[4,128,256]{2,1,0:T(8,128)(2,1)S(1)}, u32[]{:S(2)}, u32[]{:S(2)}) collective-permute-start(bf16[4,128,256]{2,1,0:T(8,128)(2,1)S(1)} %get-tuple-element.70), channel_id=1, source_target_pairs={{0,6},{1,7},{2,0},{3,1},{4,2},{5,3},{6,4},{7,5},{8,14},{9,15},{10,... | collective-permute-start | bytes 786440 | tf_op jit(solution)/shard_map/ppermute | solution.py:50
  25.4 13.0 %collective-permute-start.13 = (bf16[4,128,256]{2,1,0:T(8,128)(2,1)S(1)}, bf16[4,128,256]{2,1,0:T(8,128)(2,1)S(1)}, u32[]{:S(2)}, u32[]{:S(2)}) collective-permute-start(bf16[4,128,256]{2,1,0:T(8,128)(2,1)S(1)} %get-tuple-element.71), channel_id=1, source_target_pairs={{0,1},{1,0},{2,3},{3,2},{4,5},{5,4},{6,7},{7,6},{8,9},{9,8},{10,11... | collective-permute-start | bytes 786440 | tf_op jit(solution)/shard_map/ppermute | solution.py:50
  29.7 9.4 %collective-permute-start.14 = (bf16[4,128,256]{2,1,0:T(8,128)(2,1)S(1)}, bf16[4,128,256]{2,1,0:T(8,128)(2,1)S(1)}, u32[]{:S(2)}, u32[]{:S(2)}) collective-permute-start(bf16[4,128,256]{2,1,0:T(8,128)(2,1)S(1)} %get-tuple-element.72), channel_id=1, source_target_pairs={{0,24},{8,16},{16,8},{24,0},{1,25},{9,17},{17,9},{25,1},{2,26},{10... | collective-permute-start | bytes 786440 | tf_op jit(solution)/shard_map/ppermute | solution.py:50
  31.2 7.8 %collective-permute-start.9 = (f32[4,384]{1,0:T(4,128)S(1)}, f32[4,384]{1,0:T(4,128)S(1)}, u32[]{:S(2)}, u32[]{:S(2)}) collective-permute-start(f32[4,384]{1,0:T(4,128)S(1)} %get-tuple-element.67), channel_id=1, source_target_pairs={{0,8},{8,0},{16,24},{24,16},{1,9},{9,1},{17,25},{25,17},{2,10},{10... | collective-permute-start | bytes 18440 | tf_op jit(solution)/shard_map/ppermute | solution.py:50
  41.5 11.2 %collective-permute-start.15 = (bf16[4,128,256]{2,1,0:T(8,128)(2,1)S(1)}, bf16[4,128,256]{2,1,0:T(8,128)(2,1)S(1)}, u32[]{:S(2)}, u32[]{:S(2)}) collective-permute-start(bf16[4,128,256]{2,1,0:T(8,128)(2,1)S(1)} %get-tuple-element.74), channel_id=1, source_target_pairs={{0,2},{1,3},{2,4},{3,5},{4,6},{5,7},{6,0},{7,1},{8,10},{9,11},{10,... | collective-permute-start | bytes 786440 | tf_op jit(solution)/shard_map/ppermute | solution.py:50
  41.6 13.0 %collective-permute-start.16 = (bf16[4,128,256]{2,1,0:T(8,128)(2,1)S(1)}, bf16[4,128,256]{2,1,0:T(8,128)(2,1)S(1)}, u32[]{:S(2)}, u32[]{:S(2)}) collective-permute-start(bf16[4,128,256]{2,1,0:T(8,128)(2,1)S(1)} %get-tuple-element.75), channel_id=1, source_target_pairs={{0,7},{1,2},{2,1},{3,4},{4,3},{5,6},{6,5},{7,0},{8,15},{9,10},{10,... | collective-permute-start | bytes 786440 | tf_op jit(solution)/shard_map/ppermute | solution.py:50
  43.9 17.0 %collective-permute-start.17 = (bf16[4,128,256]{2,1,0:T(8,128)(2,1)S(1)}, bf16[4,128,256]{2,1,0:T(8,128)(2,1)S(1)}, u32[]{:S(2)}, u32[]{:S(2)}) collective-permute-start(bf16[4,128,256]{2,1,0:T(8,128)(2,1)S(1)} %get-tuple-element.76), channel_id=1, source_target_pairs={{0,6},{1,7},{2,0},{3,1},{4,2},{5,3},{6,4},{7,5},{8,14},{9,15},{10,... | collective-permute-start | bytes 786440 | tf_op jit(solution)/shard_map/ppermute | solution.py:50
  45.4 15.4 %collective-permute-start.18 = (bf16[4,128,256]{2,1,0:T(8,128)(2,1)S(1)}, bf16[4,128,256]{2,1,0:T(8,128)(2,1)S(1)}, u32[]{:S(2)}, u32[]{:S(2)}) collective-permute-start(bf16[4,128,256]{2,1,0:T(8,128)(2,1)S(1)} %get-tuple-element.77), channel_id=1, source_target_pairs={{0,8},{8,0},{16,24},{24,16},{1,9},{9,1},{17,25},{25,17},{2,10},{10... | collective-permute-start | bytes 786440 | tf_op jit(solution)/shard_map/ppermute | solution.py:50
  45.9 14.9 %collective-permute-start.19 = (bf16[4,128,256]{2,1,0:T(8,128)(2,1)S(1)}, bf16[4,128,256]{2,1,0:T(8,128)(2,1)S(1)}, u32[]{:S(2)}, u32[]{:S(2)}) collective-permute-start(bf16[4,128,256]{2,1,0:T(8,128)(2,1)S(1)} %get-tuple-element.78), channel_id=1, source_target_pairs={{0,24},{8,16},{16,8},{24,0},{1,25},{9,17},{17,9},{25,1},{2,26},{10... | collective-permute-start | bytes 786440 | tf_op jit(solution)/shard_map/ppermute | solution.py:50
  52.7 8.1 %collective-permute-start.20 = (bf16[4,128,256]{2,1,0:T(8,128)(2,1)S(1)}, bf16[4,128,256]{2,1,0:T(8,128)(2,1)S(1)}, u32[]{:S(2)}, u32[]{:S(2)}) collective-permute-start(bf16[4,128,256]{2,1,0:T(8,128)(2,1)S(1)} %get-tuple-element.79), channel_id=1, source_target_pairs={{0,1},{1,0},{2,3},{3,2},{4,5},{5,4},{6,7},{7,6},{8,9},{9,8},{10,11... | collective-permute-start | bytes 786440 | tf_op jit(solution)/shard_map/ppermute | solution.py:50
  63.1 13.2 %collective-permute-start.21 = (bf16[4,128,256]{2,1,0:T(8,128)(2,1)S(1)}, bf16[4,128,256]{2,1,0:T(8,128)(2,1)S(1)}, u32[]{:S(2)}, u32[]{:S(2)}) collective-permute-start(bf16[4,128,256]{2,1,0:T(8,128)(2,1)S(1)} %get-tuple-element.82), channel_id=1, source_target_pairs={{0,8},{8,0},{16,24},{24,16},{1,9},{9,1},{17,25},{25,17},{2,10},{10... | collective-permute-start | bytes 786440 | tf_op jit(solution)/shard_map/ppermute | solution.py:50
  63.7 12.6 %collective-permute-start.22 = (bf16[4,128,256]{2,1,0:T(8,128)(2,1)S(1)}, bf16[4,128,256]{2,1,0:T(8,128)(2,1)S(1)}, u32[]{:S(2)}, u32[]{:S(2)}) collective-permute-start(bf16[4,128,256]{2,1,0:T(8,128)(2,1)S(1)} %get-tuple-element.83), channel_id=1, source_target_pairs={{0,2},{1,3},{2,4},{3,5},{4,6},{5,7},{6,0},{7,1},{8,10},{9,11},{10,... | collective-permute-start | bytes 786440 | tf_op jit(solution)/shard_map/ppermute | solution.py:50
  66.6 6.1 %collective-permute-start.26 = (bf16[32,256]{1,0:T(8,128)(2,1)S(1)}, bf16[32,256]{1,0:T(8,128)(2,1)S(1)}, u32[]{:S(2)}, u32[]{:S(2)}) collective-permute-start(bf16[32,256]{1,0:T(8,128)(2,1)S(1)} %pad_maximum_fusion.1.rest_2_), channel_id=1, source_target_pairs={{0,6},{1,7},{2,4},{3,5},{4,2},{5,3},{6,0},{7,1},{8,14},{9,15},{10,... | collective-permute-start | bytes 49160 | tf_op jit(solution)/shard_map/ppermute | solution.py:55
  68.7 6.3 %collective-permute-start.24 = (bf16[32,256]{1,0:T(8,128)(2,1)S(1)}, bf16[32,256]{1,0:T(8,128)(2,1)S(1)}, u32[]{:S(2)}, u32[]{:S(2)}) collective-permute-start(bf16[32,256]{1,0:T(8,128)(2,1)S(1)} %pad_maximum_fusion.1.rest_2_), channel_id=1, source_target_pairs={{0,2},{1,3},{2,0},{3,1},{4,6},{5,7},{6,4},{7,5},{8,10},{9,11},{10,... | collective-permute-start | bytes 49160 | tf_op jit(solution)/shard_map/ppermute | solution.py:55
  72.7 10.5 %collective-permute-start.28 = (bf16[4,128,256]{2,1,0:T(8,128)(2,1)S(1)}, bf16[4,128,256]{2,1,0:T(8,128)(2,1)S(1)}, u32[]{:S(2)}, u32[]{:S(2)}) collective-permute-start(bf16[4,128,256]{2,1,0:T(8,128)(2,1)S(1)} %get-tuple-element.88), channel_id=1, source_target_pairs={{0,7},{1,2},{2,1},{3,4},{4,3},{5,6},{6,5},{7,0},{8,15},{9,10},{10,... | collective-permute-start | bytes 786440 | tf_op jit(solution)/shard_map/ppermute | solution.py:50
  73.4 13.1 %collective-permute-start.29 = (bf16[4,128,256]{2,1,0:T(8,128)(2,1)S(1)}, bf16[4,128,256]{2,1,0:T(8,128)(2,1)S(1)}, u32[]{:S(2)}, u32[]{:S(2)}) collective-permute-start(bf16[4,128,256]{2,1,0:T(8,128)(2,1)S(1)} %get-tuple-element.89), channel_id=1, source_target_pairs={{0,6},{1,7},{2,0},{3,1},{4,2},{5,3},{6,4},{7,5},{8,14},{9,15},{10,... | collective-permute-start | bytes 786440 | tf_op jit(solution)/shard_map/ppermute | solution.py:50
  75.1 11.4 %collective-permute-start.30 = (bf16[4,128,256]{2,1,0:T(8,128)(2,1)S(1)}, bf16[4,128,256]{2,1,0:T(8,128)(2,1)S(1)}, u32[]{:S(2)}, u32[]{:S(2)}) collective-permute-start(bf16[4,128,256]{2,1,0:T(8,128)(2,1)S(1)} %get-tuple-element.90), channel_id=1, source_target_pairs={{0,1},{1,0},{2,3},{3,2},{4,5},{5,4},{6,7},{7,6},{8,9},{9,8},{10,11... | collective-permute-start | bytes 786440 | tf_op jit(solution)/shard_map/ppermute | solution.py:50
  77.4 9.3 %collective-permute-start.31 = (bf16[4,128,256]{2,1,0:T(8,128)(2,1)S(1)}, bf16[4,128,256]{2,1,0:T(8,128)(2,1)S(1)}, u32[]{:S(2)}, u32[]{:S(2)}) collective-permute-start(bf16[4,128,256]{2,1,0:T(8,128)(2,1)S(1)} %get-tuple-element.91), channel_id=1, source_target_pairs={{0,24},{8,16},{16,8},{24,0},{1,25},{9,17},{17,9},{25,1},{2,26},{10... | collective-permute-start | bytes 786440 | tf_op jit(solution)/shard_map/ppermute | solution.py:50
  79.7 6.9 %collective-permute-start.27 = (f32[4,384]{1,0:T(4,128)S(1)}, f32[4,384]{1,0:T(4,128)S(1)}, u32[]{:S(2)}, u32[]{:S(2)}) collective-permute-start(f32[4,384]{1,0:T(4,128)S(1)} %get-tuple-element.87), channel_id=1, source_target_pairs={{0,8},{8,0},{16,24},{24,16},{1,9},{9,1},{17,25},{25,17},{2,10},{10... | collective-permute-start | bytes 18440 | tf_op jit(solution)/shard_map/ppermute | solution.py:50
  89.1 11.3 %collective-permute-start.32 = (bf16[4,128,256]{2,1,0:T(8,128)(2,1)S(1)}, bf16[4,128,256]{2,1,0:T(8,128)(2,1)S(1)}, u32[]{:S(2)}, u32[]{:S(2)}) collective-permute-start(bf16[4,128,256]{2,1,0:T(8,128)(2,1)S(1)} %get-tuple-element.93), channel_id=1, source_target_pairs={{0,2},{1,3},{2,4},{3,5},{4,6},{5,7},{6,0},{7,1},{8,10},{9,11},{10,... | collective-permute-start | bytes 786440 | tf_op jit(solution)/shard_map/ppermute | solution.py:50
  90.1 13.0 %collective-permute-start.33 = (bf16[4,128,256]{2,1,0:T(8,128)(2,1)S(1)}, bf16[4,128,256]{2,1,0:T(8,128)(2,1)S(1)}, u32[]{:S(2)}, u32[]{:S(2)}) collective-permute-start(bf16[4,128,256]{2,1,0:T(8,128)(2,1)S(1)} %get-tuple-element.94), channel_id=1, source_target_pairs={{0,7},{1,2},{2,1},{3,4},{4,3},{5,6},{6,5},{7,0},{8,15},{9,10},{10,... | collective-permute-start | bytes 786440 | tf_op jit(solution)/shard_map/ppermute | solution.py:50
  92.0 16.6 %collective-permute-start.34 = (bf16[4,128,256]{2,1,0:T(8,128)(2,1)S(1)}, bf16[4,128,256]{2,1,0:T(8,128)(2,1)S(1)}, u32[]{:S(2)}, u32[]{:S(2)}) collective-permute-start(bf16[4,128,256]{2,1,0:T(8,128)(2,1)S(1)} %get-tuple-element.95), channel_id=1, source_target_pairs={{0,6},{1,7},{2,0},{3,1},{4,2},{5,3},{6,4},{7,5},{8,14},{9,15},{10,... | collective-permute-start | bytes 786440 | tf_op jit(solution)/shard_map/ppermute | solution.py:50
  93.7 14.9 %collective-permute-start.35 = (bf16[4,128,256]{2,1,0:T(8,128)(2,1)S(1)}, bf16[4,128,256]{2,1,0:T(8,128)(2,1)S(1)}, u32[]{:S(2)}, u32[]{:S(2)}) collective-permute-start(bf16[4,128,256]{2,1,0:T(8,128)(2,1)S(1)} %get-tuple-element.96), channel_id=1, source_target_pairs={{0,8},{8,0},{16,24},{24,16},{1,9},{9,1},{17,25},{25,17},{2,10},{10... | collective-permute-start | bytes 786440 | tf_op jit(solution)/shard_map/ppermute | solution.py:50
  95.2 13.4 %collective-permute-start.36 = (bf16[4,128,256]{2,1,0:T(8,128)(2,1)S(1)}, bf16[4,128,256]{2,1,0:T(8,128)(2,1)S(1)}, u32[]{:S(2)}, u32[]{:S(2)}) collective-permute-start(bf16[4,128,256]{2,1,0:T(8,128)(2,1)S(1)} %get-tuple-element.97), channel_id=1, source_target_pairs={{0,24},{8,16},{16,8},{24,0},{1,25},{9,17},{17,9},{25,1},{2,26},{10... | collective-permute-start | bytes 786440 | tf_op jit(solution)/shard_map/ppermute | solution.py:50
  100.3 8.3 %collective-permute-start.37 = (bf16[4,128,256]{2,1,0:T(8,128)(2,1)S(1)}, bf16[4,128,256]{2,1,0:T(8,128)(2,1)S(1)}, u32[]{:S(2)}, u32[]{:S(2)}) collective-permute-start(bf16[4,128,256]{2,1,0:T(8,128)(2,1)S(1)} %get-tuple-element.98), channel_id=1, source_target_pairs={{0,1},{1,0},{2,3},{3,2},{4,5},{5,4},{6,7},{7,6},{8,9},{9,8},{10,11... | collective-permute-start | bytes 786440 | tf_op jit(solution)/shard_map/ppermute | solution.py:50
  (12 other events, 158.3 us)
